TPU v7x, 32 devices: a whole 2x2x4 slice. The times are simulated.
32 devices in a mesh: groups: 2 (over y), seq: 4 (over z), tp: 4 (over x, core).
Axes of the slice: x: 2, y: 2, z: 4, core: 2. Of those that a mesh axis runs over, the one named last changes fastest.
Arguments:
- hidden: bfloat16 [8, 192, 8192], P(('groups', 'seq')), parts along dimension 0, may hold values from -6 to 6
- queries: bfloat16 [8, 192, 4096], P(('groups', 'seq'), None, 'tp'), parts along dimension 0, may hold values from -6 to 6
- w_key: bfloat16 [8192, 512], P('seq', 'tp'), may hold values from -0.0625 to 0.0625
- w_value: bfloat16 [8192, 512], P('seq', 'tp'), may hold values from -0.0625 to 0.0625
- store_keys: bfloat16 [64, 128, 512], P(('groups', 'seq'), None, 'tp'), parts along dimension 0, may hold values from -160 to 160
- store_values: bfloat16 [64, 128, 512], P(('groups', 'seq'), None, 'tp'), parts along dimension 0, may hold values from -6 to 6
- request_docs: int32 [8, 16], P('groups'), parts along dimension 0, may hold values from 0 to 31, as said below
- doc_lengths: int32 [64], P('groups'), parts along dimension 0, may hold values from 48 to 128, as said below
- recompute_rows: int32 [8, 16, 12], P(('groups', 'seq')), parts along dimension 0, may hold values from 0 to 127, as said below
Outputs:
- mixed: bfloat16 [8, 192, 4096], P(('groups', 'seq'), None, 'tp'), parts along dimension 0
- returned: bfloat16 [8, 4, 4, 12, 2, 512], P(('groups', 'seq'), None, None, None, None, 'tp'), parts along dimension 0
There are 2 independent parts, one for each index of `groups`. A program takes and returns all parts, laid end to end along the dimension named above; an argument that names none is the same for every part. Nothing has to cross between parts.
Inputs may be any that keep to these rules, and one draw needn't show every extreme that they name: `request_docs`: the 16 documents of a request are distinct; no owner holds more than 4 of them, and some owner holds exactly 4 in every request. `doc_lengths`: some document has exactly 128 tokens. `recompute_rows`: the 12 positions of one document in one request are distinct and below that document's length.
All inputs are finite; a program needn't handle non-finite values.
Results may differ from a plain program's by a relative error of at most 0.0052.
Values may be sent and summed in bfloat16 or wider, within the bound.
No kernel may reach another device: no remote copies, remote signals or barrier semaphores. Data moves between devices by JAX's collectives and lax.ppermute only.
A program may use at most 64 MiB of HBM per device.

v0:
```python
import math

import jax
import jax.numpy as jnp
from jax import lax
from jax.sharding import PartitionSpec as P


def owner_ranks(owners):
    count = owners.shape[1]
    same_owner = owners[:, :, None] == owners[:, None, :]
    earlier = jnp.arange(count)[None, :] < jnp.arange(count)[:, None]
    return jnp.sum((same_owner & earlier[None]).astype(jnp.int32), axis=2)


def shards(
    hidden,
    queries,
    w_key,
    w_value,
    store_keys,
    store_values,
    request_docs,
    doc_lengths,
    recompute_rows,
):
    my_index = lax.axis_index("seq")
    seq_count = lax.axis_size("seq")
    slot_count = store_keys.shape[0]
    capacity = slot_count // 2
    doc_count = request_docs.shape[1]
    doc_len = store_keys.shape[1]
    head_dim = store_keys.shape[2]
    row_states = hidden[0]
    row_count = row_states.shape[0]
    row_ids = recompute_rows[0]
    per_doc = row_ids.shape[1]
    owners = request_docs // slot_count
    ranks = owner_ranks(owners)
    my_docs = lax.dynamic_index_in_dim(request_docs, my_index, 0, keepdims=False)
    my_owners = my_docs // slot_count
    my_ranks = lax.dynamic_index_in_dim(ranks, my_index, 0, keepdims=False)

    def add_rows(weight_block):
        return jnp.dot(row_states, weight_block, preferred_element_type=jnp.float32)

    weight_blocks = (
        lax.all_gather(w_key, "seq", axis=0, tiled=True),
        lax.all_gather(w_value, "seq", axis=0, tiled=True),
    )
    fresh_k, fresh_v = tuple((add_rows(block) for block in weight_blocks))
    fresh_k = fresh_k.astype(jnp.bfloat16)
    fresh_v = fresh_v.astype(jnp.bfloat16)
    all_k, all_v = (
        lax.all_gather(store_keys, "seq", axis=0, tiled=True),
        lax.all_gather(store_values, "seq", axis=0, tiled=True),
    )
    doc_k = all_k[my_docs]
    doc_v = all_v[my_docs]
    doc_column = jnp.arange(doc_count, dtype=jnp.int32)[:, None]
    doc_k = doc_k.at[doc_column, row_ids].set(fresh_k.reshape(doc_count, per_doc, head_dim))
    doc_v = doc_v.at[doc_column, row_ids].set(fresh_v.reshape(doc_count, per_doc, head_dim))
    positions = jnp.arange(doc_len, dtype=jnp.int32)
    in_length = positions[None, :] < doc_lengths[my_docs][:, None]
    key_place = (doc_column * doc_len + positions[None, :]).reshape(doc_count * doc_len)
    query_place = (doc_column * doc_len + row_ids).reshape(row_count)
    allowed = in_length.reshape(doc_count * doc_len)[None, :] & (
        key_place[None, :] <= query_place[:, None]
    )
    row_queries = queries[0]
    group_size = row_queries.shape[1] // head_dim
    q_heads = row_queries.reshape(row_count, group_size, head_dim).transpose(1, 0, 2)
    context_k = doc_k.reshape(doc_count * doc_len, head_dim)
    context_v = doc_v.reshape(doc_count * doc_len, head_dim)
    score_scale = 1.0 / math.sqrt(head_dim)

    def one_head(q_one):
        scores = (
            jnp.einsum("qd,kd->qk", q_one, context_k, preferred_element_type=jnp.float32)
            * score_scale
        )
        scores = jnp.where(allowed, scores, -jnp.inf)
        row_max = jnp.max(scores, axis=-1, keepdims=True)
        powers = jnp.exp(scores - row_max)
        row_sum = jnp.sum(powers, axis=-1, keepdims=True)
        probs = (powers / row_sum).astype(jnp.bfloat16)
        return jnp.dot(probs, context_v, preferred_element_type=jnp.float32).astype(jnp.bfloat16)

    outputs = lax.map(one_head, q_heads)
    mixed = outputs.transpose(1, 0, 2).reshape(row_count, group_size * head_dim)
    fresh_kv = jnp.stack([fresh_k, fresh_v], axis=1).reshape(doc_count, per_doc, 2, head_dim)
    chosen = (my_owners[None, None, :] == jnp.arange(seq_count)[:, None, None]) & (
        my_ranks[None, None, :] == jnp.arange(capacity)[None, :, None]
    )
    doc_pick = jnp.sum(jnp.where(chosen, jnp.arange(doc_count)[None, None, :], 0), axis=2)
    present_back = jnp.any(chosen, axis=2)[:, :, None, None, None]
    outgoing = jnp.where(present_back, fresh_kv[doc_pick], jnp.zeros((), jnp.bfloat16))
    returned = lax.all_to_all(outgoing, "seq", split_axis=0, concat_axis=0, tiled=True)
    return (mixed[None], returned[None])


def solution(mesh):
    return jax.shard_map(
        shards,
        mesh=mesh,
        in_specs=(
            P(("groups", "seq"), None, None),
            P(("groups", "seq"), None, "tp"),
            P("seq", "tp"),
            P("seq", "tp"),
            P(("groups", "seq"), None, "tp"),
            P(("groups", "seq"), None, "tp"),
            P("groups", None),
            P("groups"),
            P(("groups", "seq"), None, None),
        ),
        out_specs=(
            P(("groups", "seq"), None, "tp"),
            P(("groups", "seq"), None, None, None, None, "tp"),
        ),
        check_vma=False,
    )
```

profile of v0, /device:TPU:0, one launch (start us, length us, event | category | flops | bytes accessed | tf_op | source)
XLA Modules:
  0.0 246.7 jit_solution(9826383513066390597)
XLA Ops:
  12.5 1.3 or_select_fusion
  13.8 1.4 copy.23
  17.2 1.4 add.88
  23.8 16.5 %all-gather.5.cloned.1.call-done = bf16[32,128,128]{2,1,0:T(8,128)(2,1)} async-done(((bf16[8,128,128]{2,1,0:T(8,128)(2,1)}), bf16[32,128,128]{2,1,0:T(8,128)(2,1)}) %all-gather.5.cloned.1.call-update) | async-done | bytes 1048592 | tf_op jit(solution)/shard_map/all_gather | solution.py:55
  40.3 2.6 %gather_fusion = bf16[16,128,128]{2,1,0:T(8,128)(2,1)} fusion(bf16[32,128,128]{2,1,0:T(8,128)(2,1)} %all-gather.5.cloned.1.call-done, s32[1024]{0:T(1024)S(1)} %pad_clamp_fusion.1), kind=kCustom, calls=%fused_computation | custom fusion | bytes 1048640 | tf_op jit(solution)/shard_map/gather | solution.py:58
  42.9 26.4 %all-gather.9.cloned.1.call-done = bf16[32,128,128]{2,1,0:T(8,128)(2,1)} async-done(((bf16[8,128,128]{2,1,0:T(8,128)(2,1)}), bf16[32,128,128]{2,1,0:T(8,128)(2,1)}) %all-gather.9.cloned.1.call-update) | async-done | bytes 1048592 | tf_op jit(solution)/shard_map/all_gather | solution.py:56
  69.3 2.7 %gather_fusion.2 = bf16[16,128,128]{2,1,0:T(8,128)(2,1)} fusion(bf16[32,128,128]{2,1,0:T(8,128)(2,1)} %all-gather.9.cloned.1.call-done, s32[1024]{0:T(1024)S(1)} %pad_clamp_fusion.1), kind=kCustom, calls=%fused_computation.2 | custom fusion | bytes 1048640 | tf_op jit(solution)/shard_map/gather | solution.py:59
  72.0 44.4 %all-gather.11.cloned.1.call-done = bf16[8192,128]{1,0:T(8,128)(2,1)} async-done(((bf16[2048,128]{1,0:T(8,128)(2,1)}), bf16[8192,128]{1,0:T(8,128)(2,1)}) %all-gather.11.cloned.1.call-update) | async-done | bytes 2097168 | tf_op jit(solution)/shard_map/all_gather | solution.py:49
  116.4 2.6 %fusion.16 = bf16[192,128]{1,0:T(8,128)(2,1)S(1)} fusion(bf16[8192,128]{1,0:T(8,128)(2,1)} %all-gather.11.cloned.1.call-done, bf16[1,192,8192]{2,1,0:T(8,128)(2,1)S(1)} %copy-done), kind=kOutput, calls=%fused_computation.23 | convolution fusion | flops 402677760 | bytes 5292032 | tf_op jit(solution)/shard_map/dot_general | solution.py:45
  119.0 43.5 %all-gather.7.cloned.1.call-done = bf16[8192,128]{1,0:T(8,128)(2,1)} async-done(((bf16[2048,128]{1,0:T(8,128)(2,1)}), bf16[8192,128]{1,0:T(8,128)(2,1)}) %all-gather.7.cloned.1.call-update) | async-done | bytes 2097168 | tf_op jit(solution)/shard_map/all_gather | solution.py:48
  162.5 2.6 %fusion.13 = bf16[192,128]{1,0:T(8,128)(2,1)S(1)} fusion(bf16[8192,128]{1,0:T(8,128)(2,1)} %all-gather.7.cloned.1.call-done, bf16[1,192,8192]{2,1,0:T(8,128)(2,1)S(1)} %copy-done), kind=kOutput, calls=%fused_computation.22 | convolution fusion | flops 402677760 | bytes 5292032 | tf_op jit(solution)/shard_map/dot_general | solution.py:45
  166.5 3.9 %all-to-all-start = ((bf16[4,4,12,2,128]{4,3,2,1,0:T(2,128)(2,1)}), bf16[4,4,12,2,128]{4,3,2,1,0:T(2,128)(2,1)}, u32[]{:S(2)}, u32[]{:S(2)}) async-start(bf16[4,4,12,2,128]{4,3,2,1,0:T(2,128)(2,1)} %broadcast_select_fusion), calls=%async_computation | async-start | bytes 196608 | tf_op jit(solution)/shard_map/all_to_all | solution.py:98
  170.4 20.1 %scatter_fusion = bf16[16,128,128]{2,1,0:T(8,128)(2,1)} fusion(bf16[16,128,128]{2,1,0:T(8,128)(2,1)} %gather_fusion, s32[192]{0:T(256)S(1)} %reshape.268, bf16[192,128]{1,0:T(8,128)(2,1)S(1)} %fusion.13), kind=kCustom, calls=%fused_computation.4 | custom fusion | bytes 148992 | tf_op jit(solution)/shard_map/scatter | solution.py:61
  190.5 20.2 %scatter_fusion.1 = bf16[16,128,128]{2,1,0:T(8,128)(2,1)} fusion(bf16[16,128,128]{2,1,0:T(8,128)(2,1)} %gather_fusion.2, s32[192]{0:T(256)S(1)} %reshape.268, bf16[192,128]{1,0:T(8,128)(2,1)S(1)} %fusion.16), kind=kCustom, calls=%fused_computation.5 | custom fusion | bytes 148992 | tf_op jit(solution)/shard_map/scatter | solution.py:62
  210.7 25.7 %while.11 = (s32[]{:T(128)}, bf16[8,192,128]{2,1,0:T(8,128)(2,1)}, bf16[8,192,128]{2,1,0:T(8,128)(2,1)}, bf16[2048,128]{1,0:T(8,128)(2,1)}, bf16[2048,128]{1,0:T...) while((s32[]{:T(128)}, bf16[8,192,128]{2,1,0:T(8,128)(2,1)}, ...), condition=%wide.region_5.6_spmd.clone, body=%wide.region_2.5_spmd.clone.sunk | while | flops 205282944 | bytes 7978617 | solution.py:89
  210.7 1.7 fusion.38
  213.9 1.7 fusion.38
  217.1 1.7 fusion.38
  220.4 1.7 fusion.38
  223.6 1.7 fusion.38
  226.8 1.7 fusion.38
  230.0 1.7 fusion.38
  233.2 1.7 fusion.38
  238.6 1.6 copy.42
  (91 shorter events, 27.7 us)
Async XLA Ops:
  7.2 109.2 %copy-start = (bf16[1,192,8192]{2,1,0:T(8,128)(2,1)S(1)}, bf16[1,192,8192]{2,1,0:T(8,128)(2,1)}, u32[]{:S(2)}) copy-start(bf16[1,192,8192]{2,1,0:T(8,128)(2,1)} %param.11) | copy-start | bytes 9437188
  7.2 2.8 %copy-start.7 = (s32[4,16]{1,0:T(4,128)S(1)}, s32[4,16]{1,0:T(4,128)}, u32[]{:S(2)}) copy-start(s32[4,16]{1,0:T(4,128)} %param.17) | copy-start | bytes 772
  7.2 12.0 %copy-start.3 = (bf16[1,192,1024]{2,1,0:T(8,128)(2,1)S(1)}, bf16[1,192,1024]{2,1,0:T(8,128)(2,1)}, u32[]{:S(2)}) copy-start(bf16[1,192,1024]{2,1,0:T(8,128)(2,1)} %param.12) | copy-start | bytes 1179652
  7.2 33.1 %all-gather.5.cloned.1.call-start = ((), (), s32[]{:S(2)}) async-start(), calls=%async_computation.1 | async-start | bytes 1310720 | tf_op jit(solution)/shard_map/all_gather | solution.py:55
  7.9 12.9 %copy-start.1 = (s32[32]{0:T(128)S(1)}, s32[32]{0:T(128)}, u32[]{:S(2)}) copy-start(s32[32]{0:T(128)} %param.18) | copy-start | bytes 388
  7.9 61.4 %all-gather.9.cloned.1.call-start = ((), (), s32[]{:S(2)}) async-start(), calls=%async_computation.3 | async-start | bytes 1310720 | tf_op jit(solution)/shard_map/all_gather | solution.py:56
  8.7 107.7 %all-gather.11.cloned.1.call-start = ((), (), s32[]{:S(2)}) async-start(), calls=%async_computation.4 | async-start | bytes 2621440 | tf_op jit(solution)/shard_map/all_gather | solution.py:49
  9.4 153.0 %all-gather.7.cloned.1.call-start = ((), (), s32[]{:S(2)}) async-start(), calls=%async_computation.2 | async-start | bytes 2621440 | tf_op jit(solution)/shard_map/all_gather | solution.py:48
  10.3 0.5 copy-start.8
  10.3 0.7 copy-start.9
  15.9 0.6 copy-start.6
  19.2 2.3 copy-start.4
  19.2 2.3 copy-start.5
  166.5 72.1 %all-to-all-start = ((bf16[4,4,12,2,128]{4,3,2,1,0:T(2,128)(2,1)}), bf16[4,4,12,2,128]{4,3,2,1,0:T(2,128)(2,1)}, u32[]{:S(2)}, u32[]{:S(2)}) async-start(bf16[4,4,12,2,128]{4,3,2,1,0:T(2,128)(2,1)} %broadcast_select_fusion), calls=%async_computation | async-start | bytes 196608 | tf_op jit(solution)/shard_map/all_to_all | solution.py:98
  210.7 2.1 copy-start.2
  213.9 2.1 copy-start.2
  217.1 2.1 copy-start.2
  220.4 2.1 copy-start.2
  223.6 2.1 copy-start.2
  226.8 2.1 copy-start.2
  230.0 2.1 copy-start.2
  233.2 2.1 copy-start.2
Sparse Core Ops, SparseCore 0:
  9.6 30.6 all-gather.4
  41.8 27.4 all-gather.8
  70.9 45.4 all-gather.10
  117.8 44.6 all-gather.6
where the time goes:
time: 248 us; the launch traced here: 247 us
  waiting for transfers between devices  133 us (54%)
  local copies, waits for them, and re-layouts  59 us (24%)
  matrix products  27.7 us (11%)
  between operations  14 us (6%)
  other arithmetic  8.46 us (3%)
  starting transfers between devices  4.08 us (2%)
    all_gather x1, waiting for transfers between devices, shards(): lax.all_gather(w_value, 'seq', axis=0, tiled=True)  44.4 us
    all_gather x1, waiting for transfers between devices, shards(): lax.all_gather(w_key, 'seq', axis=0, tiled=True)  43.5 us
    all_gather x1, waiting for transfers between devices, shards(): lax.all_gather(store_values, 'seq', axis=0, tiled=True)  26.4 us
    scatter x1, local copies, waits for them, and re-layouts, shards(): doc_v.at[doc_column, row_ids]  20.2 us
    scatter x1, local copies, waits for them, and re-layouts, shards(): doc_k.at[doc_column, row_ids]  20.1 us
    all_gather x1, waiting for transfers between devices, shards(): lax.all_gather(store_keys, 'seq', axis=0, tiled=True)  16.5 us
    dot_general x8, matrix products, one_head(): jnp.einsum('qd,kd->qk', q_one, context_k, preferred_element_type=jnp.floa...  13.8 us
    dot_general x8, matrix products, one_head(): jnp.dot(probs, context_v, preferred_element_type=jnp.float32)  8.83 us
  transfers between devices with their start and end apart: 5, of which 4 were waited for; matrix products, arithmetic and copies ran while one was open for 36% of the time, Pallas kernels for 0%

commit v1 on v0

v1 whole, which is shorter than its diff:
```python
import functools
import math

import jax
import jax.numpy as jnp
from jax import lax
from jax.experimental import pallas as pl
from jax.experimental.pallas import tpu as pltpu
from jax.sharding import PartitionSpec as P

ANY = pl.BlockSpec(memory_space=pl.ANY)
SMEM = pl.BlockSpec(memory_space=pltpu.SMEM)
VMEM = pl.BlockSpec(memory_space=pltpu.VMEM)
MASKED = -1e30


def cut_kernel(hidden, w_key, w_value, w_out, h_out, sems):
    group = lax.axis_index("groups")
    me = lax.axis_index("seq")
    core = lax.rem(lax.axis_index("tp"), 2)
    depth = w_key.shape[0]
    half = w_out.shape[1]
    rows = h_out.shape[1]
    copies = []
    for i, weight in enumerate((w_key, w_value)):
        source = weight.at[pl.ds(pl.multiple_of(group * half, half), half)]
        copies.append(pltpu.make_async_copy(source, w_out.at[i], sems.at[i]))
    first = me + 1 - 2 * lax.rem(me, 2)
    second = lax.rem(first + 2, 4)
    for i, block in enumerate((first, second)):
        source = hidden.at[
            0,
            pl.ds(pl.multiple_of(core * rows, rows), rows),
            pl.ds(pl.multiple_of(block * depth, depth), depth),
        ]
        copies.append(pltpu.make_async_copy(source, h_out.at[i], sems.at[2 + i]))
    for copy in copies:
        copy.start()
    for copy in copies:
        copy.wait()


def cut(hidden, w_key, w_value):
    depth = w_key.shape[0]
    return pl.pallas_call(
        cut_kernel,
        out_shape=(
            jax.ShapeDtypeStruct((2, depth // 2, w_key.shape[1]), jnp.bfloat16),
            jax.ShapeDtypeStruct((2, hidden.shape[1] // 2, depth), jnp.bfloat16),
        ),
        in_specs=[ANY] * 3,
        out_specs=(ANY, ANY),
        scratch_shapes=[pltpu.SemaphoreType.DMA((4,))],
        name="cut",
    )(hidden, w_key, w_value)


def docs_kernel(by_owner, request_docs, store_keys, store_values, *rest):
    outs, (picks, sems) = rest[:-2], rest[-2:]
    me = lax.axis_index("seq")
    requests, doc_count = request_docs.shape
    slots = store_keys.shape[0]
    capacity = slots // 2

    def one_request(r, carry):
        for c in range(capacity):
            picks[r, c] = 0

        def one_doc(j, count):
            doc = request_docs[r, j]
            mine = lax.div(doc, slots) == me

            @pl.when(mine)
            def _():
                picks[r, jnp.minimum(count, capacity - 1)] = lax.rem(doc, slots)

            return count + mine.astype(jnp.int32)

        lax.fori_loop(0, doc_count, one_doc, jnp.int32(0), unroll=True)
        return carry

    lax.fori_loop(0, requests, one_request, 0)

    def send(r, out, sem):
        for c in range(capacity):
            slot = picks[r, c]
            pltpu.make_async_copy(store_keys.at[slot], out.at[c, 0], sem).start()
            pltpu.make_async_copy(store_values.at[slot], out.at[c, 1], sem).start()

    if by_owner:
        out = outs[0]

        def one_send(r, carry):
            send(r, out.at[r], sems.at[0])
            return carry

        lax.fori_loop(0, requests, one_send, 0)
    else:
        for i, out in enumerate(outs):
            send(lax.bitwise_xor(me, i + 1), out, sems.at[i])
    for i, out in enumerate(outs):
        pltpu.make_async_copy(out, out, sems.at[i]).wait()


def cut_docs(request_docs, store_keys, store_values, by_owner):
    requests = request_docs.shape[0]
    capacity = store_keys.shape[0] // 2
    one = (capacity, 2) + store_keys.shape[1:]
    if by_owner:
        shapes = (jax.ShapeDtypeStruct((requests,) + one, jnp.bfloat16),)
    else:
        shapes = (jax.ShapeDtypeStruct(one, jnp.bfloat16),) * (requests - 1)
    return pl.pallas_call(
        functools.partial(docs_kernel, by_owner),
        out_shape=shapes,
        in_specs=[SMEM, ANY, ANY],
        out_specs=(ANY,) * len(shapes),
        scratch_shapes=[
            pltpu.SMEM((requests, capacity), jnp.int32),
            pltpu.SemaphoreType.DMA((len(shapes),)),
        ],
        name="cut_docs",
    )(request_docs, store_keys, store_values)


def project_kernel(hidden, w_key, w_value, w_mine, w_other, h_mine, h_other, own, part, w, h, sems):
    group = lax.axis_index("groups")
    me = lax.axis_index("seq")
    core = lax.rem(lax.axis_index("tp"), 2)
    depth, width = w_key.shape
    half = depth // 2
    rows = hidden.shape[1]
    far = lax.rem(me + 2, 4)
    copies = []

    def copy(source, target):
        copies.append(pltpu.make_async_copy(source, target, sems.at[len(copies)]))

    for i, weight in enumerate((w_key, w_value)):
        columns = pl.ds(i * width, width)
        copy(weight, w.at[pl.ds(0, depth), columns])
        for held, place in ((w_mine, group), (w_other, 1 - group)):
            copy(held.at[i], w.at[pl.ds(pl.multiple_of(depth + place * half, half), half), columns])
    for i, block in enumerate((me, far)):
        columns = pl.ds(i * depth, depth)
        copy(
            hidden.at[0, :, pl.ds(pl.multiple_of(block * depth, depth), depth)],
            h.at[pl.ds(0, rows), columns],
        )
        for held, place in ((h_mine, core), (h_other, 1 - core)):
            start = rows + place * (rows // 2)
            copy(held.at[i], h.at[pl.ds(pl.multiple_of(start, rows // 2), rows // 2), columns])
    for one in copies:
        one.start()
    for one in copies:
        one.wait()
    total = jnp.dot(h[...], w[...], preferred_element_type=jnp.float32)
    own[...] = total[:rows]
    part[...] = total[rows:].astype(part.dtype)


def project(hidden, w_key, w_value, w_mine, w_other, h_mine, h_other):
    depth, width = w_key.shape
    rows = hidden.shape[1]
    return pl.pallas_call(
        project_kernel,
        out_shape=(
            jax.ShapeDtypeStruct((rows, 2 * width), jnp.float32),
            jax.ShapeDtypeStruct((rows, 2 * width), jnp.bfloat16),
        ),
        in_specs=[ANY] * 7,
        out_specs=(VMEM, VMEM),
        scratch_shapes=[
            pltpu.VMEM((2 * depth, 2 * width), jnp.bfloat16),
            pltpu.VMEM((2 * rows, 2 * depth), jnp.bfloat16),
            pltpu.SemaphoreType.DMA((12,)),
        ],
        compiler_params=pltpu.CompilerParams(vmem_limit_bytes=32 * 1024 * 1024),
        name="project",
    )(hidden, w_key, w_value, w_mine, w_other, h_mine, h_other)


def attend_kernel(
    by_owner, request_docs, queries, fresh, key_bias, row_place, key_place, *rest
):
    sources, (mixed, context_k, context_v, counts, sems) = rest[:-5], rest[-5:]
    me = lax.axis_index("seq")
    doc_count = request_docs.shape[1]
    head_dim = context_k.shape[1]
    doc_len = context_k.shape[0] // doc_count
    row_count = queries.shape[1]
    per_doc = row_count // doc_count
    heads = queries.shape[2] // head_dim
    owners = request_docs.shape[0]
    slots = sources[0].shape[0] if not by_owner else 2 * sources[0].shape[1]

    for o in range(owners):
        counts[o] = 0

    def one_doc(j, carry):
        doc = request_docs[me, j]
        owner = lax.div(doc, slots)
        rank = counts[owner]
        counts[owner] = rank + 1
        place = pl.ds(pl.multiple_of(j * doc_len, doc_len), doc_len)

        def fetch(key_source, value_source):
            pltpu.make_async_copy(key_source, context_k.at[place], sems.at[0]).start()
            pltpu.make_async_copy(value_source, context_v.at[place], sems.at[1]).start()

        if by_owner:
            fetch(sources[0].at[owner, rank, 0], sources[0].at[owner, rank, 1])
        else:
            away = lax.bitwise_xor(me, owner)

            @pl.when(away == 0)
            def _():
                slot = lax.rem(doc, slots)
                fetch(sources[0].at[slot], sources[1].at[slot])

            for k in range(1, owners):

                @pl.when(away == k)
                def _():
                    fetch(sources[1 + k].at[rank, 0], sources[1 + k].at[rank, 1])

        return carry

    lax.fori_loop(0, doc_count, one_doc, 0)
    pltpu.make_async_copy(context_k, context_k, sems.at[0]).wait()
    pltpu.make_async_copy(context_v, context_v, sems.at[1]).wait()

    scale = math.log2(math.e) / math.sqrt(head_dim)
    fresh_k = fresh[:, :head_dim]
    fresh_v = fresh[:, head_dim:]
    step = 4 if doc_count % 4 == 0 else 1
    block_rows = step * per_doc
    block_keys = step * doc_len
    slot_place = lax.broadcasted_iota(jnp.int32, (1, block_keys), 1)
    contract_last = (((1,), (1,)), ((), ()))
    for b in range(doc_count // step):
        rows = slice(b * block_rows, (b + 1) * block_rows)
        q = jnp.concatenate(
            [queries[0, rows, h * head_dim : (h + 1) * head_dim] for h in range(heads)], axis=0
        )
        own_place = row_place[rows, :]

        def masked(keys, bias):
            scores = lax.dot_general(q, keys, contract_last, preferred_element_type=jnp.float32)
            scores = (scores * scale).reshape(heads, block_rows, keys.shape[0])
            return (scores + bias[None]).reshape(heads * block_rows, keys.shape[0])

        chunks, values = [], []
        for c in range(b + 1):
            keys = slice(c * block_keys, (c + 1) * block_keys)
            bias = jnp.broadcast_to(key_bias[:, keys], (block_rows, block_keys))
            if c == b:
                bias = jnp.where(slot_place + c * block_keys <= own_place, bias, MASKED)
            chunks.append(masked(context_k[keys, :], bias))
            values.append(context_v[keys, :])
        bias = jnp.where(key_place[...] <= own_place, 0.0, MASKED)
        chunks.append(masked(fresh_k, bias))
        values.append(fresh_v)
        row_max = functools.reduce(
            jnp.maximum, [jnp.max(one, axis=1, keepdims=True) for one in chunks]
        )
        total = jnp.zeros((heads * block_rows, head_dim), jnp.float32)
        row_sum = jnp.zeros((heads * block_rows, 1), jnp.float32)
        for one, value in zip(chunks, values):
            powers = jnp.exp2(one - row_max)
            row_sum += jnp.sum(powers, axis=1, keepdims=True)
            total += jnp.dot(
                powers.astype(jnp.bfloat16), value, preferred_element_type=jnp.float32
            )
        result = (total / row_sum).astype(mixed.dtype)
        for h in range(heads):
            mixed[0, rows, h * head_dim : (h + 1) * head_dim] = result[
                h * block_rows : (h + 1) * block_rows
            ]


def attend(request_docs, queries, fresh, key_bias, row_place, key_place, sources, by_owner):
    head_dim = fresh.shape[1] // 2
    context = key_bias.shape[1]
    return pl.pallas_call(
        functools.partial(attend_kernel, by_owner),
        out_shape=jax.ShapeDtypeStruct(queries.shape, jnp.bfloat16),
        in_specs=[SMEM] + [VMEM] * 5 + [ANY] * len(sources),
        out_specs=VMEM,
        scratch_shapes=[
            pltpu.VMEM((context, head_dim), jnp.bfloat16),
            pltpu.VMEM((context, head_dim), jnp.bfloat16),
            pltpu.SMEM((request_docs.shape[0],), jnp.int32),
            pltpu.SemaphoreType.DMA((2,)),
        ],
        compiler_params=pltpu.CompilerParams(vmem_limit_bytes=32 * 1024 * 1024),
        name="attend",
    )(request_docs, queries, fresh, key_bias, row_place, key_place, *sources)


def shards(
    pairs,
    hidden,
    queries,
    w_key,
    w_value,
    store_keys,
    store_values,
    request_docs,
    doc_lengths,
    recompute_rows,
):
    my_index = lax.axis_index("seq")
    seq_count = lax.axis_size("seq")
    slot_count, doc_len, head_dim = store_keys.shape
    capacity = slot_count // 2
    doc_count = request_docs.shape[1]
    row_ids = recompute_rows[0]
    per_doc = row_ids.shape[1]
    row_count = doc_count * per_doc

    if pairs:
        def swap(array, axis, apart):
            count = lax.axis_size(axis)
            return lax.ppermute(array, axis, [(i, i ^ apart) for i in range(count)])

        w_send, h_send = cut(hidden, w_key, w_value)
        w_mine = swap(w_send, "seq", 2)
        h_mine = swap(h_send, "seq", 1)
        docs = cut_docs(request_docs, store_keys, store_values, False)
        docs = [swap(doc, "seq", k + 1) for k, doc in enumerate(docs)]
        w_other = swap(w_mine, "groups", 1)
        h_other = swap(h_mine, "tp", 1)
        own, part = project(hidden, w_key, w_value, w_mine, w_other, h_mine, h_other)
        fresh = (own + swap(part, "seq", 1).astype(jnp.float32)).astype(jnp.bfloat16)
        sources = (store_keys, store_values, *docs)
    else:
        (docs,) = cut_docs(request_docs, store_keys, store_values, True)
        sources = (lax.all_to_all(docs, "seq", split_axis=0, concat_axis=0, tiled=True),)
        weights = lax.all_gather(
            jnp.concatenate([w_key, w_value], axis=1), "seq", axis=0, tiled=True
        )
        fresh = jnp.dot(hidden[0], weights, preferred_element_type=jnp.float32)
        fresh = fresh.astype(jnp.bfloat16)

    my_docs = lax.dynamic_index_in_dim(request_docs, my_index, 0, keepdims=False)
    owners = my_docs // slot_count
    earlier = jnp.arange(doc_count)[None, :] < jnp.arange(doc_count)[:, None]
    ranks = jnp.sum(((owners[:, None] == owners[None, :]) & earlier).astype(jnp.int32), axis=1)
    positions = jnp.arange(doc_len, dtype=jnp.int32)
    held = positions[None, :] < doc_lengths[my_docs][:, None]
    held &= jnp.all(positions[None, None, :] != row_ids[:, :, None], axis=1)
    key_bias = jnp.where(held, 0.0, MASKED).astype(jnp.float32).reshape(1, doc_count * doc_len)
    place = jnp.arange(doc_count, dtype=jnp.int32)[:, None] * doc_len + row_ids
    mixed = attend(
        request_docs,
        queries,
        fresh,
        key_bias,
        place.reshape(row_count, 1),
        place.reshape(1, row_count),
        sources,
        not pairs,
    )

    slot_of_row = jnp.repeat(owners * capacity + ranks, per_doc) * per_doc + jnp.tile(
        jnp.arange(per_doc), doc_count
    )
    slots = jnp.arange(seq_count * capacity * per_doc)
    pick = (slots[:, None] == slot_of_row[None, :]).astype(jnp.bfloat16)
    outgoing = jnp.dot(pick, fresh, preferred_element_type=jnp.float32).astype(jnp.bfloat16)
    outgoing = outgoing.reshape(seq_count, capacity, per_doc, 2 * head_dim)
    returned = lax.all_to_all(outgoing, "seq", split_axis=0, concat_axis=0, tiled=True)
    returned = returned.reshape(seq_count, capacity, per_doc, 2, head_dim)
    return (mixed, returned[None])


def solution(mesh):
    pairs = mesh.shape["seq"] == 4 and mesh.shape["groups"] == 2 and mesh.shape["tp"] % 2 == 0
    return jax.shard_map(
        functools.partial(shards, pairs),
        mesh=mesh,
        in_specs=(
            P(("groups", "seq"), None, None),
            P(("groups", "seq"), None, "tp"),
            P("seq", "tp"),
            P("seq", "tp"),
            P(("groups", "seq"), None, "tp"),
            P(("groups", "seq"), None, "tp"),
            P("groups", None),
            P("groups"),
            P(("groups", "seq"), None, None),
        ),
        out_specs=(
            P(("groups", "seq"), None, "tp"),
            P(("groups", "seq"), None, None, None, None, "tp"),
        ),
        check_vma=False,
    )
```

time: 248 us -> 120 us (0.48)
  waiting for transfers between devices: 133 us -> 16.2 us
  Pallas kernels: 0 us -> 77 us
  local copies, waits for them, and re-layouts: 59 us -> 6.9 us
  matrix products: 27.7 us -> 0.17 us
  starting transfers between devices: 4.08 us -> 17.7 us
  between operations: 14 us -> 0.88 us
  other arithmetic: 8.46 us -> 0.52 us
    all_gather x4 -> x0, waiting for transfers between devices: 131 us -> none  [the longest x1 44.4 us: shards(): lax.all_gather(w_value, 'seq', axis=0, tiled=True)]
    pallas_call x0 -> x4, Pallas kernels: none -> 77 us  [the longest x1 40.9 us: cut(): pl.pallas_call(cut_kernel, out_shape=(jax.ShapeDtypeStruct((2, depth // 2...]
    scatter x2 -> x0, local copies, waits for them, and re-layouts: 40.3 us -> none  [the longest x1 20.2 us: shards(): doc_v.at[doc_column, row_ids]]
    dot_general x18 -> x1, matrix products: 27.7 us -> 0.17 us  [shards(): jnp.dot(pick, fresh, preferred_element_type=jnp.float32)]
    ppermute x0 -> x8, waiting for transfers between devices: none -> 16.2 us  [swap(): return lax.ppermute(array, axis, [(i, i ^ apart) for i in range(count)])]
    ppermute x0 -> x8, starting transfers between devices: none -> 11.9 us  [swap(): return lax.ppermute(array, axis, [(i, i ^ apart) for i in range(count)])]
    gather x4 -> x1, local copies, waits for them, and re-layouts: 6.55 us -> 0.66 us  [shards(): held = positions[None, :] < doc_lengths[my_docs][:, None]]
    reduce_sum x10 -> x1, other arithmetic: 3.33 us -> 0.18 us  [shards(): jnp.sum(((owners[:, None] == owners[None, :]) & earlier).astype(jnp.int32...]
  transfers between devices with their start and end apart: 5 -> 9, of which waited for: 4 -> 2; matrix products, arithmetic and copies ran while one was open for 36% -> 2% of each run, Pallas kernels for 0% -> 30%
where the time goes in v1:
time: 120 us; the launch traced here: 119 us
  Pallas kernels  77 us (64%)
  starting transfers between devices  17.7 us (15%)
  waiting for transfers between devices  16.2 us (14%)
  local copies, waits for them, and re-layouts  6.9 us (6%)
    pallas_call x1, Pallas kernels, cut(): pl.pallas_call(cut_kernel, out_shape=(jax.ShapeDtypeStruct((2, depth // 2...  40.9 us
    pallas_call x1, Pallas kernels, cut_docs(): pl.pallas_call(functools.partial(docs_kernel, by_owner), out_shape=shapes...  26.1 us
    ppermute x8, waiting for transfers between devices, swap(): return lax.ppermute(array, axis, [(i, i ^ apart) for i in range(count)])  16.2 us
    ppermute x8, starting transfers between devices, swap(): return lax.ppermute(array, axis, [(i, i ^ apart) for i in range(count)])  11.9 us
    pallas_call x1, Pallas kernels, attend(): pl.pallas_call(functools.partial(attend_kernel, by_owner), out_shape=jax....  7.12 us
    all_to_all x1, starting transfers between devices, shards(): lax.all_to_all(outgoing, 'seq', split_axis=0, concat_axis=0, tiled=True)  5.85 us
    unnamed x21, local copies, waits for them, and re-layouts  4.84 us
    pallas_call x1, Pallas kernels, project(): pl.pallas_call(project_kernel, out_shape=(jax.ShapeDtypeStruct((rows, 2 *...  2.9 us
  transfers between devices with their start and end apart: 9, of which 2 were waited for; matrix products, arithmetic and copies ran while one was open for 2% of the time, Pallas kernels for 30%

profile of v1, /device:TPU:0, one launch (start us, length us, event | category | flops | bytes accessed | tf_op | source)
XLA Modules:
  0.0 119.3 jit_solution(12208117959791509238)
XLA Ops:
  0.7 40.9 %cut.1 = (bf16[2,1024,128]{2,1,0:T(8,128)(2,1)}, bf16[2,96,2048]{2,1,0:T(8,128)(2,1)}) custom-call(bf16[1,192,8192]{2,1,0:T(8,128)(2,1)} %hidden.3, bf16[2048,128]{1,0:T(8,128)(2,1)} %w_key.3, bf16[2048,128]{1,0:T(8,128)(2,1)} %w_value.3), custom_call_target="tpu_custom_call" | custom-call | tf_op jit(solution)/shard_map/cut/pallas_call | solution.py:45
  41.5 3.1 %collective-permute-start.2 = (bf16[2,96,2048]{2,1,0:T(8,128)(2,1)}, bf16[2,96,2048]{2,1,0:T(8,128)(2,1)}, u32[]{:S(2)}, u32[]{:S(2)}) collective-permute-start(bf16[2,96,2048]{2,1,0:T(8,128)(2,1)} %get-tuple-element.10), channel_id=1, source_target_pairs={{0,4},{4,0},{8,12},{12,8},{1,5},{5,1},{9,13},{13,9},{2,6},{6,2},{1... | collective-permute-start | bytes 2359304 | tf_op jit(solution)/shard_map/ppermute | solution.py:325
  44.6 2.6 %collective-permute-start = (bf16[2,1024,128]{2,1,0:T(8,128)(2,1)}, bf16[2,1024,128]{2,1,0:T(8,128)(2,1)}, u32[]{:S(2)}, u32[]{:S(2)}) collective-permute-start(bf16[2,1024,128]{2,1,0:T(8,128)(2,1)} %get-tuple-element.9), channel_id=1, source_target_pairs={{0,8},{4,12},{8,0},{12,4},{1,9},{5,13},{9,1},{13,5},{2,10},{6,14},... | collective-permute-start | bytes 1572872 | tf_op jit(solution)/shard_map/ppermute | solution.py:325
  47.2 26.1 %cut_docs.1 = (bf16[4,2,128,128]{3,2,1,0:T(8,128)(2,1)}, bf16[4,2,128,128]{3,2,1,0:T(8,128)(2,1)}, bf16[4,2,128,128]{3,2,1,0:T(8,128)(2,1)}) custom-call(s32[4,16]{1,0:T(4,128)} %request_docs.3, bf16[8,128,128]{2,1,0:T(8,128)(2,1)} %rest_0_.1, bf16[8,128,128]{2,1,0:T(8,128)(2,1)} %rest_1_.1), custom_call_target="tpu_custom_call" | custom-call | tf_op jit(solution)/shard_map/cut_docs/pallas_call | solution.py:113
  73.3 0.5 collective-permute-start.5
  73.8 3.9 %collective-permute-start.7 = (bf16[4,2,128,128]{3,2,1,0:T(8,128)(2,1)}, bf16[4,2,128,128]{3,2,1,0:T(8,128)(2,1)}, u32[]{:S(2)}, u32[]{:S(2)}) collective-permute-start(bf16[4,2,128,128]{3,2,1,0:T(8,128)(2,1)} %get-tuple-element.15), channel_id=1, source_target_pairs={{0,12},{4,8},{8,4},{12,0},{1,13},{5,9},{9,5},{13,1},{2,14},{6,10},... | collective-permute-start | bytes 786440 | tf_op jit(solution)/shard_map/ppermute | solution.py:325
  77.9 0.2 convert_reduce_fusion
  78.2 1.6 %collective-permute-start.1 = (bf16[2,1024,128]{2,1,0:T(8,128)(2,1)}, bf16[2,1024,128]{2,1,0:T(8,128)(2,1)}, u32[]{:S(2)}, u32[]{:S(2)}) collective-permute-start(bf16[2,1024,128]{2,1,0:T(8,128)(2,1)} %collective-permute-done.w_mine), channel_id=1, source_target_pairs={{0,16},{16,0},{1,17},{17,1},{2,18},{18,2},{3,19},{19,3},{4,20},{20... | collective-permute-start | bytes 1572872 | tf_op jit(solution)/shard_map/ppermute | solution.py:325
  80.2 0.1 copy.36.row_place
  80.4 0.1 add.76
  80.6 0.7 gather_fusion
  81.2 11.7 %collective-permute-done.1.w_other = bf16[2,1024,128]{2,1,0:T(8,128)(2,1)} collective-permute-done((bf16[2,1024,128]{2,1,0:T(8,128)(2,1)}, bf16[2,1024,128]{2,1,0:T(8,128)(2,1)}, u32[]{:S(2)}, u32[]{:S(2)}) %collective-permute-start.1) | collective-permute-done | bytes 524320 | tf_op jit(solution)/shard_map/ppermute | solution.py:325
  92.9 1.0 copy-done.2
  93.9 1.0 copy-done.3
  95.0 2.9 %project.1 = (f32[192,256]{1,0:T(8,128)S(1)}, bf16[192,256]{1,0:T(8,128)(2,1)S(1)}) custom-call(bf16[1,192,8192]{2,1,0:T(8,128)(2,1)S(1)} %copy-done.1, bf16[2048,128]{1,0:T(8,128)(2,1)S(1)} %copy-done.2, bf16[2048,128]{1,0:T(8,128)(2,1)S(1)} %copy-done.3, bf16[2,1024,128]{2,1,0:T(8,128)(2,1)} %collective-permute-done.w_mine, ...), custom_call_target="tpu_custom_call" | custom-call | tf_op jit(solution)/shard_map/project/pallas_call | solution.py:165
  98.0 0.1 fusion.1
  98.1 4.5 %collective-permute-done.4 = bf16[192,256]{1,0:T(8,128)(2,1)S(1)} collective-permute-done((bf16[192,256]{1,0:T(8,128)(2,1)S(1)}, bf16[192,256]{1,0:T(8,128)(2,1)S(1)}, u32[]{:S(2)}, u32[]{:S(2)}) %collective-permute-start.4) | collective-permute-done | bytes 98336 | tf_op jit(solution)/shard_map/ppermute | solution.py:325
  102.6 0.2 convolution_convert_fusion
  102.8 0.7 copy.37
  103.5 5.8 %all-to-all-start = ((bf16[4,4,12,256]{3,1,2,0:T(4,128)(2,1)}), bf16[4,4,12,256]{3,1,2,0:T(4,128)(2,1)S(1)}, u32[]{:S(2)}, u32[]{:S(2)}) async-start(bf16[4,4,12,256]{3,1,2,0:T(4,128)(2,1)} %copy.37), calls=%async_computation | async-start | bytes 196608 | tf_op jit(solution)/shard_map/all_to_all | solution.py:373
  109.5 0.9 copy-done.5
  110.4 1.0 copy-done.6
  111.4 7.1 %attend.1 = bf16[1,192,1024]{2,1,0:T(8,128)(2,1)} custom-call(s32[4,16]{1,0:T(4,128)S(1)} %copy-done.7, bf16[1,192,1024]{2,1,0:T(8,128)(2,1)S(1)} %copy-done.6, bf16[192,256]{1,0:T(8,128)(2,1)S(1)} %add_convert_fusion.fresh, f32[1,2048]{1,0:T(1,128)S(1)} %bitcast.23, s32[192,1]{1,0:T(8,128)S(1)} %copy.36.row_place, s32[1,192]{1,0:T(1,128)S(1)} %add.73.key_place, ...), custom_call_target="tpu_custom_call" | custom-call | tf_op jit(solution)/shard_map/attend/pallas_call | solution.py:285
  118.6 0.7 copy.38
  (44 shorter events, 1.0 us)
Async XLA Ops:
  0.6 79.9 %copy-start = (s32[32]{0:T(128)S(1)}, s32[32]{0:T(128)}, u32[]{:S(2)}) copy-start(s32[32]{0:T(128)} %param.16) | copy-start | bytes 388
  0.6 92.3 %copy-start.1 = (bf16[1,192,8192]{2,1,0:T(8,128)(2,1)S(1)}, bf16[1,192,8192]{2,1,0:T(8,128)(2,1)}, u32[]{:S(2)}) copy-start(bf16[1,192,8192]{2,1,0:T(8,128)(2,1)} %hidden.3) | copy-start | bytes 9437188
  0.7 77.1 %copy-start.7 = (s32[4,16]{1,0:T(4,128)S(1)}, s32[4,16]{1,0:T(4,128)}, u32[]{:S(2)}) copy-start(s32[4,16]{1,0:T(4,128)} %request_docs.3) | copy-start | bytes 772
  0.7 77.4 %copy-start.8 = (s32[1,16,12]{1,0,2:T(1,128)S(1)}, s32[1,16,12]{1,0,2:T(1,128)}, u32[]{:S(2)}) copy-start(s32[1,16,12]{1,0,2:T(1,128)} %param.17) | copy-start | bytes 2308
  41.5 36.3 %collective-permute-start.2 = (bf16[2,96,2048]{2,1,0:T(8,128)(2,1)}, bf16[2,96,2048]{2,1,0:T(8,128)(2,1)}, u32[]{:S(2)}, u32[]{:S(2)}) collective-permute-start(bf16[2,96,2048]{2,1,0:T(8,128)(2,1)} %get-tuple-element.10), channel_id=1, source_target_pairs={{0,4},{4,0},{8,12},{12,8},{1,5},{5,1},{9,13},{13,9},{2,6},{6,2},{1... | collective-permute-start | bytes 2359304 | tf_op jit(solution)/shard_map/ppermute | solution.py:325
  44.6 33.6 %collective-permute-start = (bf16[2,1024,128]{2,1,0:T(8,128)(2,1)}, bf16[2,1024,128]{2,1,0:T(8,128)(2,1)}, u32[]{:S(2)}, u32[]{:S(2)}) collective-permute-start(bf16[2,1024,128]{2,1,0:T(8,128)(2,1)} %get-tuple-element.9), channel_id=1, source_target_pairs={{0,8},{4,12},{8,0},{12,4},{1,9},{5,13},{9,1},{13,5},{2,10},{6,14},... | collective-permute-start | bytes 1572872 | tf_op jit(solution)/shard_map/ppermute | solution.py:325
  73.3 36.1 %collective-permute-start.5 = (bf16[4,2,128,128]{3,2,1,0:T(8,128)(2,1)}, bf16[4,2,128,128]{3,2,1,0:T(8,128)(2,1)}, u32[]{:S(2)}, u32[]{:S(2)}) collective-permute-start(bf16[4,2,128,128]{3,2,1,0:T(8,128)(2,1)} %get-tuple-element.13), channel_id=1, source_target_pairs={{0,4},{4,0},{8,12},{12,8},{1,5},{5,1},{9,13},{13,9},{2,6},{6,2},{1... | collective-permute-start | bytes 786440 | tf_op jit(solution)/shard_map/ppermute | solution.py:325
  73.8 35.6 %collective-permute-start.6 = (bf16[4,2,128,128]{3,2,1,0:T(8,128)(2,1)}, bf16[4,2,128,128]{3,2,1,0:T(8,128)(2,1)}, u32[]{:S(2)}, u32[]{:S(2)}) collective-permute-start(bf16[4,2,128,128]{3,2,1,0:T(8,128)(2,1)} %get-tuple-element.14), channel_id=1, source_target_pairs={{0,8},{4,12},{8,0},{12,4},{1,9},{5,13},{9,1},{13,5},{2,10},{6,14},... | collective-permute-start | bytes 786440 | tf_op jit(solution)/shard_map/ppermute | solution.py:325
  73.8 35.6 %collective-permute-start.7 = (bf16[4,2,128,128]{3,2,1,0:T(8,128)(2,1)}, bf16[4,2,128,128]{3,2,1,0:T(8,128)(2,1)}, u32[]{:S(2)}, u32[]{:S(2)}) collective-permute-start(bf16[4,2,128,128]{3,2,1,0:T(8,128)(2,1)} %get-tuple-element.15), channel_id=1, source_target_pairs={{0,12},{4,8},{8,4},{12,0},{1,13},{5,9},{9,5},{13,1},{2,14},{6,10},... | collective-permute-start | bytes 786440 | tf_op jit(solution)/shard_map/ppermute | solution.py:325
  77.8 15.1 %collective-permute-start.3 = (bf16[2,96,2048]{2,1,0:T(8,128)(2,1)}, bf16[2,96,2048]{2,1,0:T(8,128)(2,1)}, u32[]{:S(2)}, u32[]{:S(2)}) collective-permute-start(bf16[2,96,2048]{2,1,0:T(8,128)(2,1)} %collective-permute-done.2.h_mine), channel_id=1, source_target_pairs={{0,1},{1,0},{2,3},{3,2},{4,5},{5,4},{6,7},{7,6},{8,9},{9,8},{10,11... | collective-permute-start | bytes 2359304 | tf_op jit(solution)/shard_map/ppermute | solution.py:325
  78.2 14.7 %collective-permute-start.1 = (bf16[2,1024,128]{2,1,0:T(8,128)(2,1)}, bf16[2,1024,128]{2,1,0:T(8,128)(2,1)}, u32[]{:S(2)}, u32[]{:S(2)}) collective-permute-start(bf16[2,1024,128]{2,1,0:T(8,128)(2,1)} %collective-permute-done.w_mine), channel_id=1, source_target_pairs={{0,16},{16,0},{1,17},{17,1},{2,18},{18,2},{3,19},{19,3},{4,20},{20... | collective-permute-start | bytes 1572872 | tf_op jit(solution)/shard_map/ppermute | solution.py:325
  92.9 1.0 copy-start.2
  93.9 1.0 copy-start.3
  95.0 14.5 %copy-start.4 = (bf16[8,128,128]{2,1,0:T(8,128)(2,1)S(1)}, bf16[8,128,128]{2,1,0:T(8,128)(2,1)}, u32[]{:S(2)}) copy-start(bf16[8,128,128]{2,1,0:T(8,128)(2,1)} %rest_0_.1) | copy-start | bytes 786436
  97.9 4.7 %collective-permute-start.4 = (bf16[192,256]{1,0:T(8,128)(2,1)S(1)}, bf16[192,256]{1,0:T(8,128)(2,1)S(1)}, u32[]{:S(2)}, u32[]{:S(2)}) collective-permute-start(bf16[192,256]{1,0:T(8,128)(2,1)S(1)} %get-tuple-element.12), channel_id=1, source_target_pairs={{0,4},{4,0},{8,12},{12,8},{1,5},{5,1},{9,13},{13,9},{2,6},{6,2},{1... | collective-permute-start | bytes 294920 | tf_op jit(solution)/shard_map/ppermute | solution.py:325
  103.5 15.0 %all-to-all-start = ((bf16[4,4,12,256]{3,1,2,0:T(4,128)(2,1)}), bf16[4,4,12,256]{3,1,2,0:T(4,128)(2,1)S(1)}, u32[]{:S(2)}, u32[]{:S(2)}) async-start(bf16[4,4,12,256]{3,1,2,0:T(4,128)(2,1)} %copy.37), calls=%async_computation | async-start | bytes 196608 | tf_op jit(solution)/shard_map/all_to_all | solution.py:373
  109.5 1.0 copy-start.5
  110.4 1.0 copy-start.6

commit v2 on v1

--- a/solution.py
+++ b/solution.py
@@ -49,7 +49,7 @@
             jax.ShapeDtypeStruct((2, hidden.shape[1] // 2, depth), jnp.bfloat16),
         ),
         in_specs=[ANY] * 3,
-        out_specs=(ANY, ANY),
+        out_specs=(VMEM, VMEM),
         scratch_shapes=[pltpu.SemaphoreType.DMA((4,))],
         name="cut",
     )(hidden, w_key, w_value)
@@ -114,7 +114,7 @@
         functools.partial(docs_kernel, by_owner),
         out_shape=shapes,
         in_specs=[SMEM, ANY, ANY],
-        out_specs=(ANY,) * len(shapes),
+        out_specs=(VMEM,) * len(shapes),
         scratch_shapes=[
             pltpu.SMEM((requests, capacity), jnp.int32),
             pltpu.SemaphoreType.DMA((len(shapes),)),

time: 120 us -> 83.4 us (0.70)
  Pallas kernels: 77 us -> 15.6 us
  waiting for transfers between devices: 16.2 us -> 41.3 us
    pallas_call x1, Pallas kernels: 40.9 us -> 2.55 us  [cut(): pl.pallas_call(cut_kernel, out_shape=(jax.ShapeDtypeStruct((2, depth // 2...]
    ppermute x8, waiting for transfers between devices: 16.2 us -> 41.3 us  [swap(): return lax.ppermute(array, axis, [(i, i ^ apart) for i in range(count)])]
    pallas_call x1, Pallas kernels: 26.1 us -> 3.13 us  [cut_docs(): pl.pallas_call(functools.partial(docs_kernel, by_owner), out_shape=shapes...]
  transfers between devices with their start and end apart: 9 -> 9, of which waited for: 2 -> 3; matrix products, arithmetic and copies ran while one was open for 2% -> 3% of each run, Pallas kernels for 30% -> 16%
where the time goes in v2:
time: 83.4 us; the launch traced here: 82.7 us
  waiting for transfers between devices  41.3 us (50%)
  starting transfers between devices  17.3 us (21%)
  Pallas kernels  15.6 us (19%)
  local copies, waits for them, and re-layouts  6.9 us (8%)
  between operations  0.87 us (1%)
    ppermute x8, waiting for transfers between devices, swap(): return lax.ppermute(array, axis, [(i, i ^ apart) for i in range(count)])  41.3 us
    ppermute x8, starting transfers between devices, swap(): return lax.ppermute(array, axis, [(i, i ^ apart) for i in range(count)])  12.3 us
    pallas_call x1, Pallas kernels, attend(): pl.pallas_call(functools.partial(attend_kernel, by_owner), out_shape=jax....  7.01 us
    all_to_all x1, starting transfers between devices, shards(): lax.all_to_all(outgoing, 'seq', split_axis=0, concat_axis=0, tiled=True)  5.08 us
    unnamed x21, local copies, waits for them, and re-layouts  4.84 us
    pallas_call x1, Pallas kernels, cut_docs(): pl.pallas_call(functools.partial(docs_kernel, by_owner), out_shape=shapes...  3.13 us
    pallas_call x1, Pallas kernels, project(): pl.pallas_call(project_kernel, out_shape=(jax.ShapeDtypeStruct((rows, 2 *...  2.9 us
    pallas_call x1, Pallas kernels, cut(): pl.pallas_call(cut_kernel, out_shape=(jax.ShapeDtypeStruct((2, depth // 2...  2.55 us
  transfers between devices with their start and end apart: 9, of which 3 were waited for; matrix products, arithmetic and copies ran while one was open for 3% of the time, Pallas kernels for 16%

profile of v2, /device:TPU:0, one launch (start us, length us, event | category | flops | bytes accessed | tf_op | source)
XLA Modules:
  0.0 82.7 jit_solution(8292775177544603520)
XLA Ops:
  0.7 2.6 %cut.1 = (bf16[2,1024,128]{2,1,0:T(8,128)(2,1)}, bf16[2,96,2048]{2,1,0:T(8,128)(2,1)}) custom-call(bf16[1,192,8192]{2,1,0:T(8,128)(2,1)} %hidden.3, bf16[2048,128]{1,0:T(8,128)(2,1)} %w_key.3, bf16[2048,128]{1,0:T(8,128)(2,1)} %w_value.3), custom_call_target="tpu_custom_call" | custom-call | tf_op jit(solution)/shard_map/cut/pallas_call | solution.py:45
  3.2 3.1 %collective-permute-start.2 = (bf16[2,96,2048]{2,1,0:T(8,128)(2,1)}, bf16[2,96,2048]{2,1,0:T(8,128)(2,1)}, u32[]{:S(2)}, u32[]{:S(2)}) collective-permute-start(bf16[2,96,2048]{2,1,0:T(8,128)(2,1)} %get-tuple-element.10), channel_id=1, source_target_pairs={{0,4},{4,0},{8,12},{12,8},{1,5},{5,1},{9,13},{13,9},{2,6},{6,2},{1... | collective-permute-start | bytes 2359304 | tf_op jit(solution)/shard_map/ppermute | solution.py:325
  6.3 2.6 %collective-permute-start = (bf16[2,1024,128]{2,1,0:T(8,128)(2,1)}, bf16[2,1024,128]{2,1,0:T(8,128)(2,1)}, u32[]{:S(2)}, u32[]{:S(2)}) collective-permute-start(bf16[2,1024,128]{2,1,0:T(8,128)(2,1)} %get-tuple-element.9), channel_id=1, source_target_pairs={{0,8},{4,12},{8,0},{12,4},{1,9},{5,13},{9,1},{13,5},{2,10},{6,14},... | collective-permute-start | bytes 1572872 | tf_op jit(solution)/shard_map/ppermute | solution.py:325
  8.9 3.1 %cut_docs.1 = (bf16[4,2,128,128]{3,2,1,0:T(8,128)(2,1)}, bf16[4,2,128,128]{3,2,1,0:T(8,128)(2,1)}, bf16[4,2,128,128]{3,2,1,0:T(8,128)(2,1)}) custom-call(s32[4,16]{1,0:T(4,128)} %request_docs.3, bf16[8,128,128]{2,1,0:T(8,128)(2,1)} %rest_0_.1, bf16[8,128,128]{2,1,0:T(8,128)(2,1)} %rest_1_.1), custom_call_target="tpu_custom_call" | custom-call | tf_op jit(solution)/shard_map/cut_docs/pallas_call | solution.py:113
  12.1 0.5 collective-permute-start.5
  12.6 3.9 %collective-permute-start.7 = (bf16[4,2,128,128]{3,2,1,0:T(8,128)(2,1)}, bf16[4,2,128,128]{3,2,1,0:T(8,128)(2,1)}, u32[]{:S(2)}, u32[]{:S(2)}) collective-permute-start(bf16[4,2,128,128]{3,2,1,0:T(8,128)(2,1)} %get-tuple-element.15), channel_id=1, source_target_pairs={{0,12},{4,8},{8,4},{12,0},{1,13},{5,9},{9,5},{13,1},{2,14},{6,10},... | collective-permute-start | bytes 786440 | tf_op jit(solution)/shard_map/ppermute | solution.py:325
  16.5 25.3 %collective-permute-done.2.h_mine = bf16[2,96,2048]{2,1,0:T(8,128)(2,1)} collective-permute-done((bf16[2,96,2048]{2,1,0:T(8,128)(2,1)}, bf16[2,96,2048]{2,1,0:T(8,128)(2,1)}, u32[]{:S(2)}, u32[]{:S(2)}) %collective-permute-start.2) | collective-permute-done | bytes 786464 | tf_op jit(solution)/shard_map/ppermute | solution.py:325
  41.9 0.2 convert_reduce_fusion
  42.2 2.1 %collective-permute-start.1 = (bf16[2,1024,128]{2,1,0:T(8,128)(2,1)}, bf16[2,1024,128]{2,1,0:T(8,128)(2,1)}, u32[]{:S(2)}, u32[]{:S(2)}) collective-permute-start(bf16[2,1024,128]{2,1,0:T(8,128)(2,1)} %collective-permute-done.w_mine), channel_id=1, source_target_pairs={{0,16},{16,0},{1,17},{17,1},{2,18},{18,2},{3,19},{19,3},{4,20},{20... | collective-permute-start | bytes 1572872 | tf_op jit(solution)/shard_map/ppermute | solution.py:325
  44.7 0.1 copy.36.row_place
  44.9 0.1 add.76
  45.0 0.7 gather_fusion
  45.7 11.5 %collective-permute-done.1.w_other = bf16[2,1024,128]{2,1,0:T(8,128)(2,1)} collective-permute-done((bf16[2,1024,128]{2,1,0:T(8,128)(2,1)}, bf16[2,1024,128]{2,1,0:T(8,128)(2,1)}, u32[]{:S(2)}, u32[]{:S(2)}) %collective-permute-start.1) | collective-permute-done | bytes 524320 | tf_op jit(solution)/shard_map/ppermute | solution.py:325
  57.2 1.0 %copy-done.2 = bf16[2048,128]{1,0:T(8,128)(2,1)S(1)} copy-done((bf16[2048,128]{1,0:T(8,128)(2,1)S(1)}, bf16[2048,128]{1,0:T(8,128)(2,1)}, u32[]{:S(2)}) %copy-start.2) | copy-done | bytes 524312
  58.2 1.0 %copy-done.3 = bf16[2048,128]{1,0:T(8,128)(2,1)S(1)} copy-done((bf16[2048,128]{1,0:T(8,128)(2,1)S(1)}, bf16[2048,128]{1,0:T(8,128)(2,1)}, u32[]{:S(2)}) %copy-start.3) | copy-done | bytes 524312
  59.2 2.9 %project.1 = (f32[192,256]{1,0:T(8,128)S(1)}, bf16[192,256]{1,0:T(8,128)(2,1)S(1)}) custom-call(bf16[1,192,8192]{2,1,0:T(8,128)(2,1)S(1)} %copy-done.1, bf16[2048,128]{1,0:T(8,128)(2,1)S(1)} %copy-done.2, bf16[2048,128]{1,0:T(8,128)(2,1)S(1)} %copy-done.3, bf16[2,1024,128]{2,1,0:T(8,128)(2,1)} %collective-permute-done.w_mine, ...), custom_call_target="tpu_custom_call" | custom-call | tf_op jit(solution)/shard_map/project/pallas_call | solution.py:165
  62.3 4.5 %collective-permute-done.4 = bf16[192,256]{1,0:T(8,128)(2,1)S(1)} collective-permute-done((bf16[192,256]{1,0:T(8,128)(2,1)S(1)}, bf16[192,256]{1,0:T(8,128)(2,1)S(1)}, u32[]{:S(2)}, u32[]{:S(2)}) %collective-permute-start.4) | collective-permute-done | bytes 98336 | tf_op jit(solution)/shard_map/ppermute | solution.py:325
  66.9 0.2 convolution_convert_fusion
  67.1 0.7 copy.37
  67.8 5.1 %all-to-all-start = ((bf16[4,4,12,256]{3,1,2,0:T(4,128)(2,1)}), bf16[4,4,12,256]{3,1,2,0:T(4,128)(2,1)S(1)}, u32[]{:S(2)}, u32[]{:S(2)}) async-start(bf16[4,4,12,256]{3,1,2,0:T(4,128)(2,1)} %copy.37), calls=%async_computation | async-start | bytes 196608 | tf_op jit(solution)/shard_map/all_to_all | solution.py:373
  73.0 0.9 %copy-done.5 = bf16[8,128,128]{2,1,0:T(8,128)(2,1)S(1)} copy-done((bf16[8,128,128]{2,1,0:T(8,128)(2,1)S(1)}, bf16[8,128,128]{2,1,0:T(8,128)(2,1)}, u32[]{:S(2)}) %copy-start.5) | copy-done | bytes 262168
  73.9 1.0 %copy-done.6 = bf16[1,192,1024]{2,1,0:T(8,128)(2,1)S(1)} copy-done((bf16[1,192,1024]{2,1,0:T(8,128)(2,1)S(1)}, bf16[1,192,1024]{2,1,0:T(8,128)(2,1)}, u32[]{:S(2)}) %copy-start.6) | copy-done | bytes 393240
  74.9 7.0 %attend.1 = bf16[1,192,1024]{2,1,0:T(8,128)(2,1)} custom-call(s32[4,16]{1,0:T(4,128)S(1)} %copy-done.7, bf16[1,192,1024]{2,1,0:T(8,128)(2,1)S(1)} %copy-done.6, bf16[192,256]{1,0:T(8,128)(2,1)S(1)} %add_convert_fusion.fresh, f32[1,2048]{1,0:T(1,128)S(1)} %bitcast.23, s32[192,1]{1,0:T(8,128)S(1)} %copy.36.row_place, s32[1,192]{1,0:T(1,128)S(1)} %add.73.key_place, ...), custom_call_target="tpu_custom_call" | custom-call | tf_op jit(solution)/shard_map/attend/pallas_call | solution.py:285
  82.0 0.7 copy.38
  (44 shorter events, 1.0 us)
Async XLA Ops:
  0.6 44.4 %copy-start = (s32[32]{0:T(128)S(1)}, s32[32]{0:T(128)}, u32[]{:S(2)}) copy-start(s32[32]{0:T(128)} %param.16) | copy-start | bytes 388
  0.6 56.5 %copy-start.1 = (bf16[1,192,8192]{2,1,0:T(8,128)(2,1)S(1)}, bf16[1,192,8192]{2,1,0:T(8,128)(2,1)}, u32[]{:S(2)}) copy-start(bf16[1,192,8192]{2,1,0:T(8,128)(2,1)} %hidden.3) | copy-start | bytes 9437188
  0.7 15.9 %copy-start.7 = (s32[4,16]{1,0:T(4,128)S(1)}, s32[4,16]{1,0:T(4,128)}, u32[]{:S(2)}) copy-start(s32[4,16]{1,0:T(4,128)} %request_docs.3) | copy-start | bytes 772
  0.7 41.4 %copy-start.8 = (s32[1,16,12]{1,0,2:T(1,128)S(1)}, s32[1,16,12]{1,0,2:T(1,128)}, u32[]{:S(2)}) copy-start(s32[1,16,12]{1,0,2:T(1,128)} %param.17) | copy-start | bytes 2308
  3.2 38.6 %collective-permute-start.2 = (bf16[2,96,2048]{2,1,0:T(8,128)(2,1)}, bf16[2,96,2048]{2,1,0:T(8,128)(2,1)}, u32[]{:S(2)}, u32[]{:S(2)}) collective-permute-start(bf16[2,96,2048]{2,1,0:T(8,128)(2,1)} %get-tuple-element.10), channel_id=1, source_target_pairs={{0,4},{4,0},{8,12},{12,8},{1,5},{5,1},{9,13},{13,9},{2,6},{6,2},{1... | collective-permute-start | bytes 2359304 | tf_op jit(solution)/shard_map/ppermute | solution.py:325
  6.3 35.8 %collective-permute-start = (bf16[2,1024,128]{2,1,0:T(8,128)(2,1)}, bf16[2,1024,128]{2,1,0:T(8,128)(2,1)}, u32[]{:S(2)}, u32[]{:S(2)}) collective-permute-start(bf16[2,1024,128]{2,1,0:T(8,128)(2,1)} %get-tuple-element.9), channel_id=1, source_target_pairs={{0,8},{4,12},{8,0},{12,4},{1,9},{5,13},{9,1},{13,5},{2,10},{6,14},... | collective-permute-start | bytes 1572872 | tf_op jit(solution)/shard_map/ppermute | solution.py:325
  12.1 60.9 %collective-permute-start.5 = (bf16[4,2,128,128]{3,2,1,0:T(8,128)(2,1)}, bf16[4,2,128,128]{3,2,1,0:T(8,128)(2,1)}, u32[]{:S(2)}, u32[]{:S(2)}) collective-permute-start(bf16[4,2,128,128]{3,2,1,0:T(8,128)(2,1)} %get-tuple-element.13), channel_id=1, source_target_pairs={{0,4},{4,0},{8,12},{12,8},{1,5},{5,1},{9,13},{13,9},{2,6},{6,2},{1... | collective-permute-start | bytes 786440 | tf_op jit(solution)/shard_map/ppermute | solution.py:325
  12.6 60.4 %collective-permute-start.6 = (bf16[4,2,128,128]{3,2,1,0:T(8,128)(2,1)}, bf16[4,2,128,128]{3,2,1,0:T(8,128)(2,1)}, u32[]{:S(2)}, u32[]{:S(2)}) collective-permute-start(bf16[4,2,128,128]{3,2,1,0:T(8,128)(2,1)} %get-tuple-element.14), channel_id=1, source_target_pairs={{0,8},{4,12},{8,0},{12,4},{1,9},{5,13},{9,1},{13,5},{2,10},{6,14},... | collective-permute-start | bytes 786440 | tf_op jit(solution)/shard_map/ppermute | solution.py:325
  12.6 60.4 %collective-permute-start.7 = (bf16[4,2,128,128]{3,2,1,0:T(8,128)(2,1)}, bf16[4,2,128,128]{3,2,1,0:T(8,128)(2,1)}, u32[]{:S(2)}, u32[]{:S(2)}) collective-permute-start(bf16[4,2,128,128]{3,2,1,0:T(8,128)(2,1)} %get-tuple-element.15), channel_id=1, source_target_pairs={{0,12},{4,8},{8,4},{12,0},{1,13},{5,9},{9,5},{13,1},{2,14},{6,10},... | collective-permute-start | bytes 786440 | tf_op jit(solution)/shard_map/ppermute | solution.py:325
  41.9 15.3 %collective-permute-start.3 = (bf16[2,96,2048]{2,1,0:T(8,128)(2,1)}, bf16[2,96,2048]{2,1,0:T(8,128)(2,1)}, u32[]{:S(2)}, u32[]{:S(2)}) collective-permute-start(bf16[2,96,2048]{2,1,0:T(8,128)(2,1)} %collective-permute-done.2.h_mine), channel_id=1, source_target_pairs={{0,1},{1,0},{2,3},{3,2},{4,5},{5,4},{6,7},{7,6},{8,9},{9,8},{10,11... | collective-permute-start | bytes 2359304 | tf_op jit(solution)/shard_map/ppermute | solution.py:325
  42.2 15.0 %collective-permute-start.1 = (bf16[2,1024,128]{2,1,0:T(8,128)(2,1)}, bf16[2,1024,128]{2,1,0:T(8,128)(2,1)}, u32[]{:S(2)}, u32[]{:S(2)}) collective-permute-start(bf16[2,1024,128]{2,1,0:T(8,128)(2,1)} %collective-permute-done.w_mine), channel_id=1, source_target_pairs={{0,16},{16,0},{1,17},{17,1},{2,18},{18,2},{3,19},{19,3},{4,20},{20... | collective-permute-start | bytes 1572872 | tf_op jit(solution)/shard_map/ppermute | solution.py:325
  57.2 1.0 %copy-start.2 = (bf16[2048,128]{1,0:T(8,128)(2,1)S(1)}, bf16[2048,128]{1,0:T(8,128)(2,1)}, u32[]{:S(2)}) copy-start(bf16[2048,128]{1,0:T(8,128)(2,1)} %w_key.3) | copy-start | bytes 1572868
  58.2 1.0 %copy-start.3 = (bf16[2048,128]{1,0:T(8,128)(2,1)S(1)}, bf16[2048,128]{1,0:T(8,128)(2,1)}, u32[]{:S(2)}) copy-start(bf16[2048,128]{1,0:T(8,128)(2,1)} %w_value.3) | copy-start | bytes 1572868
  59.2 13.7 %copy-start.4 = (bf16[8,128,128]{2,1,0:T(8,128)(2,1)S(1)}, bf16[8,128,128]{2,1,0:T(8,128)(2,1)}, u32[]{:S(2)}) copy-start(bf16[8,128,128]{2,1,0:T(8,128)(2,1)} %rest_0_.1) | copy-start | bytes 786436
  62.2 4.7 %collective-permute-start.4 = (bf16[192,256]{1,0:T(8,128)(2,1)S(1)}, bf16[192,256]{1,0:T(8,128)(2,1)S(1)}, u32[]{:S(2)}, u32[]{:S(2)}) collective-permute-start(bf16[192,256]{1,0:T(8,128)(2,1)S(1)} %get-tuple-element.12), channel_id=1, source_target_pairs={{0,4},{4,0},{8,12},{12,8},{1,5},{5,1},{9,13},{13,9},{2,6},{6,2},{1... | collective-permute-start | bytes 294920 | tf_op jit(solution)/shard_map/ppermute | solution.py:325
  67.8 14.2 %all-to-all-start = ((bf16[4,4,12,256]{3,1,2,0:T(4,128)(2,1)}), bf16[4,4,12,256]{3,1,2,0:T(4,128)(2,1)S(1)}, u32[]{:S(2)}, u32[]{:S(2)}) async-start(bf16[4,4,12,256]{3,1,2,0:T(4,128)(2,1)} %copy.37), calls=%async_computation | async-start | bytes 196608 | tf_op jit(solution)/shard_map/all_to_all | solution.py:373
  73.0 1.0 %copy-start.5 = (bf16[8,128,128]{2,1,0:T(8,128)(2,1)S(1)}, bf16[8,128,128]{2,1,0:T(8,128)(2,1)}, u32[]{:S(2)}) copy-start(bf16[8,128,128]{2,1,0:T(8,128)(2,1)} %rest_1_.1) | copy-start | bytes 786436
  73.9 1.0 %copy-start.6 = (bf16[1,192,1024]{2,1,0:T(8,128)(2,1)S(1)}, bf16[1,192,1024]{2,1,0:T(8,128)(2,1)}, u32[]{:S(2)}) copy-start(bf16[1,192,1024]{2,1,0:T(8,128)(2,1)} %queries.1) | copy-start | bytes 1179652

commit v3 on v2

--- a/solution.py
+++ b/solution.py
@@ -14,45 +14,55 @@
 MASKED = -1e30
 
 
-def cut_kernel(hidden, w_key, w_value, w_out, h_out, sems):
-    group = lax.axis_index("groups")
+def cut_kernel(hidden, h_out, staged, sems):
     me = lax.axis_index("seq")
     core = lax.rem(lax.axis_index("tp"), 2)
-    depth = w_key.shape[0]
-    half = w_out.shape[1]
-    rows = h_out.shape[1]
-    copies = []
-    for i, weight in enumerate((w_key, w_value)):
-        source = weight.at[pl.ds(pl.multiple_of(group * half, half), half)]
-        copies.append(pltpu.make_async_copy(source, w_out.at[i], sems.at[i]))
+    rows, depth = h_out.shape[1:]
     first = me + 1 - 2 * lax.rem(me, 2)
     second = lax.rem(first + 2, 4)
+    fetches, stores = [], []
     for i, block in enumerate((first, second)):
         source = hidden.at[
             0,
             pl.ds(pl.multiple_of(core * rows, rows), rows),
             pl.ds(pl.multiple_of(block * depth, depth), depth),
         ]
-        copies.append(pltpu.make_async_copy(source, h_out.at[i], sems.at[2 + i]))
-    for copy in copies:
-        copy.start()
-    for copy in copies:
-        copy.wait()
-
-
-def cut(hidden, w_key, w_value):
-    depth = w_key.shape[0]
+        fetches.append(pltpu.make_async_copy(source, staged.at[i], sems.at[i]))
+        stores.append(pltpu.make_async_copy(staged.at[i], h_out.at[i], sems.at[2 + i]))
+    for fetch in fetches:
+        fetch.start()
+    for fetch, store in zip(fetches, stores):
+        fetch.wait()
+        store.start()
+    for store in stores:
+        store.wait()
+
+
+def cut(hidden, depth):
+    shape = (2, hidden.shape[1] // 2, depth)
     return pl.pallas_call(
         cut_kernel,
-        out_shape=(
-            jax.ShapeDtypeStruct((2, depth // 2, w_key.shape[1]), jnp.bfloat16),
-            jax.ShapeDtypeStruct((2, hidden.shape[1] // 2, depth), jnp.bfloat16),
-        ),
-        in_specs=[ANY] * 3,
-        out_specs=(VMEM, VMEM),
-        scratch_shapes=[pltpu.SemaphoreType.DMA((4,))],
+        out_shape=jax.ShapeDtypeStruct(shape, jnp.bfloat16),
+        in_specs=[ANY],
+        out_specs=ANY,
+        scratch_shapes=[pltpu.VMEM(shape, jnp.bfloat16), pltpu.SemaphoreType.DMA((4,))],
         name="cut",
-    )(hidden, w_key, w_value)
+    )(hidden)
+
+
+def gate_kernel(*refs):
+    pass
+
+
+def gate(arrays, first):
+    return pl.pallas_call(
+        gate_kernel,
+        out_shape=tuple(jax.ShapeDtypeStruct(one.shape, one.dtype) for one in arrays),
+        in_specs=[ANY] * (len(arrays) + len(first)),
+        out_specs=(ANY,) * len(arrays),
+        input_output_aliases={i: i for i in range(len(arrays))},
+        name="gate",
+    )(*arrays, *first)
 
 
 def docs_kernel(by_owner, request_docs, store_keys, store_values, *rest):
@@ -123,43 +133,56 @@
     )(request_docs, store_keys, store_values)
 
 
-def project_kernel(hidden, w_key, w_value, w_mine, w_other, h_mine, h_other, own, part, w, h, sems):
+def project_kernel(
+    hidden, w_key, w_value, k_far, v_far, k_swapped, v_swapped, h_mine, h_other, own, part, w, h, sems
+):
     group = lax.axis_index("groups")
     me = lax.axis_index("seq")
     core = lax.rem(lax.axis_index("tp"), 2)
     depth, width = w_key.shape
-    half = depth // 2
     rows = hidden.shape[1]
     far = lax.rem(me + 2, 4)
-    copies = []
-
-    def copy(source, target):
-        copies.append(pltpu.make_async_copy(source, target, sems.at[len(copies)]))
-
-    for i, weight in enumerate((w_key, w_value)):
-        columns = pl.ds(i * width, width)
-        copy(weight, w.at[pl.ds(0, depth), columns])
-        for held, place in ((w_mine, group), (w_other, 1 - group)):
-            copy(held.at[i], w.at[pl.ds(pl.multiple_of(depth + place * half, half), half), columns])
+    near = pl.ds(0, depth)
+    rest = pl.ds(depth, depth)
+    keys = pl.ds(0, width)
+    values = pl.ds(width, width)
+    copies = [
+        pltpu.make_async_copy(w_key, w.at[near, keys], sems.at[0]),
+        pltpu.make_async_copy(w_value, w.at[near, values], sems.at[1]),
+    ]
     for i, block in enumerate((me, far)):
         columns = pl.ds(i * depth, depth)
-        copy(
-            hidden.at[0, :, pl.ds(pl.multiple_of(block * depth, depth), depth)],
-            h.at[pl.ds(0, rows), columns],
+        source = hidden.at[0, :, pl.ds(pl.multiple_of(block * depth, depth), depth)]
+        copies.append(
+            pltpu.make_async_copy(source, h.at[pl.ds(0, rows), columns], sems.at[2 + 3 * i])
         )
-        for held, place in ((h_mine, core), (h_other, 1 - core)):
-            start = rows + place * (rows // 2)
-            copy(held.at[i], h.at[pl.ds(pl.multiple_of(start, rows // 2), rows // 2), columns])
+        for k, (held, place) in enumerate(((h_mine, core), (h_other, 1 - core))):
+            start = pl.multiple_of(rows + place * (rows // 2), rows // 2)
+            target = h.at[pl.ds(start, rows // 2), columns]
+            copies.append(pltpu.make_async_copy(held.at[i], target, sems.at[3 + 3 * i + k]))
     for one in copies:
         one.start()
+
+    @pl.when(group == 0)
+    def _():
+        pltpu.make_async_copy(k_far, w.at[rest, keys], sems.at[8]).start()
+        pltpu.make_async_copy(v_swapped, w.at[rest, values], sems.at[9]).start()
+
+    @pl.when(group != 0)
+    def _():
+        pltpu.make_async_copy(k_swapped, w.at[rest, keys], sems.at[8]).start()
+        pltpu.make_async_copy(v_far, w.at[rest, values], sems.at[9]).start()
+
     for one in copies:
         one.wait()
+    pltpu.make_async_copy(k_far, w.at[rest, keys], sems.at[8]).wait()
+    pltpu.make_async_copy(v_far, w.at[rest, values], sems.at[9]).wait()
     total = jnp.dot(h[...], w[...], preferred_element_type=jnp.float32)
     own[...] = total[:rows]
     part[...] = total[rows:].astype(part.dtype)
 
 
-def project(hidden, w_key, w_value, w_mine, w_other, h_mine, h_other):
+def project(hidden, w_key, w_value, *arrived):
     depth, width = w_key.shape
     rows = hidden.shape[1]
     return pl.pallas_call(
@@ -168,16 +191,16 @@
             jax.ShapeDtypeStruct((rows, 2 * width), jnp.float32),
             jax.ShapeDtypeStruct((rows, 2 * width), jnp.bfloat16),
         ),
-        in_specs=[ANY] * 7,
+        in_specs=[ANY] * (3 + len(arrived)),
         out_specs=(VMEM, VMEM),
         scratch_shapes=[
             pltpu.VMEM((2 * depth, 2 * width), jnp.bfloat16),
             pltpu.VMEM((2 * rows, 2 * depth), jnp.bfloat16),
-            pltpu.SemaphoreType.DMA((12,)),
+            pltpu.SemaphoreType.DMA((10,)),
         ],
         compiler_params=pltpu.CompilerParams(vmem_limit_bytes=32 * 1024 * 1024),
         name="project",
-    )(hidden, w_key, w_value, w_mine, w_other, h_mine, h_other)
+    )(hidden, w_key, w_value, *arrived)
 
 
 def attend_kernel(
@@ -324,14 +347,19 @@
             count = lax.axis_size(axis)
             return lax.ppermute(array, axis, [(i, i ^ apart) for i in range(count)])
 
-        w_send, h_send = cut(hidden, w_key, w_value)
-        w_mine = swap(w_send, "seq", 2)
-        h_mine = swap(h_send, "seq", 1)
+        both = ("groups", "seq")
+        k_far = lax.ppermute(w_key, both, [(s, s ^ 2) for s in range(4)])
+        v_far = lax.ppermute(w_value, both, [(4 + s, 4 + (s ^ 2)) for s in range(4)])
+        h_mine = swap(cut(hidden, w_key.shape[0]), "seq", 1)
+        k_swapped = lax.ppermute(k_far, "groups", [(0, 1)])
+        v_swapped = lax.ppermute(v_far, "groups", [(1, 0)])
         docs = cut_docs(request_docs, store_keys, store_values, False)
+        docs = gate(docs, (k_far, v_far))
         docs = [swap(doc, "seq", k + 1) for k, doc in enumerate(docs)]
-        w_other = swap(w_mine, "groups", 1)
         h_other = swap(h_mine, "tp", 1)
-        own, part = project(hidden, w_key, w_value, w_mine, w_other, h_mine, h_other)
+        own, part = project(
+            hidden, w_key, w_value, k_far, v_far, k_swapped, v_swapped, h_mine, h_other
+        )
         fresh = (own + swap(part, "seq", 1).astype(jnp.float32)).astype(jnp.bfloat16)
         sources = (store_keys, store_values, *docs)
     else:

time: 83.4 us -> 98 us (1.18)
  the two profiles are of different devices: /device:TPU:0 before, /device:TPU:16 now
where the time goes in v3:
time: 98 us; the launch traced here: 97.5 us
  waiting for transfers between devices  49.8 us (51%)
  starting transfers between devices  23.6 us (24%)
  Pallas kernels  15.8 us (16%)
  local copies, waits for them, and re-layouts  6.16 us (6%)
  other arithmetic  1.18 us (1%)
    ppermute x6, waiting for transfers between devices, swap(): return lax.ppermute(array, axis, [(i, i ^ apart) for i in range(count)])  40.1 us
    ppermute x6, starting transfers between devices, swap(): return lax.ppermute(array, axis, [(i, i ^ apart) for i in range(count)])  7.74 us
    pallas_call x1, Pallas kernels, attend(): pl.pallas_call(functools.partial(attend_kernel, by_owner), out_shape=jax....  7.41 us
    all_to_all x1, starting transfers between devices, shards(): lax.all_to_all(outgoing, 'seq', split_axis=0, concat_axis=0, tiled=True)  6.6 us
    ppermute x1, waiting for transfers between devices, shards(): v_swapped = lax.ppermute(v_far, 'groups', [(1, 0)])  4.9 us
    ppermute x1, waiting for transfers between devices, shards(): k_swapped = lax.ppermute(k_far, 'groups', [(0, 1)])  4.8 us
    ppermute x1, starting transfers between devices, shards(): k_swapped = lax.ppermute(k_far, 'groups', [(0, 1)])  4.23 us
    unnamed x25, local copies, waits for them, and re-layouts  3.53 us
  transfers between devices with their start and end apart: 11, of which 6 were waited for; matrix products, arithmetic and copies ran while one was open for 5% of the time, Pallas kernels for 11%

profile of v3, /device:TPU:16, one launch (start us, length us, event | category | flops | bytes accessed | tf_op | source)
XLA Modules:
  0.0 97.5 jit_solution(5433494922276494070)
XLA Ops:
  0.7 2.1 %cut.1 = bf16[2,96,2048]{2,1,0:T(8,128)(2,1)} custom-call(bf16[1,192,8192]{2,1,0:T(8,128)(2,1)} %hidden.3), custom_call_target="tpu_custom_call" | custom-call | tf_op jit(solution)/shard_map/cut/pallas_call | solution.py:43
  2.8 1.6 %collective-permute-start.4 = (bf16[2,96,2048]{2,1,0:T(8,128)(2,1)}, bf16[2,96,2048]{2,1,0:T(8,128)(2,1)}, u32[]{:S(2)}, u32[]{:S(2)}) collective-permute-start(bf16[2,96,2048]{2,1,0:T(8,128)(2,1)} %cut.1), channel_id=1, source_target_pairs={{0,4},{4,0},{8,12},{12,8},{1,5},{5,1},{9,13},{13,9},{2,6},{6,2},{1... | collective-permute-start | bytes 2359304 | tf_op jit(solution)/shard_map/ppermute | solution.py:348
  4.5 2.2 %collective-permute-start = (bf16[2048,128]{1,0:T(8,128)(2,1)}, bf16[2048,128]{1,0:T(8,128)(2,1)}, u32[]{:S(2)}, u32[]{:S(2)}) collective-permute-start(bf16[2048,128]{1,0:T(8,128)(2,1)} %w_key.1), channel_id=1, source_target_pairs={{0,8},{4,12},{8,0},{12,4},{1,9},{5,13},{9,1},{13,5},{2,10},{6,14},... | collective-permute-start | bytes 1572872 | tf_op jit(solution)/shard_map/ppermute | solution.py:351
  6.7 1.5 %collective-permute-start.1 = (bf16[2048,128]{1,0:T(8,128)(2,1)}, bf16[2048,128]{1,0:T(8,128)(2,1)}, u32[]{:S(2)}, u32[]{:S(2)}) collective-permute-start(bf16[2048,128]{1,0:T(8,128)(2,1)} %w_value.1), channel_id=1, source_target_pairs={{16,24},{20,28},{24,16},{28,20},{17,25},{21,29},{25,17},{29,21},{1... | collective-permute-start | bytes 1572872 | tf_op jit(solution)/shard_map/ppermute | solution.py:352
  8.2 24.6 %collective-permute-done.4.h_mine = bf16[2,96,2048]{2,1,0:T(8,128)(2,1)} collective-permute-done((bf16[2,96,2048]{2,1,0:T(8,128)(2,1)}, bf16[2,96,2048]{2,1,0:T(8,128)(2,1)}, u32[]{:S(2)}, u32[]{:S(2)}) %collective-permute-start.4) | collective-permute-done | bytes 786464 | tf_op jit(solution)/shard_map/ppermute | solution.py:348
  33.7 4.2 %collective-permute-start.2 = (bf16[2048,128]{1,0:T(8,128)(2,1)}, bf16[2048,128]{1,0:T(8,128)(2,1)}, u32[]{:S(2)}, u32[]{:S(2)}) collective-permute-start(bf16[2048,128]{1,0:T(8,128)(2,1)} %collective-permute-done.k_far.refs_3_), channel_id=1, source_target_pairs={{0,16},{1,17},{2,18},{3,19},{4,20},{5,21},{6,22},{7,23},{8,24},{9,... | collective-permute-start | bytes 1572872 | tf_op jit(solution)/shard_map/ppermute | solution.py:354
  37.9 1.3 %collective-permute-start.3 = (bf16[2048,128]{1,0:T(8,128)(2,1)}, bf16[2048,128]{1,0:T(8,128)(2,1)}, u32[]{:S(2)}, u32[]{:S(2)}) collective-permute-start(bf16[2048,128]{1,0:T(8,128)(2,1)} %collective-permute-done.1.v_far.refs_4_), channel_id=1, source_target_pairs={{16,0},{17,1},{18,2},{19,3},{20,4},{21,5},{22,6},{23,7},{24,8},{25... | collective-permute-start | bytes 1572872 | tf_op jit(solution)/shard_map/ppermute | solution.py:355
  40.0 3.2 %cut_docs.1 = (bf16[4,2,128,128]{3,2,1,0:T(8,128)(2,1)}, bf16[4,2,128,128]{3,2,1,0:T(8,128)(2,1)}, bf16[4,2,128,128]{3,2,1,0:T(8,128)(2,1)}) custom-call(s32[4,16]{1,0:T(4,128)} %request_docs.3, bf16[8,128,128]{2,1,0:T(8,128)(2,1)} %rest_0_.1, bf16[8,128,128]{2,1,0:T(8,128)(2,1)} %rest_1_.1), custom_call_target="tpu_custom_call" | custom-call | tf_op jit(solution)/shard_map/cut_docs/pallas_call | solution.py:123
  43.2 1.2 %gather_fusion = s32[16]{0:T(128)} fusion(s32[32]{0:T(128)S(1)} %copy-done, s32[1024]{0:T(1024)S(1)} %pad_clamp_fusion), kind=kCustom, calls=%fused_computation | custom fusion | bytes 192 | tf_op jit(solution)/shard_map/gather | solution.py:379
  44.5 4.8 %collective-permute-done.2.k_swapped = bf16[2048,128]{1,0:T(8,128)(2,1)} collective-permute-done((bf16[2048,128]{1,0:T(8,128)(2,1)}, bf16[2048,128]{1,0:T(8,128)(2,1)}, u32[]{:S(2)}, u32[]{:S(2)}) %collective-permute-start.2) | collective-permute-done | bytes 524320 | tf_op jit(solution)/shard_map/ppermute | solution.py:354
  49.3 4.9 %collective-permute-done.3.v_swapped = bf16[2048,128]{1,0:T(8,128)(2,1)} collective-permute-done((bf16[2048,128]{1,0:T(8,128)(2,1)}, bf16[2048,128]{1,0:T(8,128)(2,1)}, u32[]{:S(2)}, u32[]{:S(2)}) %collective-permute-start.3) | collective-permute-done | bytes 524320 | tf_op jit(solution)/shard_map/ppermute | solution.py:355
  54.2 1.0 %copy-done.4 = bf16[2048,128]{1,0:T(8,128)(2,1)S(1)} copy-done((bf16[2048,128]{1,0:T(8,128)(2,1)S(1)}, bf16[2048,128]{1,0:T(8,128)(2,1)}, u32[]{:S(2)}) %copy-start.4) | copy-done | bytes 524312
  55.2 1.0 %copy-done.5 = bf16[2048,128]{1,0:T(8,128)(2,1)S(1)} copy-done((bf16[2048,128]{1,0:T(8,128)(2,1)S(1)}, bf16[2048,128]{1,0:T(8,128)(2,1)}, u32[]{:S(2)}) %copy-start.5) | copy-done | bytes 524312
  56.3 3.0 %project.1 = (f32[192,256]{1,0:T(8,128)S(1)}, bf16[192,256]{1,0:T(8,128)(2,1)S(1)}) custom-call(bf16[1,192,8192]{2,1,0:T(8,128)(2,1)S(1)} %copy-done.1, bf16[2048,128]{1,0:T(8,128)(2,1)S(1)} %copy-done.4, bf16[2048,128]{1,0:T(8,128)(2,1)S(1)} %copy-done.5, bf16[2048,128]{1,0:T(8,128)(2,1)} %collective-permute-done.k_far.refs_3_, ...), custom_call_target="tpu_custom_call" | custom-call | tf_op jit(solution)/shard_map/project/pallas_call | solution.py:188
  59.4 2.5 %collective-permute-start.6 = (bf16[192,256]{1,0:T(8,128)(2,1)S(1)}, bf16[192,256]{1,0:T(8,128)(2,1)S(1)}, u32[]{:S(2)}, u32[]{:S(2)}) collective-permute-start(bf16[192,256]{1,0:T(8,128)(2,1)S(1)} %get-tuple-element.11), channel_id=1, source_target_pairs={{0,4},{4,0},{8,12},{12,8},{1,5},{5,1},{9,13},{13,9},{2,6},{6,2},{1... | collective-permute-start | bytes 294920 | tf_op jit(solution)/shard_map/ppermute | solution.py:348
  62.1 0.8 collective-permute-start.8
  62.9 2.7 %collective-permute-start.9 = (bf16[4,2,128,128]{3,2,1,0:T(8,128)(2,1)}, bf16[4,2,128,128]{3,2,1,0:T(8,128)(2,1)S(1)}, u32[]{:S(2)}, u32[]{:S(2)}) collective-permute-start(bf16[4,2,128,128]{3,2,1,0:T(8,128)(2,1)} %get-tuple-element.17), channel_id=1, source_target_pairs={{0,12},{4,8},{8,4},{12,0},{1,13},{5,9},{9,5},{13,1},{2,14},{6,10},... | collective-permute-start | bytes 786440 | tf_op jit(solution)/shard_map/ppermute | solution.py:348
  65.6 2.2 %collective-permute-done.6 = bf16[192,256]{1,0:T(8,128)(2,1)S(1)} collective-permute-done((bf16[192,256]{1,0:T(8,128)(2,1)S(1)}, bf16[192,256]{1,0:T(8,128)(2,1)S(1)}, u32[]{:S(2)}, u32[]{:S(2)}) %collective-permute-start.6) | collective-permute-done | bytes 98336 | tf_op jit(solution)/shard_map/ppermute | solution.py:348
  68.7 6.6 %all-to-all-start = ((bf16[4,4,12,256]{3,1,2,0:T(4,128)(2,1)}), bf16[4,4,12,256]{3,1,2,0:T(4,128)(2,1)S(1)}, u32[]{:S(2)}, u32[]{:S(2)}) async-start(bf16[4,4,12,256]{3,1,2,0:T(4,128)(2,1)} %copy.40), calls=%async_computation | async-start | bytes 196608 | tf_op jit(solution)/shard_map/all_to_all | solution.py:401
  75.3 0.7 fusion.3
  76.1 5.8 %collective-permute-done.8.rest_3_ = bf16[4,2,128,128]{3,2,1,0:T(8,128)(2,1)S(1)} collective-permute-done((bf16[4,2,128,128]{3,2,1,0:T(8,128)(2,1)}, bf16[4,2,128,128]{3,2,1,0:T(8,128)(2,1)S(1)}, u32[]{:S(2)}, u32[]{:S(2)}) %collective-permute-start.8) | collective-permute-done | bytes 262176 | tf_op jit(solution)/shard_map/ppermute | solution.py:348
  81.8 7.5 %collective-permute-done.9.rest_4_ = bf16[4,2,128,128]{3,2,1,0:T(8,128)(2,1)S(1)} collective-permute-done((bf16[4,2,128,128]{3,2,1,0:T(8,128)(2,1)}, bf16[4,2,128,128]{3,2,1,0:T(8,128)(2,1)S(1)}, u32[]{:S(2)}, u32[]{:S(2)}) %collective-permute-start.9) | collective-permute-done | bytes 262176 | tf_op jit(solution)/shard_map/ppermute | solution.py:348
  89.3 7.4 %attend.1 = bf16[1,192,1024]{2,1,0:T(8,128)(2,1)} custom-call(s32[4,16]{1,0:T(4,128)S(1)} %copy-done.8, bf16[1,192,1024]{2,1,0:T(8,128)(2,1)S(1)} %copy-done.6, bf16[192,256]{1,0:T(8,128)(2,1)S(1)} %add_convert_fusion.fresh, f32[1,2048]{1,0:T(1,128)S(1)} %bitcast.23, s32[192,1]{1,0:T(8,128)S(1)} %copy.39.row_place, s32[1,192]{1,0:T(1,128)S(1)} %add.73.key_place, ...), custom_call_target="tpu_custom_call" | custom-call | tf_op jit(solution)/shard_map/attend/pallas_call | solution.py:308
  96.8 0.7 copy.41
  (53 shorter events, 2.8 us)
Async XLA Ops:
  0.6 42.6 %copy-start = (s32[32]{0:T(128)S(1)}, s32[32]{0:T(128)}, u32[]{:S(2)}) copy-start(s32[32]{0:T(128)} %param.16) | copy-start | bytes 388
  0.6 53.5 %copy-start.1 = (bf16[1,192,8192]{2,1,0:T(8,128)(2,1)S(1)}, bf16[1,192,8192]{2,1,0:T(8,128)(2,1)}, u32[]{:S(2)}) copy-start(bf16[1,192,8192]{2,1,0:T(8,128)(2,1)} %hidden.3) | copy-start | bytes 9437188
  0.7 7.5 %copy-start.7 = (s32[4,16]{1,0:T(4,128)S(1)}, s32[4,16]{1,0:T(4,128)}, u32[]{:S(2)}) copy-start(s32[4,16]{1,0:T(4,128)} %request_docs.3) | copy-start | bytes 772
  0.7 42.5 %copy-start.8 = (s32[4,16]{1,0:T(4,128)S(1)}, s32[4,16]{1,0:T(4,128)}, u32[]{:S(2)}) copy-start(s32[4,16]{1,0:T(4,128)} %request_docs.3) | copy-start | bytes 772
  0.7 32.3 %copy-start.10 = (s32[1,16,12]{1,0,2:T(1,128)S(1)}, s32[1,16,12]{1,0,2:T(1,128)}, u32[]{:S(2)}) copy-start(s32[1,16,12]{1,0,2:T(1,128)} %param.17) | copy-start | bytes 2308
  2.8 30.0 %collective-permute-start.4 = (bf16[2,96,2048]{2,1,0:T(8,128)(2,1)}, bf16[2,96,2048]{2,1,0:T(8,128)(2,1)}, u32[]{:S(2)}, u32[]{:S(2)}) collective-permute-start(bf16[2,96,2048]{2,1,0:T(8,128)(2,1)} %cut.1), channel_id=1, source_target_pairs={{0,4},{4,0},{8,12},{12,8},{1,5},{5,1},{9,13},{13,9},{2,6},{6,2},{1... | collective-permute-start | bytes 2359304 | tf_op jit(solution)/shard_map/ppermute | solution.py:348
  4.5 29.2 %collective-permute-start = (bf16[2048,128]{1,0:T(8,128)(2,1)}, bf16[2048,128]{1,0:T(8,128)(2,1)}, u32[]{:S(2)}, u32[]{:S(2)}) collective-permute-start(bf16[2048,128]{1,0:T(8,128)(2,1)} %w_key.1), channel_id=1, source_target_pairs={{0,8},{4,12},{8,0},{12,4},{1,9},{5,13},{9,1},{13,5},{2,10},{6,14},... | collective-permute-start | bytes 1572872 | tf_op jit(solution)/shard_map/ppermute | solution.py:351
  6.7 31.2 %collective-permute-start.1 = (bf16[2048,128]{1,0:T(8,128)(2,1)}, bf16[2048,128]{1,0:T(8,128)(2,1)}, u32[]{:S(2)}, u32[]{:S(2)}) collective-permute-start(bf16[2048,128]{1,0:T(8,128)(2,1)} %w_value.1), channel_id=1, source_target_pairs={{16,24},{20,28},{24,16},{28,20},{17,25},{21,29},{25,17},{29,21},{1... | collective-permute-start | bytes 1572872 | tf_op jit(solution)/shard_map/ppermute | solution.py:352
  32.8 21.4 %collective-permute-start.5 = (bf16[2,96,2048]{2,1,0:T(8,128)(2,1)}, bf16[2,96,2048]{2,1,0:T(8,128)(2,1)}, u32[]{:S(2)}, u32[]{:S(2)}) collective-permute-start(bf16[2,96,2048]{2,1,0:T(8,128)(2,1)} %collective-permute-done.4.h_mine), channel_id=1, source_target_pairs={{0,1},{1,0},{2,3},{3,2},{4,5},{5,4},{6,7},{7,6},{8,9},{9,8},{10,11... | collective-permute-start | bytes 2359304 | tf_op jit(solution)/shard_map/ppermute | solution.py:348
  33.7 15.6 %collective-permute-start.2 = (bf16[2048,128]{1,0:T(8,128)(2,1)}, bf16[2048,128]{1,0:T(8,128)(2,1)}, u32[]{:S(2)}, u32[]{:S(2)}) collective-permute-start(bf16[2048,128]{1,0:T(8,128)(2,1)} %collective-permute-done.k_far.refs_3_), channel_id=1, source_target_pairs={{0,16},{1,17},{2,18},{3,19},{4,20},{5,21},{6,22},{7,23},{8,24},{9,... | collective-permute-start | bytes 1572872 | tf_op jit(solution)/shard_map/ppermute | solution.py:354
  37.9 16.3 %collective-permute-start.3 = (bf16[2048,128]{1,0:T(8,128)(2,1)}, bf16[2048,128]{1,0:T(8,128)(2,1)}, u32[]{:S(2)}, u32[]{:S(2)}) collective-permute-start(bf16[2048,128]{1,0:T(8,128)(2,1)} %collective-permute-done.1.v_far.refs_4_), channel_id=1, source_target_pairs={{16,0},{17,1},{18,2},{19,3},{20,4},{21,5},{22,6},{23,7},{24,8},{25... | collective-permute-start | bytes 1572872 | tf_op jit(solution)/shard_map/ppermute | solution.py:355
  54.2 1.0 %copy-start.4 = (bf16[2048,128]{1,0:T(8,128)(2,1)S(1)}, bf16[2048,128]{1,0:T(8,128)(2,1)}, u32[]{:S(2)}) copy-start(bf16[2048,128]{1,0:T(8,128)(2,1)} %w_key.1) | copy-start | bytes 1572868
  55.2 1.0 %copy-start.5 = (bf16[2048,128]{1,0:T(8,128)(2,1)S(1)}, bf16[2048,128]{1,0:T(8,128)(2,1)}, u32[]{:S(2)}) copy-start(bf16[2048,128]{1,0:T(8,128)(2,1)} %w_value.1) | copy-start | bytes 1572868
  56.3 5.6 %copy-start.9 = (s32[1,16,12]{1,2,0:T(8,128)S(1)}, s32[1,16,12]{1,2,0:T(8,128)}, u32[]{:S(2)}) copy-start(s32[1,16,12]{1,2,0:T(8,128)} %copy.44) | copy-start | bytes 2308
  59.3 30.0 %copy-start.2 = (bf16[8,128,128]{2,1,0:T(8,128)(2,1)S(1)}, bf16[8,128,128]{2,1,0:T(8,128)(2,1)}, u32[]{:S(2)}) copy-start(bf16[8,128,128]{2,1,0:T(8,128)(2,1)} %rest_0_.1) | copy-start | bytes 786436
  59.3 30.0 %copy-start.3 = (bf16[8,128,128]{2,1,0:T(8,128)(2,1)S(1)}, bf16[8,128,128]{2,1,0:T(8,128)(2,1)}, u32[]{:S(2)}) copy-start(bf16[8,128,128]{2,1,0:T(8,128)(2,1)} %rest_1_.1) | copy-start | bytes 786436
  59.3 30.0 %copy-start.6 = (bf16[1,192,1024]{2,1,0:T(8,128)(2,1)S(1)}, bf16[1,192,1024]{2,1,0:T(8,128)(2,1)}, u32[]{:S(2)}) copy-start(bf16[1,192,1024]{2,1,0:T(8,128)(2,1)} %queries.1) | copy-start | bytes 1179652
  59.4 8.4 %collective-permute-start.6 = (bf16[192,256]{1,0:T(8,128)(2,1)S(1)}, bf16[192,256]{1,0:T(8,128)(2,1)S(1)}, u32[]{:S(2)}, u32[]{:S(2)}) collective-permute-start(bf16[192,256]{1,0:T(8,128)(2,1)S(1)} %get-tuple-element.11), channel_id=1, source_target_pairs={{0,4},{4,0},{8,12},{12,8},{1,5},{5,1},{9,13},{13,9},{2,6},{6,2},{1... | collective-permute-start | bytes 294920 | tf_op jit(solution)/shard_map/ppermute | solution.py:348
  62.0 14.1 %collective-permute-start.7 = (bf16[4,2,128,128]{3,2,1,0:T(8,128)(2,1)}, bf16[4,2,128,128]{3,2,1,0:T(8,128)(2,1)S(1)}, u32[]{:S(2)}, u32[]{:S(2)}) collective-permute-start(bf16[4,2,128,128]{3,2,1,0:T(8,128)(2,1)} %get-tuple-element.15), channel_id=1, source_target_pairs={{0,4},{4,0},{8,12},{12,8},{1,5},{5,1},{9,13},{13,9},{2,6},{6,2},{1... | collective-permute-start | bytes 786440 | tf_op jit(solution)/shard_map/ppermute | solution.py:348
  62.1 19.7 %collective-permute-start.8 = (bf16[4,2,128,128]{3,2,1,0:T(8,128)(2,1)}, bf16[4,2,128,128]{3,2,1,0:T(8,128)(2,1)S(1)}, u32[]{:S(2)}, u32[]{:S(2)}) collective-permute-start(bf16[4,2,128,128]{3,2,1,0:T(8,128)(2,1)} %get-tuple-element.16), channel_id=1, source_target_pairs={{0,8},{4,12},{8,0},{12,4},{1,9},{5,13},{9,1},{13,5},{2,10},{6,14},... | collective-permute-start | bytes 786440 | tf_op jit(solution)/shard_map/ppermute | solution.py:348
  62.9 26.4 %collective-permute-start.9 = (bf16[4,2,128,128]{3,2,1,0:T(8,128)(2,1)}, bf16[4,2,128,128]{3,2,1,0:T(8,128)(2,1)S(1)}, u32[]{:S(2)}, u32[]{:S(2)}) collective-permute-start(bf16[4,2,128,128]{3,2,1,0:T(8,128)(2,1)} %get-tuple-element.17), channel_id=1, source_target_pairs={{0,12},{4,8},{8,4},{12,0},{1,13},{5,9},{9,5},{13,1},{2,14},{6,10},... | collective-permute-start | bytes 786440 | tf_op jit(solution)/shard_map/ppermute | solution.py:348
  68.7 28.0 %all-to-all-start = ((bf16[4,4,12,256]{3,1,2,0:T(4,128)(2,1)}), bf16[4,4,12,256]{3,1,2,0:T(4,128)(2,1)S(1)}, u32[]{:S(2)}, u32[]{:S(2)}) async-start(bf16[4,4,12,256]{3,1,2,0:T(4,128)(2,1)} %copy.40), calls=%async_computation | async-start | bytes 196608 | tf_op jit(solution)/shard_map/all_to_all | solution.py:401

commit v4 on v3

--- a/solution.py
+++ b/solution.py
@@ -54,15 +54,15 @@
     pass
 
 
-def gate(arrays, first):
+def gate(arrays):
     return pl.pallas_call(
         gate_kernel,
         out_shape=tuple(jax.ShapeDtypeStruct(one.shape, one.dtype) for one in arrays),
-        in_specs=[ANY] * (len(arrays) + len(first)),
+        in_specs=[ANY] * len(arrays),
         out_specs=(ANY,) * len(arrays),
         input_output_aliases={i: i for i in range(len(arrays))},
         name="gate",
-    )(*arrays, *first)
+    )(*arrays)
 
 
 def docs_kernel(by_owner, request_docs, store_keys, store_values, *rest):
@@ -199,6 +199,7 @@
             pltpu.SemaphoreType.DMA((10,)),
         ],
         compiler_params=pltpu.CompilerParams(vmem_limit_bytes=32 * 1024 * 1024),
+        cost_estimate=pl.CostEstimate(flops=1, bytes_accessed=1, transcendentals=0),
         name="project",
     )(hidden, w_key, w_value, *arrived)
 
@@ -351,17 +352,17 @@
         k_far = lax.ppermute(w_key, both, [(s, s ^ 2) for s in range(4)])
         v_far = lax.ppermute(w_value, both, [(4 + s, 4 + (s ^ 2)) for s in range(4)])
         h_mine = swap(cut(hidden, w_key.shape[0]), "seq", 1)
+        (docs,) = cut_docs(request_docs, store_keys, store_values, True)
+        docs, k_far, v_far = gate((docs, k_far, v_far))
         k_swapped = lax.ppermute(k_far, "groups", [(0, 1)])
         v_swapped = lax.ppermute(v_far, "groups", [(1, 0)])
-        docs = cut_docs(request_docs, store_keys, store_values, False)
-        docs = gate(docs, (k_far, v_far))
-        docs = [swap(doc, "seq", k + 1) for k, doc in enumerate(docs)]
+        docs = lax.all_to_all(docs, "seq", split_axis=0, concat_axis=0, tiled=True)
         h_other = swap(h_mine, "tp", 1)
         own, part = project(
             hidden, w_key, w_value, k_far, v_far, k_swapped, v_swapped, h_mine, h_other
         )
         fresh = (own + swap(part, "seq", 1).astype(jnp.float32)).astype(jnp.bfloat16)
-        sources = (store_keys, store_values, *docs)
+        sources = (docs,)
     else:
         (docs,) = cut_docs(request_docs, store_keys, store_values, True)
         sources = (lax.all_to_all(docs, "seq", split_axis=0, concat_axis=0, tiled=True),)
@@ -388,7 +389,7 @@
         place.reshape(row_count, 1),
         place.reshape(1, row_count),
         sources,
-        not pairs,
+        True,
     )
 
     slot_of_row = jnp.repeat(owners * capacity + ranks, per_doc) * per_doc + jnp.tile(

time: 98 us -> 113 us (1.15)
  the two profiles are of different devices: /device:TPU:16 before, /device:TPU:0 now
where the time goes in v4:
time: 113 us; the launch traced here: 112 us
  waiting for transfers between devices  62.8 us (56%)
  starting transfers between devices  17.4 us (15%)
  Pallas kernels  15.5 us (14%)
  blocking collectives  10.5 us (9%)
  local copies, waits for them, and re-layouts  4.32 us (4%)
    ppermute x3, waiting for transfers between devices, swap(): return lax.ppermute(array, axis, [(i, i ^ apart) for i in range(count)])  27.6 us
    all_to_all x1, waiting for transfers between devices, shards(): docs = lax.all_to_all(docs, 'seq', split_axis=0, concat_axis=0, tiled=True)  20.6 us
    ppermute x1, waiting for transfers between devices, shards(): k_swapped = lax.ppermute(k_far, 'groups', [(0, 1)])  10.6 us
    all_to_all x1, blocking collectives, shards(): lax.all_to_all(outgoing, 'seq', split_axis=0, concat_axis=0, tiled=True)  10.5 us
    pallas_call x1, Pallas kernels, attend(): pl.pallas_call(functools.partial(attend_kernel, by_owner), out_shape=jax....  7.12 us
    ppermute x1, starting transfers between devices, shards(): k_far = lax.ppermute(w_key, both, [(s, s ^ 2) for s in range(4)])  4.49 us
    ppermute x1, waiting for transfers between devices, shards(): v_swapped = lax.ppermute(v_far, 'groups', [(1, 0)])  4.04 us
    all_to_all x1, starting transfers between devices, shards(): docs = lax.all_to_all(docs, 'seq', split_axis=0, concat_axis=0, tiled=True)  3.52 us
  transfers between devices with their start and end apart: 8, of which 5 were waited for; matrix products, arithmetic and copies ran while one was open for 2% of the time, Pallas kernels for 3%

profile of v4, /device:TPU:0, one launch (start us, length us, event | category | flops | bytes accessed | tf_op | source)
XLA Modules:
  0.0 112.1 jit_solution(2471003978637307893)
XLA Ops:
  0.7 2.1 %cut.1 = bf16[2,96,2048]{2,1,0:T(8,128)(2,1)} custom-call(bf16[1,192,8192]{2,1,0:T(8,128)(2,1)} %hidden.3), custom_call_target="tpu_custom_call" | custom-call | tf_op jit(solution)/shard_map/cut/pallas_call | solution.py:43
  2.8 3.1 %collective-permute-start.4 = (bf16[2,96,2048]{2,1,0:T(8,128)(2,1)}, bf16[2,96,2048]{2,1,0:T(8,128)(2,1)}, u32[]{:S(2)}, u32[]{:S(2)}) collective-permute-start(bf16[2,96,2048]{2,1,0:T(8,128)(2,1)} %cut.1), channel_id=1, source_target_pairs={{0,4},{4,0},{8,12},{12,8},{1,5},{5,1},{9,13},{13,9},{2,6},{6,2},{1... | collective-permute-start | bytes 2359304 | tf_op jit(solution)/shard_map/ppermute | solution.py:349
  5.8 4.5 %collective-permute-start = (bf16[2048,128]{1,0:T(8,128)(2,1)}, bf16[2048,128]{1,0:T(8,128)(2,1)}, u32[]{:S(2)}, u32[]{:S(2)}) collective-permute-start(bf16[2048,128]{1,0:T(8,128)(2,1)} %w_key.1), channel_id=1, source_target_pairs={{0,8},{4,12},{8,0},{12,4},{1,9},{5,13},{9,1},{13,5},{2,10},{6,14},... | collective-permute-start | bytes 1572872 | tf_op jit(solution)/shard_map/ppermute | solution.py:352
  10.3 1.5 %collective-permute-start.1 = (bf16[2048,128]{1,0:T(8,128)(2,1)}, bf16[2048,128]{1,0:T(8,128)(2,1)}, u32[]{:S(2)}, u32[]{:S(2)}) collective-permute-start(bf16[2048,128]{1,0:T(8,128)(2,1)} %w_value.1), channel_id=1, source_target_pairs={{16,24},{20,28},{24,16},{28,20},{17,25},{21,29},{25,17},{29,21},{1... | collective-permute-start | bytes 1572872 | tf_op jit(solution)/shard_map/ppermute | solution.py:353
  11.8 23.1 %collective-permute-done.4.h_mine = bf16[2,96,2048]{2,1,0:T(8,128)(2,1)} collective-permute-done((bf16[2,96,2048]{2,1,0:T(8,128)(2,1)}, bf16[2,96,2048]{2,1,0:T(8,128)(2,1)}, u32[]{:S(2)}, u32[]{:S(2)}) %collective-permute-start.4) | collective-permute-done | bytes 786464 | tf_op jit(solution)/shard_map/ppermute | solution.py:349
  34.9 3.5 %cut_docs.1.refs_0_ = bf16[4,4,2,128,128]{4,3,2,1,0:T(8,128)(2,1)} custom-call(s32[4,16]{1,0:T(4,128)} %request_docs.3, bf16[8,128,128]{2,1,0:T(8,128)(2,1)} %store_keys.1, bf16[8,128,128]{2,1,0:T(8,128)(2,1)} %store_values.1), custom_call_target="tpu_custom_call" | custom-call | tf_op jit(solution)/shard_map/cut_docs/pallas_call | solution.py:123
  38.4 3.5 %collective-permute-start.2 = (bf16[2048,128]{1,0:T(8,128)(2,1)}, bf16[2048,128]{1,0:T(8,128)(2,1)S(1)}, u32[]{:S(2)}, u32[]{:S(2)}) collective-permute-start(bf16[2048,128]{1,0:T(8,128)(2,1)} %get-tuple-element.7.k_far), channel_id=1, source_target_pairs={{0,16},{1,17},{2,18},{3,19},{4,20},{5,21},{6,22},{7,23},{8,24},{9,... | collective-permute-start | bytes 1572872 | tf_op jit(solution)/shard_map/ppermute | solution.py:357
  41.9 1.3 %collective-permute-start.3 = (bf16[2048,128]{1,0:T(8,128)(2,1)}, bf16[2048,128]{1,0:T(8,128)(2,1)S(1)}, u32[]{:S(2)}, u32[]{:S(2)}) collective-permute-start(bf16[2048,128]{1,0:T(8,128)(2,1)} %get-tuple-element.8.v_far), channel_id=1, source_target_pairs={{16,0},{17,1},{18,2},{19,3},{20,4},{21,5},{22,6},{23,7},{24,8},{25... | collective-permute-start | bytes 1572872 | tf_op jit(solution)/shard_map/ppermute | solution.py:358
  43.3 0.2 convert_reduce_fusion
  43.5 10.6 %collective-permute-done.2.k_swapped = bf16[2048,128]{1,0:T(8,128)(2,1)S(1)} collective-permute-done((bf16[2048,128]{1,0:T(8,128)(2,1)}, bf16[2048,128]{1,0:T(8,128)(2,1)S(1)}, u32[]{:S(2)}, u32[]{:S(2)}) %collective-permute-start.2) | collective-permute-done | bytes 524320 | tf_op jit(solution)/shard_map/ppermute | solution.py:357
  54.0 4.0 %collective-permute-done.3.v_swapped = bf16[2048,128]{1,0:T(8,128)(2,1)S(1)} collective-permute-done((bf16[2048,128]{1,0:T(8,128)(2,1)}, bf16[2048,128]{1,0:T(8,128)(2,1)S(1)}, u32[]{:S(2)}, u32[]{:S(2)}) %collective-permute-start.3) | collective-permute-done | bytes 524320 | tf_op jit(solution)/shard_map/ppermute | solution.py:358
  58.1 1.0 copy-done.2
  59.1 1.0 copy-done.3
  60.2 2.9 %project.1 = (f32[192,256]{1,0:T(8,128)S(1)}, bf16[192,256]{1,0:T(8,128)(2,1)S(1)}) custom-call(bf16[1,192,8192]{2,1,0:T(8,128)(2,1)S(1)} %copy-done.1, bf16[2048,128]{1,0:T(8,128)(2,1)S(1)} %copy-done.2, bf16[2048,128]{1,0:T(8,128)(2,1)S(1)} %copy-done.3, bf16[2048,128]{1,0:T(8,128)(2,1)} %get-tuple-element.7.k_far, ...), custom_call_target="tpu_custom_call" | custom-call | flops 1 | bytes 1 | tf_op jit(solution)/shard_map/project/pallas_call | solution.py:188
  63.3 4.4 %collective-permute-done.6 = bf16[192,256]{1,0:T(8,128)(2,1)S(1)} collective-permute-done((bf16[192,256]{1,0:T(8,128)(2,1)S(1)}, bf16[192,256]{1,0:T(8,128)(2,1)S(1)}, u32[]{:S(2)}, u32[]{:S(2)}) %collective-permute-start.6) | collective-permute-done | bytes 98336 | tf_op jit(solution)/shard_map/ppermute | solution.py:349
  67.8 0.2 convolution_convert_fusion
  68.0 10.5 %all_to_all.10 = bf16[4,4,12,256]{3,1,2,0:T(4,128)(2,1)S(1)} all-to-all(bf16[4,4,12,256]{3,1,2,0:T(4,128)(2,1)S(1)} %copy.40), channel_id=1, replica_groups=mesh['groups'=2,'seq'=4,'tp'=4] {'seq'}, dimensions={0} | all-to-all | bytes 196608 | tf_op jit(solution)/shard_map/all_to_all | solution.py:402
  78.5 3.5 %all-to-all-start = ((bf16[4,4,2,128,128]{4,3,2,1,0:T(8,128)(2,1)}), bf16[4,4,2,128,128]{4,3,2,1,0:T(8,128)(2,1)S(1)}, u32[]{:S(2)}, u32[]{:S(2)}) async-start(bf16[4,4,2,128,128]{4,3,2,1,0:T(8,128)(2,1)} %get-tuple-element.11), calls=%async_computation | async-start | bytes 2097152 | tf_op jit(solution)/shard_map/all_to_all | solution.py:359
  82.6 0.1 copy.39.row_place
  82.8 0.7 gather_fusion
  83.4 0.1 fusion.1
  83.7 0.7 copy.41
  84.4 20.6 %all-to-all-done.rest_0_ = bf16[4,4,2,128,128]{4,3,2,1,0:T(8,128)(2,1)S(1)} async-done(((bf16[4,4,2,128,128]{4,3,2,1,0:T(8,128)(2,1)}), bf16[4,4,2,128,128]{4,3,2,1,0:T(8,128)(2,1)S(1)}, u32[]{:S(2)}, u32[]{:S(2)}) %all-to-all-start) | async-done | bytes 1048608 | tf_op jit(solution)/shard_map/all_to_all | solution.py:359
  105.0 7.1 %attend.1 = bf16[1,192,1024]{2,1,0:T(8,128)(2,1)} custom-call(s32[4,16]{1,0:T(4,128)S(1)} %copy-done.5, bf16[1,192,1024]{2,1,0:T(8,128)(2,1)S(1)} %copy-done.4, bf16[192,256]{1,0:T(8,128)(2,1)S(1)} %add_convert_fusion.fresh, f32[1,2048]{1,0:T(1,128)S(1)} %bitcast.23, s32[192,1]{1,0:T(8,128)S(1)} %copy.39.row_place, s32[1,192]{1,0:T(1,128)S(1)} %add.73.key_place, ...), custom_call_target="tpu_custom_call" | custom-call | tf_op jit(solution)/shard_map/attend/pallas_call | solution.py:309
  (40 shorter events, 1.1 us)
Async XLA Ops:
  0.6 82.1 %copy-start = (s32[32]{0:T(128)S(1)}, s32[32]{0:T(128)}, u32[]{:S(2)}) copy-start(s32[32]{0:T(128)} %param.16) | copy-start | bytes 388
  0.6 57.4 %copy-start.1 = (bf16[1,192,8192]{2,1,0:T(8,128)(2,1)S(1)}, bf16[1,192,8192]{2,1,0:T(8,128)(2,1)}, u32[]{:S(2)}) copy-start(bf16[1,192,8192]{2,1,0:T(8,128)(2,1)} %hidden.3) | copy-start | bytes 9437188
  0.7 42.6 %copy-start.5 = (s32[4,16]{1,0:T(4,128)S(1)}, s32[4,16]{1,0:T(4,128)}, u32[]{:S(2)}) copy-start(s32[4,16]{1,0:T(4,128)} %request_docs.3) | copy-start | bytes 772
  2.8 32.2 %collective-permute-start.4 = (bf16[2,96,2048]{2,1,0:T(8,128)(2,1)}, bf16[2,96,2048]{2,1,0:T(8,128)(2,1)}, u32[]{:S(2)}, u32[]{:S(2)}) collective-permute-start(bf16[2,96,2048]{2,1,0:T(8,128)(2,1)} %cut.1), channel_id=1, source_target_pairs={{0,4},{4,0},{8,12},{12,8},{1,5},{5,1},{9,13},{13,9},{2,6},{6,2},{1... | collective-permute-start | bytes 2359304 | tf_op jit(solution)/shard_map/ppermute | solution.py:349
  5.8 32.6 %collective-permute-start = (bf16[2048,128]{1,0:T(8,128)(2,1)}, bf16[2048,128]{1,0:T(8,128)(2,1)}, u32[]{:S(2)}, u32[]{:S(2)}) collective-permute-start(bf16[2048,128]{1,0:T(8,128)(2,1)} %w_key.1), channel_id=1, source_target_pairs={{0,8},{4,12},{8,0},{12,4},{1,9},{5,13},{9,1},{13,5},{2,10},{6,14},... | collective-permute-start | bytes 1572872 | tf_op jit(solution)/shard_map/ppermute | solution.py:352
  10.3 28.1 %collective-permute-start.1 = (bf16[2048,128]{1,0:T(8,128)(2,1)}, bf16[2048,128]{1,0:T(8,128)(2,1)}, u32[]{:S(2)}, u32[]{:S(2)}) collective-permute-start(bf16[2048,128]{1,0:T(8,128)(2,1)} %w_value.1), channel_id=1, source_target_pairs={{16,24},{20,28},{24,16},{28,20},{17,25},{21,29},{25,17},{29,21},{1... | collective-permute-start | bytes 1572872 | tf_op jit(solution)/shard_map/ppermute | solution.py:353
  34.9 23.1 %collective-permute-start.5 = (bf16[2,96,2048]{2,1,0:T(8,128)(2,1)}, bf16[2,96,2048]{2,1,0:T(8,128)(2,1)}, u32[]{:S(2)}, u32[]{:S(2)}) collective-permute-start(bf16[2,96,2048]{2,1,0:T(8,128)(2,1)} %collective-permute-done.4.h_mine), channel_id=1, source_target_pairs={{0,1},{1,0},{2,3},{3,2},{4,5},{5,4},{6,7},{7,6},{8,9},{9,8},{10,11... | collective-permute-start | bytes 2359304 | tf_op jit(solution)/shard_map/ppermute | solution.py:349
  38.4 15.6 %collective-permute-start.2 = (bf16[2048,128]{1,0:T(8,128)(2,1)}, bf16[2048,128]{1,0:T(8,128)(2,1)S(1)}, u32[]{:S(2)}, u32[]{:S(2)}) collective-permute-start(bf16[2048,128]{1,0:T(8,128)(2,1)} %get-tuple-element.7.k_far), channel_id=1, source_target_pairs={{0,16},{1,17},{2,18},{3,19},{4,20},{5,21},{6,22},{7,23},{8,24},{9,... | collective-permute-start | bytes 1572872 | tf_op jit(solution)/shard_map/ppermute | solution.py:357
  41.9 16.2 %collective-permute-start.3 = (bf16[2048,128]{1,0:T(8,128)(2,1)}, bf16[2048,128]{1,0:T(8,128)(2,1)S(1)}, u32[]{:S(2)}, u32[]{:S(2)}) collective-permute-start(bf16[2048,128]{1,0:T(8,128)(2,1)} %get-tuple-element.8.v_far), channel_id=1, source_target_pairs={{16,0},{17,1},{18,2},{19,3},{20,4},{21,5},{22,6},{23,7},{24,8},{25... | collective-permute-start | bytes 1572872 | tf_op jit(solution)/shard_map/ppermute | solution.py:358
  58.1 1.0 copy-start.2
  59.1 1.0 copy-start.3
  63.0 19.0 %copy-start.6 = (s32[1,16,12]{1,0,2:T(1,128)S(1)}, s32[1,16,12]{1,0,2:T(1,128)}, u32[]{:S(2)}) copy-start(s32[1,16,12]{1,0,2:T(1,128)} %param.17) | copy-start | bytes 2308
  63.0 42.0 %copy-start.4 = (bf16[1,192,1024]{2,1,0:T(8,128)(2,1)S(1)}, bf16[1,192,1024]{2,1,0:T(8,128)(2,1)}, u32[]{:S(2)}) copy-start(bf16[1,192,1024]{2,1,0:T(8,128)(2,1)} %queries.1) | copy-start | bytes 1179652
  63.0 4.7 %collective-permute-start.6 = (bf16[192,256]{1,0:T(8,128)(2,1)S(1)}, bf16[192,256]{1,0:T(8,128)(2,1)S(1)}, u32[]{:S(2)}, u32[]{:S(2)}) collective-permute-start(bf16[192,256]{1,0:T(8,128)(2,1)S(1)} %get-tuple-element.10), channel_id=1, source_target_pairs={{0,4},{4,0},{8,12},{12,8},{1,5},{5,1},{9,13},{13,9},{2,6},{6,2},{1... | collective-permute-start | bytes 294920 | tf_op jit(solution)/shard_map/ppermute | solution.py:349
  78.5 26.5 %all-to-all-start = ((bf16[4,4,2,128,128]{4,3,2,1,0:T(8,128)(2,1)}), bf16[4,4,2,128,128]{4,3,2,1,0:T(8,128)(2,1)S(1)}, u32[]{:S(2)}, u32[]{:S(2)}) async-start(bf16[4,4,2,128,128]{4,3,2,1,0:T(8,128)(2,1)} %get-tuple-element.11), calls=%async_computation | async-start | bytes 2097152 | tf_op jit(solution)/shard_map/all_to_all | solution.py:359

commit v5 on v4

--- a/solution.py
+++ b/solution.py
@@ -12,6 +12,31 @@
 SMEM = pl.BlockSpec(memory_space=pltpu.SMEM)
 VMEM = pl.BlockSpec(memory_space=pltpu.VMEM)
 MASKED = -1e30
+
+
+def pick_kernel(w_key, w_value, w_out, sem):
+    group = lax.axis_index("groups")
+
+    @pl.when(group == 0)
+    def _():
+        pltpu.make_async_copy(w_key, w_out, sem).start()
+
+    @pl.when(group != 0)
+    def _():
+        pltpu.make_async_copy(w_value, w_out, sem).start()
+
+    pltpu.make_async_copy(w_key, w_out, sem).wait()
+
+
+def pick_weights(w_key, w_value):
+    return pl.pallas_call(
+        pick_kernel,
+        out_shape=jax.ShapeDtypeStruct(w_key.shape, jnp.bfloat16),
+        in_specs=[ANY, ANY],
+        out_specs=VMEM,
+        scratch_shapes=[pltpu.SemaphoreType.DMA],
+        name="pick_weights",
+    )(w_key, w_value)
 
 
 def cut_kernel(hidden, h_out, staged, sems):
@@ -134,7 +159,7 @@
 
 
 def project_kernel(
-    hidden, w_key, w_value, k_far, v_far, k_swapped, v_swapped, h_mine, h_other, own, part, w, h, sems
+    hidden, w_key, w_value, w_far, w_swapped, h_mine, h_other, own, part, w, h, sems
 ):
     group = lax.axis_index("groups")
     me = lax.axis_index("seq")
@@ -163,20 +188,15 @@
     for one in copies:
         one.start()
 
-    @pl.when(group == 0)
-    def _():
-        pltpu.make_async_copy(k_far, w.at[rest, keys], sems.at[8]).start()
-        pltpu.make_async_copy(v_swapped, w.at[rest, values], sems.at[9]).start()
-
-    @pl.when(group != 0)
-    def _():
-        pltpu.make_async_copy(k_swapped, w.at[rest, keys], sems.at[8]).start()
-        pltpu.make_async_copy(v_far, w.at[rest, values], sems.at[9]).start()
-
+    first = pl.multiple_of(group * width, width)
+    second = pl.multiple_of((1 - group) * width, width)
+    for i, (held, column) in enumerate(((w_far, first), (w_swapped, second))):
+        copies.append(
+            pltpu.make_async_copy(held, w.at[rest, pl.ds(column, width)], sems.at[8 + i])
+        )
+        copies[-1].start()
     for one in copies:
         one.wait()
-    pltpu.make_async_copy(k_far, w.at[rest, keys], sems.at[8]).wait()
-    pltpu.make_async_copy(v_far, w.at[rest, values], sems.at[9]).wait()
     total = jnp.dot(h[...], w[...], preferred_element_type=jnp.float32)
     own[...] = total[:rows]
     part[...] = total[rows:].astype(part.dtype)
@@ -204,19 +224,17 @@
     )(hidden, w_key, w_value, *arrived)
 
 
-def attend_kernel(
-    by_owner, request_docs, queries, fresh, key_bias, row_place, key_place, *rest
+def assemble_kernel(
+    by_owner, request_docs, held, spare, *rest
 ):
-    sources, (mixed, context_k, context_v, counts, sems) = rest[:-5], rest[-5:]
+    sources, (keys, values, counts, sems) = rest[:-4], rest[-4:]
     me = lax.axis_index("seq")
     doc_count = request_docs.shape[1]
-    head_dim = context_k.shape[1]
-    doc_len = context_k.shape[0] // doc_count
-    row_count = queries.shape[1]
-    per_doc = row_count // doc_count
-    heads = queries.shape[2] // head_dim
+    head_dim = keys.shape[1] // 2
+    doc_len = keys.shape[0] // doc_count
     owners = request_docs.shape[0]
     slots = sources[0].shape[0] if not by_owner else 2 * sources[0].shape[1]
+    left = pl.ds(0, head_dim)
 
     for o in range(owners):
         counts[o] = 0
@@ -229,8 +247,8 @@
         place = pl.ds(pl.multiple_of(j * doc_len, doc_len), doc_len)
 
         def fetch(key_source, value_source):
-            pltpu.make_async_copy(key_source, context_k.at[place], sems.at[0]).start()
-            pltpu.make_async_copy(value_source, context_v.at[place], sems.at[1]).start()
+            pltpu.make_async_copy(key_source, keys.at[place, left], sems.at[0]).start()
+            pltpu.make_async_copy(value_source, values.at[place, left], sems.at[1]).start()
 
         if by_owner:
             fetch(sources[0].at[owner, rank, 0], sources[0].at[owner, rank, 1])
@@ -251,75 +269,107 @@
         return carry
 
     lax.fori_loop(0, doc_count, one_doc, 0)
-    pltpu.make_async_copy(context_k, context_k, sems.at[0]).wait()
-    pltpu.make_async_copy(context_v, context_v, sems.at[1]).wait()
-
+    pltpu.make_async_copy(keys.at[:, left], keys.at[:, left], sems.at[0]).wait()
+    pltpu.make_async_copy(values.at[:, left], values.at[:, left], sems.at[1]).wait()
+    spares = jnp.dot(spare[...], keys[:, :head_dim], preferred_element_type=jnp.float32)
+    spares = spares.astype(jnp.bfloat16)
+    for j in range(doc_count):
+        place = slice(j * doc_len, (j + 1) * doc_len)
+        used = held[place, :]
+        key = jnp.where(used > 0, keys[place, :head_dim], spares[j : j + 1, :])
+        keys[place, :head_dim] = key
+        keys[place, head_dim:] = key
+        values[place, :head_dim] = values[place, :head_dim] * used
+        values[place, head_dim:] = used
+
+
+def assemble(request_docs, held, spare, sources, by_owner):
+    context, head_dim = held.shape
+    wide = jax.ShapeDtypeStruct((context, 2 * head_dim), jnp.bfloat16)
+    return pl.pallas_call(
+        functools.partial(assemble_kernel, by_owner),
+        out_shape=(wide, wide),
+        in_specs=[SMEM, VMEM, VMEM] + [ANY] * len(sources),
+        out_specs=(VMEM, VMEM),
+        scratch_shapes=[
+            pltpu.SMEM((request_docs.shape[0],), jnp.int32),
+            pltpu.SemaphoreType.DMA((2,)),
+        ],
+        compiler_params=pltpu.CompilerParams(vmem_limit_bytes=32 * 1024 * 1024),
+        cost_estimate=pl.CostEstimate(flops=0, bytes_accessed=16 * 1024 * 1024, transcendentals=0),
+        name="assemble",
+    )(request_docs, held, spare, *sources)
+
+
+def attend_kernel(queries, fresh, keys, values, key_bias, row_place, key_place, mixed):
+    row_count = queries.shape[1]
+    head_dim = fresh.shape[1] // 2
+    heads = queries.shape[2] // head_dim
+    step = 4
+    blocks = key_bias.shape[1] // (step * 128)
+    block_rows = row_count // blocks
+    block_keys = key_bias.shape[1] // blocks
     scale = math.log2(math.e) / math.sqrt(head_dim)
-    fresh_k = fresh[:, :head_dim]
-    fresh_v = fresh[:, head_dim:]
-    step = 4 if doc_count % 4 == 0 else 1
-    block_rows = step * per_doc
-    block_keys = step * doc_len
+    fresh_k = jnp.concatenate([fresh[:, :head_dim]] * 2, axis=1)
+    fresh_v = jnp.concatenate([fresh[:, head_dim:], jnp.ones_like(fresh[:, head_dim:])], axis=1)
     slot_place = lax.broadcasted_iota(jnp.int32, (1, block_keys), 1)
     contract_last = (((1,), (1,)), ((), ()))
-    for b in range(doc_count // step):
+    for b in range(blocks):
         rows = slice(b * block_rows, (b + 1) * block_rows)
         q = jnp.concatenate(
             [queries[0, rows, h * head_dim : (h + 1) * head_dim] for h in range(heads)], axis=0
         )
+        q = q.astype(jnp.float32) * scale
+        high = q.astype(jnp.bfloat16)
+        low = (q - high.astype(jnp.float32)).astype(jnp.bfloat16)
+        q = jnp.concatenate([high, low], axis=1)
         own_place = row_place[rows, :]
 
-        def masked(keys, bias):
-            scores = lax.dot_general(q, keys, contract_last, preferred_element_type=jnp.float32)
-            scores = (scores * scale).reshape(heads, block_rows, keys.shape[0])
-            return (scores + bias[None]).reshape(heads * block_rows, keys.shape[0])
-
-        chunks, values = [], []
-        for c in range(b + 1):
-            keys = slice(c * block_keys, (c + 1) * block_keys)
-            bias = jnp.broadcast_to(key_bias[:, keys], (block_rows, block_keys))
-            if c == b:
-                bias = jnp.where(slot_place + c * block_keys <= own_place, bias, MASKED)
-            chunks.append(masked(context_k[keys, :], bias))
-            values.append(context_v[keys, :])
-        bias = jnp.where(key_place[...] <= own_place, 0.0, MASKED)
-        chunks.append(masked(fresh_k, bias))
-        values.append(fresh_v)
+        def scores(some_keys):
+            return lax.dot_general(
+                q, some_keys, contract_last, preferred_element_type=jnp.float32
+            )
+
+        def masked(some_keys, allowed):
+            shape = (heads, block_rows, some_keys.shape[0])
+            kept = jnp.where(allowed[None], scores(some_keys).reshape(shape), MASKED)
+            return kept.reshape(heads * block_rows, some_keys.shape[0])
+
+        chunks, sides = [], []
+        for c in range(b):
+            part = slice(c * block_keys, (c + 1) * block_keys)
+            chunks.append(scores(keys[part, :]))
+            sides.append(values[part, :])
+        part = slice(b * block_keys, (b + 1) * block_keys)
+        allowed = (slot_place + b * block_keys <= own_place) & (key_bias[:, part] == 0)
+        chunks.append(masked(keys[part, :], allowed))
+        sides.append(values[part, :])
+        chunks.append(masked(fresh_k, key_place[...] <= own_place))
+        sides.append(fresh_v)
         row_max = functools.reduce(
             jnp.maximum, [jnp.max(one, axis=1, keepdims=True) for one in chunks]
         )
-        total = jnp.zeros((heads * block_rows, head_dim), jnp.float32)
-        row_sum = jnp.zeros((heads * block_rows, 1), jnp.float32)
-        for one, value in zip(chunks, values):
-            powers = jnp.exp2(one - row_max)
-            row_sum += jnp.sum(powers, axis=1, keepdims=True)
-            total += jnp.dot(
-                powers.astype(jnp.bfloat16), value, preferred_element_type=jnp.float32
-            )
-        result = (total / row_sum).astype(mixed.dtype)
+        total = jnp.zeros((heads * block_rows, 2 * head_dim), jnp.float32)
+        for one, side in zip(chunks, sides):
+            powers = jnp.exp2(one - row_max).astype(jnp.bfloat16)
+            total += jnp.dot(powers, side, preferred_element_type=jnp.float32)
+        result = (total[:, :head_dim] / total[:, head_dim:]).astype(mixed.dtype)
         for h in range(heads):
             mixed[0, rows, h * head_dim : (h + 1) * head_dim] = result[
                 h * block_rows : (h + 1) * block_rows
             ]
 
 
-def attend(request_docs, queries, fresh, key_bias, row_place, key_place, sources, by_owner):
-    head_dim = fresh.shape[1] // 2
-    context = key_bias.shape[1]
-    return pl.pallas_call(
-        functools.partial(attend_kernel, by_owner),
+def attend(queries, fresh, keys, values, key_bias, row_place, key_place):
+    return pl.pallas_call(
+        attend_kernel,
         out_shape=jax.ShapeDtypeStruct(queries.shape, jnp.bfloat16),
-        in_specs=[SMEM] + [VMEM] * 5 + [ANY] * len(sources),
+        in_specs=[VMEM] * 7,
         out_specs=VMEM,
-        scratch_shapes=[
-            pltpu.VMEM((context, head_dim), jnp.bfloat16),
-            pltpu.VMEM((context, head_dim), jnp.bfloat16),
-            pltpu.SMEM((request_docs.shape[0],), jnp.int32),
-            pltpu.SemaphoreType.DMA((2,)),
-        ],
         compiler_params=pltpu.CompilerParams(vmem_limit_bytes=32 * 1024 * 1024),
+        cost_estimate=pl.CostEstimate(flops=1, bytes_accessed=1, transcendentals=0),
         name="attend",
-    )(request_docs, queries, fresh, key_bias, row_place, key_place, *sources)
+    )(queries, fresh, keys, values, key_bias, row_place, key_place)
 
 
 def shards(
@@ -348,21 +398,16 @@
             count = lax.axis_size(axis)
             return lax.ppermute(array, axis, [(i, i ^ apart) for i in range(count)])
 
-        both = ("groups", "seq")
-        k_far = lax.ppermute(w_key, both, [(s, s ^ 2) for s in range(4)])
-        v_far = lax.ppermute(w_value, both, [(4 + s, 4 + (s ^ 2)) for s in range(4)])
+        w_far = swap(pick_weights(w_key, w_value), "seq", 2)
         h_mine = swap(cut(hidden, w_key.shape[0]), "seq", 1)
-        (docs,) = cut_docs(request_docs, store_keys, store_values, True)
-        docs, k_far, v_far = gate((docs, k_far, v_far))
-        k_swapped = lax.ppermute(k_far, "groups", [(0, 1)])
-        v_swapped = lax.ppermute(v_far, "groups", [(1, 0)])
-        docs = lax.all_to_all(docs, "seq", split_axis=0, concat_axis=0, tiled=True)
+        docs = cut_docs(request_docs, store_keys, store_values, False)
+        *docs, w_far = gate((*docs, w_far))
+        w_swapped = swap(w_far, "groups", 1)
+        docs = [swap(doc, "seq", k + 1) for k, doc in enumerate(docs)]
         h_other = swap(h_mine, "tp", 1)
-        own, part = project(
-            hidden, w_key, w_value, k_far, v_far, k_swapped, v_swapped, h_mine, h_other
-        )
+        own, part = project(hidden, w_key, w_value, w_far, w_swapped, h_mine, h_other)
         fresh = (own + swap(part, "seq", 1).astype(jnp.float32)).astype(jnp.bfloat16)
-        sources = (docs,)
+        sources = (store_keys, store_values, *docs)
     else:
         (docs,) = cut_docs(request_docs, store_keys, store_values, True)
         sources = (lax.all_to_all(docs, "seq", split_axis=0, concat_axis=0, tiled=True),)
@@ -381,15 +426,21 @@
     held &= jnp.all(positions[None, None, :] != row_ids[:, :, None], axis=1)
     key_bias = jnp.where(held, 0.0, MASKED).astype(jnp.float32).reshape(1, doc_count * doc_len)
     place = jnp.arange(doc_count, dtype=jnp.int32)[:, None] * doc_len + row_ids
+    context = doc_count * doc_len
+    used = held.astype(jnp.bfloat16).reshape(context, 1)
+    first_used = jnp.argmax(held, axis=1) + jnp.arange(doc_count) * doc_len
+    spare = (jnp.arange(context)[None, :] == first_used[:, None]).astype(jnp.bfloat16)
+    keys, values = assemble(
+        request_docs, jnp.broadcast_to(used, (context, head_dim)), spare, sources, not pairs
+    )
     mixed = attend(
-        request_docs,
         queries,
         fresh,
+        keys,
+        values,
         key_bias,
         place.reshape(row_count, 1),
         place.reshape(1, row_count),
-        sources,
-        True,
     )
 
     slot_of_row = jnp.repeat(owners * capacity + ranks, per_doc) * per_doc + jnp.tile(

time: 113 us -> 99.1 us (0.88)
  the two profiles are of different devices: /device:TPU:0 before, /device:TPU:14 now
where the time goes in v5:
time: 99.1 us; the launch traced here: 98.6 us
  waiting for transfers between devices  52.4 us (53%)
  starting transfers between devices  18.6 us (19%)
  Pallas kernels  17.2 us (17%)
  local copies, waits for them, and re-layouts  6.9 us (7%)
  other arithmetic  2.3 us (2%)
    ppermute x8, waiting for transfers between devices, swap(): return lax.ppermute(array, axis, [(i, i ^ apart) for i in range(count)])  52.4 us
    ppermute x8, starting transfers between devices, swap(): return lax.ppermute(array, axis, [(i, i ^ apart) for i in range(count)])  9.84 us
    all_to_all x1, starting transfers between devices, shards(): lax.all_to_all(outgoing, 'seq', split_axis=0, concat_axis=0, tiled=True)  8.81 us
    pallas_call x1, Pallas kernels, attend(): pl.pallas_call(attend_kernel, out_shape=jax.ShapeDtypeStruct(queries.shap...  4.82 us
    unnamed x25, local copies, waits for them, and re-layouts  4.52 us
    pallas_call x1, Pallas kernels, project(): pl.pallas_call(project_kernel, out_shape=(jax.ShapeDtypeStruct((rows, 2 *...  3.65 us
    pallas_call x1, Pallas kernels, cut_docs(): pl.pallas_call(functools.partial(docs_kernel, by_owner), out_shape=shapes...  3.13 us
  transfers between devices with their start and end apart: 9, of which 4 were waited for; matrix products, arithmetic and copies ran while one was open for 5% of the time, Pallas kernels for 12%

profile of v5, /device:TPU:14, one launch (start us, length us, event | category | flops | bytes accessed | tf_op | source)
XLA Modules:
  0.0 98.6 jit_solution(5189471243038749325)
XLA Ops:
  0.7 1.9 %pick_weights.1 = bf16[2048,128]{1,0:T(8,128)(2,1)} custom-call(bf16[2048,128]{1,0:T(8,128)(2,1)} %w_key.3, bf16[2048,128]{1,0:T(8,128)(2,1)} %w_value.3), custom_call_target="tpu_custom_call" | custom-call | tf_op jit(solution)/shard_map/pick_weights/pallas_call | solution.py:32
  2.6 2.7 %collective-permute-start = (bf16[2048,128]{1,0:T(8,128)(2,1)}, bf16[2048,128]{1,0:T(8,128)(2,1)}, u32[]{:S(2)}, u32[]{:S(2)}) collective-permute-start(bf16[2048,128]{1,0:T(8,128)(2,1)} %pick_weights.1), channel_id=1, source_target_pairs={{0,8},{4,12},{8,0},{12,4},{1,9},{5,13},{9,1},{13,5},{2,10},{6,14},... | collective-permute-start | bytes 1572872 | tf_op jit(solution)/shard_map/ppermute | solution.py:399
  5.2 1.9 %cut.1 = bf16[2,96,2048]{2,1,0:T(8,128)(2,1)} custom-call(bf16[1,192,8192]{2,1,0:T(8,128)(2,1)} %hidden.3), custom_call_target="tpu_custom_call" | custom-call | tf_op jit(solution)/shard_map/cut/pallas_call | solution.py:68
  7.9 0.7 gather_fusion
  8.8 0.7 iota_reduce_fusion
  9.5 25.1 %collective-permute-done.2.h_mine = bf16[2,96,2048]{2,1,0:T(8,128)(2,1)} collective-permute-done((bf16[2,96,2048]{2,1,0:T(8,128)(2,1)}, bf16[2,96,2048]{2,1,0:T(8,128)(2,1)}, u32[]{:S(2)}, u32[]{:S(2)}) %collective-permute-start.2) | collective-permute-done | bytes 786464 | tf_op jit(solution)/shard_map/ppermute | solution.py:399
  34.7 3.1 %cut_docs.1 = (bf16[4,2,128,128]{3,2,1,0:T(8,128)(2,1)}, bf16[4,2,128,128]{3,2,1,0:T(8,128)(2,1)}, bf16[4,2,128,128]{3,2,1,0:T(8,128)(2,1)}) custom-call(s32[4,16]{1,0:T(4,128)} %request_docs.3, bf16[8,128,128]{2,1,0:T(8,128)(2,1)} %rest_0_.1, bf16[8,128,128]{2,1,0:T(8,128)(2,1)} %rest_1_.1), custom_call_target="tpu_custom_call" | custom-call | tf_op jit(solution)/shard_map/cut_docs/pallas_call | solution.py:148
  37.9 0.6 collective-permute-start.1
  38.6 14.0 %collective-permute-done.1.w_swapped = bf16[2048,128]{1,0:T(8,128)(2,1)} collective-permute-done((bf16[2048,128]{1,0:T(8,128)(2,1)}, bf16[2048,128]{1,0:T(8,128)(2,1)}, u32[]{:S(2)}, u32[]{:S(2)}) %collective-permute-start.1) | collective-permute-done | bytes 524320 | tf_op jit(solution)/shard_map/ppermute | solution.py:399
  52.6 1.0 %copy-done.2 = bf16[2048,128]{1,0:T(8,128)(2,1)S(1)} copy-done((bf16[2048,128]{1,0:T(8,128)(2,1)S(1)}, bf16[2048,128]{1,0:T(8,128)(2,1)}, u32[]{:S(2)}) %copy-start.2) | copy-done | bytes 524312
  53.6 1.0 %copy-done.3 = bf16[2048,128]{1,0:T(8,128)(2,1)S(1)} copy-done((bf16[2048,128]{1,0:T(8,128)(2,1)S(1)}, bf16[2048,128]{1,0:T(8,128)(2,1)}, u32[]{:S(2)}) %copy-start.3) | copy-done | bytes 524312
  54.7 3.7 %project.1 = (f32[192,256]{1,0:T(8,128)S(1)}, bf16[192,256]{1,0:T(8,128)(2,1)}) custom-call(bf16[1,192,8192]{2,1,0:T(8,128)(2,1)S(1)} %copy-done.1, bf16[2048,128]{1,0:T(8,128)(2,1)S(1)} %copy-done.2, bf16[2048,128]{1,0:T(8,128)(2,1)S(1)} %copy-done.3, bf16[2048,128]{1,0:T(8,128)(2,1)} %get-tuple-element.17.w_far, ...), custom_call_target="tpu_custom_call" | custom-call | flops 1 | bytes 1 | tf_op jit(solution)/shard_map/project/pallas_call | solution.py:208
  58.3 0.7 copy-done.7
  59.0 2.5 %collective-permute-start.4 = (bf16[192,256]{1,0:T(8,128)(2,1)}, bf16[192,256]{1,0:T(8,128)(2,1)S(1)}, u32[]{:S(2)}, u32[]{:S(2)}) collective-permute-start(bf16[192,256]{1,0:T(8,128)(2,1)} %get-tuple-element.19), channel_id=1, source_target_pairs={{0,4},{4,0},{8,12},{12,8},{1,5},{5,1},{9,13},{13,9},{2,6},{6,2},{1... | collective-permute-start | bytes 294920 | tf_op jit(solution)/shard_map/ppermute | solution.py:399
  62.3 3.0 %collective-permute-start.6 = (bf16[4,2,128,128]{3,2,1,0:T(8,128)(2,1)}, bf16[4,2,128,128]{3,2,1,0:T(8,128)(2,1)S(1)}, u32[]{:S(2)}, u32[]{:S(2)}) collective-permute-start(bf16[4,2,128,128]{3,2,1,0:T(8,128)(2,1)} %get-tuple-element.22), channel_id=1, source_target_pairs={{0,8},{4,12},{8,0},{12,4},{1,9},{5,13},{9,1},{13,5},{2,10},{6,14},... | collective-permute-start | bytes 786440 | tf_op jit(solution)/shard_map/ppermute | solution.py:399
  65.8 0.9 add_convert_fusion.fresh
  66.9 0.7 copy.41
  67.6 8.8 %all-to-all-start = ((bf16[4,4,12,256]{3,1,2,0:T(4,128)(2,1)}), bf16[4,4,12,256]{3,1,2,0:T(4,128)(2,1)S(1)}, u32[]{:S(2)}, u32[]{:S(2)}) async-start(bf16[4,4,12,256]{3,1,2,0:T(4,128)(2,1)} %copy.41), calls=%async_computation | async-start | bytes 196608 | tf_op jit(solution)/shard_map/all_to_all | solution.py:453
  76.5 8.2 %collective-permute-done.6.rest_3_ = bf16[4,2,128,128]{3,2,1,0:T(8,128)(2,1)S(1)} collective-permute-done((bf16[4,2,128,128]{3,2,1,0:T(8,128)(2,1)}, bf16[4,2,128,128]{3,2,1,0:T(8,128)(2,1)S(1)}, u32[]{:S(2)}, u32[]{:S(2)}) %collective-permute-start.6) | collective-permute-done | bytes 262176 | tf_op jit(solution)/shard_map/ppermute | solution.py:399
  84.7 5.2 %collective-permute-done.7.rest_4_ = bf16[4,2,128,128]{3,2,1,0:T(8,128)(2,1)S(1)} collective-permute-done((bf16[4,2,128,128]{3,2,1,0:T(8,128)(2,1)}, bf16[4,2,128,128]{3,2,1,0:T(8,128)(2,1)S(1)}, u32[]{:S(2)}, u32[]{:S(2)}) %collective-permute-start.7) | collective-permute-done | bytes 262176 | tf_op jit(solution)/shard_map/ppermute | solution.py:399
  90.2 0.9 copy-done.5
  91.2 1.8 %assemble.1 = (bf16[2048,256]{1,0:T(8,128)(2,1)S(1)}, bf16[2048,256]{1,0:T(8,128)(2,1)S(1)}) custom-call(s32[4,16]{1,0:T(4,128)S(1)} %copy-done.9, bf16[2048,128]{1,0:T(8,128)(2,1)S(1)} %broadcast_in_dim.12.held, bf16[16,2048]{1,0:T(8,128)(2,1)S(1)} %fusion.spare, bf16[8,128,128]{2,1,0:T(8,128)(2,1)S(1)} %copy-done.4, bf16[8,128,128]{2,1,0:T(8,128)(2,1)S(1)} %copy-done.5, ...), custom_call_target="tpu_custom_call" | custom-call | bytes 16777216 | tf_op jit(solution)/shard_map/assemble/pallas_call | solution.py:289
  93.0 4.8 %attend.1 = bf16[1,192,1024]{2,1,0:T(8,128)(2,1)} custom-call(bf16[1,192,1024]{2,1,0:T(8,128)(2,1)S(1)} %copy-done.6, bf16[192,256]{1,0:T(8,128)(2,1)S(1)} %add_convert_fusion.fresh, bf16[2048,256]{1,0:T(8,128)(2,1)S(1)} %get-tuple-element.24.keys, bf16[2048,256]{1,0:T(8,128)(2,1)S(1)} %get-tuple-element.25.values, f32[1,2048]{1,0:T(1,128)S(1)} %bitcast.25, ...), custom_call_target="tpu_custom_call" | custom-call | flops 1 | bytes 1 | tf_op jit(solution)/shard_map/attend/pallas_call | solution.py:364
  97.9 0.7 copy.42
  (56 shorter events, 3.1 us)
Async XLA Ops:
  0.6 7.2 %copy-start = (s32[32]{0:T(128)S(1)}, s32[32]{0:T(128)}, u32[]{:S(2)}) copy-start(s32[32]{0:T(128)} %param.16) | copy-start | bytes 388
  0.6 7.0 %copy-start.8 = (s32[4,16]{1,0:T(4,128)S(1)}, s32[4,16]{1,0:T(4,128)}, u32[]{:S(2)}) copy-start(s32[4,16]{1,0:T(4,128)} %request_docs.3) | copy-start | bytes 772
  0.7 7.1 %copy-start.10 = (s32[1,16,12]{1,0,2:T(1,128)S(1)}, s32[1,16,12]{1,0,2:T(1,128)}, u32[]{:S(2)}) copy-start(s32[1,16,12]{1,0,2:T(1,128)} %param.17) | copy-start | bytes 2308
  2.6 50.0 %copy-start.1 = (bf16[1,192,8192]{2,1,0:T(8,128)(2,1)S(1)}, bf16[1,192,8192]{2,1,0:T(8,128)(2,1)}, u32[]{:S(2)}) copy-start(bf16[1,192,8192]{2,1,0:T(8,128)(2,1)} %hidden.3) | copy-start | bytes 9437188
  2.6 35.3 %collective-permute-start = (bf16[2048,128]{1,0:T(8,128)(2,1)}, bf16[2048,128]{1,0:T(8,128)(2,1)}, u32[]{:S(2)}, u32[]{:S(2)}) collective-permute-start(bf16[2048,128]{1,0:T(8,128)(2,1)} %pick_weights.1), channel_id=1, source_target_pairs={{0,8},{4,12},{8,0},{12,4},{1,9},{5,13},{9,1},{13,5},{2,10},{6,14},... | collective-permute-start | bytes 1572872 | tf_op jit(solution)/shard_map/ppermute | solution.py:399
  7.2 27.5 %collective-permute-start.2 = (bf16[2,96,2048]{2,1,0:T(8,128)(2,1)}, bf16[2,96,2048]{2,1,0:T(8,128)(2,1)}, u32[]{:S(2)}, u32[]{:S(2)}) collective-permute-start(bf16[2,96,2048]{2,1,0:T(8,128)(2,1)} %cut.1), channel_id=1, source_target_pairs={{0,4},{4,0},{8,12},{12,8},{1,5},{5,1},{9,13},{13,9},{2,6},{6,2},{1... | collective-permute-start | bytes 2359304 | tf_op jit(solution)/shard_map/ppermute | solution.py:399
  34.6 18.0 %collective-permute-start.3 = (bf16[2,96,2048]{2,1,0:T(8,128)(2,1)}, bf16[2,96,2048]{2,1,0:T(8,128)(2,1)}, u32[]{:S(2)}, u32[]{:S(2)}) collective-permute-start(bf16[2,96,2048]{2,1,0:T(8,128)(2,1)} %collective-permute-done.2.h_mine), channel_id=1, source_target_pairs={{0,1},{1,0},{2,3},{3,2},{4,5},{5,4},{6,7},{7,6},{8,9},{9,8},{10,11... | collective-permute-start | bytes 2359304 | tf_op jit(solution)/shard_map/ppermute | solution.py:399
  37.9 14.7 %collective-permute-start.1 = (bf16[2048,128]{1,0:T(8,128)(2,1)}, bf16[2048,128]{1,0:T(8,128)(2,1)}, u32[]{:S(2)}, u32[]{:S(2)}) collective-permute-start(bf16[2048,128]{1,0:T(8,128)(2,1)} %get-tuple-element.17.w_far), channel_id=1, source_target_pairs={{0,16},{16,0},{1,17},{17,1},{2,18},{18,2},{3,19},{19,3},{4,20},{20... | collective-permute-start | bytes 1572872 | tf_op jit(solution)/shard_map/ppermute | solution.py:399
  38.5 51.7 %copy-start.9 = (s32[4,16]{1,0:T(4,128)S(1)}, s32[4,16]{1,0:T(4,128)}, u32[]{:S(2)}) copy-start(s32[4,16]{1,0:T(4,128)} %request_docs.3) | copy-start | bytes 772
  52.6 1.0 %copy-start.2 = (bf16[2048,128]{1,0:T(8,128)(2,1)S(1)}, bf16[2048,128]{1,0:T(8,128)(2,1)}, u32[]{:S(2)}) copy-start(bf16[2048,128]{1,0:T(8,128)(2,1)} %w_key.3) | copy-start | bytes 1572868
  53.6 1.0 %copy-start.3 = (bf16[2048,128]{1,0:T(8,128)(2,1)S(1)}, bf16[2048,128]{1,0:T(8,128)(2,1)}, u32[]{:S(2)}) copy-start(bf16[2048,128]{1,0:T(8,128)(2,1)} %w_value.3) | copy-start | bytes 1572868
  54.7 35.5 %copy-start.4 = (bf16[8,128,128]{2,1,0:T(8,128)(2,1)S(1)}, bf16[8,128,128]{2,1,0:T(8,128)(2,1)}, u32[]{:S(2)}) copy-start(bf16[8,128,128]{2,1,0:T(8,128)(2,1)} %rest_0_.1) | copy-start | bytes 786436
  58.3 0.7 copy-start.7
  59.0 34.0 %copy-start.6 = (bf16[1,192,1024]{2,1,0:T(8,128)(2,1)S(1)}, bf16[1,192,1024]{2,1,0:T(8,128)(2,1)}, u32[]{:S(2)}) copy-start(bf16[1,192,1024]{2,1,0:T(8,128)(2,1)} %queries.1) | copy-start | bytes 1179652
  59.0 6.8 %collective-permute-start.4 = (bf16[192,256]{1,0:T(8,128)(2,1)}, bf16[192,256]{1,0:T(8,128)(2,1)S(1)}, u32[]{:S(2)}, u32[]{:S(2)}) collective-permute-start(bf16[192,256]{1,0:T(8,128)(2,1)} %get-tuple-element.19), channel_id=1, source_target_pairs={{0,4},{4,0},{8,12},{12,8},{1,5},{5,1},{9,13},{13,9},{2,6},{6,2},{1... | collective-permute-start | bytes 294920 | tf_op jit(solution)/shard_map/ppermute | solution.py:399
  62.2 14.3 %collective-permute-start.5 = (bf16[4,2,128,128]{3,2,1,0:T(8,128)(2,1)}, bf16[4,2,128,128]{3,2,1,0:T(8,128)(2,1)S(1)}, u32[]{:S(2)}, u32[]{:S(2)}) collective-permute-start(bf16[4,2,128,128]{3,2,1,0:T(8,128)(2,1)} %get-tuple-element.21), channel_id=1, source_target_pairs={{0,4},{4,0},{8,12},{12,8},{1,5},{5,1},{9,13},{13,9},{2,6},{6,2},{1... | collective-permute-start | bytes 786440 | tf_op jit(solution)/shard_map/ppermute | solution.py:399
  62.3 22.4 %collective-permute-start.6 = (bf16[4,2,128,128]{3,2,1,0:T(8,128)(2,1)}, bf16[4,2,128,128]{3,2,1,0:T(8,128)(2,1)S(1)}, u32[]{:S(2)}, u32[]{:S(2)}) collective-permute-start(bf16[4,2,128,128]{3,2,1,0:T(8,128)(2,1)} %get-tuple-element.22), channel_id=1, source_target_pairs={{0,8},{4,12},{8,0},{12,4},{1,9},{5,13},{9,1},{13,5},{2,10},{6,14},... | collective-permute-start | bytes 786440 | tf_op jit(solution)/shard_map/ppermute | solution.py:399
  65.3 24.5 %collective-permute-start.7 = (bf16[4,2,128,128]{3,2,1,0:T(8,128)(2,1)}, bf16[4,2,128,128]{3,2,1,0:T(8,128)(2,1)S(1)}, u32[]{:S(2)}, u32[]{:S(2)}) collective-permute-start(bf16[4,2,128,128]{3,2,1,0:T(8,128)(2,1)} %get-tuple-element.23), channel_id=1, source_target_pairs={{0,12},{4,8},{8,4},{12,0},{1,13},{5,9},{9,5},{13,1},{2,14},{6,10},... | collective-permute-start | bytes 786440 | tf_op jit(solution)/shard_map/ppermute | solution.py:399
  67.6 30.2 %all-to-all-start = ((bf16[4,4,12,256]{3,1,2,0:T(4,128)(2,1)}), bf16[4,4,12,256]{3,1,2,0:T(4,128)(2,1)S(1)}, u32[]{:S(2)}, u32[]{:S(2)}) async-start(bf16[4,4,12,256]{3,1,2,0:T(4,128)(2,1)} %copy.41), calls=%async_computation | async-start | bytes 196608 | tf_op jit(solution)/shard_map/all_to_all | solution.py:453
  90.2 1.0 copy-start.5

commit v6 on v5

--- a/solution.py
+++ b/solution.py
@@ -9,70 +9,51 @@
 from jax.sharding import PartitionSpec as P
 
 ANY = pl.BlockSpec(memory_space=pl.ANY)
+HBM = pl.BlockSpec(memory_space=pltpu.HBM)
 SMEM = pl.BlockSpec(memory_space=pltpu.SMEM)
 VMEM = pl.BlockSpec(memory_space=pltpu.VMEM)
 MASKED = -1e30
 
 
-def pick_kernel(w_key, w_value, w_out, sem):
+def pick_kernel(w_key, w_value, w_out, staged, sems):
     group = lax.axis_index("groups")
-
-    @pl.when(group == 0)
-    def _():
-        pltpu.make_async_copy(w_key, w_out, sem).start()
-
-    @pl.when(group != 0)
-    def _():
-        pltpu.make_async_copy(w_value, w_out, sem).start()
-
-    pltpu.make_async_copy(w_key, w_out, sem).wait()
+    pieces = staged.shape[0]
+    rows = staged.shape[1]
+
+    def fetch(i, weight):
+        source = weight.at[pl.ds(i * rows, rows)]
+        return pltpu.make_async_copy(source, staged.at[i], sems.at[0, i])
+
+    for chosen, weight in ((0, w_key), (1, w_value)):
+
+        @pl.when(group == chosen)
+        def _():
+            for i in range(pieces):
+                fetch(i, weight).start()
+
+    stores = []
+    for i in range(pieces):
+        fetch(i, w_key).wait()
+        target = w_out.at[pl.ds(i * rows, rows)]
+        stores.append(pltpu.make_async_copy(staged.at[i], target, sems.at[1, i]))
+        stores[-1].start()
+    for store in stores:
+        store.wait()
 
 
 def pick_weights(w_key, w_value):
+    pieces = 4
     return pl.pallas_call(
         pick_kernel,
         out_shape=jax.ShapeDtypeStruct(w_key.shape, jnp.bfloat16),
-        in_specs=[ANY, ANY],
-        out_specs=VMEM,
-        scratch_shapes=[pltpu.SemaphoreType.DMA],
+        in_specs=[HBM, HBM],
+        out_specs=HBM,
+        scratch_shapes=[
+            pltpu.VMEM((pieces, w_key.shape[0] // pieces, w_key.shape[1]), jnp.bfloat16),
+            pltpu.SemaphoreType.DMA((2, pieces)),
+        ],
         name="pick_weights",
     )(w_key, w_value)
-
-
-def cut_kernel(hidden, h_out, staged, sems):
-    me = lax.axis_index("seq")
-    core = lax.rem(lax.axis_index("tp"), 2)
-    rows, depth = h_out.shape[1:]
-    first = me + 1 - 2 * lax.rem(me, 2)
-    second = lax.rem(first + 2, 4)
-    fetches, stores = [], []
-    for i, block in enumerate((first, second)):
-        source = hidden.at[
-            0,
-            pl.ds(pl.multiple_of(core * rows, rows), rows),
-            pl.ds(pl.multiple_of(block * depth, depth), depth),
-        ]
-        fetches.append(pltpu.make_async_copy(source, staged.at[i], sems.at[i]))
-        stores.append(pltpu.make_async_copy(staged.at[i], h_out.at[i], sems.at[2 + i]))
-    for fetch in fetches:
-        fetch.start()
-    for fetch, store in zip(fetches, stores):
-        fetch.wait()
-        store.start()
-    for store in stores:
-        store.wait()
-
-
-def cut(hidden, depth):
-    shape = (2, hidden.shape[1] // 2, depth)
-    return pl.pallas_call(
-        cut_kernel,
-        out_shape=jax.ShapeDtypeStruct(shape, jnp.bfloat16),
-        in_specs=[ANY],
-        out_specs=ANY,
-        scratch_shapes=[pltpu.VMEM(shape, jnp.bfloat16), pltpu.SemaphoreType.DMA((4,))],
-        name="cut",
-    )(hidden)
 
 
 def gate_kernel(*refs):
@@ -86,16 +67,35 @@
         in_specs=[ANY] * len(arrays),
         out_specs=(ANY,) * len(arrays),
         input_output_aliases={i: i for i in range(len(arrays))},
+        compiler_params=pltpu.CompilerParams(vmem_limit_bytes=1 * 1024 * 1024),
         name="gate",
     )(*arrays)
 
 
-def docs_kernel(by_owner, request_docs, store_keys, store_values, *rest):
-    outs, (picks, sems) = rest[:-2], rest[-2:]
+def cut_kernel(by_owner, request_docs, store_keys, store_values, *rest):
+    if by_owner:
+        out, picks, sems = rest
+        outs = (out,)
+    else:
+        hidden, h_out, *outs, picks, sems = rest
     me = lax.axis_index("seq")
     requests, doc_count = request_docs.shape
     slots = store_keys.shape[0]
     capacity = slots // 2
+    h_copies = []
+    if not by_owner:
+        core = lax.rem(lax.axis_index("tp"), 2)
+        rows, depth = h_out.shape[1:]
+        first = me + 1 - 2 * lax.rem(me, 2)
+        second = lax.rem(first + 2, 4)
+        for i, block in enumerate((first, second)):
+            source = hidden.at[
+                0,
+                pl.ds(pl.multiple_of(core * rows, rows), rows),
+                pl.ds(pl.multiple_of(block * depth, depth), depth),
+            ]
+            h_copies.append(pltpu.make_async_copy(source, h_out.at[i], sems.at[len(outs) + i]))
+            h_copies[-1].start()
 
     def one_request(r, carry):
         for c in range(capacity):
@@ -123,39 +123,42 @@
             pltpu.make_async_copy(store_values.at[slot], out.at[c, 1], sem).start()
 
     if by_owner:
-        out = outs[0]
 
         def one_send(r, carry):
-            send(r, out.at[r], sems.at[0])
+            send(r, outs[0].at[r], sems.at[0])
             return carry
 
         lax.fori_loop(0, requests, one_send, 0)
     else:
         for i, out in enumerate(outs):
             send(lax.bitwise_xor(me, i + 1), out, sems.at[i])
+    for copy in h_copies:
+        copy.wait()
     for i, out in enumerate(outs):
         pltpu.make_async_copy(out, out, sems.at[i]).wait()
 
 
-def cut_docs(request_docs, store_keys, store_values, by_owner):
+def cut(request_docs, store_keys, store_values, hidden, depth):
     requests = request_docs.shape[0]
     capacity = store_keys.shape[0] // 2
     one = (capacity, 2) + store_keys.shape[1:]
-    if by_owner:
-        shapes = (jax.ShapeDtypeStruct((requests,) + one, jnp.bfloat16),)
+    if hidden is None:
+        shapes = ((requests,) + one,)
+        inputs = (store_keys, store_values)
     else:
-        shapes = (jax.ShapeDtypeStruct(one, jnp.bfloat16),) * (requests - 1)
-    return pl.pallas_call(
-        functools.partial(docs_kernel, by_owner),
-        out_shape=shapes,
-        in_specs=[SMEM, ANY, ANY],
+        shapes = ((2, hidden.shape[1] // 2, depth),) + (one,) * (requests - 1)
+        inputs = (store_keys, store_values, hidden)
+    return pl.pallas_call(
+        functools.partial(cut_kernel, hidden is None),
+        out_shape=tuple(jax.ShapeDtypeStruct(one, jnp.bfloat16) for one in shapes),
+        in_specs=[SMEM] + [HBM] * len(inputs),
         out_specs=(VMEM,) * len(shapes),
         scratch_shapes=[
             pltpu.SMEM((requests, capacity), jnp.int32),
-            pltpu.SemaphoreType.DMA((len(shapes),)),
+            pltpu.SemaphoreType.DMA((len(shapes) + 1,)),
         ],
-        name="cut_docs",
-    )(request_docs, store_keys, store_values)
+        name="cut",
+    )(request_docs, *inputs)
 
 
 def project_kernel(
@@ -211,7 +214,7 @@
             jax.ShapeDtypeStruct((rows, 2 * width), jnp.float32),
             jax.ShapeDtypeStruct((rows, 2 * width), jnp.bfloat16),
         ),
-        in_specs=[ANY] * (3 + len(arrived)),
+        in_specs=[HBM] * (3 + len(arrived)),
         out_specs=(VMEM, VMEM),
         scratch_shapes=[
             pltpu.VMEM((2 * depth, 2 * width), jnp.bfloat16),
@@ -289,7 +292,7 @@
     return pl.pallas_call(
         functools.partial(assemble_kernel, by_owner),
         out_shape=(wide, wide),
-        in_specs=[SMEM, VMEM, VMEM] + [ANY] * len(sources),
+        in_specs=[SMEM, VMEM, VMEM] + [HBM] * len(sources),
         out_specs=(VMEM, VMEM),
         scratch_shapes=[
             pltpu.SMEM((request_docs.shape[0],), jnp.int32),
@@ -299,6 +302,26 @@
         cost_estimate=pl.CostEstimate(flops=0, bytes_accessed=16 * 1024 * 1024, transcendentals=0),
         name="assemble",
     )(request_docs, held, spare, *sources)
+
+
+def finish_kernel(own, arrived, slot_row, fresh, outgoing):
+    total = (own[...] + arrived[...].astype(jnp.float32)).astype(jnp.bfloat16)
+    fresh[...] = total
+    rows = lax.broadcasted_iota(jnp.int32, (1, total.shape[0]), 1)
+    pick = (rows == slot_row[...]).astype(jnp.bfloat16)
+    outgoing[...] = jnp.dot(pick, total, preferred_element_type=jnp.float32).astype(jnp.bfloat16)
+
+
+def finish(own, arrived, slot_row):
+    shapes = (own.shape, (slot_row.shape[0], own.shape[1]))
+    return pl.pallas_call(
+        finish_kernel,
+        out_shape=tuple(jax.ShapeDtypeStruct(one, jnp.bfloat16) for one in shapes),
+        in_specs=[VMEM] * 3,
+        out_specs=(VMEM, VMEM),
+        compiler_params=pltpu.CompilerParams(vmem_limit_bytes=16 * 1024 * 1024),
+        name="finish",
+    )(own, arrived, slot_row)
 
 
 def attend_kernel(queries, fresh, keys, values, key_bias, row_place, key_place, mixed):
@@ -399,23 +422,23 @@
             return lax.ppermute(array, axis, [(i, i ^ apart) for i in range(count)])
 
         w_far = swap(pick_weights(w_key, w_value), "seq", 2)
-        h_mine = swap(cut(hidden, w_key.shape[0]), "seq", 1)
-        docs = cut_docs(request_docs, store_keys, store_values, False)
+        h_send, *docs = cut(request_docs, store_keys, store_values, hidden, w_key.shape[0])
+        h_mine = swap(h_send, "seq", 1)
         *docs, w_far = gate((*docs, w_far))
         w_swapped = swap(w_far, "groups", 1)
         docs = [swap(doc, "seq", k + 1) for k, doc in enumerate(docs)]
         h_other = swap(h_mine, "tp", 1)
         own, part = project(hidden, w_key, w_value, w_far, w_swapped, h_mine, h_other)
-        fresh = (own + swap(part, "seq", 1).astype(jnp.float32)).astype(jnp.bfloat16)
+        arrived = swap(part, "seq", 1)
         sources = (store_keys, store_values, *docs)
     else:
-        (docs,) = cut_docs(request_docs, store_keys, store_values, True)
+        (docs,) = cut(request_docs, store_keys, store_values, None, 0)
         sources = (lax.all_to_all(docs, "seq", split_axis=0, concat_axis=0, tiled=True),)
         weights = lax.all_gather(
             jnp.concatenate([w_key, w_value], axis=1), "seq", axis=0, tiled=True
         )
-        fresh = jnp.dot(hidden[0], weights, preferred_element_type=jnp.float32)
-        fresh = fresh.astype(jnp.bfloat16)
+        own = jnp.dot(hidden[0], weights, preferred_element_type=jnp.float32)
+        arrived = jnp.zeros(own.shape, jnp.bfloat16)
 
     my_docs = lax.dynamic_index_in_dim(request_docs, my_index, 0, keepdims=False)
     owners = my_docs // slot_count
@@ -433,6 +456,11 @@
     keys, values = assemble(
         request_docs, jnp.broadcast_to(used, (context, head_dim)), spare, sources, not pairs
     )
+    row_of_slot = owners * capacity + ranks
+    chosen = row_of_slot[None, :] == jnp.arange(seq_count * capacity)[:, None]
+    entry = jnp.max(jnp.where(chosen, jnp.arange(doc_count)[None, :], -doc_count), axis=1)
+    slot_row = entry[:, None] * per_doc + jnp.arange(per_doc)[None, :]
+    fresh, outgoing = finish(own, arrived, slot_row.reshape(-1, 1))
     mixed = attend(
         queries,
         fresh,
@@ -443,12 +471,6 @@
         place.reshape(1, row_count),
     )
 
-    slot_of_row = jnp.repeat(owners * capacity + ranks, per_doc) * per_doc + jnp.tile(
-        jnp.arange(per_doc), doc_count
-    )
-    slots = jnp.arange(seq_count * capacity * per_doc)
-    pick = (slots[:, None] == slot_of_row[None, :]).astype(jnp.bfloat16)
-    outgoing = jnp.dot(pick, fresh, preferred_element_type=jnp.float32).astype(jnp.bfloat16)
     outgoing = outgoing.reshape(seq_count, capacity, per_doc, 2 * head_dim)
     returned = lax.all_to_all(outgoing, "seq", split_axis=0, concat_axis=0, tiled=True)
     returned = returned.reshape(seq_count, capacity, per_doc, 2, head_dim)

time: 99.1 us -> 82.6 us (0.83)
  the two profiles are of different devices: /device:TPU:14 before, /device:TPU:0 now
where the time goes in v6:
time: 82.6 us; the launch traced here: 82 us
  waiting for transfers between devices  38.3 us (46%)
  Pallas kernels  15.9 us (19%)
  starting transfers between devices  15.8 us (19%)
  local copies, waits for them, and re-layouts  9.6 us (12%)
  other arithmetic  1.48 us (2%)
  between operations  0.92 us (1%)
    ppermute x8, waiting for transfers between devices, swap(): return lax.ppermute(array, axis, [(i, i ^ apart) for i in range(count)])  38.3 us
    ppermute x8, starting transfers between devices, swap(): return lax.ppermute(array, axis, [(i, i ^ apart) for i in range(count)])  11.8 us
    unnamed x29, local copies, waits for them, and re-layouts  6.34 us
    pallas_call x1, Pallas kernels, attend(): pl.pallas_call(attend_kernel, out_shape=jax.ShapeDtypeStruct(queries.shap...  4.74 us
    all_to_all x1, starting transfers between devices, shards(): lax.all_to_all(outgoing, 'seq', split_axis=0, concat_axis=0, tiled=True)  3.92 us
    pallas_call x1, Pallas kernels, cut(): pl.pallas_call(functools.partial(cut_kernel, hidden is None), out_shape=t...  3.44 us
    pallas_call x1, Pallas kernels, project(): pl.pallas_call(project_kernel, out_shape=(jax.ShapeDtypeStruct((rows, 2 *...  3.27 us
    pallas_call x1, Pallas kernels, assemble(): pl.pallas_call(functools.partial(assemble_kernel, by_owner), out_shape=(w...  2.42 us
  transfers between devices with their start and end apart: 9, of which 3 were waited for; matrix products, arithmetic and copies ran while one was open for 5% of the time, Pallas kernels for 17%

profile of v6, /device:TPU:0, one launch (start us, length us, event | category | flops | bytes accessed | tf_op | source)
XLA Modules:
  0.0 82.0 jit_solution(9109788201067019228)
XLA Ops:
  0.7 1.8 %pick_weights.1 = bf16[2048,128]{1,0:T(8,128)(2,1)} custom-call(bf16[2048,128]{1,0:T(8,128)(2,1)} %w_key.3, bf16[2048,128]{1,0:T(8,128)(2,1)} %w_value.3), custom_call_target="tpu_custom_call" | custom-call | tf_op jit(solution)/shard_map/pick_weights/pallas_call | solution.py:46
  2.5 4.1 %collective-permute-start = (bf16[2048,128]{1,0:T(8,128)(2,1)}, bf16[2048,128]{1,0:T(8,128)(2,1)}, u32[]{:S(2)}, u32[]{:S(2)}) collective-permute-start(bf16[2048,128]{1,0:T(8,128)(2,1)} %pick_weights.1), channel_id=1, source_target_pairs={{0,8},{4,12},{8,0},{12,4},{1,9},{5,13},{9,1},{13,5},{2,10},{6,14},... | collective-permute-start | bytes 1572872 | tf_op jit(solution)/shard_map/ppermute | solution.py:422
  6.6 3.4 %cut.1 = (bf16[2,96,2048]{2,1,0:T(8,128)(2,1)}, bf16[4,2,128,128]{3,2,1,0:T(8,128)(2,1)}, bf16[4,2,128,128]{3,2,1,0:T(8,128)(2,1)}, bf16[4,2,128,128]{3,2,1,0:T(8,128)(2,1)}) custom-call(s32[4,16]{1,0:T(4,128)} %request_docs.3, bf16[8,128,128]{2,1,0:T(8,128)(2,1)} %rest_0_.3, bf16[8,128,128]{2,1,0:T(8,128)(2,1)} %rest_1_.1, bf16[1,192,8192]{2,1,0:T(8,128)(2,1)} %hidden.1), custom_call_target="tpu_custom_call" | custom-call | tf_op jit(solution)/shard_map/cut/pallas_call | solution.py:151
  10.1 1.7 %collective-permute-start.2 = (bf16[2,96,2048]{2,1,0:T(8,128)(2,1)}, bf16[2,96,2048]{2,1,0:T(8,128)(2,1)}, u32[]{:S(2)}, u32[]{:S(2)}) collective-permute-start(bf16[2,96,2048]{2,1,0:T(8,128)(2,1)} %get-tuple-element.21), channel_id=1, source_target_pairs={{0,4},{4,0},{8,12},{12,8},{1,5},{5,1},{9,13},{13,9},{2,6},{6,2},{1... | collective-permute-start | bytes 2359304 | tf_op jit(solution)/shard_map/ppermute | solution.py:422
  13.0 0.7 iota_reduce_fusion
  13.7 25.8 %collective-permute-done.2.h_mine = bf16[2,96,2048]{2,1,0:T(8,128)(2,1)} collective-permute-done((bf16[2,96,2048]{2,1,0:T(8,128)(2,1)}, bf16[2,96,2048]{2,1,0:T(8,128)(2,1)}, u32[]{:S(2)}, u32[]{:S(2)}) %collective-permute-start.2) | collective-permute-done | bytes 786464 | tf_op jit(solution)/shard_map/ppermute | solution.py:422
  39.6 1.6 %collective-permute-start.1 = (bf16[2048,128]{1,0:T(8,128)(2,1)}, bf16[2048,128]{1,0:T(8,128)(2,1)S(1)}, u32[]{:S(2)}, u32[]{:S(2)}) collective-permute-start(bf16[2048,128]{1,0:T(8,128)(2,1)} %get-tuple-element.20.w_far), channel_id=1, source_target_pairs={{0,16},{16,0},{1,17},{17,1},{2,18},{18,2},{3,19},{19,3},{4,20},{20... | collective-permute-start | bytes 1572872 | tf_op jit(solution)/shard_map/ppermute | solution.py:422
  41.4 3.0 %collective-permute-start.6 = (bf16[4,2,128,128]{3,2,1,0:T(8,128)(2,1)}, bf16[4,2,128,128]{3,2,1,0:T(8,128)(2,1)}, u32[]{:S(2)}, u32[]{:S(2)}) collective-permute-start(bf16[4,2,128,128]{3,2,1,0:T(8,128)(2,1)} %get-tuple-element.27), channel_id=1, source_target_pairs={{0,8},{4,12},{8,0},{12,4},{1,9},{5,13},{9,1},{13,5},{2,10},{6,14},... | collective-permute-start | bytes 786440 | tf_op jit(solution)/shard_map/ppermute | solution.py:422
  44.4 1.4 %collective-permute-start.7 = (bf16[4,2,128,128]{3,2,1,0:T(8,128)(2,1)}, bf16[4,2,128,128]{3,2,1,0:T(8,128)(2,1)}, u32[]{:S(2)}, u32[]{:S(2)}) collective-permute-start(bf16[4,2,128,128]{3,2,1,0:T(8,128)(2,1)} %get-tuple-element.28), channel_id=1, source_target_pairs={{0,12},{4,8},{8,4},{12,0},{1,13},{5,9},{9,5},{13,1},{2,14},{6,10},... | collective-permute-start | bytes 786440 | tf_op jit(solution)/shard_map/ppermute | solution.py:422
  45.8 8.4 %collective-permute-done.1.w_swapped = bf16[2048,128]{1,0:T(8,128)(2,1)S(1)} collective-permute-done((bf16[2048,128]{1,0:T(8,128)(2,1)}, bf16[2048,128]{1,0:T(8,128)(2,1)S(1)}, u32[]{:S(2)}, u32[]{:S(2)}) %collective-permute-start.1) | collective-permute-done | bytes 524320 | tf_op jit(solution)/shard_map/ppermute | solution.py:422
  54.2 1.0 %copy-done.2 = bf16[2048,128]{1,0:T(8,128)(2,1)S(1)} copy-done((bf16[2048,128]{1,0:T(8,128)(2,1)S(1)}, bf16[2048,128]{1,0:T(8,128)(2,1)}, u32[]{:S(2)}) %copy-start.2) | copy-done | bytes 524312
  55.2 1.0 %copy-done.3 = bf16[2048,128]{1,0:T(8,128)(2,1)S(1)} copy-done((bf16[2048,128]{1,0:T(8,128)(2,1)S(1)}, bf16[2048,128]{1,0:T(8,128)(2,1)}, u32[]{:S(2)}) %copy-start.3) | copy-done | bytes 524312
  56.3 3.3 %project.1 = (f32[192,256]{1,0:T(8,128)S(1)}, bf16[192,256]{1,0:T(8,128)(2,1)}) custom-call(bf16[1,192,8192]{2,1,0:T(8,128)(2,1)S(1)} %copy-done.1, bf16[2048,128]{1,0:T(8,128)(2,1)S(1)} %copy-done.2, bf16[2048,128]{1,0:T(8,128)(2,1)S(1)} %copy-done.3, bf16[2048,128]{1,0:T(8,128)(2,1)} %get-tuple-element.20.w_far, ...), custom_call_target="tpu_custom_call" | custom-call | flops 1 | bytes 1 | tf_op jit(solution)/shard_map/project/pallas_call | solution.py:211
  59.5 0.7 copy-done.7
  61.0 4.1 %collective-permute-done.4.arrived = bf16[192,256]{1,0:T(8,128)(2,1)S(1)} collective-permute-done((bf16[192,256]{1,0:T(8,128)(2,1)}, bf16[192,256]{1,0:T(8,128)(2,1)S(1)}, u32[]{:S(2)}, u32[]{:S(2)}) %collective-permute-start.4) | collective-permute-done | bytes 98336 | tf_op jit(solution)/shard_map/ppermute | solution.py:422
  65.0 0.9 %copy-done.8 = f32[192,256]{1,0:T(8,128)S(1)} copy-done((f32[192,256]{1,0:T(8,128)S(1)}, f32[192,256]{1,0:T(8,128)}, u32[]{:S(2)}) %copy-start.8) | copy-done | bytes 196632
  66.2 0.7 copy.45
  66.9 3.9 %all-to-all-start = ((bf16[4,4,12,256]{3,1,2,0:T(4,128)(2,1)}), bf16[4,4,12,256]{3,1,2,0:T(4,128)(2,1)}, u32[]{:S(2)}, u32[]{:S(2)}) async-start(bf16[4,4,12,256]{3,1,2,0:T(4,128)(2,1)} %copy.45), calls=%async_computation | async-start | bytes 196608 | tf_op jit(solution)/shard_map/all_to_all | solution.py:475
  71.3 0.9 %copy-done.5 = bf16[8,128,128]{2,1,0:T(8,128)(2,1)S(1)} copy-done((bf16[8,128,128]{2,1,0:T(8,128)(2,1)S(1)}, bf16[8,128,128]{2,1,0:T(8,128)(2,1)}, u32[]{:S(2)}) %copy-start.5) | copy-done | bytes 262168
  72.2 2.4 %assemble.1 = (bf16[2048,256]{1,0:T(8,128)(2,1)S(1)}, bf16[2048,256]{1,0:T(8,128)(2,1)S(1)}) custom-call(s32[4,16]{1,0:T(4,128)S(1)} %copy-done.11, bf16[2048,128]{1,0:T(8,128)(2,1)S(1)} %broadcast_in_dim.17.held, bf16[16,2048]{1,0:T(8,128)(2,1)S(1)} %fusion.spare, bf16[8,128,128]{2,1,0:T(8,128)(2,1)S(1)} %copy-done.4, bf16[8,128,128]{2,1,0:T(8,128)(2,1)S(1)} %copy-done.5, ...), custom_call_target="tpu_custom_call" | custom-call | bytes 16777216 | tf_op jit(solution)/shard_map/assemble/pallas_call | solution.py:292
  74.7 0.9 %copy-done.10 = bf16[192,256]{1,0:T(8,128)(2,1)S(1)} copy-done((bf16[192,256]{1,0:T(8,128)(2,1)S(1)}, bf16[192,256]{1,0:T(8,128)(2,1)}, u32[]{:S(2)}) %copy-start.10) | copy-done | bytes 98328
  75.6 4.7 %attend.1 = bf16[1,192,1024]{2,1,0:T(8,128)(2,1)} custom-call(bf16[1,192,1024]{2,1,0:T(8,128)(2,1)S(1)} %copy-done.6, bf16[192,256]{1,0:T(8,128)(2,1)S(1)} %copy-done.10, bf16[2048,256]{1,0:T(8,128)(2,1)S(1)} %get-tuple-element.29.keys, bf16[2048,256]{1,0:T(8,128)(2,1)S(1)} %get-tuple-element.30.values, f32[1,2048]{1,0:T(1,128)S(1)} %bitcast.28, ...), custom_call_target="tpu_custom_call" | custom-call | flops 1 | bytes 1 | tf_op jit(solution)/shard_map/attend/pallas_call | solution.py:387
  80.3 0.9 %broadcast_in_dim_reshape.3 = bf16[1,4,4,12,2,128]{5,4,2,3,1,0:T(2,128)(2,1)S(1)} reshape(bf16[4,4,12,256]{3,1,2,0:T(4,128)(2,1)} %all-to-all-done) | data formatting | bytes 196608 | tf_op jit(solution)/shard_map/broadcast_in_dim;reshape | solution.py:477
  81.3 0.7 copy.46
  (60 shorter events, 2.9 us)
Async XLA Ops:
  0.6 11.5 %copy-start = (s32[32]{0:T(128)S(1)}, s32[32]{0:T(128)}, u32[]{:S(2)}) copy-start(s32[32]{0:T(128)} %param.16) | copy-start | bytes 388
  0.6 11.1 %copy-start.11 = (s32[4,16]{1,0:T(4,128)S(1)}, s32[4,16]{1,0:T(4,128)}, u32[]{:S(2)}) copy-start(s32[4,16]{1,0:T(4,128)} %request_docs.3) | copy-start | bytes 772
  0.7 11.3 %copy-start.12 = (s32[1,16,12]{1,0,2:T(1,128)S(1)}, s32[1,16,12]{1,0,2:T(1,128)}, u32[]{:S(2)}) copy-start(s32[1,16,12]{1,0,2:T(1,128)} %param.17) | copy-start | bytes 2308
  2.5 51.7 %copy-start.1 = (bf16[1,192,8192]{2,1,0:T(8,128)(2,1)S(1)}, bf16[1,192,8192]{2,1,0:T(8,128)(2,1)}, u32[]{:S(2)}) copy-start(bf16[1,192,8192]{2,1,0:T(8,128)(2,1)} %hidden.1) | copy-start | bytes 9437188
  2.5 37.1 %collective-permute-start = (bf16[2048,128]{1,0:T(8,128)(2,1)}, bf16[2048,128]{1,0:T(8,128)(2,1)}, u32[]{:S(2)}, u32[]{:S(2)}) collective-permute-start(bf16[2048,128]{1,0:T(8,128)(2,1)} %pick_weights.1), channel_id=1, source_target_pairs={{0,8},{4,12},{8,0},{12,4},{1,9},{5,13},{9,1},{13,5},{2,10},{6,14},... | collective-permute-start | bytes 1572872 | tf_op jit(solution)/shard_map/ppermute | solution.py:422
  10.1 29.5 %collective-permute-start.2 = (bf16[2,96,2048]{2,1,0:T(8,128)(2,1)}, bf16[2,96,2048]{2,1,0:T(8,128)(2,1)}, u32[]{:S(2)}, u32[]{:S(2)}) collective-permute-start(bf16[2,96,2048]{2,1,0:T(8,128)(2,1)} %get-tuple-element.21), channel_id=1, source_target_pairs={{0,4},{4,0},{8,12},{12,8},{1,5},{5,1},{9,13},{13,9},{2,6},{6,2},{1... | collective-permute-start | bytes 2359304 | tf_op jit(solution)/shard_map/ppermute | solution.py:422
  39.5 14.6 %collective-permute-start.3 = (bf16[2,96,2048]{2,1,0:T(8,128)(2,1)}, bf16[2,96,2048]{2,1,0:T(8,128)(2,1)S(1)}, u32[]{:S(2)}, u32[]{:S(2)}) collective-permute-start(bf16[2,96,2048]{2,1,0:T(8,128)(2,1)} %collective-permute-done.2.h_mine), channel_id=1, source_target_pairs={{0,1},{1,0},{2,3},{3,2},{4,5},{5,4},{6,7},{7,6},{8,9},{9,8},{10,11... | collective-permute-start | bytes 2359304 | tf_op jit(solution)/shard_map/ppermute | solution.py:422
  39.6 14.6 %collective-permute-start.1 = (bf16[2048,128]{1,0:T(8,128)(2,1)}, bf16[2048,128]{1,0:T(8,128)(2,1)S(1)}, u32[]{:S(2)}, u32[]{:S(2)}) collective-permute-start(bf16[2048,128]{1,0:T(8,128)(2,1)} %get-tuple-element.20.w_far), channel_id=1, source_target_pairs={{0,16},{16,0},{1,17},{17,1},{2,18},{18,2},{3,19},{19,3},{4,20},{20... | collective-permute-start | bytes 1572872 | tf_op jit(solution)/shard_map/ppermute | solution.py:422
  41.3 29.6 %collective-permute-start.5 = (bf16[4,2,128,128]{3,2,1,0:T(8,128)(2,1)}, bf16[4,2,128,128]{3,2,1,0:T(8,128)(2,1)}, u32[]{:S(2)}, u32[]{:S(2)}) collective-permute-start(bf16[4,2,128,128]{3,2,1,0:T(8,128)(2,1)} %get-tuple-element.26), channel_id=1, source_target_pairs={{0,4},{4,0},{8,12},{12,8},{1,5},{5,1},{9,13},{13,9},{2,6},{6,2},{1... | collective-permute-start | bytes 786440 | tf_op jit(solution)/shard_map/ppermute | solution.py:422
  41.4 29.5 %collective-permute-start.6 = (bf16[4,2,128,128]{3,2,1,0:T(8,128)(2,1)}, bf16[4,2,128,128]{3,2,1,0:T(8,128)(2,1)}, u32[]{:S(2)}, u32[]{:S(2)}) collective-permute-start(bf16[4,2,128,128]{3,2,1,0:T(8,128)(2,1)} %get-tuple-element.27), channel_id=1, source_target_pairs={{0,8},{4,12},{8,0},{12,4},{1,9},{5,13},{9,1},{13,5},{2,10},{6,14},... | collective-permute-start | bytes 786440 | tf_op jit(solution)/shard_map/ppermute | solution.py:422
  44.4 26.5 %collective-permute-start.7 = (bf16[4,2,128,128]{3,2,1,0:T(8,128)(2,1)}, bf16[4,2,128,128]{3,2,1,0:T(8,128)(2,1)}, u32[]{:S(2)}, u32[]{:S(2)}) collective-permute-start(bf16[4,2,128,128]{3,2,1,0:T(8,128)(2,1)} %get-tuple-element.28), channel_id=1, source_target_pairs={{0,12},{4,8},{8,4},{12,0},{1,13},{5,9},{9,5},{13,1},{2,14},{6,10},... | collective-permute-start | bytes 786440 | tf_op jit(solution)/shard_map/ppermute | solution.py:422
  54.2 1.0 %copy-start.2 = (bf16[2048,128]{1,0:T(8,128)(2,1)S(1)}, bf16[2048,128]{1,0:T(8,128)(2,1)}, u32[]{:S(2)}) copy-start(bf16[2048,128]{1,0:T(8,128)(2,1)} %w_key.3) | copy-start | bytes 1572868
  55.2 1.0 %copy-start.3 = (bf16[2048,128]{1,0:T(8,128)(2,1)S(1)}, bf16[2048,128]{1,0:T(8,128)(2,1)}, u32[]{:S(2)}) copy-start(bf16[2048,128]{1,0:T(8,128)(2,1)} %w_value.3) | copy-start | bytes 1572868
  56.3 15.0 %copy-start.4 = (bf16[8,128,128]{2,1,0:T(8,128)(2,1)S(1)}, bf16[8,128,128]{2,1,0:T(8,128)(2,1)}, u32[]{:S(2)}) copy-start(bf16[8,128,128]{2,1,0:T(8,128)(2,1)} %rest_0_.3) | copy-start | bytes 786436
  59.5 0.7 copy-start.7
  60.2 14.5 %copy-start.6 = (bf16[1,192,1024]{2,1,0:T(8,128)(2,1)S(1)}, bf16[1,192,1024]{2,1,0:T(8,128)(2,1)}, u32[]{:S(2)}) copy-start(bf16[1,192,1024]{2,1,0:T(8,128)(2,1)} %queries.1) | copy-start | bytes 1179652
  60.2 4.8 %collective-permute-start.4 = (bf16[192,256]{1,0:T(8,128)(2,1)}, bf16[192,256]{1,0:T(8,128)(2,1)S(1)}, u32[]{:S(2)}, u32[]{:S(2)}) collective-permute-start(bf16[192,256]{1,0:T(8,128)(2,1)} %get-tuple-element.23), channel_id=1, source_target_pairs={{0,4},{4,0},{8,12},{12,8},{1,5},{5,1},{9,13},{13,9},{2,6},{6,2},{1... | collective-permute-start | bytes 294920 | tf_op jit(solution)/shard_map/ppermute | solution.py:422
  65.0 0.9 %copy-start.8 = (f32[192,256]{1,0:T(8,128)S(1)}, f32[192,256]{1,0:T(8,128)}, u32[]{:S(2)}) copy-start(f32[192,256]{1,0:T(8,128)} %copy-done.7) | copy-start | bytes 589828
  66.2 4.8 %copy-start.9 = (bf16[192,256]{1,0:T(8,128)(2,1)}, bf16[192,256]{1,0:T(8,128)(2,1)S(1)}, u32[]{:S(2)}) copy-start(bf16[192,256]{1,0:T(8,128)(2,1)S(1)} %get-tuple-element.24.fresh) | copy-start | bytes 294916
  66.9 13.4 %all-to-all-start = ((bf16[4,4,12,256]{3,1,2,0:T(4,128)(2,1)}), bf16[4,4,12,256]{3,1,2,0:T(4,128)(2,1)}, u32[]{:S(2)}, u32[]{:S(2)}) async-start(bf16[4,4,12,256]{3,1,2,0:T(4,128)(2,1)} %copy.45), calls=%async_computation | async-start | bytes 196608 | tf_op jit(solution)/shard_map/all_to_all | solution.py:475
  71.3 1.0 %copy-start.5 = (bf16[8,128,128]{2,1,0:T(8,128)(2,1)S(1)}, bf16[8,128,128]{2,1,0:T(8,128)(2,1)}, u32[]{:S(2)}) copy-start(bf16[8,128,128]{2,1,0:T(8,128)(2,1)} %rest_1_.1) | copy-start | bytes 786436
  74.7 0.9 %copy-start.10 = (bf16[192,256]{1,0:T(8,128)(2,1)S(1)}, bf16[192,256]{1,0:T(8,128)(2,1)}, u32[]{:S(2)}) copy-start(bf16[192,256]{1,0:T(8,128)(2,1)} %copy-done.9) | copy-start | bytes 294916

commit v7 on v6

--- a/solution.py
+++ b/solution.py
@@ -15,14 +15,20 @@
 MASKED = -1e30
 
 
-def pick_kernel(w_key, w_value, w_out, staged, sems):
+def in_hbm(array):
+    return pltpu.with_memory_space_constraint(array, pltpu.HBM)
+
+
+def send_kernel(hidden, w_key, w_value, w_out, h_out, w_held, h_held, w_sems, h_sems):
     group = lax.axis_index("groups")
-    pieces = staged.shape[0]
-    rows = staged.shape[1]
+    me = lax.axis_index("seq")
+    quarter = lax.axis_index("tp")
+    pieces, piece = w_held.shape[:2]
+    rows, depth = h_out.shape[1:]
 
     def fetch(i, weight):
-        source = weight.at[pl.ds(i * rows, rows)]
-        return pltpu.make_async_copy(source, staged.at[i], sems.at[0, i])
+        source = weight.at[pl.ds(i * piece, piece)]
+        return pltpu.make_async_copy(source, w_held.at[i], w_sems.at[0, i])
 
     for chosen, weight in ((0, w_key), (1, w_value)):
 
@@ -31,29 +37,50 @@
             for i in range(pieces):
                 fetch(i, weight).start()
 
+    first = me + 1 - 2 * lax.rem(me, 2)
     stores = []
+    h_fetches = []
+    for i, block in enumerate((first, lax.rem(first + 2, 4))):
+        source = hidden.at[
+            0,
+            pl.ds(pl.multiple_of(quarter * rows, rows), rows),
+            pl.ds(pl.multiple_of(block * depth, depth), depth),
+        ]
+        h_fetches.append(pltpu.make_async_copy(source, h_held.at[i], h_sems.at[0, i]))
+        h_fetches[-1].start()
     for i in range(pieces):
         fetch(i, w_key).wait()
-        target = w_out.at[pl.ds(i * rows, rows)]
-        stores.append(pltpu.make_async_copy(staged.at[i], target, sems.at[1, i]))
+        target = w_out.at[pl.ds(i * piece, piece)]
+        stores.append(pltpu.make_async_copy(w_held.at[i], target, w_sems.at[1, i]))
+        stores[-1].start()
+    for i, one in enumerate(h_fetches):
+        one.wait()
+        stores.append(pltpu.make_async_copy(h_held.at[i], h_out.at[i], h_sems.at[1, i]))
         stores[-1].start()
     for store in stores:
         store.wait()
 
 
-def pick_weights(w_key, w_value):
+def pick_sent(hidden, w_key, w_value):
+    depth, width = w_key.shape
     pieces = 4
-    return pl.pallas_call(
-        pick_kernel,
-        out_shape=jax.ShapeDtypeStruct(w_key.shape, jnp.bfloat16),
-        in_specs=[HBM, HBM],
-        out_specs=HBM,
+    h_shape = (2, hidden.shape[1] // 4, depth)
+    return pl.pallas_call(
+        send_kernel,
+        out_shape=(
+            jax.ShapeDtypeStruct(w_key.shape, jnp.bfloat16),
+            jax.ShapeDtypeStruct(h_shape, jnp.bfloat16),
+        ),
+        in_specs=[ANY] * 3,
+        out_specs=(ANY, ANY),
         scratch_shapes=[
-            pltpu.VMEM((pieces, w_key.shape[0] // pieces, w_key.shape[1]), jnp.bfloat16),
+            pltpu.VMEM((pieces, depth // pieces, width), jnp.bfloat16),
+            pltpu.VMEM(h_shape, jnp.bfloat16),
             pltpu.SemaphoreType.DMA((2, pieces)),
+            pltpu.SemaphoreType.DMA((2, 2)),
         ],
-        name="pick_weights",
-    )(w_key, w_value)
+        name="pick_sent",
+    )(hidden, w_key, w_value)
 
 
 def gate_kernel(*refs):
@@ -67,35 +94,16 @@
         in_specs=[ANY] * len(arrays),
         out_specs=(ANY,) * len(arrays),
         input_output_aliases={i: i for i in range(len(arrays))},
-        compiler_params=pltpu.CompilerParams(vmem_limit_bytes=1 * 1024 * 1024),
         name="gate",
     )(*arrays)
 
 
-def cut_kernel(by_owner, request_docs, store_keys, store_values, *rest):
-    if by_owner:
-        out, picks, sems = rest
-        outs = (out,)
-    else:
-        hidden, h_out, *outs, picks, sems = rest
+def docs_kernel(by_owner, request_docs, store_keys, store_values, *rest):
+    *outs, picks, sems = rest
     me = lax.axis_index("seq")
     requests, doc_count = request_docs.shape
     slots = store_keys.shape[0]
     capacity = slots // 2
-    h_copies = []
-    if not by_owner:
-        core = lax.rem(lax.axis_index("tp"), 2)
-        rows, depth = h_out.shape[1:]
-        first = me + 1 - 2 * lax.rem(me, 2)
-        second = lax.rem(first + 2, 4)
-        for i, block in enumerate((first, second)):
-            source = hidden.at[
-                0,
-                pl.ds(pl.multiple_of(core * rows, rows), rows),
-                pl.ds(pl.multiple_of(block * depth, depth), depth),
-            ]
-            h_copies.append(pltpu.make_async_copy(source, h_out.at[i], sems.at[len(outs) + i]))
-            h_copies[-1].start()
 
     def one_request(r, carry):
         for c in range(capacity):
@@ -132,99 +140,116 @@
     else:
         for i, out in enumerate(outs):
             send(lax.bitwise_xor(me, i + 1), out, sems.at[i])
-    for copy in h_copies:
-        copy.wait()
     for i, out in enumerate(outs):
         pltpu.make_async_copy(out, out, sems.at[i]).wait()
 
 
-def cut(request_docs, store_keys, store_values, hidden, depth):
+def pick_docs(request_docs, store_keys, store_values, by_owner):
     requests = request_docs.shape[0]
     capacity = store_keys.shape[0] // 2
     one = (capacity, 2) + store_keys.shape[1:]
-    if hidden is None:
-        shapes = ((requests,) + one,)
-        inputs = (store_keys, store_values)
-    else:
-        shapes = ((2, hidden.shape[1] // 2, depth),) + (one,) * (requests - 1)
-        inputs = (store_keys, store_values, hidden)
-    return pl.pallas_call(
-        functools.partial(cut_kernel, hidden is None),
+    shapes = ((requests,) + one,) if by_owner else (one,) * (requests - 1)
+    return pl.pallas_call(
+        functools.partial(docs_kernel, by_owner),
         out_shape=tuple(jax.ShapeDtypeStruct(one, jnp.bfloat16) for one in shapes),
-        in_specs=[SMEM] + [HBM] * len(inputs),
+        in_specs=[SMEM, ANY, ANY],
         out_specs=(VMEM,) * len(shapes),
         scratch_shapes=[
             pltpu.SMEM((requests, capacity), jnp.int32),
-            pltpu.SemaphoreType.DMA((len(shapes) + 1,)),
+            pltpu.SemaphoreType.DMA((len(shapes),)),
         ],
-        name="cut",
-    )(request_docs, *inputs)
-
-
-def project_kernel(
-    hidden, w_key, w_value, w_far, w_swapped, h_mine, h_other, own, part, w, h, sems
-):
+        name="pick_docs",
+    )(request_docs, store_keys, store_values)
+
+
+def lay_rows(hidden, quarters, block, depth, h, copy):
+    mine = lax.axis_index("tp")
+    rows = hidden.shape[1]
+    piece = rows // len(quarters)
+    start = pl.multiple_of(block * depth, depth)
+    copy(hidden.at[0, :, pl.ds(start, depth)], h.at[pl.ds(0, rows)])
+    for k, quarter in enumerate(quarters):
+        start = pl.multiple_of(rows + lax.bitwise_xor(mine, k) * piece, piece)
+        copy(quarter, h.at[pl.ds(start, piece)])
+
+
+def near_kernel(hidden, w_key, w_value, *rest):
+    *quarters, total, w, h, sems = rest
+    depth, width = w_key.shape
+    copies = []
+
+    def copy(source, target):
+        copies.append(pltpu.make_async_copy(source, target, sems.at[len(copies)]))
+        copies[-1].start()
+
+    for i, held in enumerate((w_key, w_value)):
+        copy(held, w.at[:, pl.ds(i * width, width)])
+    quarters = [quarter.at[0] for quarter in quarters]
+    lay_rows(hidden, quarters, lax.axis_index("seq"), depth, h, copy)
+    for one in copies:
+        one.wait()
+    total[...] = jnp.dot(h[...], w[...], preferred_element_type=jnp.float32)
+
+
+def far_kernel(hidden, w_far, w_swapped, near, *rest):
+    *quarters, own, part, w, h, sems, held_own, own_sem = rest
     group = lax.axis_index("groups")
-    me = lax.axis_index("seq")
-    core = lax.rem(lax.axis_index("tp"), 2)
+    depth, width = w_far.shape
+    rows = hidden.shape[1]
+    copies = []
+
+    def copy(source, target):
+        copies.append(pltpu.make_async_copy(source, target, sems.at[len(copies)]))
+        copies[-1].start()
+
+    for held, place in ((w_far, group), (w_swapped, 1 - group)):
+        copy(held, w.at[:, pl.ds(pl.multiple_of(place * width, width), width)])
+    quarters = [quarter.at[1] for quarter in quarters]
+    lay_rows(hidden, quarters, lax.rem(lax.axis_index("seq") + 2, 4), depth, h, copy)
+    for one in copies:
+        one.wait()
+    total = near[...] + jnp.dot(h[...], w[...], preferred_element_type=jnp.float32)
+    held_own[...] = total[:rows]
+    store = pltpu.make_async_copy(held_own, own, own_sem)
+    store.start()
+    part[...] = total[rows:].astype(part.dtype)
+    store.wait()
+
+
+def project(hidden, w_key, w_value, w_far, w_swapped, quarters):
     depth, width = w_key.shape
     rows = hidden.shape[1]
-    far = lax.rem(me + 2, 4)
-    near = pl.ds(0, depth)
-    rest = pl.ds(depth, depth)
-    keys = pl.ds(0, width)
-    values = pl.ds(width, width)
-    copies = [
-        pltpu.make_async_copy(w_key, w.at[near, keys], sems.at[0]),
-        pltpu.make_async_copy(w_value, w.at[near, values], sems.at[1]),
+    scratch = [
+        pltpu.VMEM((depth, 2 * width), jnp.bfloat16),
+        pltpu.VMEM((2 * rows, depth), jnp.bfloat16),
+        pltpu.SemaphoreType.DMA((3 + len(quarters),)),
     ]
-    for i, block in enumerate((me, far)):
-        columns = pl.ds(i * depth, depth)
-        source = hidden.at[0, :, pl.ds(pl.multiple_of(block * depth, depth), depth)]
-        copies.append(
-            pltpu.make_async_copy(source, h.at[pl.ds(0, rows), columns], sems.at[2 + 3 * i])
-        )
-        for k, (held, place) in enumerate(((h_mine, core), (h_other, 1 - core))):
-            start = pl.multiple_of(rows + place * (rows // 2), rows // 2)
-            target = h.at[pl.ds(start, rows // 2), columns]
-            copies.append(pltpu.make_async_copy(held.at[i], target, sems.at[3 + 3 * i + k]))
-    for one in copies:
-        one.start()
-
-    first = pl.multiple_of(group * width, width)
-    second = pl.multiple_of((1 - group) * width, width)
-    for i, (held, column) in enumerate(((w_far, first), (w_swapped, second))):
-        copies.append(
-            pltpu.make_async_copy(held, w.at[rest, pl.ds(column, width)], sems.at[8 + i])
-        )
-        copies[-1].start()
-    for one in copies:
-        one.wait()
-    total = jnp.dot(h[...], w[...], preferred_element_type=jnp.float32)
-    own[...] = total[:rows]
-    part[...] = total[rows:].astype(part.dtype)
-
-
-def project(hidden, w_key, w_value, *arrived):
-    depth, width = w_key.shape
-    rows = hidden.shape[1]
-    return pl.pallas_call(
-        project_kernel,
+    settings = dict(
+        compiler_params=pltpu.CompilerParams(vmem_limit_bytes=16 * 1024 * 1024),
+        cost_estimate=pl.CostEstimate(flops=1, bytes_accessed=1, transcendentals=0),
+    )
+    near = pl.pallas_call(
+        near_kernel,
+        out_shape=jax.ShapeDtypeStruct((2 * rows, 2 * width), jnp.float32),
+        in_specs=[ANY] * (3 + len(quarters)),
+        out_specs=VMEM,
+        scratch_shapes=scratch,
+        name="project_near",
+        **settings,
+    )(hidden, in_hbm(w_key), in_hbm(w_value), *quarters)
+    return pl.pallas_call(
+        far_kernel,
         out_shape=(
             jax.ShapeDtypeStruct((rows, 2 * width), jnp.float32),
             jax.ShapeDtypeStruct((rows, 2 * width), jnp.bfloat16),
         ),
-        in_specs=[HBM] * (3 + len(arrived)),
-        out_specs=(VMEM, VMEM),
-        scratch_shapes=[
-            pltpu.VMEM((2 * depth, 2 * width), jnp.bfloat16),
-            pltpu.VMEM((2 * rows, 2 * depth), jnp.bfloat16),
-            pltpu.SemaphoreType.DMA((10,)),
-        ],
-        compiler_params=pltpu.CompilerParams(vmem_limit_bytes=32 * 1024 * 1024),
-        cost_estimate=pl.CostEstimate(flops=1, bytes_accessed=1, transcendentals=0),
-        name="project",
-    )(hidden, w_key, w_value, *arrived)
+        in_specs=[ANY] * 3 + [VMEM] + [ANY] * len(quarters),
+        out_specs=(ANY, VMEM),
+        scratch_shapes=scratch
+        + [pltpu.VMEM((rows, 2 * width), jnp.float32), pltpu.SemaphoreType.DMA],
+        name="project_far",
+        **settings,
+    )(hidden, w_far, w_swapped, near, *quarters)
 
 
 def assemble_kernel(
@@ -304,21 +329,109 @@
     )(request_docs, held, spare, *sources)
 
 
-def finish_kernel(own, arrived, slot_row, fresh, outgoing):
-    total = (own[...] + arrived[...].astype(jnp.float32)).astype(jnp.bfloat16)
+def plan_kernel(
+    capacity, slots, request_docs, doc_lengths, rows, held, spare, key_bias, row_place, key_place, slot_row, counts
+):
+    me = lax.axis_index("seq")
+    per_doc, _, doc_count = rows.shape
+    doc_len = held.shape[0] // doc_count
+    row_count = row_place.shape[0]
+    docs = lax.broadcasted_iota(jnp.int32, (1, doc_count), 1)
+    lengths = jnp.zeros((1, doc_count), jnp.int32)
+    places = jnp.zeros((1, doc_count), jnp.int32)
+    for o in range(counts.shape[0]):
+        counts[o] = 0
+    for j in range(doc_count):
+        doc = request_docs[me, j]
+        owner = lax.div(doc, slots)
+        rank = counts[owner]
+        counts[owner] = rank + 1
+        lengths = jnp.where(docs == j, doc_lengths[doc], lengths)
+        places = jnp.where(docs == j, owner * capacity + rank, places)
+    slot = lax.broadcasted_iota(jnp.int32, (doc_len, doc_count), 0)
+    used = slot < lengths
+    for i in range(per_doc):
+        used &= slot != rows[i]
+    used = used.astype(jnp.float32)
+    first = jnp.min(jnp.where(used > 0, slot, doc_len), axis=0, keepdims=True)
+    firsts = (slot == first).astype(jnp.bfloat16)
+    eye = lax.broadcasted_iota(jnp.int32, (doc_count, doc_count), 0) == docs
+    across = (((1,), (1,)), ((), ()))
+
+    def turned(columns):
+        return lax.dot_general(
+            eye.astype(jnp.bfloat16), columns, across, preferred_element_type=jnp.float32
+        )
+
+    bias = jnp.where(turned(used.astype(jnp.bfloat16)) > 0, 0.0, MASKED)
+    firsts = turned(firsts)
+    doc = lax.broadcasted_iota(jnp.int32, (doc_count, 1), 0)
+    for j in range(doc_count):
+        part = slice(j * doc_len, (j + 1) * doc_len)
+        held[part, :] = jnp.broadcast_to(used[:, j : j + 1], (doc_len, held.shape[1])).astype(
+            held.dtype
+        )
+        key_bias[:, part] = bias[j : j + 1, :]
+        spare[:, part] = jnp.where(doc == j, firsts, 0.0).astype(spare.dtype)
+    row = lax.broadcasted_iota(jnp.int32, (row_count, doc_count), 0)
+    start = per_doc * lax.broadcasted_iota(jnp.int32, (row_count, doc_count), 1)
+    of_doc = (row >= start) & (row < start + per_doc)
+    nth = jnp.sum(jnp.where(of_doc, row - start, 0), axis=1, keepdims=True)
+    chosen = jnp.zeros((row_count, doc_count), jnp.int32)
+    for i in range(per_doc):
+        chosen = jnp.where(nth == i, rows[i], chosen)
+    chosen = jnp.where(of_doc, chosen + doc_len * docs, 0)
+    column = jnp.sum(chosen, axis=1, keepdims=True)
+    goes = nth + per_doc * jnp.sum(jnp.where(of_doc, places, 0), axis=1, keepdims=True)
+    row_place[...] = column
+    square = (row_count, row_count)
+    same = lax.broadcasted_iota(jnp.int32, square, 0) == lax.broadcasted_iota(jnp.int32, square, 1)
+    key_place[...] = jnp.sum(jnp.where(same, column, 0), axis=0, keepdims=True)
+    slot_row[...] = jnp.sum(jnp.where(same, goes, 0), axis=0, keepdims=True)
+
+
+def plan(request_docs, doc_lengths, recompute_rows, slots, head_dim, doc_len):
+    _, doc_count, per_doc = recompute_rows.shape
+    rows = doc_count * per_doc
+    context = doc_count * doc_len
+    shapes = (
+        ((context, head_dim), jnp.bfloat16),
+        ((doc_count, context), jnp.bfloat16),
+        ((1, context), jnp.float32),
+        ((rows, 1), jnp.int32),
+        ((1, rows), jnp.int32),
+        ((1, rows), jnp.int32),
+    )
+    return pl.pallas_call(
+        functools.partial(plan_kernel, slots // 2, slots),
+        out_shape=tuple(jax.ShapeDtypeStruct(*one) for one in shapes),
+        in_specs=[SMEM, SMEM, VMEM],
+        out_specs=(VMEM,) * len(shapes),
+        scratch_shapes=[pltpu.SMEM((request_docs.shape[0],), jnp.int32)],
+        compiler_params=pltpu.CompilerParams(vmem_limit_bytes=16 * 1024 * 1024),
+        name="plan",
+    )(request_docs, doc_lengths, jnp.transpose(recompute_rows, (2, 0, 1)))
+
+
+def finish_kernel(own, arrived, slot_row, fresh, outgoing, held, sem):
+    fetch = pltpu.make_async_copy(own, held, sem)
+    fetch.start()
+    fetch.wait()
+    total = (held[...] + arrived[...].astype(jnp.float32)).astype(jnp.bfloat16)
     fresh[...] = total
-    rows = lax.broadcasted_iota(jnp.int32, (1, total.shape[0]), 1)
-    pick = (rows == slot_row[...]).astype(jnp.bfloat16)
+    slots = lax.broadcasted_iota(jnp.int32, (outgoing.shape[0], 1), 0)
+    pick = (slots == slot_row[...]).astype(jnp.bfloat16)
     outgoing[...] = jnp.dot(pick, total, preferred_element_type=jnp.float32).astype(jnp.bfloat16)
 
 
-def finish(own, arrived, slot_row):
-    shapes = (own.shape, (slot_row.shape[0], own.shape[1]))
+def finish(own, arrived, slot_row, slots):
+    shapes = (own.shape, (slots, own.shape[1]))
     return pl.pallas_call(
         finish_kernel,
         out_shape=tuple(jax.ShapeDtypeStruct(one, jnp.bfloat16) for one in shapes),
-        in_specs=[VMEM] * 3,
+        in_specs=[ANY, VMEM, VMEM],
         out_specs=(VMEM, VMEM),
+        scratch_shapes=[pltpu.VMEM(own.shape, jnp.float32), pltpu.SemaphoreType.DMA],
         compiler_params=pltpu.CompilerParams(vmem_limit_bytes=16 * 1024 * 1024),
         name="finish",
     )(own, arrived, slot_row)
@@ -407,32 +520,30 @@
     doc_lengths,
     recompute_rows,
 ):
-    my_index = lax.axis_index("seq")
     seq_count = lax.axis_size("seq")
     slot_count, doc_len, head_dim = store_keys.shape
     capacity = slot_count // 2
-    doc_count = request_docs.shape[1]
-    row_ids = recompute_rows[0]
-    per_doc = row_ids.shape[1]
-    row_count = doc_count * per_doc
+    per_doc = recompute_rows.shape[2]
 
     if pairs:
         def swap(array, axis, apart):
             count = lax.axis_size(axis)
             return lax.ppermute(array, axis, [(i, i ^ apart) for i in range(count)])
 
-        w_far = swap(pick_weights(w_key, w_value), "seq", 2)
-        h_send, *docs = cut(request_docs, store_keys, store_values, hidden, w_key.shape[0])
+        w_send, h_send = pick_sent(hidden, w_key, w_value)
+        w_far = swap(w_send, "seq", 2)
         h_mine = swap(h_send, "seq", 1)
+        docs = pick_docs(request_docs, store_keys, store_values, False)
         *docs, w_far = gate((*docs, w_far))
         w_swapped = swap(w_far, "groups", 1)
         docs = [swap(doc, "seq", k + 1) for k, doc in enumerate(docs)]
-        h_other = swap(h_mine, "tp", 1)
-        own, part = project(hidden, w_key, w_value, w_far, w_swapped, h_mine, h_other)
+        h_chip = swap(h_mine, "tp", 2)
+        quarters = (h_mine, swap(h_mine, "tp", 1), h_chip, swap(h_chip, "tp", 1))
+        own, part = project(hidden, w_key, w_value, w_far, w_swapped, quarters)
         arrived = swap(part, "seq", 1)
         sources = (store_keys, store_values, *docs)
     else:
-        (docs,) = cut(request_docs, store_keys, store_values, None, 0)
+        (docs,) = pick_docs(request_docs, store_keys, store_values, True)
         sources = (lax.all_to_all(docs, "seq", split_axis=0, concat_axis=0, tiled=True),)
         weights = lax.all_gather(
             jnp.concatenate([w_key, w_value], axis=1), "seq", axis=0, tiled=True
@@ -440,45 +551,23 @@
         own = jnp.dot(hidden[0], weights, preferred_element_type=jnp.float32)
         arrived = jnp.zeros(own.shape, jnp.bfloat16)
 
-    my_docs = lax.dynamic_index_in_dim(request_docs, my_index, 0, keepdims=False)
-    owners = my_docs // slot_count
-    earlier = jnp.arange(doc_count)[None, :] < jnp.arange(doc_count)[:, None]
-    ranks = jnp.sum(((owners[:, None] == owners[None, :]) & earlier).astype(jnp.int32), axis=1)
-    positions = jnp.arange(doc_len, dtype=jnp.int32)
-    held = positions[None, :] < doc_lengths[my_docs][:, None]
-    held &= jnp.all(positions[None, None, :] != row_ids[:, :, None], axis=1)
-    key_bias = jnp.where(held, 0.0, MASKED).astype(jnp.float32).reshape(1, doc_count * doc_len)
-    place = jnp.arange(doc_count, dtype=jnp.int32)[:, None] * doc_len + row_ids
-    context = doc_count * doc_len
-    used = held.astype(jnp.bfloat16).reshape(context, 1)
-    first_used = jnp.argmax(held, axis=1) + jnp.arange(doc_count) * doc_len
-    spare = (jnp.arange(context)[None, :] == first_used[:, None]).astype(jnp.bfloat16)
-    keys, values = assemble(
-        request_docs, jnp.broadcast_to(used, (context, head_dim)), spare, sources, not pairs
+    held, spare, key_bias, row_place, key_place, slot_row = plan(
+        request_docs, doc_lengths, recompute_rows, slot_count, head_dim, doc_len
     )
-    row_of_slot = owners * capacity + ranks
-    chosen = row_of_slot[None, :] == jnp.arange(seq_count * capacity)[:, None]
-    entry = jnp.max(jnp.where(chosen, jnp.arange(doc_count)[None, :], -doc_count), axis=1)
-    slot_row = entry[:, None] * per_doc + jnp.arange(per_doc)[None, :]
-    fresh, outgoing = finish(own, arrived, slot_row.reshape(-1, 1))
-    mixed = attend(
-        queries,
-        fresh,
-        keys,
-        values,
-        key_bias,
-        place.reshape(row_count, 1),
-        place.reshape(1, row_count),
-    )
-
-    outgoing = outgoing.reshape(seq_count, capacity, per_doc, 2 * head_dim)
+    if pairs:
+        sources = tuple(in_hbm(one) for one in sources)
+    keys, values = assemble(request_docs, held, spare, sources, not pairs)
+    fresh, outgoing = finish(own, arrived, slot_row, seq_count * capacity * per_doc)
+    mixed = attend(queries, fresh, keys, values, key_bias, row_place, key_place)
+
+    outgoing = outgoing.reshape(seq_count, capacity * per_doc, 2 * head_dim)
     returned = lax.all_to_all(outgoing, "seq", split_axis=0, concat_axis=0, tiled=True)
     returned = returned.reshape(seq_count, capacity, per_doc, 2, head_dim)
     return (mixed, returned[None])
 
 
 def solution(mesh):
-    pairs = mesh.shape["seq"] == 4 and mesh.shape["groups"] == 2 and mesh.shape["tp"] % 2 == 0
+    pairs = mesh.shape["seq"] == 4 and mesh.shape["groups"] == 2 and mesh.shape["tp"] == 4
     return jax.shard_map(
         functools.partial(shards, pairs),
         mesh=mesh,

time: 82.6 us -> 70.7 us (0.86)
  local copies, waits for them, and re-layouts: 9.6 us -> 1.68 us
  waiting for transfers between devices: 38.3 us -> 30.9 us
  Pallas kernels: 15.9 us -> 19.5 us
  other arithmetic: 1.48 us -> 0 us
  starting transfers between devices: 15.8 us -> 17.2 us
    ppermute x8 -> x10, waiting for transfers between devices: 38.3 us -> 30.9 us  [swap(): return lax.ppermute(array, axis, [(i, i ^ apart) for i in range(count)])]
    unnamed x29 -> x10, local copies, waits for them, and re-layouts: 6.34 us -> 1.01 us
    pallas_call x3 -> x5, Pallas kernels: 8.53 us -> 11.3 us  [the longest x1 3.14 us: pick_docs(): pl.pallas_call(functools.partial(docs_kernel, by_owner), out_shape=tuple(...]
    ppermute x8 -> x10, starting transfers between devices: 11.8 us -> 13.4 us  [swap(): return lax.ppermute(array, axis, [(i, i ^ apart) for i in range(count)])]
    pallas_call x1, Pallas kernels: 0.21 us -> 1.05 us  [finish(): pl.pallas_call(finish_kernel, out_shape=tuple((jax.ShapeDtypeStruct(one,...]
  transfers between devices with their start and end apart: 9 -> 11, of which waited for: 3 -> 5; matrix products, arithmetic and copies ran while one was open for 5% -> 0% of each run, Pallas kernels for 17% -> 25%
where the time goes in v7:
time: 70.7 us; the launch traced here: 70.1 us
  waiting for transfers between devices  30.9 us (44%)
  Pallas kernels  19.5 us (28%)
  starting transfers between devices  17.2 us (24%)
  local copies, waits for them, and re-layouts  1.68 us (2%)
  between operations  0.78 us (1%)
    ppermute x10, waiting for transfers between devices, swap(): return lax.ppermute(array, axis, [(i, i ^ apart) for i in range(count)])  30.9 us
    ppermute x10, starting transfers between devices, swap(): return lax.ppermute(array, axis, [(i, i ^ apart) for i in range(count)])  13.4 us
    pallas_call x1, Pallas kernels, attend(): pl.pallas_call(attend_kernel, out_shape=jax.ShapeDtypeStruct(queries.shap...  4.84 us
    all_to_all x1, starting transfers between devices, shards(): lax.all_to_all(outgoing, 'seq', split_axis=0, concat_axis=0, tiled=True)  3.86 us
    pallas_call x1, Pallas kernels, pick_docs(): pl.pallas_call(functools.partial(docs_kernel, by_owner), out_shape=tuple(...  3.14 us
    pallas_call x1, Pallas kernels, project(): pl.pallas_call(far_kernel, out_shape=(jax.ShapeDtypeStruct((rows, 2 * wid...  2.55 us
    pallas_call x1, Pallas kernels, assemble(): pl.pallas_call(functools.partial(assemble_kernel, by_owner), out_shape=(w...  2.33 us
    pallas_call x1, Pallas kernels, project(): pl.pallas_call(near_kernel, out_shape=jax.ShapeDtypeStruct((2 * rows, 2 *...  2.23 us
  transfers between devices with their start and end apart: 11, of which 5 were waited for; matrix products, arithmetic and copies ran while one was open for 0% of the time, Pallas kernels for 25%

profile of v7, /device:TPU:0, one launch (start us, length us, event | category | flops | bytes accessed | tf_op | source)
XLA Modules:
  0.0 70.1 jit_solution(9270932901875736229)
XLA Ops:
  0.6 2.2 %pick_sent.1 = (bf16[2048,128]{1,0:T(8,128)(2,1)}, bf16[2,48,2048]{2,1,0:T(8,128)(2,1)}) custom-call(bf16[1,192,8192]{2,1,0:T(8,128)(2,1)} %hidden.5, bf16[2048,128]{1,0:T(8,128)(2,1)} %w_key.3, bf16[2048,128]{1,0:T(8,128)(2,1)} %w_value.3), custom_call_target="tpu_custom_call" | custom-call | tf_op jit(solution)/shard_map/pick_sent/pallas_call | solution.py:68
  2.8 3.1 %collective-permute-start.2 = (bf16[2,48,2048]{2,1,0:T(8,128)(2,1)}, bf16[2,48,2048]{2,1,0:T(8,128)(2,1)S(1)}, u32[]{:S(2)}, u32[]{:S(2)}) collective-permute-start(bf16[2,48,2048]{2,1,0:T(8,128)(2,1)} %get-tuple-element.28), channel_id=1, source_target_pairs={{0,4},{4,0},{8,12},{12,8},{1,5},{5,1},{9,13},{13,9},{2,6},{6,2},{1... | collective-permute-start | bytes 1179656 | tf_op jit(solution)/shard_map/ppermute | solution.py:531
  5.9 2.6 %collective-permute-start = (bf16[2048,128]{1,0:T(8,128)(2,1)}, bf16[2048,128]{1,0:T(8,128)(2,1)}, u32[]{:S(2)}, u32[]{:S(2)}) collective-permute-start(bf16[2048,128]{1,0:T(8,128)(2,1)} %get-tuple-element.26), channel_id=1, source_target_pairs={{0,8},{4,12},{8,0},{12,4},{1,9},{5,13},{9,1},{13,5},{2,10},{6,14},... | collective-permute-start | bytes 1572872 | tf_op jit(solution)/shard_map/ppermute | solution.py:531
  8.5 15.0 %collective-permute-done.2.rest_0_ = bf16[2,48,2048]{2,1,0:T(8,128)(2,1)S(1)} collective-permute-done((bf16[2,48,2048]{2,1,0:T(8,128)(2,1)}, bf16[2,48,2048]{2,1,0:T(8,128)(2,1)S(1)}, u32[]{:S(2)}, u32[]{:S(2)}) %collective-permute-start.2) | collective-permute-done | bytes 393248 | tf_op jit(solution)/shard_map/ppermute | solution.py:531
  23.6 1.7 %collective-permute-start.4 = (bf16[2,48,2048]{2,1,0:T(8,128)(2,1)S(1)}, bf16[2,48,2048]{2,1,0:T(8,128)(2,1)}, u32[]{:S(2)}, u32[]{:S(2)}) collective-permute-start(bf16[2,48,2048]{2,1,0:T(8,128)(2,1)S(1)} %collective-permute-done.2.rest_0_), channel_id=1, source_target_pairs={{0,2},{1,3},{2,0},{3,1},{4,6},{5,7},{6,4},{7,5},{8,10},{9,11},{10,... | collective-permute-start | bytes 1179656 | tf_op jit(solution)/shard_map/ppermute | solution.py:531
  25.2 3.1 %pick_docs.1 = (bf16[4,2,128,128]{3,2,1,0:T(8,128)(2,1)}, bf16[4,2,128,128]{3,2,1,0:T(8,128)(2,1)}, bf16[4,2,128,128]{3,2,1,0:T(8,128)(2,1)}) custom-call(s32[4,16]{1,0:T(4,128)} %request_docs.5, bf16[8,128,128]{2,1,0:T(8,128)(2,1)} %rest_0_.1, bf16[8,128,128]{2,1,0:T(8,128)(2,1)} %rest_1_.1), custom_call_target="tpu_custom_call" | custom-call | tf_op jit(solution)/shard_map/pick_docs/pallas_call | solution.py:152
  28.4 3.4 %collective-permute-done.refs_3_ = bf16[2048,128]{1,0:T(8,128)(2,1)} collective-permute-done((bf16[2048,128]{1,0:T(8,128)(2,1)}, bf16[2048,128]{1,0:T(8,128)(2,1)}, u32[]{:S(2)}, u32[]{:S(2)}) %collective-permute-start) | collective-permute-done | bytes 524320 | tf_op jit(solution)/shard_map/ppermute | solution.py:531
  31.8 1.6 %collective-permute-start.1 = (bf16[2048,128]{1,0:T(8,128)(2,1)}, bf16[2048,128]{1,0:T(8,128)(2,1)S(1)}, u32[]{:S(2)}, u32[]{:S(2)}) collective-permute-start(bf16[2048,128]{1,0:T(8,128)(2,1)} %get-tuple-element.27.w_far), channel_id=1, source_target_pairs={{0,16},{16,0},{1,17},{17,1},{2,18},{18,2},{3,19},{19,3},{4,20},{20... | collective-permute-start | bytes 1572872 | tf_op jit(solution)/shard_map/ppermute | solution.py:531
  33.4 0.7 collective-permute-done.4.rest_2_
  34.1 2.9 %collective-permute-start.8 = (bf16[4,2,128,128]{3,2,1,0:T(8,128)(2,1)}, bf16[4,2,128,128]{3,2,1,0:T(8,128)(2,1)}, u32[]{:S(2)}, u32[]{:S(2)}) collective-permute-start(bf16[4,2,128,128]{3,2,1,0:T(8,128)(2,1)} %get-tuple-element.36), channel_id=1, source_target_pairs={{0,8},{4,12},{8,0},{12,4},{1,9},{5,13},{9,1},{13,5},{2,10},{6,14},... | collective-permute-start | bytes 786440 | tf_op jit(solution)/shard_map/ppermute | solution.py:531
  37.0 1.5 %collective-permute-start.9 = (bf16[4,2,128,128]{3,2,1,0:T(8,128)(2,1)}, bf16[4,2,128,128]{3,2,1,0:T(8,128)(2,1)}, u32[]{:S(2)}, u32[]{:S(2)}) collective-permute-start(bf16[4,2,128,128]{3,2,1,0:T(8,128)(2,1)} %get-tuple-element.37), channel_id=1, source_target_pairs={{0,12},{4,8},{8,4},{12,0},{1,13},{5,9},{9,5},{13,1},{2,14},{6,10},... | collective-permute-start | bytes 786440 | tf_op jit(solution)/shard_map/ppermute | solution.py:531
  38.5 2.2 %project_near.1.near = f32[384,256]{1,0:T(8,128)S(1)} custom-call(bf16[1,192,8192]{2,1,0:T(8,128)(2,1)S(1)} %copy-done, bf16[2048,128]{1,0:T(8,128)(2,1)} %w_key.3, bf16[2048,128]{1,0:T(8,128)(2,1)} %w_value.3, bf16[2,48,2048]{2,1,0:T(8,128)(2,1)S(1)} %collective-permute-done.2.rest_0_, bf16[2,48,2048]{2,1,0:T(8,128)(2,1)S(1)} %collective-permute-done.3.rest_1_, ...), custom_call_target="tpu_custom_call" | custom-call | flops 1 | bytes 1 | tf_op jit(solution)/shard_map/project_near/pallas_call | solution.py:231
  40.7 0.0 copy-start.3
  40.7 3.8 %collective-permute-done.1.w_swapped = bf16[2048,128]{1,0:T(8,128)(2,1)S(1)} collective-permute-done((bf16[2048,128]{1,0:T(8,128)(2,1)}, bf16[2048,128]{1,0:T(8,128)(2,1)S(1)}, u32[]{:S(2)}, u32[]{:S(2)}) %collective-permute-start.1) | collective-permute-done | bytes 524320 | tf_op jit(solution)/shard_map/ppermute | solution.py:531
  44.5 2.6 %project_far.1 = (f32[192,256]{1,0:T(8,128)S(1)}, bf16[192,256]{1,0:T(8,128)(2,1)S(1)}) custom-call(bf16[1,192,8192]{2,1,0:T(8,128)(2,1)S(1)} %copy-done, bf16[2048,128]{1,0:T(8,128)(2,1)} %get-tuple-element.27.w_far, bf16[2048,128]{1,0:T(8,128)(2,1)S(1)} %collective-permute-done.1.w_swapped, f32[384,256]{1,0:T(8,128)S(1)} %project_near.1.near, ...), custom_call_target="tpu_custom_call" | custom-call | flops 1 | bytes 1 | tf_op jit(solution)/shard_map/project_far/pallas_call | solution.py:240
  47.1 0.1 collective-permute-start.6
  47.2 1.2 %plan.1 = (bf16[2048,128]{1,0:T(8,128)(2,1)S(1)}, bf16[16,2048]{1,0:T(8,128)(2,1)S(1)}, f32[1,2048]{1,0:T(1,128)S(1)}, s32[192,1]{1,0:T(8,128)S(1)}, s32[1,192]{1,0:T(1,128)S(1)}, /*index=5*/s32[1,192]{1,0:T(1,128)S(1)}) custom-call(s32[4,16]{1,0:T(4,128)S(1)} %copy-done.2, s32[32]{0:T(128)S(1)} %copy-done.4, s32[12,1,16]{2,1,0:T(1,128)S(1)} %bitcast.2), custom_call_target="tpu_custom_call" | custom-call | tf_op jit(solution)/shard_map/plan/pallas_call | solution.py:405
  48.4 7.9 %collective-permute-done.6.arrived = bf16[192,256]{1,0:T(8,128)(2,1)S(1)} collective-permute-done((bf16[192,256]{1,0:T(8,128)(2,1)S(1)}, bf16[192,256]{1,0:T(8,128)(2,1)S(1)}, u32[]{:S(2)}, u32[]{:S(2)}) %collective-permute-start.6) | collective-permute-done | bytes 98336 | tf_op jit(solution)/shard_map/ppermute | solution.py:531
  56.3 1.0 %finish.1 = (bf16[192,256]{1,0:T(8,128)(2,1)S(1)}, bf16[192,256]{1,0:T(8,128)(2,1)}) custom-call(f32[192,256]{1,0:T(8,128)S(1)} %get-tuple-element.29.own, bf16[192,256]{1,0:T(8,128)(2,1)S(1)} %collective-permute-done.6.arrived, s32[1,192]{1,0:T(1,128)S(1)} %get-tuple-element.31.slot_row), custom_call_target="tpu_custom_call" | custom-call | tf_op jit(solution)/shard_map/finish/pallas_call | solution.py:429
  57.4 3.9 %all-to-all-start = ((bf16[4,48,256]{2,1,0:T(8,128)(2,1)}), bf16[4,48,256]{2,1,0:T(8,128)(2,1)S(1)}, u32[]{:S(2)}, u32[]{:S(2)}) async-start(bf16[4,48,256]{2,1,0:T(8,128)(2,1)} %bitcast.1), calls=%async_computation | async-start | bytes 196608 | tf_op jit(solution)/shard_map/all_to_all | solution.py:564
  61.3 2.3 %assemble.1 = (bf16[2048,256]{1,0:T(8,128)(2,1)S(1)}, bf16[2048,256]{1,0:T(8,128)(2,1)S(1)}) custom-call(s32[4,16]{1,0:T(4,128)S(1)} %copy-done.2, bf16[2048,128]{1,0:T(8,128)(2,1)S(1)} %get-tuple-element.33.held, bf16[16,2048]{1,0:T(8,128)(2,1)S(1)} %get-tuple-element.34.spare, bf16[8,128,128]{2,1,0:T(8,128)(2,1)} %rest_0_.1, bf16[8,128,128]{2,1,0:T(8,128)(2,1)} %rest_1_.1, ...), custom_call_target="tpu_custom_call" | custom-call | bytes 16777216 | tf_op jit(solution)/shard_map/assemble/pallas_call | solution.py:317
  63.6 1.0 %copy-done.1 = bf16[1,192,1024]{2,1,0:T(8,128)(2,1)S(1)} copy-done((bf16[1,192,1024]{2,1,0:T(8,128)(2,1)S(1)}, bf16[1,192,1024]{2,1,0:T(8,128)(2,1)}, u32[]{:S(2)}) %copy-start.1) | copy-done | bytes 393240
  64.6 4.8 %attend.1 = bf16[1,192,1024]{2,1,0:T(8,128)(2,1)} custom-call(bf16[1,192,1024]{2,1,0:T(8,128)(2,1)S(1)} %copy-done.1, bf16[192,256]{1,0:T(8,128)(2,1)S(1)} %get-tuple-element.32.fresh, bf16[2048,256]{1,0:T(8,128)(2,1)S(1)} %get-tuple-element.38.keys, bf16[2048,256]{1,0:T(8,128)(2,1)S(1)} %get-tuple-element.39.values, ...), custom_call_target="tpu_custom_call" | custom-call | flops 1 | bytes 1 | tf_op jit(solution)/shard_map/attend/pallas_call | solution.py:500
  69.5 0.7 broadcast_in_dim_reshape.3
  (18 shorter events, 0.0 us)
Async XLA Ops:
  0.6 37.8 %copy-start = (bf16[1,192,8192]{2,1,0:T(8,128)(2,1)S(1)}, bf16[1,192,8192]{2,1,0:T(8,128)(2,1)}, u32[]{:S(2)}) copy-start(bf16[1,192,8192]{2,1,0:T(8,128)(2,1)} %hidden.5) | copy-start | bytes 9437188
  2.8 20.7 %collective-permute-start.2 = (bf16[2,48,2048]{2,1,0:T(8,128)(2,1)}, bf16[2,48,2048]{2,1,0:T(8,128)(2,1)S(1)}, u32[]{:S(2)}, u32[]{:S(2)}) collective-permute-start(bf16[2,48,2048]{2,1,0:T(8,128)(2,1)} %get-tuple-element.28), channel_id=1, source_target_pairs={{0,4},{4,0},{8,12},{12,8},{1,5},{5,1},{9,13},{13,9},{2,6},{6,2},{1... | collective-permute-start | bytes 1179656 | tf_op jit(solution)/shard_map/ppermute | solution.py:531
  5.9 25.9 %collective-permute-start = (bf16[2048,128]{1,0:T(8,128)(2,1)}, bf16[2048,128]{1,0:T(8,128)(2,1)}, u32[]{:S(2)}, u32[]{:S(2)}) collective-permute-start(bf16[2048,128]{1,0:T(8,128)(2,1)} %get-tuple-element.26), channel_id=1, source_target_pairs={{0,8},{4,12},{8,0},{12,4},{1,9},{5,13},{9,1},{13,5},{2,10},{6,14},... | collective-permute-start | bytes 1572872 | tf_op jit(solution)/shard_map/ppermute | solution.py:531
  23.6 10.5 %collective-permute-start.4 = (bf16[2,48,2048]{2,1,0:T(8,128)(2,1)S(1)}, bf16[2,48,2048]{2,1,0:T(8,128)(2,1)}, u32[]{:S(2)}, u32[]{:S(2)}) collective-permute-start(bf16[2,48,2048]{2,1,0:T(8,128)(2,1)S(1)} %collective-permute-done.2.rest_0_), channel_id=1, source_target_pairs={{0,2},{1,3},{2,0},{3,1},{4,6},{5,7},{6,4},{7,5},{8,10},{9,11},{10,... | collective-permute-start | bytes 1179656 | tf_op jit(solution)/shard_map/ppermute | solution.py:531
  31.8 12.7 %collective-permute-start.1 = (bf16[2048,128]{1,0:T(8,128)(2,1)}, bf16[2048,128]{1,0:T(8,128)(2,1)S(1)}, u32[]{:S(2)}, u32[]{:S(2)}) collective-permute-start(bf16[2048,128]{1,0:T(8,128)(2,1)} %get-tuple-element.27.w_far), channel_id=1, source_target_pairs={{0,16},{16,0},{1,17},{17,1},{2,18},{18,2},{3,19},{19,3},{4,20},{20... | collective-permute-start | bytes 1572872 | tf_op jit(solution)/shard_map/ppermute | solution.py:531
  33.4 3.6 %collective-permute-start.3 = (bf16[2,48,2048]{2,1,0:T(8,128)(2,1)S(1)}, bf16[2,48,2048]{2,1,0:T(8,128)(2,1)S(1)}, u32[]{:S(2)}, u32[]{:S(2)}) collective-permute-start(bf16[2,48,2048]{2,1,0:T(8,128)(2,1)S(1)} %collective-permute-done.2.rest_0_), channel_id=1, source_target_pairs={{0,1},{1,0},{2,3},{3,2},{4,5},{5,4},{6,7},{7,6},{8,9},{9,8},{10,11... | collective-permute-start | bytes 1179656 | tf_op jit(solution)/shard_map/ppermute | solution.py:531
  34.1 4.4 %collective-permute-start.5 = (bf16[2,48,2048]{2,1,0:T(8,128)(2,1)}, bf16[2,48,2048]{2,1,0:T(8,128)(2,1)S(1)}, u32[]{:S(2)}, u32[]{:S(2)}) collective-permute-start(bf16[2,48,2048]{2,1,0:T(8,128)(2,1)} %collective-permute-done.4.rest_2_), channel_id=1, source_target_pairs={{0,1},{1,0},{2,3},{3,2},{4,5},{5,4},{6,7},{7,6},{8,9},{9,8},{10,11... | collective-permute-start | bytes 1179656 | tf_op jit(solution)/shard_map/ppermute | solution.py:531
  34.1 27.2 %collective-permute-start.7 = (bf16[4,2,128,128]{3,2,1,0:T(8,128)(2,1)}, bf16[4,2,128,128]{3,2,1,0:T(8,128)(2,1)}, u32[]{:S(2)}, u32[]{:S(2)}) collective-permute-start(bf16[4,2,128,128]{3,2,1,0:T(8,128)(2,1)} %get-tuple-element.35), channel_id=1, source_target_pairs={{0,4},{4,0},{8,12},{12,8},{1,5},{5,1},{9,13},{13,9},{2,6},{6,2},{1... | collective-permute-start | bytes 786440 | tf_op jit(solution)/shard_map/ppermute | solution.py:531
  34.1 27.2 %collective-permute-start.8 = (bf16[4,2,128,128]{3,2,1,0:T(8,128)(2,1)}, bf16[4,2,128,128]{3,2,1,0:T(8,128)(2,1)}, u32[]{:S(2)}, u32[]{:S(2)}) collective-permute-start(bf16[4,2,128,128]{3,2,1,0:T(8,128)(2,1)} %get-tuple-element.36), channel_id=1, source_target_pairs={{0,8},{4,12},{8,0},{12,4},{1,9},{5,13},{9,1},{13,5},{2,10},{6,14},... | collective-permute-start | bytes 786440 | tf_op jit(solution)/shard_map/ppermute | solution.py:531
  37.0 24.3 %collective-permute-start.9 = (bf16[4,2,128,128]{3,2,1,0:T(8,128)(2,1)}, bf16[4,2,128,128]{3,2,1,0:T(8,128)(2,1)}, u32[]{:S(2)}, u32[]{:S(2)}) collective-permute-start(bf16[4,2,128,128]{3,2,1,0:T(8,128)(2,1)} %get-tuple-element.37), channel_id=1, source_target_pairs={{0,12},{4,8},{8,4},{12,0},{1,13},{5,9},{9,5},{13,1},{2,14},{6,10},... | collective-permute-start | bytes 786440 | tf_op jit(solution)/shard_map/ppermute | solution.py:531
  40.7 6.5 %copy-start.2 = (s32[4,16]{1,0:T(4,128)S(1)}, s32[4,16]{1,0:T(4,128)}, u32[]{:S(2)}) copy-start(s32[4,16]{1,0:T(4,128)} %request_docs.5) | copy-start | bytes 772
  40.7 6.5 %copy-start.3 = (s32[1,16,12]{1,0,2:T(1,128)S(1)}, s32[1,16,12]{1,0,2:T(1,128)}, u32[]{:S(2)}) copy-start(s32[1,16,12]{1,0,2:T(1,128)} %param.17) | copy-start | bytes 2308
  40.7 6.5 %copy-start.4 = (s32[32]{0:T(128)S(1)}, s32[32]{0:T(128)}, u32[]{:S(2)}) copy-start(s32[32]{0:T(128)} %doc_lengths.1) | copy-start | bytes 388
  47.1 9.3 %collective-permute-start.6 = (bf16[192,256]{1,0:T(8,128)(2,1)S(1)}, bf16[192,256]{1,0:T(8,128)(2,1)S(1)}, u32[]{:S(2)}, u32[]{:S(2)}) collective-permute-start(bf16[192,256]{1,0:T(8,128)(2,1)S(1)} %get-tuple-element.30), channel_id=1, source_target_pairs={{0,4},{4,0},{8,12},{12,8},{1,5},{5,1},{9,13},{13,9},{2,6},{6,2},{1... | collective-permute-start | bytes 294920 | tf_op jit(solution)/shard_map/ppermute | solution.py:531
  57.4 12.1 %all-to-all-start = ((bf16[4,48,256]{2,1,0:T(8,128)(2,1)}), bf16[4,48,256]{2,1,0:T(8,128)(2,1)S(1)}, u32[]{:S(2)}, u32[]{:S(2)}) async-start(bf16[4,48,256]{2,1,0:T(8,128)(2,1)} %bitcast.1), calls=%async_computation | async-start | bytes 196608 | tf_op jit(solution)/shard_map/all_to_all | solution.py:564
  63.6 1.0 %copy-start.1 = (bf16[1,192,1024]{2,1,0:T(8,128)(2,1)S(1)}, bf16[1,192,1024]{2,1,0:T(8,128)(2,1)}, u32[]{:S(2)}) copy-start(bf16[1,192,1024]{2,1,0:T(8,128)(2,1)} %queries.1) | copy-start | bytes 1179652

commit v8 on v7

--- a/solution.py
+++ b/solution.py
@@ -19,12 +19,12 @@
     return pltpu.with_memory_space_constraint(array, pltpu.HBM)
 
 
-def send_kernel(hidden, w_key, w_value, w_out, h_out, w_held, h_held, w_sems, h_sems):
+def send_kernel(hidden, w_key, w_value, w_out, h_near, h_far, w_held, h_held, w_sems, h_sems):
     group = lax.axis_index("groups")
     me = lax.axis_index("seq")
     quarter = lax.axis_index("tp")
     pieces, piece = w_held.shape[:2]
-    rows, depth = h_out.shape[1:]
+    rows, depth = h_near.shape
 
     def fetch(i, weight):
         source = weight.at[pl.ds(i * piece, piece)]
@@ -55,7 +55,8 @@
         stores[-1].start()
     for i, one in enumerate(h_fetches):
         one.wait()
-        stores.append(pltpu.make_async_copy(h_held.at[i], h_out.at[i], h_sems.at[1, i]))
+        target = (h_near, h_far)[i]
+        stores.append(pltpu.make_async_copy(h_held.at[i], target, h_sems.at[1, i]))
         stores[-1].start()
     for store in stores:
         store.wait()
@@ -64,18 +65,19 @@
 def pick_sent(hidden, w_key, w_value):
     depth, width = w_key.shape
     pieces = 4
-    h_shape = (2, hidden.shape[1] // 4, depth)
+    h_shape = (hidden.shape[1] // 4, depth)
     return pl.pallas_call(
         send_kernel,
         out_shape=(
             jax.ShapeDtypeStruct(w_key.shape, jnp.bfloat16),
             jax.ShapeDtypeStruct(h_shape, jnp.bfloat16),
+            jax.ShapeDtypeStruct(h_shape, jnp.bfloat16),
         ),
         in_specs=[ANY] * 3,
-        out_specs=(ANY, ANY),
+        out_specs=(ANY,) * 3,
         scratch_shapes=[
             pltpu.VMEM((pieces, depth // pieces, width), jnp.bfloat16),
-            pltpu.VMEM(h_shape, jnp.bfloat16),
+            pltpu.VMEM((2,) + h_shape, jnp.bfloat16),
             pltpu.SemaphoreType.DMA((2, pieces)),
             pltpu.SemaphoreType.DMA((2, 2)),
         ],
@@ -87,15 +89,16 @@
     pass
 
 
-def gate(arrays):
+def gate(arrays, first=()):
     return pl.pallas_call(
         gate_kernel,
         out_shape=tuple(jax.ShapeDtypeStruct(one.shape, one.dtype) for one in arrays),
-        in_specs=[ANY] * len(arrays),
+        in_specs=[ANY] * (len(arrays) + len(first)),
         out_specs=(ANY,) * len(arrays),
         input_output_aliases={i: i for i in range(len(arrays))},
+        compiler_params=pltpu.CompilerParams(vmem_limit_bytes=1024 * 1024),
         name="gate",
-    )(*arrays)
+    )(*(in_hbm(one) for one in arrays), *first)
 
 
 def docs_kernel(by_owner, request_docs, store_keys, store_values, *rest):
@@ -184,7 +187,6 @@
 
     for i, held in enumerate((w_key, w_value)):
         copy(held, w.at[:, pl.ds(i * width, width)])
-    quarters = [quarter.at[0] for quarter in quarters]
     lay_rows(hidden, quarters, lax.axis_index("seq"), depth, h, copy)
     for one in copies:
         one.wait()
@@ -204,7 +206,6 @@
 
     for held, place in ((w_far, group), (w_swapped, 1 - group)):
         copy(held, w.at[:, pl.ds(pl.multiple_of(place * width, width), width)])
-    quarters = [quarter.at[1] for quarter in quarters]
     lay_rows(hidden, quarters, lax.rem(lax.axis_index("seq") + 2, 4), depth, h, copy)
     for one in copies:
         one.wait()
@@ -216,7 +217,7 @@
     store.wait()
 
 
-def project(hidden, w_key, w_value, w_far, w_swapped, quarters):
+def project(hidden, w_key, w_value, w_far, w_swapped, quarters, far_quarters):
     depth, width = w_key.shape
     rows = hidden.shape[1]
     scratch = [
@@ -249,84 +250,7 @@
         + [pltpu.VMEM((rows, 2 * width), jnp.float32), pltpu.SemaphoreType.DMA],
         name="project_far",
         **settings,
-    )(hidden, w_far, w_swapped, near, *quarters)
-
-
-def assemble_kernel(
-    by_owner, request_docs, held, spare, *rest
-):
-    sources, (keys, values, counts, sems) = rest[:-4], rest[-4:]
-    me = lax.axis_index("seq")
-    doc_count = request_docs.shape[1]
-    head_dim = keys.shape[1] // 2
-    doc_len = keys.shape[0] // doc_count
-    owners = request_docs.shape[0]
-    slots = sources[0].shape[0] if not by_owner else 2 * sources[0].shape[1]
-    left = pl.ds(0, head_dim)
-
-    for o in range(owners):
-        counts[o] = 0
-
-    def one_doc(j, carry):
-        doc = request_docs[me, j]
-        owner = lax.div(doc, slots)
-        rank = counts[owner]
-        counts[owner] = rank + 1
-        place = pl.ds(pl.multiple_of(j * doc_len, doc_len), doc_len)
-
-        def fetch(key_source, value_source):
-            pltpu.make_async_copy(key_source, keys.at[place, left], sems.at[0]).start()
-            pltpu.make_async_copy(value_source, values.at[place, left], sems.at[1]).start()
-
-        if by_owner:
-            fetch(sources[0].at[owner, rank, 0], sources[0].at[owner, rank, 1])
-        else:
-            away = lax.bitwise_xor(me, owner)
-
-            @pl.when(away == 0)
-            def _():
-                slot = lax.rem(doc, slots)
-                fetch(sources[0].at[slot], sources[1].at[slot])
-
-            for k in range(1, owners):
-
-                @pl.when(away == k)
-                def _():
-                    fetch(sources[1 + k].at[rank, 0], sources[1 + k].at[rank, 1])
-
-        return carry
-
-    lax.fori_loop(0, doc_count, one_doc, 0)
-    pltpu.make_async_copy(keys.at[:, left], keys.at[:, left], sems.at[0]).wait()
-    pltpu.make_async_copy(values.at[:, left], values.at[:, left], sems.at[1]).wait()
-    spares = jnp.dot(spare[...], keys[:, :head_dim], preferred_element_type=jnp.float32)
-    spares = spares.astype(jnp.bfloat16)
-    for j in range(doc_count):
-        place = slice(j * doc_len, (j + 1) * doc_len)
-        used = held[place, :]
-        key = jnp.where(used > 0, keys[place, :head_dim], spares[j : j + 1, :])
-        keys[place, :head_dim] = key
-        keys[place, head_dim:] = key
-        values[place, :head_dim] = values[place, :head_dim] * used
-        values[place, head_dim:] = used
-
-
-def assemble(request_docs, held, spare, sources, by_owner):
-    context, head_dim = held.shape
-    wide = jax.ShapeDtypeStruct((context, 2 * head_dim), jnp.bfloat16)
-    return pl.pallas_call(
-        functools.partial(assemble_kernel, by_owner),
-        out_shape=(wide, wide),
-        in_specs=[SMEM, VMEM, VMEM] + [HBM] * len(sources),
-        out_specs=(VMEM, VMEM),
-        scratch_shapes=[
-            pltpu.SMEM((request_docs.shape[0],), jnp.int32),
-            pltpu.SemaphoreType.DMA((2,)),
-        ],
-        compiler_params=pltpu.CompilerParams(vmem_limit_bytes=32 * 1024 * 1024),
-        cost_estimate=pl.CostEstimate(flops=0, bytes_accessed=16 * 1024 * 1024, transcendentals=0),
-        name="assemble",
-    )(request_docs, held, spare, *sources)
+    )(hidden, w_far, w_swapped, near, *far_quarters)
 
 
 def plan_kernel(
@@ -437,33 +361,103 @@
     )(own, arrived, slot_row)
 
 
-def attend_kernel(queries, fresh, keys, values, key_bias, row_place, key_place, mixed):
-    row_count = queries.shape[1]
-    head_dim = fresh.shape[1] // 2
-    heads = queries.shape[2] // head_dim
-    step = 4
-    blocks = key_bias.shape[1] // (step * 128)
-    block_rows = row_count // blocks
-    block_keys = key_bias.shape[1] // blocks
+def attend_kernel(
+    by_owner, request_docs, queries, fresh, held, spare, key_bias, row_place, key_place, *rest
+):
+    sources, (mixed, raw, q, keys, values, counts, sems, q_sem) = rest[:-8], rest[-8:]
+    me = lax.axis_index("seq")
+    doc_count = request_docs.shape[1]
+    head_dim = keys.shape[1] // 2
+    doc_len = keys.shape[0] // doc_count
+    owners = request_docs.shape[0]
+    slots = sources[0].shape[0] if not by_owner else 2 * sources[0].shape[1]
+    step = doc_count // sems.shape[1]
+    blocks = doc_count // step
+    block_rows = mixed.shape[1] // blocks
+    block_keys = step * doc_len
+    heads = mixed.shape[2] // head_dim
+    left = pl.ds(0, head_dim)
+
+    fetch_queries = pltpu.make_async_copy(queries, raw, q_sem)
+    fetch_queries.start()
+    for o in range(owners):
+        counts[o] = 0
+
+    def one_doc(j, carry):
+        doc = request_docs[me, j]
+        owner = lax.div(doc, slots)
+        rank = counts[owner]
+        counts[owner] = rank + 1
+        place = pl.ds(pl.multiple_of(j * doc_len, doc_len), doc_len)
+        block = lax.div(j, step)
+
+        def fetch(key_source, value_source):
+            pltpu.make_async_copy(key_source, keys.at[place, left], sems.at[0, block]).start()
+            pltpu.make_async_copy(value_source, values.at[place, left], sems.at[1, block]).start()
+
+        if by_owner:
+            fetch(sources[0].at[owner, rank, 0], sources[0].at[owner, rank, 1])
+        else:
+            away = lax.bitwise_xor(me, owner)
+
+            @pl.when(away == 0)
+            def _():
+                slot = lax.rem(doc, slots)
+                fetch(sources[0].at[slot], sources[1].at[slot])
+
+            for k in range(1, owners):
+
+                @pl.when(away == k)
+                def _():
+                    fetch(sources[1 + k].at[rank, 0], sources[1 + k].at[rank, 1])
+
+        return carry
+
+    lax.fori_loop(0, doc_count, one_doc, 0)
+
+    fetch_queries.wait()
     scale = math.log2(math.e) / math.sqrt(head_dim)
+    for b in range(blocks):
+        for h in range(heads):
+            here = raw[0, b * block_rows : (b + 1) * block_rows, h * head_dim : (h + 1) * head_dim]
+            here = here.astype(jnp.float32) * scale
+            high = here.astype(jnp.bfloat16)
+            place = slice((b * heads + h) * block_rows, (b * heads + h + 1) * block_rows)
+            q[place, :head_dim] = high
+            q[place, head_dim:] = (here - high.astype(jnp.float32)).astype(jnp.bfloat16)
+
+    for b in range(blocks):
+        block = pl.ds(b * block_keys, block_keys)
+        for i, context in enumerate((keys, values)):
+            pltpu.make_async_copy(
+                context.at[block, left], context.at[block, left], sems.at[i, b]
+            ).wait()
+    for b in range(blocks):
+        block = slice(b * block_keys, (b + 1) * block_keys)
+        spares = jnp.dot(
+            spare[:, block], keys[block, :head_dim], preferred_element_type=jnp.float32
+        ).astype(jnp.bfloat16)
+        for j in range(b * step, (b + 1) * step):
+            place = slice(j * doc_len, (j + 1) * doc_len)
+            used = held[place, :]
+            key = jnp.where(used > 0, keys[place, :head_dim], spares[j : j + 1, :])
+            keys[place, :head_dim] = key
+            keys[place, head_dim:] = key
+            values[place, :head_dim] = values[place, :head_dim] * used
+            values[place, head_dim:] = used
+
     fresh_k = jnp.concatenate([fresh[:, :head_dim]] * 2, axis=1)
     fresh_v = jnp.concatenate([fresh[:, head_dim:], jnp.ones_like(fresh[:, head_dim:])], axis=1)
     slot_place = lax.broadcasted_iota(jnp.int32, (1, block_keys), 1)
     contract_last = (((1,), (1,)), ((), ()))
     for b in range(blocks):
         rows = slice(b * block_rows, (b + 1) * block_rows)
-        q = jnp.concatenate(
-            [queries[0, rows, h * head_dim : (h + 1) * head_dim] for h in range(heads)], axis=0
-        )
-        q = q.astype(jnp.float32) * scale
-        high = q.astype(jnp.bfloat16)
-        low = (q - high.astype(jnp.float32)).astype(jnp.bfloat16)
-        q = jnp.concatenate([high, low], axis=1)
+        q_here = q[b * heads * block_rows : (b + 1) * heads * block_rows, :]
         own_place = row_place[rows, :]
 
         def scores(some_keys):
             return lax.dot_general(
-                q, some_keys, contract_last, preferred_element_type=jnp.float32
+                q_here, some_keys, contract_last, preferred_element_type=jnp.float32
             )
 
         def masked(some_keys, allowed):
@@ -496,16 +490,36 @@
             ]
 
 
-def attend(queries, fresh, keys, values, key_bias, row_place, key_place):
+def attend(request_docs, queries, fresh, held, spare, key_bias, row_place, key_place, sources, by_owner):
+    context, head_dim = held.shape
+    rows = queries.shape[1] * queries.shape[2] // head_dim
     return pl.pallas_call(
-        attend_kernel,
+        functools.partial(attend_kernel, by_owner),
         out_shape=jax.ShapeDtypeStruct(queries.shape, jnp.bfloat16),
-        in_specs=[VMEM] * 7,
+        in_specs=[SMEM, ANY] + [VMEM] * 6 + [ANY] * len(sources),
         out_specs=VMEM,
+        scratch_shapes=[
+            pltpu.VMEM(queries.shape, jnp.bfloat16),
+            pltpu.VMEM((rows, 2 * head_dim), jnp.bfloat16),
+            pltpu.VMEM((context, 2 * head_dim), jnp.bfloat16),
+            pltpu.VMEM((context, 2 * head_dim), jnp.bfloat16),
+            pltpu.SMEM((request_docs.shape[0],), jnp.int32),
+            pltpu.SemaphoreType.DMA((2, 4)),
+            pltpu.SemaphoreType.DMA,
+        ],
         compiler_params=pltpu.CompilerParams(vmem_limit_bytes=32 * 1024 * 1024),
-        cost_estimate=pl.CostEstimate(flops=1, bytes_accessed=1, transcendentals=0),
         name="attend",
-    )(queries, fresh, keys, values, key_bias, row_place, key_place)
+    )(
+        request_docs,
+        in_hbm(queries),
+        fresh,
+        held,
+        spare,
+        key_bias,
+        row_place,
+        key_place,
+        *(in_hbm(one) for one in sources),
+    )
 
 
 def shards(
@@ -530,16 +544,22 @@
             count = lax.axis_size(axis)
             return lax.ppermute(array, axis, [(i, i ^ apart) for i in range(count)])
 
-        w_send, h_send = pick_sent(hidden, w_key, w_value)
+        w_send, *h_send = pick_sent(hidden, w_key, w_value)
         w_far = swap(w_send, "seq", 2)
-        h_mine = swap(h_send, "seq", 1)
-        docs = pick_docs(request_docs, store_keys, store_values, False)
-        *docs, w_far = gate((*docs, w_far))
+        doc_1, doc_2, doc_3 = pick_docs(request_docs, store_keys, store_values, False)
+
+        def spread(sent):
+            mine = swap(sent, "seq", 1)
+            chip = swap(mine, "tp", 2)
+            return mine, swap(mine, "tp", 1), chip, swap(chip, "tp", 1)
+
+        quarters = tuple(spread(one) for one in h_send)
+        (doc_1,) = gate((doc_1,), (quarters[1][0],))
+        doc_1 = swap(doc_1, "seq", 1)
+        doc_2, doc_3, w_far = gate((doc_2, doc_3, w_far), (doc_1, *quarters[0], *quarters[1]))
+        docs = (doc_1, swap(doc_2, "seq", 2), swap(doc_3, "seq", 3))
         w_swapped = swap(w_far, "groups", 1)
-        docs = [swap(doc, "seq", k + 1) for k, doc in enumerate(docs)]
-        h_chip = swap(h_mine, "tp", 2)
-        quarters = (h_mine, swap(h_mine, "tp", 1), h_chip, swap(h_chip, "tp", 1))
-        own, part = project(hidden, w_key, w_value, w_far, w_swapped, quarters)
+        own, part = project(hidden, w_key, w_value, w_far, w_swapped, *quarters)
         arrived = swap(part, "seq", 1)
         sources = (store_keys, store_values, *docs)
     else:
@@ -554,11 +574,19 @@
     held, spare, key_bias, row_place, key_place, slot_row = plan(
         request_docs, doc_lengths, recompute_rows, slot_count, head_dim, doc_len
     )
-    if pairs:
-        sources = tuple(in_hbm(one) for one in sources)
-    keys, values = assemble(request_docs, held, spare, sources, not pairs)
     fresh, outgoing = finish(own, arrived, slot_row, seq_count * capacity * per_doc)
-    mixed = attend(queries, fresh, keys, values, key_bias, row_place, key_place)
+    mixed = attend(
+        request_docs,
+        queries,
+        fresh,
+        held,
+        spare,
+        key_bias,
+        row_place,
+        key_place,
+        sources,
+        not pairs,
+    )
 
     outgoing = outgoing.reshape(seq_count, capacity * per_doc, 2 * head_dim)
     returned = lax.all_to_all(outgoing, "seq", split_axis=0, concat_axis=0, tiled=True)

time: 70.7 us -> 74.7 us (1.057)
  starting transfers between devices: 17.2 us -> 20.5 us
  waiting for transfers between devices: 30.9 us -> 33.1 us
  local copies, waits for them, and re-layouts: 1.68 us -> 0.7 us
    ppermute x10 -> x14, starting transfers between devices: 13.4 us -> 16.4 us  [swap(): return lax.ppermute(array, axis, [(i, i ^ apart) for i in range(count)])]
    ppermute x10 -> x14, waiting for transfers between devices: 30.9 us -> 33.1 us  [swap(): return lax.ppermute(array, axis, [(i, i ^ apart) for i in range(count)])]
    unnamed x10, local copies, waits for them, and re-layouts: 1.01 us -> 0.03 us
    pallas_call x2 -> x1, Pallas kernels: 7.17 us -> 6.96 us  [attend(): pl.pallas_call(functools.partial(attend_kernel, by_owner), out_shape=jax....]
  transfers between devices with their start and end apart: 11 -> 15, of which waited for: 5 -> 6; matrix products, arithmetic and copies ran while one was open for 0% -> 0% of each run, Pallas kernels for 25% -> 23%
where the time goes in v8:
time: 74.7 us; the launch traced here: 74.3 us
  waiting for transfers between devices  33.1 us (44%)
  starting transfers between devices  20.5 us (27%)
  Pallas kernels  19.2 us (26%)
  between operations  0.78 us (1%)
    ppermute x14, waiting for transfers between devices, swap(): return lax.ppermute(array, axis, [(i, i ^ apart) for i in range(count)])  33.1 us
    ppermute x14, starting transfers between devices, swap(): return lax.ppermute(array, axis, [(i, i ^ apart) for i in range(count)])  16.4 us
    pallas_call x1, Pallas kernels, attend(): pl.pallas_call(functools.partial(attend_kernel, by_owner), out_shape=jax....  6.96 us
    all_to_all x1, starting transfers between devices, shards(): lax.all_to_all(outgoing, 'seq', split_axis=0, concat_axis=0, tiled=True)  4.15 us
    pallas_call x1, Pallas kernels, pick_docs(): pl.pallas_call(functools.partial(docs_kernel, by_owner), out_shape=tuple(...  3.2 us
    pallas_call x1, Pallas kernels, project(): pl.pallas_call(far_kernel, out_shape=(jax.ShapeDtypeStruct((rows, 2 * wid...  2.35 us
    pallas_call x1, Pallas kernels, project(): pl.pallas_call(near_kernel, out_shape=jax.ShapeDtypeStruct((2 * rows, 2 *...  2.22 us
    pallas_call x1, Pallas kernels, pick_sent(): pl.pallas_call(send_kernel, out_shape=(jax.ShapeDtypeStruct(w_key.shape,...  2.18 us
  transfers between devices with their start and end apart: 15, of which 6 were waited for; matrix products, arithmetic and copies ran while one was open for 0% of the time, Pallas kernels for 23%

profile of v8, /device:TPU:0, one launch (start us, length us, event | category | flops | bytes accessed | tf_op | source)
XLA Modules:
  0.0 74.3 jit_solution(9008343676794198268)
XLA Ops:
  0.6 2.2 %pick_sent.1 = (bf16[2048,128]{1,0:T(8,128)(2,1)}, bf16[48,2048]{1,0:T(8,128)(2,1)}, bf16[48,2048]{1,0:T(8,128)(2,1)}) custom-call(bf16[1,192,8192]{2,1,0:T(8,128)(2,1)} %hidden.5, bf16[2048,128]{1,0:T(8,128)(2,1)} %w_key.3, bf16[2048,128]{1,0:T(8,128)(2,1)} %w_value.3), custom_call_target="tpu_custom_call" | custom-call | tf_op jit(solution)/shard_map/pick_sent/pallas_call | solution.py:69
  2.8 3.1 %collective-permute-start.1 = (bf16[48,2048]{1,0:T(8,128)(2,1)}, bf16[48,2048]{1,0:T(8,128)(2,1)S(1)}, u32[]{:S(2)}, u32[]{:S(2)}) collective-permute-start(bf16[48,2048]{1,0:T(8,128)(2,1)} %get-tuple-element.25), channel_id=1, source_target_pairs={{0,4},{4,0},{8,12},{12,8},{1,5},{5,1},{9,13},{13,9},{2,6},{6,2},{1... | collective-permute-start | bytes 589832 | tf_op jit(solution)/shard_map/ppermute | solution.py:545
  6.0 3.0 %collective-permute-start = (bf16[2048,128]{1,0:T(8,128)(2,1)}, bf16[2048,128]{1,0:T(8,128)(2,1)}, u32[]{:S(2)}, u32[]{:S(2)}) collective-permute-start(bf16[2048,128]{1,0:T(8,128)(2,1)} %get-tuple-element.23), channel_id=1, source_target_pairs={{0,8},{4,12},{8,0},{12,4},{1,9},{5,13},{9,1},{13,5},{2,10},{6,14},... | collective-permute-start | bytes 1572872 | tf_op jit(solution)/shard_map/ppermute | solution.py:545
  9.0 11.1 %collective-permute-done.1.refs_1_.refs_8_.rest_0_ = bf16[48,2048]{1,0:T(8,128)(2,1)S(1)} collective-permute-done((bf16[48,2048]{1,0:T(8,128)(2,1)}, bf16[48,2048]{1,0:T(8,128)(2,1)S(1)}, u32[]{:S(2)}, u32[]{:S(2)}) %collective-permute-start.1) | collective-permute-done | bytes 196640 | tf_op jit(solution)/shard_map/ppermute | solution.py:545
  20.1 1.9 %collective-permute-start.8 = (bf16[48,2048]{1,0:T(8,128)(2,1)S(1)}, bf16[48,2048]{1,0:T(8,128)(2,1)}, u32[]{:S(2)}, u32[]{:S(2)}) collective-permute-start(bf16[48,2048]{1,0:T(8,128)(2,1)S(1)} %collective-permute-done.1.refs_1_.refs_8_.rest_0_), channel_id=1, source_target_pairs={{0,2},{1,3},{2,0},{3,1},{4,6},{5,7},{6,4},{7,5},{8,10},{9,11},{10,... | collective-permute-start | bytes 589832 | tf_op jit(solution)/shard_map/ppermute | solution.py:545
  22.0 1.5 %collective-permute-done.3.refs_4_.rest_0_ = bf16[48,2048]{1,0:T(8,128)(2,1)S(1)} collective-permute-done((bf16[48,2048]{1,0:T(8,128)(2,1)}, bf16[48,2048]{1,0:T(8,128)(2,1)S(1)}, u32[]{:S(2)}, u32[]{:S(2)}) %collective-permute-start.3) | collective-permute-done | bytes 196640 | tf_op jit(solution)/shard_map/ppermute | solution.py:545
  23.4 1.6 %collective-permute-start.5 = (bf16[48,2048]{1,0:T(8,128)(2,1)S(1)}, bf16[48,2048]{1,0:T(8,128)(2,1)}, u32[]{:S(2)}, u32[]{:S(2)}) collective-permute-start(bf16[48,2048]{1,0:T(8,128)(2,1)S(1)} %collective-permute-done.3.refs_4_.rest_0_), channel_id=1, source_target_pairs={{0,2},{1,3},{2,0},{3,1},{4,6},{5,7},{6,4},{7,5},{8,10},{9,11},{10,... | collective-permute-start | bytes 589832 | tf_op jit(solution)/shard_map/ppermute | solution.py:545
  25.0 3.2 %pick_docs.1 = (bf16[4,2,128,128]{3,2,1,0:T(8,128)(2,1)}, bf16[4,2,128,128]{3,2,1,0:T(8,128)(2,1)}, bf16[4,2,128,128]{3,2,1,0:T(8,128)(2,1)}) custom-call(s32[4,16]{1,0:T(4,128)} %request_docs.5, bf16[8,128,128]{2,1,0:T(8,128)(2,1)} %rest_0_.1, bf16[8,128,128]{2,1,0:T(8,128)(2,1)} %rest_1_.1), custom_call_target="tpu_custom_call" | custom-call | tf_op jit(solution)/shard_map/pick_docs/pallas_call | solution.py:155
  28.3 0.6 collective-permute-start.4
  28.9 1.1 %collective-permute-done.5.refs_6_.rest_2_ = bf16[48,2048]{1,0:T(8,128)(2,1)} collective-permute-done((bf16[48,2048]{1,0:T(8,128)(2,1)S(1)}, bf16[48,2048]{1,0:T(8,128)(2,1)}, u32[]{:S(2)}, u32[]{:S(2)}) %collective-permute-start.5) | collective-permute-done | bytes 196640 | tf_op jit(solution)/shard_map/ppermute | solution.py:545
  30.0 0.5 collective-permute-start.6
  30.6 6.9 %collective-permute-done.2.refs_3_.rest_2_ = bf16[4,2,128,128]{3,2,1,0:T(8,128)(2,1)S(1)} collective-permute-done((bf16[4,2,128,128]{3,2,1,0:T(8,128)(2,1)}, bf16[4,2,128,128]{3,2,1,0:T(8,128)(2,1)S(1)}, u32[]{:S(2)}, u32[]{:S(2)}) %collective-permute-start.2) | collective-permute-done | bytes 262176 | tf_op jit(solution)/shard_map/ppermute | solution.py:545
  37.5 1.7 %collective-permute-start.10 = (bf16[2048,128]{1,0:T(8,128)(2,1)}, bf16[2048,128]{1,0:T(8,128)(2,1)S(1)}, u32[]{:S(2)}, u32[]{:S(2)}) collective-permute-start(bf16[2048,128]{1,0:T(8,128)(2,1)} %get-tuple-element.27.w_far), channel_id=1, source_target_pairs={{0,16},{16,0},{1,17},{17,1},{2,18},{18,2},{3,19},{19,3},{4,20},{20... | collective-permute-start | bytes 1572872 | tf_op jit(solution)/shard_map/ppermute | solution.py:545
  39.2 1.8 %collective-permute-start.12 = (bf16[4,2,128,128]{3,2,1,0:T(8,128)(2,1)}, bf16[4,2,128,128]{3,2,1,0:T(8,128)(2,1)}, u32[]{:S(2)}, u32[]{:S(2)}) collective-permute-start(bf16[4,2,128,128]{3,2,1,0:T(8,128)(2,1)} %get-tuple-element.37), channel_id=1, source_target_pairs={{0,8},{4,12},{8,0},{12,4},{1,9},{5,13},{9,1},{13,5},{2,10},{6,14},... | collective-permute-start | bytes 786440 | tf_op jit(solution)/shard_map/ppermute | solution.py:545
  40.9 1.8 %collective-permute-start.13 = (bf16[4,2,128,128]{3,2,1,0:T(8,128)(2,1)}, bf16[4,2,128,128]{3,2,1,0:T(8,128)(2,1)}, u32[]{:S(2)}, u32[]{:S(2)}) collective-permute-start(bf16[4,2,128,128]{3,2,1,0:T(8,128)(2,1)} %get-tuple-element.38), channel_id=1, source_target_pairs={{0,12},{4,8},{8,4},{12,0},{1,13},{5,9},{9,5},{13,1},{2,14},{6,10},... | collective-permute-start | bytes 786440 | tf_op jit(solution)/shard_map/ppermute | solution.py:545
  42.8 2.2 %project_near.1.near = f32[384,256]{1,0:T(8,128)S(1)} custom-call(bf16[1,192,8192]{2,1,0:T(8,128)(2,1)S(1)} %copy-done, bf16[2048,128]{1,0:T(8,128)(2,1)} %w_key.3, bf16[2048,128]{1,0:T(8,128)(2,1)} %w_value.3, bf16[48,2048]{1,0:T(8,128)(2,1)S(1)} %collective-permute-done.3.refs_4_.rest_0_, bf16[48,2048]{1,0:T(8,128)(2,1)S(1)} %collective-permute-done.4.refs_5_.rest_1_, ...), custom_call_target="tpu_custom_call" | custom-call | flops 1 | bytes 1 | tf_op jit(solution)/shard_map/project_near/pallas_call | solution.py:232
  45.0 6.4 %collective-permute-done.10.w_swapped = bf16[2048,128]{1,0:T(8,128)(2,1)S(1)} collective-permute-done((bf16[2048,128]{1,0:T(8,128)(2,1)}, bf16[2048,128]{1,0:T(8,128)(2,1)S(1)}, u32[]{:S(2)}, u32[]{:S(2)}) %collective-permute-start.10) | collective-permute-done | bytes 524320 | tf_op jit(solution)/shard_map/ppermute | solution.py:545
  51.4 2.4 %project_far.1 = (f32[192,256]{1,0:T(8,128)S(1)}, bf16[192,256]{1,0:T(8,128)(2,1)S(1)}) custom-call(bf16[1,192,8192]{2,1,0:T(8,128)(2,1)S(1)} %copy-done, bf16[2048,128]{1,0:T(8,128)(2,1)} %get-tuple-element.27.w_far, bf16[2048,128]{1,0:T(8,128)(2,1)S(1)} %collective-permute-done.10.w_swapped, f32[384,256]{1,0:T(8,128)S(1)} %project_near.1.near, ...), custom_call_target="tpu_custom_call" | custom-call | flops 1 | bytes 1 | tf_op jit(solution)/shard_map/project_far/pallas_call | solution.py:241
  54.0 1.2 %plan.1 = (bf16[2048,128]{1,0:T(8,128)(2,1)S(1)}, bf16[16,2048]{1,0:T(8,128)(2,1)S(1)}, f32[1,2048]{1,0:T(1,128)S(1)}, s32[192,1]{1,0:T(8,128)S(1)}, s32[1,192]{1,0:T(1,128)S(1)}, /*index=5*/s32[1,192]{1,0:T(1,128)S(1)}) custom-call(s32[4,16]{1,0:T(4,128)S(1)} %copy-done.2, s32[32]{0:T(128)S(1)} %copy-done.4, s32[12,1,16]{2,1,0:T(1,128)S(1)} %bitcast.2), custom_call_target="tpu_custom_call" | custom-call | tf_op jit(solution)/shard_map/plan/pallas_call | solution.py:329
  55.3 6.2 %collective-permute-done.11.arrived = bf16[192,256]{1,0:T(8,128)(2,1)S(1)} collective-permute-done((bf16[192,256]{1,0:T(8,128)(2,1)S(1)}, bf16[192,256]{1,0:T(8,128)(2,1)S(1)}, u32[]{:S(2)}, u32[]{:S(2)}) %collective-permute-start.11) | collective-permute-done | bytes 98336 | tf_op jit(solution)/shard_map/ppermute | solution.py:545
  61.4 1.0 %finish.1 = (bf16[192,256]{1,0:T(8,128)(2,1)S(1)}, bf16[192,256]{1,0:T(8,128)(2,1)}) custom-call(f32[192,256]{1,0:T(8,128)S(1)} %get-tuple-element.28.own, bf16[192,256]{1,0:T(8,128)(2,1)S(1)} %collective-permute-done.11.arrived, s32[1,192]{1,0:T(1,128)S(1)} %get-tuple-element.30.slot_row), custom_call_target="tpu_custom_call" | custom-call | tf_op jit(solution)/shard_map/finish/pallas_call | solution.py:353
  62.5 4.1 %all-to-all-start = ((bf16[4,48,256]{2,1,0:T(8,128)(2,1)}), bf16[4,48,256]{2,1,0:T(8,128)(2,1)S(1)}, u32[]{:S(2)}, u32[]{:S(2)}) async-start(bf16[4,48,256]{2,1,0:T(8,128)(2,1)} %bitcast.1), calls=%async_computation | async-start | bytes 196608 | tf_op jit(solution)/shard_map/all_to_all | solution.py:592
  66.6 7.0 %attend.1 = bf16[1,192,1024]{2,1,0:T(8,128)(2,1)} custom-call(s32[4,16]{1,0:T(4,128)S(1)} %copy-done.2, bf16[1,192,1024]{2,1,0:T(8,128)(2,1)} %queries.1, bf16[192,256]{1,0:T(8,128)(2,1)S(1)} %get-tuple-element.31.fresh, bf16[2048,128]{1,0:T(8,128)(2,1)S(1)} %get-tuple-element.32.held, bf16[16,2048]{1,0:T(8,128)(2,1)S(1)} %get-tuple-element.33.spare, ...), custom_call_target="tpu_custom_call" | custom-call | tf_op jit(solution)/shard_map/attend/pallas_call | solution.py:496
  73.6 0.7 broadcast_in_dim_reshape.3
  (26 shorter events, 0.5 us)
Async XLA Ops:
  0.6 42.1 %copy-start = (bf16[1,192,8192]{2,1,0:T(8,128)(2,1)S(1)}, bf16[1,192,8192]{2,1,0:T(8,128)(2,1)}, u32[]{:S(2)}) copy-start(bf16[1,192,8192]{2,1,0:T(8,128)(2,1)} %hidden.5) | copy-start | bytes 9437188
  2.8 17.2 %collective-permute-start.1 = (bf16[48,2048]{1,0:T(8,128)(2,1)}, bf16[48,2048]{1,0:T(8,128)(2,1)S(1)}, u32[]{:S(2)}, u32[]{:S(2)}) collective-permute-start(bf16[48,2048]{1,0:T(8,128)(2,1)} %get-tuple-element.25), channel_id=1, source_target_pairs={{0,4},{4,0},{8,12},{12,8},{1,5},{5,1},{9,13},{13,9},{2,6},{6,2},{1... | collective-permute-start | bytes 589832 | tf_op jit(solution)/shard_map/ppermute | solution.py:545
  5.9 17.5 %collective-permute-start.3 = (bf16[48,2048]{1,0:T(8,128)(2,1)}, bf16[48,2048]{1,0:T(8,128)(2,1)S(1)}, u32[]{:S(2)}, u32[]{:S(2)}) collective-permute-start(bf16[48,2048]{1,0:T(8,128)(2,1)} %get-tuple-element.26), channel_id=1, source_target_pairs={{0,4},{4,0},{8,12},{12,8},{1,5},{5,1},{9,13},{13,9},{2,6},{6,2},{1... | collective-permute-start | bytes 589832 | tf_op jit(solution)/shard_map/ppermute | solution.py:545
  6.0 31.4 %collective-permute-start = (bf16[2048,128]{1,0:T(8,128)(2,1)}, bf16[2048,128]{1,0:T(8,128)(2,1)}, u32[]{:S(2)}, u32[]{:S(2)}) collective-permute-start(bf16[2048,128]{1,0:T(8,128)(2,1)} %get-tuple-element.23), channel_id=1, source_target_pairs={{0,8},{4,12},{8,0},{12,4},{1,9},{5,13},{9,1},{13,5},{2,10},{6,14},... | collective-permute-start | bytes 1572872 | tf_op jit(solution)/shard_map/ppermute | solution.py:545
  20.1 8.3 %collective-permute-start.8 = (bf16[48,2048]{1,0:T(8,128)(2,1)S(1)}, bf16[48,2048]{1,0:T(8,128)(2,1)}, u32[]{:S(2)}, u32[]{:S(2)}) collective-permute-start(bf16[48,2048]{1,0:T(8,128)(2,1)S(1)} %collective-permute-done.1.refs_1_.refs_8_.rest_0_), channel_id=1, source_target_pairs={{0,2},{1,3},{2,0},{3,1},{4,6},{5,7},{6,4},{7,5},{8,10},{9,11},{10,... | collective-permute-start | bytes 589832 | tf_op jit(solution)/shard_map/ppermute | solution.py:545
  23.4 6.6 %collective-permute-start.5 = (bf16[48,2048]{1,0:T(8,128)(2,1)S(1)}, bf16[48,2048]{1,0:T(8,128)(2,1)}, u32[]{:S(2)}, u32[]{:S(2)}) collective-permute-start(bf16[48,2048]{1,0:T(8,128)(2,1)S(1)} %collective-permute-done.3.refs_4_.rest_0_), channel_id=1, source_target_pairs={{0,2},{1,3},{2,0},{3,1},{4,6},{5,7},{6,4},{7,5},{8,10},{9,11},{10,... | collective-permute-start | bytes 589832 | tf_op jit(solution)/shard_map/ppermute | solution.py:545
  25.0 5.0 %collective-permute-start.7 = (bf16[48,2048]{1,0:T(8,128)(2,1)S(1)}, bf16[48,2048]{1,0:T(8,128)(2,1)}, u32[]{:S(2)}, u32[]{:S(2)}) collective-permute-start(bf16[48,2048]{1,0:T(8,128)(2,1)S(1)} %collective-permute-done.1.refs_1_.refs_8_.rest_0_), channel_id=1, source_target_pairs={{0,1},{1,0},{2,3},{3,2},{4,5},{5,4},{6,7},{7,6},{8,9},{9,8},{10,11... | collective-permute-start | bytes 589832 | tf_op jit(solution)/shard_map/ppermute | solution.py:545
  28.3 9.2 %collective-permute-start.2 = (bf16[4,2,128,128]{3,2,1,0:T(8,128)(2,1)}, bf16[4,2,128,128]{3,2,1,0:T(8,128)(2,1)S(1)}, u32[]{:S(2)}, u32[]{:S(2)}) collective-permute-start(bf16[4,2,128,128]{3,2,1,0:T(8,128)(2,1)} %gate.2), channel_id=1, source_target_pairs={{0,4},{4,0},{8,12},{12,8},{1,5},{5,1},{9,13},{13,9},{2,6},{6,2},{1... | collective-permute-start | bytes 786440 | tf_op jit(solution)/shard_map/ppermute | solution.py:545
  28.3 2.2 %collective-permute-start.4 = (bf16[48,2048]{1,0:T(8,128)(2,1)S(1)}, bf16[48,2048]{1,0:T(8,128)(2,1)S(1)}, u32[]{:S(2)}, u32[]{:S(2)}) collective-permute-start(bf16[48,2048]{1,0:T(8,128)(2,1)S(1)} %collective-permute-done.3.refs_4_.rest_0_), channel_id=1, source_target_pairs={{0,1},{1,0},{2,3},{3,2},{4,5},{5,4},{6,7},{7,6},{8,9},{9,8},{10,11... | collective-permute-start | bytes 589832 | tf_op jit(solution)/shard_map/ppermute | solution.py:545
  30.0 7.4 %collective-permute-start.9 = (bf16[48,2048]{1,0:T(8,128)(2,1)}, bf16[48,2048]{1,0:T(8,128)(2,1)S(1)}, u32[]{:S(2)}, u32[]{:S(2)}) collective-permute-start(bf16[48,2048]{1,0:T(8,128)(2,1)} %collective-permute-done.8.refs_10_.rest_2_), channel_id=1, source_target_pairs={{0,1},{1,0},{2,3},{3,2},{4,5},{5,4},{6,7},{7,6},{8,9},{9,8},{10,11... | collective-permute-start | bytes 589832 | tf_op jit(solution)/shard_map/ppermute | solution.py:545
  30.0 7.4 %collective-permute-start.6 = (bf16[48,2048]{1,0:T(8,128)(2,1)}, bf16[48,2048]{1,0:T(8,128)(2,1)S(1)}, u32[]{:S(2)}, u32[]{:S(2)}) collective-permute-start(bf16[48,2048]{1,0:T(8,128)(2,1)} %collective-permute-done.5.refs_6_.rest_2_), channel_id=1, source_target_pairs={{0,1},{1,0},{2,3},{3,2},{4,5},{5,4},{6,7},{7,6},{8,9},{9,8},{10,11... | collective-permute-start | bytes 589832 | tf_op jit(solution)/shard_map/ppermute | solution.py:545
  37.4 3.5 %copy-start.1 = (bf16[4,2,128,128]{3,2,1,0:T(8,128)(2,1)}, bf16[4,2,128,128]{3,2,1,0:T(8,128)(2,1)S(1)}, u32[]{:S(2)}) copy-start(bf16[4,2,128,128]{3,2,1,0:T(8,128)(2,1)S(1)} %collective-permute-done.2.refs_3_.rest_2_) | copy-start | bytes 786436
  37.5 13.9 %collective-permute-start.10 = (bf16[2048,128]{1,0:T(8,128)(2,1)}, bf16[2048,128]{1,0:T(8,128)(2,1)S(1)}, u32[]{:S(2)}, u32[]{:S(2)}) collective-permute-start(bf16[2048,128]{1,0:T(8,128)(2,1)} %get-tuple-element.27.w_far), channel_id=1, source_target_pairs={{0,16},{16,0},{1,17},{17,1},{2,18},{18,2},{3,19},{19,3},{4,20},{20... | collective-permute-start | bytes 1572872 | tf_op jit(solution)/shard_map/ppermute | solution.py:545
  39.2 27.5 %collective-permute-start.12 = (bf16[4,2,128,128]{3,2,1,0:T(8,128)(2,1)}, bf16[4,2,128,128]{3,2,1,0:T(8,128)(2,1)}, u32[]{:S(2)}, u32[]{:S(2)}) collective-permute-start(bf16[4,2,128,128]{3,2,1,0:T(8,128)(2,1)} %get-tuple-element.37), channel_id=1, source_target_pairs={{0,8},{4,12},{8,0},{12,4},{1,9},{5,13},{9,1},{13,5},{2,10},{6,14},... | collective-permute-start | bytes 786440 | tf_op jit(solution)/shard_map/ppermute | solution.py:545
  40.9 25.7 %collective-permute-start.13 = (bf16[4,2,128,128]{3,2,1,0:T(8,128)(2,1)}, bf16[4,2,128,128]{3,2,1,0:T(8,128)(2,1)}, u32[]{:S(2)}, u32[]{:S(2)}) collective-permute-start(bf16[4,2,128,128]{3,2,1,0:T(8,128)(2,1)} %get-tuple-element.38), channel_id=1, source_target_pairs={{0,12},{4,8},{8,4},{12,0},{1,13},{5,9},{9,5},{13,1},{2,14},{6,10},... | collective-permute-start | bytes 786440 | tf_op jit(solution)/shard_map/ppermute | solution.py:545
  45.0 9.0 %copy-start.2 = (s32[4,16]{1,0:T(4,128)S(1)}, s32[4,16]{1,0:T(4,128)}, u32[]{:S(2)}) copy-start(s32[4,16]{1,0:T(4,128)} %request_docs.5) | copy-start | bytes 772
  45.0 9.0 %copy-start.3 = (s32[1,16,12]{1,0,2:T(1,128)S(1)}, s32[1,16,12]{1,0,2:T(1,128)}, u32[]{:S(2)}) copy-start(s32[1,16,12]{1,0,2:T(1,128)} %param.17) | copy-start | bytes 2308
  45.0 9.0 %copy-start.4 = (s32[32]{0:T(128)S(1)}, s32[32]{0:T(128)}, u32[]{:S(2)}) copy-start(s32[32]{0:T(128)} %doc_lengths.1) | copy-start | bytes 388
  53.7 7.7 %collective-permute-start.11 = (bf16[192,256]{1,0:T(8,128)(2,1)S(1)}, bf16[192,256]{1,0:T(8,128)(2,1)S(1)}, u32[]{:S(2)}, u32[]{:S(2)}) collective-permute-start(bf16[192,256]{1,0:T(8,128)(2,1)S(1)} %get-tuple-element.29), channel_id=1, source_target_pairs={{0,4},{4,0},{8,12},{12,8},{1,5},{5,1},{9,13},{13,9},{2,6},{6,2},{1... | collective-permute-start | bytes 294920 | tf_op jit(solution)/shard_map/ppermute | solution.py:545
  62.5 11.1 %all-to-all-start = ((bf16[4,48,256]{2,1,0:T(8,128)(2,1)}), bf16[4,48,256]{2,1,0:T(8,128)(2,1)S(1)}, u32[]{:S(2)}, u32[]{:S(2)}) async-start(bf16[4,48,256]{2,1,0:T(8,128)(2,1)} %bitcast.1), calls=%async_computation | async-start | bytes 196608 | tf_op jit(solution)/shard_map/all_to_all | solution.py:592

commit v9 on v8

--- a/solution.py
+++ b/solution.py
@@ -19,12 +19,12 @@
     return pltpu.with_memory_space_constraint(array, pltpu.HBM)
 
 
-def send_kernel(hidden, w_key, w_value, w_out, h_near, h_far, w_held, h_held, w_sems, h_sems):
+def send_kernel(hidden, w_key, w_value, w_out, h_out, w_held, h_held, w_sems, h_sems):
     group = lax.axis_index("groups")
     me = lax.axis_index("seq")
     quarter = lax.axis_index("tp")
     pieces, piece = w_held.shape[:2]
-    rows, depth = h_near.shape
+    rows, depth = h_out.shape[1:]
 
     def fetch(i, weight):
         source = weight.at[pl.ds(i * piece, piece)]
@@ -55,8 +55,7 @@
         stores[-1].start()
     for i, one in enumerate(h_fetches):
         one.wait()
-        target = (h_near, h_far)[i]
-        stores.append(pltpu.make_async_copy(h_held.at[i], target, h_sems.at[1, i]))
+        stores.append(pltpu.make_async_copy(h_held.at[i], h_out.at[i], h_sems.at[1, i]))
         stores[-1].start()
     for store in stores:
         store.wait()
@@ -65,19 +64,18 @@
 def pick_sent(hidden, w_key, w_value):
     depth, width = w_key.shape
     pieces = 4
-    h_shape = (hidden.shape[1] // 4, depth)
+    h_shape = (2, hidden.shape[1] // 4, depth)
     return pl.pallas_call(
         send_kernel,
         out_shape=(
             jax.ShapeDtypeStruct(w_key.shape, jnp.bfloat16),
             jax.ShapeDtypeStruct(h_shape, jnp.bfloat16),
-            jax.ShapeDtypeStruct(h_shape, jnp.bfloat16),
         ),
         in_specs=[ANY] * 3,
-        out_specs=(ANY,) * 3,
+        out_specs=(ANY, ANY),
         scratch_shapes=[
             pltpu.VMEM((pieces, depth // pieces, width), jnp.bfloat16),
-            pltpu.VMEM((2,) + h_shape, jnp.bfloat16),
+            pltpu.VMEM(h_shape, jnp.bfloat16),
             pltpu.SemaphoreType.DMA((2, pieces)),
             pltpu.SemaphoreType.DMA((2, 2)),
         ],
@@ -187,6 +185,7 @@
 
     for i, held in enumerate((w_key, w_value)):
         copy(held, w.at[:, pl.ds(i * width, width)])
+    quarters = [quarter.at[0] for quarter in quarters]
     lay_rows(hidden, quarters, lax.axis_index("seq"), depth, h, copy)
     for one in copies:
         one.wait()
@@ -194,7 +193,7 @@
 
 
 def far_kernel(hidden, w_far, w_swapped, near, *rest):
-    *quarters, own, part, w, h, sems, held_own, own_sem = rest
+    *quarters, own, part_k, part_v, w, h, sems, held_own, own_sem = rest
     group = lax.axis_index("groups")
     depth, width = w_far.shape
     rows = hidden.shape[1]
@@ -206,6 +205,7 @@
 
     for held, place in ((w_far, group), (w_swapped, 1 - group)):
         copy(held, w.at[:, pl.ds(pl.multiple_of(place * width, width), width)])
+    quarters = [quarter.at[1] for quarter in quarters]
     lay_rows(hidden, quarters, lax.rem(lax.axis_index("seq") + 2, 4), depth, h, copy)
     for one in copies:
         one.wait()
@@ -213,11 +213,12 @@
     held_own[...] = total[:rows]
     store = pltpu.make_async_copy(held_own, own, own_sem)
     store.start()
-    part[...] = total[rows:].astype(part.dtype)
+    part_k[...] = total[rows:, :width].astype(part_k.dtype)
+    part_v[...] = total[rows:, width:].astype(part_v.dtype)
     store.wait()
 
 
-def project(hidden, w_key, w_value, w_far, w_swapped, quarters, far_quarters):
+def project(hidden, w_key, w_value, w_far, w_swapped, quarters):
     depth, width = w_key.shape
     rows = hidden.shape[1]
     scratch = [
@@ -242,15 +243,16 @@
         far_kernel,
         out_shape=(
             jax.ShapeDtypeStruct((rows, 2 * width), jnp.float32),
-            jax.ShapeDtypeStruct((rows, 2 * width), jnp.bfloat16),
+            jax.ShapeDtypeStruct((rows, width), jnp.bfloat16),
+            jax.ShapeDtypeStruct((rows, width), jnp.bfloat16),
         ),
         in_specs=[ANY] * 3 + [VMEM] + [ANY] * len(quarters),
-        out_specs=(ANY, VMEM),
+        out_specs=(ANY, VMEM, VMEM),
         scratch_shapes=scratch
         + [pltpu.VMEM((rows, 2 * width), jnp.float32), pltpu.SemaphoreType.DMA],
         name="project_far",
         **settings,
-    )(hidden, w_far, w_swapped, near, *far_quarters)
+    )(hidden, w_far, w_swapped, near, *quarters)
 
 
 def plan_kernel(
@@ -337,11 +339,12 @@
     )(request_docs, doc_lengths, jnp.transpose(recompute_rows, (2, 0, 1)))
 
 
-def finish_kernel(own, arrived, slot_row, fresh, outgoing, held, sem):
+def finish_kernel(own, arrived_k, arrived_v, slot_row, fresh, outgoing, held, sem):
     fetch = pltpu.make_async_copy(own, held, sem)
     fetch.start()
     fetch.wait()
-    total = (held[...] + arrived[...].astype(jnp.float32)).astype(jnp.bfloat16)
+    arrived = jnp.concatenate([arrived_k[...], arrived_v[...]], axis=1)
+    total = (held[...] + arrived.astype(jnp.float32)).astype(jnp.bfloat16)
     fresh[...] = total
     slots = lax.broadcasted_iota(jnp.int32, (outgoing.shape[0], 1), 0)
     pick = (slots == slot_row[...]).astype(jnp.bfloat16)
@@ -353,12 +356,12 @@
     return pl.pallas_call(
         finish_kernel,
         out_shape=tuple(jax.ShapeDtypeStruct(one, jnp.bfloat16) for one in shapes),
-        in_specs=[ANY, VMEM, VMEM],
+        in_specs=[ANY] + [VMEM] * 3,
         out_specs=(VMEM, VMEM),
         scratch_shapes=[pltpu.VMEM(own.shape, jnp.float32), pltpu.SemaphoreType.DMA],
         compiler_params=pltpu.CompilerParams(vmem_limit_bytes=16 * 1024 * 1024),
         name="finish",
-    )(own, arrived, slot_row)
+    )(own, *arrived, slot_row)
 
 
 def attend_kernel(
@@ -405,11 +408,11 @@
                 slot = lax.rem(doc, slots)
                 fetch(sources[0].at[slot], sources[1].at[slot])
 
-            for k in range(1, owners):
+            for k, source in zip((2, 3, 1), sources[2:]):
 
                 @pl.when(away == k)
                 def _():
-                    fetch(sources[1 + k].at[rank, 0], sources[1 + k].at[rank, 1])
+                    fetch(source.at[rank, 0], source.at[rank, 1])
 
         return carry
 
@@ -544,23 +547,21 @@
             count = lax.axis_size(axis)
             return lax.ppermute(array, axis, [(i, i ^ apart) for i in range(count)])
 
-        w_send, *h_send = pick_sent(hidden, w_key, w_value)
+        w_send, h_send = pick_sent(hidden, w_key, w_value)
         w_far = swap(w_send, "seq", 2)
+        h_mine = swap(h_send, "seq", 1)
         doc_1, doc_2, doc_3 = pick_docs(request_docs, store_keys, store_values, False)
-
-        def spread(sent):
-            mine = swap(sent, "seq", 1)
-            chip = swap(mine, "tp", 2)
-            return mine, swap(mine, "tp", 1), chip, swap(chip, "tp", 1)
-
-        quarters = tuple(spread(one) for one in h_send)
-        (doc_1,) = gate((doc_1,), (quarters[1][0],))
+        h_core = swap(h_mine, "tp", 1)
+        h_chip = swap(h_mine, "tp", 2)
+        doc_1, doc_2, doc_3, w_far = gate((doc_1, doc_2, doc_3, w_far), ())
+        w_swapped = swap(w_far, "groups", 1)
+        doc_2 = swap(doc_2, "seq", 2)
+        doc_3 = swap(doc_3, "seq", 3)
         doc_1 = swap(doc_1, "seq", 1)
-        doc_2, doc_3, w_far = gate((doc_2, doc_3, w_far), (doc_1, *quarters[0], *quarters[1]))
-        docs = (doc_1, swap(doc_2, "seq", 2), swap(doc_3, "seq", 3))
-        w_swapped = swap(w_far, "groups", 1)
-        own, part = project(hidden, w_key, w_value, w_far, w_swapped, *quarters)
-        arrived = swap(part, "seq", 1)
+        docs = (doc_2, doc_3, doc_1)
+        quarters = (h_mine, h_core, h_chip, swap(h_chip, "tp", 1))
+        own, *parts = project(hidden, w_key, w_value, w_far, w_swapped, quarters)
+        arrived = [swap(one, "seq", 1) for one in parts]
         sources = (store_keys, store_values, *docs)
     else:
         (docs,) = pick_docs(request_docs, store_keys, store_values, True)
@@ -569,7 +570,7 @@
             jnp.concatenate([w_key, w_value], axis=1), "seq", axis=0, tiled=True
         )
         own = jnp.dot(hidden[0], weights, preferred_element_type=jnp.float32)
-        arrived = jnp.zeros(own.shape, jnp.bfloat16)
+        arrived = [jnp.zeros(own.shape, jnp.bfloat16)[:, :head_dim]] * 2
 
     held, spare, key_bias, row_place, key_place, slot_row = plan(
         request_docs, doc_lengths, recompute_rows, slot_count, head_dim, doc_len

time: 74.7 us -> 70.8 us (0.948)
  starting transfers between devices: 20.5 us -> 17.8 us
  waiting for transfers between devices: 33.1 us -> 31.8 us
    ppermute x14 -> x11, starting transfers between devices: 16.4 us -> 14.5 us  [swap(): return lax.ppermute(array, axis, [(i, i ^ apart) for i in range(count)])]
    ppermute x14 -> x11, waiting for transfers between devices: 33.1 us -> 31.8 us  [swap(): return lax.ppermute(array, axis, [(i, i ^ apart) for i in range(count)])]
    all_to_all x1, starting transfers between devices: 4.15 us -> 3.32 us  [shards(): lax.all_to_all(outgoing, 'seq', split_axis=0, concat_axis=0, tiled=True)]
  transfers between devices with their start and end apart: 15 -> 12, of which waited for: 6 -> 6; matrix products, arithmetic and copies ran while one was open for 0% -> 0% of each run, Pallas kernels for 23% -> 24%
where the time goes in v9:
time: 70.8 us; the launch traced here: 70.4 us
  waiting for transfers between devices  31.8 us (45%)
  Pallas kernels  19.3 us (27%)
  starting transfers between devices  17.8 us (25%)
  between operations  0.77 us (1%)
    ppermute x11, waiting for transfers between devices, swap(): return lax.ppermute(array, axis, [(i, i ^ apart) for i in range(count)])  31.8 us
    ppermute x11, starting transfers between devices, swap(): return lax.ppermute(array, axis, [(i, i ^ apart) for i in range(count)])  14.5 us
    pallas_call x1, Pallas kernels, attend(): pl.pallas_call(functools.partial(attend_kernel, by_owner), out_shape=jax....  6.95 us
    all_to_all x1, starting transfers between devices, shards(): lax.all_to_all(outgoing, 'seq', split_axis=0, concat_axis=0, tiled=True)  3.32 us
    pallas_call x1, Pallas kernels, pick_docs(): pl.pallas_call(functools.partial(docs_kernel, by_owner), out_shape=tuple(...  3.13 us
    pallas_call x1, Pallas kernels, project(): pl.pallas_call(far_kernel, out_shape=(jax.ShapeDtypeStruct((rows, 2 * wid...  2.55 us
    pallas_call x1, Pallas kernels, project(): pl.pallas_call(near_kernel, out_shape=jax.ShapeDtypeStruct((2 * rows, 2 *...  2.23 us
    pallas_call x1, Pallas kernels, pick_sent(): pl.pallas_call(send_kernel, out_shape=(jax.ShapeDtypeStruct(w_key.shape,...  2.19 us
  transfers between devices with their start and end apart: 12, of which 6 were waited for; matrix products, arithmetic and copies ran while one was open for 0% of the time, Pallas kernels for 24%

profile of v9, /device:TPU:0, one launch (start us, length us, event | category | flops | bytes accessed | tf_op | source)
XLA Modules:
  0.0 70.4 jit_solution(6508133032402776906)
XLA Ops:
  0.6 2.2 %pick_sent.1 = (bf16[2048,128]{1,0:T(8,128)(2,1)}, bf16[2,48,2048]{2,1,0:T(8,128)(2,1)}) custom-call(bf16[1,192,8192]{2,1,0:T(8,128)(2,1)} %hidden.5, bf16[2048,128]{1,0:T(8,128)(2,1)} %w_key.3, bf16[2048,128]{1,0:T(8,128)(2,1)} %w_value.3), custom_call_target="tpu_custom_call" | custom-call | tf_op jit(solution)/shard_map/pick_sent/pallas_call | solution.py:68
  2.8 3.1 %collective-permute-start.2 = (bf16[2,48,2048]{2,1,0:T(8,128)(2,1)}, bf16[2,48,2048]{2,1,0:T(8,128)(2,1)S(1)}, u32[]{:S(2)}, u32[]{:S(2)}) collective-permute-start(bf16[2,48,2048]{2,1,0:T(8,128)(2,1)} %get-tuple-element.27), channel_id=1, source_target_pairs={{0,4},{4,0},{8,12},{12,8},{1,5},{5,1},{9,13},{13,9},{2,6},{6,2},{1... | collective-permute-start | bytes 1179656 | tf_op jit(solution)/shard_map/ppermute | solution.py:548
  5.9 2.6 %collective-permute-start = (bf16[2048,128]{1,0:T(8,128)(2,1)}, bf16[2048,128]{1,0:T(8,128)(2,1)}, u32[]{:S(2)}, u32[]{:S(2)}) collective-permute-start(bf16[2048,128]{1,0:T(8,128)(2,1)} %get-tuple-element.25), channel_id=1, source_target_pairs={{0,8},{4,12},{8,0},{12,4},{1,9},{5,13},{9,1},{13,5},{2,10},{6,14},... | collective-permute-start | bytes 1572872 | tf_op jit(solution)/shard_map/ppermute | solution.py:548
  8.5 15.0 %collective-permute-done.2.rest_0_ = bf16[2,48,2048]{2,1,0:T(8,128)(2,1)S(1)} collective-permute-done((bf16[2,48,2048]{2,1,0:T(8,128)(2,1)}, bf16[2,48,2048]{2,1,0:T(8,128)(2,1)S(1)}, u32[]{:S(2)}, u32[]{:S(2)}) %collective-permute-start.2) | collective-permute-done | bytes 393248 | tf_op jit(solution)/shard_map/ppermute | solution.py:548
  23.6 1.7 %collective-permute-start.4 = (bf16[2,48,2048]{2,1,0:T(8,128)(2,1)S(1)}, bf16[2,48,2048]{2,1,0:T(8,128)(2,1)}, u32[]{:S(2)}, u32[]{:S(2)}) collective-permute-start(bf16[2,48,2048]{2,1,0:T(8,128)(2,1)S(1)} %collective-permute-done.2.rest_0_), channel_id=1, source_target_pairs={{0,2},{1,3},{2,0},{3,1},{4,6},{5,7},{6,4},{7,5},{8,10},{9,11},{10,... | collective-permute-start | bytes 1179656 | tf_op jit(solution)/shard_map/ppermute | solution.py:548
  25.2 3.1 %pick_docs.1 = (bf16[4,2,128,128]{3,2,1,0:T(8,128)(2,1)}, bf16[4,2,128,128]{3,2,1,0:T(8,128)(2,1)}, bf16[4,2,128,128]{3,2,1,0:T(8,128)(2,1)}) custom-call(s32[4,16]{1,0:T(4,128)} %request_docs.5, bf16[8,128,128]{2,1,0:T(8,128)(2,1)} %rest_0_.1, bf16[8,128,128]{2,1,0:T(8,128)(2,1)} %rest_1_.1), custom_call_target="tpu_custom_call" | custom-call | tf_op jit(solution)/shard_map/pick_docs/pallas_call | solution.py:153
  28.4 3.4 %collective-permute-done.refs_3_ = bf16[2048,128]{1,0:T(8,128)(2,1)} collective-permute-done((bf16[2048,128]{1,0:T(8,128)(2,1)}, bf16[2048,128]{1,0:T(8,128)(2,1)}, u32[]{:S(2)}, u32[]{:S(2)}) %collective-permute-start) | collective-permute-done | bytes 524320 | tf_op jit(solution)/shard_map/ppermute | solution.py:548
  31.8 1.6 %collective-permute-start.1 = (bf16[2048,128]{1,0:T(8,128)(2,1)}, bf16[2048,128]{1,0:T(8,128)(2,1)S(1)}, u32[]{:S(2)}, u32[]{:S(2)}) collective-permute-start(bf16[2048,128]{1,0:T(8,128)(2,1)} %get-tuple-element.26.w_far), channel_id=1, source_target_pairs={{0,16},{16,0},{1,17},{17,1},{2,18},{18,2},{3,19},{19,3},{4,20},{20... | collective-permute-start | bytes 1572872 | tf_op jit(solution)/shard_map/ppermute | solution.py:548
  33.4 0.7 collective-permute-done.4.rest_2_
  34.1 0.4 collective-permute-start.8
  34.5 1.9 %collective-permute-start.9 = (bf16[4,2,128,128]{3,2,1,0:T(8,128)(2,1)}, bf16[4,2,128,128]{3,2,1,0:T(8,128)(2,1)}, u32[]{:S(2)}, u32[]{:S(2)}) collective-permute-start(bf16[4,2,128,128]{3,2,1,0:T(8,128)(2,1)} %get-tuple-element.39), channel_id=1, source_target_pairs={{0,12},{4,8},{8,4},{12,0},{1,13},{5,9},{9,5},{13,1},{2,14},{6,10},... | collective-permute-start | bytes 786440 | tf_op jit(solution)/shard_map/ppermute | solution.py:548
  36.4 1.2 %collective-permute-start.10 = (bf16[4,2,128,128]{3,2,1,0:T(8,128)(2,1)}, bf16[4,2,128,128]{3,2,1,0:T(8,128)(2,1)}, u32[]{:S(2)}, u32[]{:S(2)}) collective-permute-start(bf16[4,2,128,128]{3,2,1,0:T(8,128)(2,1)} %get-tuple-element.40), channel_id=1, source_target_pairs={{0,4},{4,0},{8,12},{12,8},{1,5},{5,1},{9,13},{13,9},{2,6},{6,2},{1... | collective-permute-start | bytes 786440 | tf_op jit(solution)/shard_map/ppermute | solution.py:548
  37.6 2.2 %project_near.1.near = f32[384,256]{1,0:T(8,128)S(1)} custom-call(bf16[1,192,8192]{2,1,0:T(8,128)(2,1)S(1)} %copy-done, bf16[2048,128]{1,0:T(8,128)(2,1)} %w_key.3, bf16[2048,128]{1,0:T(8,128)(2,1)} %w_value.3, bf16[2,48,2048]{2,1,0:T(8,128)(2,1)S(1)} %collective-permute-done.2.rest_0_, bf16[2,48,2048]{2,1,0:T(8,128)(2,1)S(1)} %collective-permute-done.3.rest_1_, ...), custom_call_target="tpu_custom_call" | custom-call | flops 1 | bytes 1 | tf_op jit(solution)/shard_map/project_near/pallas_call | solution.py:233
  39.8 4.7 %collective-permute-done.1.w_swapped = bf16[2048,128]{1,0:T(8,128)(2,1)S(1)} collective-permute-done((bf16[2048,128]{1,0:T(8,128)(2,1)}, bf16[2048,128]{1,0:T(8,128)(2,1)S(1)}, u32[]{:S(2)}, u32[]{:S(2)}) %collective-permute-start.1) | collective-permute-done | bytes 524320 | tf_op jit(solution)/shard_map/ppermute | solution.py:548
  44.5 2.6 %project_far.1 = (f32[192,256]{1,0:T(8,128)S(1)}, bf16[192,128]{1,0:T(8,128)(2,1)S(1)}, bf16[192,128]{1,0:T(8,128)(2,1)S(1)}) custom-call(bf16[1,192,8192]{2,1,0:T(8,128)(2,1)S(1)} %copy-done, bf16[2048,128]{1,0:T(8,128)(2,1)} %get-tuple-element.26.w_far, bf16[2048,128]{1,0:T(8,128)(2,1)S(1)} %collective-permute-done.1.w_swapped, ...), custom_call_target="tpu_custom_call" | custom-call | flops 1 | bytes 1 | tf_op jit(solution)/shard_map/project_far/pallas_call | solution.py:242
  47.1 0.1 collective-permute-start.6
  47.2 2.0 %collective-permute-start.7 = (bf16[192,128]{1,0:T(8,128)(2,1)S(1)}, bf16[192,128]{1,0:T(8,128)(2,1)S(1)}, u32[]{:S(2)}, u32[]{:S(2)}) collective-permute-start(bf16[192,128]{1,0:T(8,128)(2,1)S(1)} %get-tuple-element.30), channel_id=1, source_target_pairs={{0,4},{4,0},{8,12},{12,8},{1,5},{5,1},{9,13},{13,9},{2,6},{6,2},{1... | collective-permute-start | bytes 147464 | tf_op jit(solution)/shard_map/ppermute | solution.py:548
  49.2 1.2 %plan.1 = (bf16[2048,128]{1,0:T(8,128)(2,1)S(1)}, bf16[16,2048]{1,0:T(8,128)(2,1)S(1)}, f32[1,2048]{1,0:T(1,128)S(1)}, s32[192,1]{1,0:T(8,128)S(1)}, s32[1,192]{1,0:T(1,128)S(1)}, /*index=5*/s32[1,192]{1,0:T(1,128)S(1)}) custom-call(s32[4,16]{1,0:T(4,128)S(1)} %copy-done.1, s32[32]{0:T(128)S(1)} %copy-done.3, s32[12,1,16]{2,1,0:T(1,128)S(1)} %bitcast.2), custom_call_target="tpu_custom_call" | custom-call | tf_op jit(solution)/shard_map/plan/pallas_call | solution.py:331
  50.4 7.4 %collective-permute-done.6.arrived_k = bf16[192,128]{1,0:T(8,128)(2,1)S(1)} collective-permute-done((bf16[192,128]{1,0:T(8,128)(2,1)S(1)}, bf16[192,128]{1,0:T(8,128)(2,1)S(1)}, u32[]{:S(2)}, u32[]{:S(2)}) %collective-permute-start.6) | collective-permute-done | bytes 49184 | tf_op jit(solution)/shard_map/ppermute | solution.py:548
  57.8 0.5 collective-permute-done.7.arrived_v
  58.3 1.0 %finish.1 = (bf16[192,256]{1,0:T(8,128)(2,1)S(1)}, bf16[192,256]{1,0:T(8,128)(2,1)}) custom-call(f32[192,256]{1,0:T(8,128)S(1)} %get-tuple-element.28.own, bf16[192,128]{1,0:T(8,128)(2,1)S(1)} %collective-permute-done.6.arrived_k, bf16[192,128]{1,0:T(8,128)(2,1)S(1)} %collective-permute-done.7.arrived_v, s32[1,192]{1,0:T(1,128)S(1)} %get-tuple-element.31.slot_row), custom_call_target="tpu_custom_call" | custom-call | tf_op jit(solution)/shard_map/finish/pallas_call | solution.py:356
  59.4 3.3 %all-to-all-start = ((bf16[4,48,256]{2,1,0:T(8,128)(2,1)}), bf16[4,48,256]{2,1,0:T(8,128)(2,1)S(1)}, u32[]{:S(2)}, u32[]{:S(2)}) async-start(bf16[4,48,256]{2,1,0:T(8,128)(2,1)} %bitcast.1), calls=%async_computation | async-start | bytes 196608 | tf_op jit(solution)/shard_map/all_to_all | solution.py:593
  62.7 7.0 %attend.1 = bf16[1,192,1024]{2,1,0:T(8,128)(2,1)} custom-call(s32[4,16]{1,0:T(4,128)S(1)} %copy-done.1, bf16[1,192,1024]{2,1,0:T(8,128)(2,1)} %queries.1, bf16[192,256]{1,0:T(8,128)(2,1)S(1)} %get-tuple-element.32.fresh, bf16[2048,128]{1,0:T(8,128)(2,1)S(1)} %get-tuple-element.33.held, bf16[16,2048]{1,0:T(8,128)(2,1)S(1)} %get-tuple-element.34.spare, ...), custom_call_target="tpu_custom_call" | custom-call | tf_op jit(solution)/shard_map/attend/pallas_call | solution.py:499
  69.7 0.7 broadcast_in_dim_reshape.3
  (17 shorter events, 0.0 us)
Async XLA Ops:
  0.6 36.9 %copy-start = (bf16[1,192,8192]{2,1,0:T(8,128)(2,1)S(1)}, bf16[1,192,8192]{2,1,0:T(8,128)(2,1)}, u32[]{:S(2)}) copy-start(bf16[1,192,8192]{2,1,0:T(8,128)(2,1)} %hidden.5) | copy-start | bytes 9437188
  2.8 20.7 %collective-permute-start.2 = (bf16[2,48,2048]{2,1,0:T(8,128)(2,1)}, bf16[2,48,2048]{2,1,0:T(8,128)(2,1)S(1)}, u32[]{:S(2)}, u32[]{:S(2)}) collective-permute-start(bf16[2,48,2048]{2,1,0:T(8,128)(2,1)} %get-tuple-element.27), channel_id=1, source_target_pairs={{0,4},{4,0},{8,12},{12,8},{1,5},{5,1},{9,13},{13,9},{2,6},{6,2},{1... | collective-permute-start | bytes 1179656 | tf_op jit(solution)/shard_map/ppermute | solution.py:548
  5.9 25.9 %collective-permute-start = (bf16[2048,128]{1,0:T(8,128)(2,1)}, bf16[2048,128]{1,0:T(8,128)(2,1)}, u32[]{:S(2)}, u32[]{:S(2)}) collective-permute-start(bf16[2048,128]{1,0:T(8,128)(2,1)} %get-tuple-element.25), channel_id=1, source_target_pairs={{0,8},{4,12},{8,0},{12,4},{1,9},{5,13},{9,1},{13,5},{2,10},{6,14},... | collective-permute-start | bytes 1572872 | tf_op jit(solution)/shard_map/ppermute | solution.py:548
  23.6 10.5 %collective-permute-start.4 = (bf16[2,48,2048]{2,1,0:T(8,128)(2,1)S(1)}, bf16[2,48,2048]{2,1,0:T(8,128)(2,1)}, u32[]{:S(2)}, u32[]{:S(2)}) collective-permute-start(bf16[2,48,2048]{2,1,0:T(8,128)(2,1)S(1)} %collective-permute-done.2.rest_0_), channel_id=1, source_target_pairs={{0,2},{1,3},{2,0},{3,1},{4,6},{5,7},{6,4},{7,5},{8,10},{9,11},{10,... | collective-permute-start | bytes 1179656 | tf_op jit(solution)/shard_map/ppermute | solution.py:548
  31.8 12.7 %collective-permute-start.1 = (bf16[2048,128]{1,0:T(8,128)(2,1)}, bf16[2048,128]{1,0:T(8,128)(2,1)S(1)}, u32[]{:S(2)}, u32[]{:S(2)}) collective-permute-start(bf16[2048,128]{1,0:T(8,128)(2,1)} %get-tuple-element.26.w_far), channel_id=1, source_target_pairs={{0,16},{16,0},{1,17},{17,1},{2,18},{18,2},{3,19},{19,3},{4,20},{20... | collective-permute-start | bytes 1572872 | tf_op jit(solution)/shard_map/ppermute | solution.py:548
  33.4 3.0 %collective-permute-start.3 = (bf16[2,48,2048]{2,1,0:T(8,128)(2,1)S(1)}, bf16[2,48,2048]{2,1,0:T(8,128)(2,1)S(1)}, u32[]{:S(2)}, u32[]{:S(2)}) collective-permute-start(bf16[2,48,2048]{2,1,0:T(8,128)(2,1)S(1)} %collective-permute-done.2.rest_0_), channel_id=1, source_target_pairs={{0,1},{1,0},{2,3},{3,2},{4,5},{5,4},{6,7},{7,6},{8,9},{9,8},{10,11... | collective-permute-start | bytes 1179656 | tf_op jit(solution)/shard_map/ppermute | solution.py:548
  34.1 3.5 %collective-permute-start.5 = (bf16[2,48,2048]{2,1,0:T(8,128)(2,1)}, bf16[2,48,2048]{2,1,0:T(8,128)(2,1)S(1)}, u32[]{:S(2)}, u32[]{:S(2)}) collective-permute-start(bf16[2,48,2048]{2,1,0:T(8,128)(2,1)} %collective-permute-done.4.rest_2_), channel_id=1, source_target_pairs={{0,1},{1,0},{2,3},{3,2},{4,5},{5,4},{6,7},{7,6},{8,9},{9,8},{10,11... | collective-permute-start | bytes 1179656 | tf_op jit(solution)/shard_map/ppermute | solution.py:548
  34.1 28.6 %collective-permute-start.8 = (bf16[4,2,128,128]{3,2,1,0:T(8,128)(2,1)}, bf16[4,2,128,128]{3,2,1,0:T(8,128)(2,1)}, u32[]{:S(2)}, u32[]{:S(2)}) collective-permute-start(bf16[4,2,128,128]{3,2,1,0:T(8,128)(2,1)} %get-tuple-element.38), channel_id=1, source_target_pairs={{0,8},{4,12},{8,0},{12,4},{1,9},{5,13},{9,1},{13,5},{2,10},{6,14},... | collective-permute-start | bytes 786440 | tf_op jit(solution)/shard_map/ppermute | solution.py:548
  34.5 28.2 %collective-permute-start.9 = (bf16[4,2,128,128]{3,2,1,0:T(8,128)(2,1)}, bf16[4,2,128,128]{3,2,1,0:T(8,128)(2,1)}, u32[]{:S(2)}, u32[]{:S(2)}) collective-permute-start(bf16[4,2,128,128]{3,2,1,0:T(8,128)(2,1)} %get-tuple-element.39), channel_id=1, source_target_pairs={{0,12},{4,8},{8,4},{12,0},{1,13},{5,9},{9,5},{13,1},{2,14},{6,10},... | collective-permute-start | bytes 786440 | tf_op jit(solution)/shard_map/ppermute | solution.py:548
  36.4 26.3 %collective-permute-start.10 = (bf16[4,2,128,128]{3,2,1,0:T(8,128)(2,1)}, bf16[4,2,128,128]{3,2,1,0:T(8,128)(2,1)}, u32[]{:S(2)}, u32[]{:S(2)}) collective-permute-start(bf16[4,2,128,128]{3,2,1,0:T(8,128)(2,1)} %get-tuple-element.40), channel_id=1, source_target_pairs={{0,4},{4,0},{8,12},{12,8},{1,5},{5,1},{9,13},{13,9},{2,6},{6,2},{1... | collective-permute-start | bytes 786440 | tf_op jit(solution)/shard_map/ppermute | solution.py:548
  39.8 9.4 %copy-start.1 = (s32[4,16]{1,0:T(4,128)S(1)}, s32[4,16]{1,0:T(4,128)}, u32[]{:S(2)}) copy-start(s32[4,16]{1,0:T(4,128)} %request_docs.5) | copy-start | bytes 772
  39.8 9.4 %copy-start.2 = (s32[1,16,12]{1,0,2:T(1,128)S(1)}, s32[1,16,12]{1,0,2:T(1,128)}, u32[]{:S(2)}) copy-start(s32[1,16,12]{1,0,2:T(1,128)} %param.17) | copy-start | bytes 2308
  39.8 9.4 %copy-start.3 = (s32[32]{0:T(128)S(1)}, s32[32]{0:T(128)}, u32[]{:S(2)}) copy-start(s32[32]{0:T(128)} %doc_lengths.1) | copy-start | bytes 388
  47.1 10.7 %collective-permute-start.6 = (bf16[192,128]{1,0:T(8,128)(2,1)S(1)}, bf16[192,128]{1,0:T(8,128)(2,1)S(1)}, u32[]{:S(2)}, u32[]{:S(2)}) collective-permute-start(bf16[192,128]{1,0:T(8,128)(2,1)S(1)} %get-tuple-element.29), channel_id=1, source_target_pairs={{0,4},{4,0},{8,12},{12,8},{1,5},{5,1},{9,13},{13,9},{2,6},{6,2},{1... | collective-permute-start | bytes 147464 | tf_op jit(solution)/shard_map/ppermute | solution.py:548
  47.2 11.1 %collective-permute-start.7 = (bf16[192,128]{1,0:T(8,128)(2,1)S(1)}, bf16[192,128]{1,0:T(8,128)(2,1)S(1)}, u32[]{:S(2)}, u32[]{:S(2)}) collective-permute-start(bf16[192,128]{1,0:T(8,128)(2,1)S(1)} %get-tuple-element.30), channel_id=1, source_target_pairs={{0,4},{4,0},{8,12},{12,8},{1,5},{5,1},{9,13},{13,9},{2,6},{6,2},{1... | collective-permute-start | bytes 147464 | tf_op jit(solution)/shard_map/ppermute | solution.py:548
  59.4 10.3 %all-to-all-start = ((bf16[4,48,256]{2,1,0:T(8,128)(2,1)}), bf16[4,48,256]{2,1,0:T(8,128)(2,1)S(1)}, u32[]{:S(2)}, u32[]{:S(2)}) async-start(bf16[4,48,256]{2,1,0:T(8,128)(2,1)} %bitcast.1), calls=%async_computation | async-start | bytes 196608 | tf_op jit(solution)/shard_map/all_to_all | solution.py:593

commit v10 on v9

--- a/solution.py
+++ b/solution.py
@@ -163,20 +163,31 @@
     )(request_docs, store_keys, store_values)
 
 
-def lay_rows(hidden, quarters, block, depth, h, copy):
-    mine = lax.axis_index("tp")
-    rows = hidden.shape[1]
-    piece = rows // len(quarters)
-    start = pl.multiple_of(block * depth, depth)
-    copy(hidden.at[0, :, pl.ds(start, depth)], h.at[pl.ds(0, rows)])
+def near_kernel(hidden, w_key, w_value, _, total, w, h, sems):
+    depth, width = w_key.shape
+    start = pl.multiple_of(lax.axis_index("seq") * depth, depth)
+    copies = [
+        pltpu.make_async_copy(w_key, w.at[:, pl.ds(0, width)], sems.at[0]),
+        pltpu.make_async_copy(w_value, w.at[:, pl.ds(width, width)], sems.at[1]),
+        pltpu.make_async_copy(hidden.at[0, :, pl.ds(start, depth)], h, sems.at[2]),
+    ]
+    for copy in copies:
+        copy.start()
+    for copy in copies:
+        copy.wait()
+    total[...] = jnp.dot(h[...], w[...], preferred_element_type=jnp.float32)
+
+
+def lay_quarters(quarters, block, rows, copy):
+    piece = rows.shape[0] // len(quarters)
     for k, quarter in enumerate(quarters):
-        start = pl.multiple_of(rows + lax.bitwise_xor(mine, k) * piece, piece)
-        copy(quarter, h.at[pl.ds(start, piece)])
-
-
-def near_kernel(hidden, w_key, w_value, *rest):
-    *quarters, total, w, h, sems = rest
-    depth, width = w_key.shape
+        start = pl.multiple_of(lax.bitwise_xor(lax.axis_index("tp"), k) * piece, piece)
+        copy(quarter.at[block], rows.at[pl.ds(start, piece)])
+
+
+def neighbour_kernel(w_key, w_value, *rest):
+    *quarters, total, w, n, sems = rest
+    width = w_key.shape[1]
     copies = []
 
     def copy(source, target):
@@ -185,18 +196,16 @@
 
     for i, held in enumerate((w_key, w_value)):
         copy(held, w.at[:, pl.ds(i * width, width)])
-    quarters = [quarter.at[0] for quarter in quarters]
-    lay_rows(hidden, quarters, lax.axis_index("seq"), depth, h, copy)
+    lay_quarters(quarters, 0, n, copy)
     for one in copies:
         one.wait()
-    total[...] = jnp.dot(h[...], w[...], preferred_element_type=jnp.float32)
-
-
-def far_kernel(hidden, w_far, w_swapped, near, *rest):
-    *quarters, own, part_k, part_v, w, h, sems, held_own, own_sem = rest
+    total[...] = jnp.dot(n[...], w[...], preferred_element_type=jnp.float32)
+
+
+def far_kernel(hidden, w_far, w_swapped, near, neighbour, *rest):
+    *quarters, own, part, w, h, n, sems, held_own, own_sem = rest
     group = lax.axis_index("groups")
     depth, width = w_far.shape
-    rows = hidden.shape[1]
     copies = []
 
     def copy(source, target):
@@ -205,54 +214,69 @@
 
     for held, place in ((w_far, group), (w_swapped, 1 - group)):
         copy(held, w.at[:, pl.ds(pl.multiple_of(place * width, width), width)])
-    quarters = [quarter.at[1] for quarter in quarters]
-    lay_rows(hidden, quarters, lax.rem(lax.axis_index("seq") + 2, 4), depth, h, copy)
+    start = pl.multiple_of(lax.rem(lax.axis_index("seq") + 2, 4) * depth, depth)
+    copy(hidden.at[0, :, pl.ds(start, depth)], h)
+    lay_quarters(quarters, 1, n, copy)
     for one in copies:
         one.wait()
-    total = near[...] + jnp.dot(h[...], w[...], preferred_element_type=jnp.float32)
-    held_own[...] = total[:rows]
+    held_own[...] = near[...] + jnp.dot(h[...], w[...], preferred_element_type=jnp.float32)
     store = pltpu.make_async_copy(held_own, own, own_sem)
     store.start()
-    part_k[...] = total[rows:, :width].astype(part_k.dtype)
-    part_v[...] = total[rows:, width:].astype(part_v.dtype)
+    total = neighbour[...] + jnp.dot(n[...], w[...], preferred_element_type=jnp.float32)
+    part[...] = total.astype(part.dtype)
     store.wait()
 
 
-def project(hidden, w_key, w_value, w_far, w_swapped, quarters):
+def project(hidden, w_key, w_value, w_far, w_swapped, quarters, first):
     depth, width = w_key.shape
     rows = hidden.shape[1]
-    scratch = [
-        pltpu.VMEM((depth, 2 * width), jnp.bfloat16),
-        pltpu.VMEM((2 * rows, depth), jnp.bfloat16),
-        pltpu.SemaphoreType.DMA((3 + len(quarters),)),
-    ]
-    settings = dict(
-        compiler_params=pltpu.CompilerParams(vmem_limit_bytes=16 * 1024 * 1024),
-        cost_estimate=pl.CostEstimate(flops=1, bytes_accessed=1, transcendentals=0),
-    )
+    sums = jax.ShapeDtypeStruct((rows, 2 * width), jnp.float32)
+    w_scratch = pltpu.VMEM((depth, 2 * width), jnp.bfloat16)
+    h_scratch = pltpu.VMEM((rows, depth), jnp.bfloat16)
+    limit = pltpu.CompilerParams(vmem_limit_bytes=16 * 1024 * 1024)
+    cheap = pl.CostEstimate(flops=1, bytes_accessed=1, transcendentals=0)
+    w_key, w_value = in_hbm(w_key), in_hbm(w_value)
     near = pl.pallas_call(
         near_kernel,
-        out_shape=jax.ShapeDtypeStruct((2 * rows, 2 * width), jnp.float32),
-        in_specs=[ANY] * (3 + len(quarters)),
+        out_shape=sums,
+        in_specs=[ANY] * 4,
         out_specs=VMEM,
-        scratch_shapes=scratch,
+        scratch_shapes=[w_scratch, h_scratch, pltpu.SemaphoreType.DMA((3,))],
+        compiler_params=limit,
+        cost_estimate=pl.CostEstimate(flops=10**10, bytes_accessed=1, transcendentals=0),
         name="project_near",
-        **settings,
-    )(hidden, in_hbm(w_key), in_hbm(w_value), *quarters)
+    )(hidden, w_key, w_value, first)
+    neighbour = pl.pallas_call(
+        neighbour_kernel,
+        out_shape=sums,
+        in_specs=[ANY] * (2 + len(quarters)),
+        out_specs=VMEM,
+        scratch_shapes=[
+            w_scratch,
+            h_scratch,
+            pltpu.SemaphoreType.DMA((2 + len(quarters),)),
+        ],
+        compiler_params=limit,
+        cost_estimate=cheap,
+        name="project_neighbour",
+    )(w_key, w_value, *quarters)
     return pl.pallas_call(
         far_kernel,
-        out_shape=(
-            jax.ShapeDtypeStruct((rows, 2 * width), jnp.float32),
-            jax.ShapeDtypeStruct((rows, width), jnp.bfloat16),
-            jax.ShapeDtypeStruct((rows, width), jnp.bfloat16),
-        ),
-        in_specs=[ANY] * 3 + [VMEM] + [ANY] * len(quarters),
-        out_specs=(ANY, VMEM, VMEM),
-        scratch_shapes=scratch
-        + [pltpu.VMEM((rows, 2 * width), jnp.float32), pltpu.SemaphoreType.DMA],
+        out_shape=(sums, jax.ShapeDtypeStruct((rows, 2 * width), jnp.bfloat16)),
+        in_specs=[ANY] * 3 + [VMEM] * 2 + [ANY] * len(quarters),
+        out_specs=(ANY, VMEM),
+        scratch_shapes=[
+            w_scratch,
+            h_scratch,
+            h_scratch,
+            pltpu.SemaphoreType.DMA((3 + len(quarters),)),
+            pltpu.VMEM((rows, 2 * width), jnp.float32),
+            pltpu.SemaphoreType.DMA,
+        ],
+        compiler_params=limit,
+        cost_estimate=cheap,
         name="project_far",
-        **settings,
-    )(hidden, w_far, w_swapped, near, *quarters)
+    )(hidden, w_far, w_swapped, near, neighbour, *quarters)
 
 
 def plan_kernel(
@@ -339,12 +363,11 @@
     )(request_docs, doc_lengths, jnp.transpose(recompute_rows, (2, 0, 1)))
 
 
-def finish_kernel(own, arrived_k, arrived_v, slot_row, fresh, outgoing, held, sem):
+def finish_kernel(own, arrived, slot_row, fresh, outgoing, held, sem):
     fetch = pltpu.make_async_copy(own, held, sem)
     fetch.start()
     fetch.wait()
-    arrived = jnp.concatenate([arrived_k[...], arrived_v[...]], axis=1)
-    total = (held[...] + arrived.astype(jnp.float32)).astype(jnp.bfloat16)
+    total = (held[...] + arrived[...].astype(jnp.float32)).astype(jnp.bfloat16)
     fresh[...] = total
     slots = lax.broadcasted_iota(jnp.int32, (outgoing.shape[0], 1), 0)
     pick = (slots == slot_row[...]).astype(jnp.bfloat16)
@@ -356,12 +379,12 @@
     return pl.pallas_call(
         finish_kernel,
         out_shape=tuple(jax.ShapeDtypeStruct(one, jnp.bfloat16) for one in shapes),
-        in_specs=[ANY] + [VMEM] * 3,
+        in_specs=[ANY, VMEM, VMEM],
         out_specs=(VMEM, VMEM),
         scratch_shapes=[pltpu.VMEM(own.shape, jnp.float32), pltpu.SemaphoreType.DMA],
         compiler_params=pltpu.CompilerParams(vmem_limit_bytes=16 * 1024 * 1024),
         name="finish",
-    )(own, *arrived, slot_row)
+    )(own, arrived, slot_row)
 
 
 def attend_kernel(
@@ -553,15 +576,13 @@
         doc_1, doc_2, doc_3 = pick_docs(request_docs, store_keys, store_values, False)
         h_core = swap(h_mine, "tp", 1)
         h_chip = swap(h_mine, "tp", 2)
-        doc_1, doc_2, doc_3, w_far = gate((doc_1, doc_2, doc_3, w_far), ())
+        doc_2, doc_3, w_far = gate((doc_2, doc_3, w_far))
         w_swapped = swap(w_far, "groups", 1)
-        doc_2 = swap(doc_2, "seq", 2)
-        doc_3 = swap(doc_3, "seq", 3)
         doc_1 = swap(doc_1, "seq", 1)
-        docs = (doc_2, doc_3, doc_1)
+        docs = (swap(doc_2, "seq", 2), swap(doc_3, "seq", 3), doc_1)
         quarters = (h_mine, h_core, h_chip, swap(h_chip, "tp", 1))
-        own, *parts = project(hidden, w_key, w_value, w_far, w_swapped, quarters)
-        arrived = [swap(one, "seq", 1) for one in parts]
+        own, part = project(hidden, w_key, w_value, w_far, w_swapped, quarters, doc_1)
+        arrived = swap(part, "seq", 1)
         sources = (store_keys, store_values, *docs)
     else:
         (docs,) = pick_docs(request_docs, store_keys, store_values, True)
@@ -570,7 +591,7 @@
             jnp.concatenate([w_key, w_value], axis=1), "seq", axis=0, tiled=True
         )
         own = jnp.dot(hidden[0], weights, preferred_element_type=jnp.float32)
-        arrived = [jnp.zeros(own.shape, jnp.bfloat16)[:, :head_dim]] * 2
+        arrived = jnp.zeros(own.shape, jnp.bfloat16)
 
     held, spare, key_bias, row_place, key_place, slot_row = plan(
         request_docs, doc_lengths, recompute_rows, slot_count, head_dim, doc_len

time: 70.8 us -> 67.3 us (0.951)
  starting transfers between devices: 17.8 us -> 14.9 us
  waiting for transfers between devices: 31.8 us -> 29.3 us
  Pallas kernels: 19.3 us -> 21.2 us
    ppermute x11 -> x10, starting transfers between devices: 14.5 us -> 11.2 us  [swap(): return lax.ppermute(array, axis, [(i, i ^ apart) for i in range(count)])]
    ppermute x11 -> x10, waiting for transfers between devices: 31.8 us -> 29.3 us  [swap(): return lax.ppermute(array, axis, [(i, i ^ apart) for i in range(count)])]
    pallas_call x2 -> x3, Pallas kernels: 4.78 us -> 6.61 us  [the longest x1 3.08 us: project(): pl.pallas_call(far_kernel, out_shape=(sums, jax.ShapeDtypeStruct((rows, 2...]
  transfers between devices with their start and end apart: 12 -> 11, of which waited for: 6 -> 6; matrix products, arithmetic and copies ran while one was open for 0% -> 0% of each run, Pallas kernels for 24% -> 28%
where the time goes in v10:
time: 67.3 us; the launch traced here: 66.9 us
  waiting for transfers between devices  29.3 us (44%)
  Pallas kernels  21.2 us (32%)
  starting transfers between devices  14.9 us (22%)
  between operations  0.78 us (1%)
  local copies, waits for them, and re-layouts  0.7 us (1%)
    ppermute x10, waiting for transfers between devices, swap(): return lax.ppermute(array, axis, [(i, i ^ apart) for i in range(count)])  29.3 us
    ppermute x10, starting transfers between devices, swap(): return lax.ppermute(array, axis, [(i, i ^ apart) for i in range(count)])  11.2 us
    pallas_call x1, Pallas kernels, attend(): pl.pallas_call(functools.partial(attend_kernel, by_owner), out_shape=jax....  6.96 us
    all_to_all x1, starting transfers between devices, shards(): lax.all_to_all(outgoing, 'seq', split_axis=0, concat_axis=0, tiled=True)  3.71 us
    pallas_call x1, Pallas kernels, pick_docs(): pl.pallas_call(functools.partial(docs_kernel, by_owner), out_shape=tuple(...  3.16 us
    pallas_call x1, Pallas kernels, project(): pl.pallas_call(far_kernel, out_shape=(sums, jax.ShapeDtypeStruct((rows, 2...  3.08 us
    pallas_call x1, Pallas kernels, pick_sent(): pl.pallas_call(send_kernel, out_shape=(jax.ShapeDtypeStruct(w_key.shape,...  2.19 us
    pallas_call x1, Pallas kernels, project(): pl.pallas_call(neighbour_kernel, out_shape=sums, in_specs=[ANY] * (2 + le...  1.92 us
  transfers between devices with their start and end apart: 11, of which 6 were waited for; matrix products, arithmetic and copies ran while one was open for 0% of the time, Pallas kernels for 28%

profile of v10, /device:TPU:0, one launch (start us, length us, event | category | flops | bytes accessed | tf_op | source)
XLA Modules:
  0.0 66.9 jit_solution(8770431536737713491)
XLA Ops:
  0.6 2.2 %pick_sent.1 = (bf16[2048,128]{1,0:T(8,128)(2,1)}, bf16[2,48,2048]{2,1,0:T(8,128)(2,1)}) custom-call(bf16[1,192,8192]{2,1,0:T(8,128)(2,1)} %hidden.5, bf16[2048,128]{1,0:T(8,128)(2,1)} %w_key.5, bf16[2048,128]{1,0:T(8,128)(2,1)} %w_value.5), custom_call_target="tpu_custom_call" | custom-call | tf_op jit(solution)/shard_map/pick_sent/pallas_call | solution.py:68
  2.8 3.1 %collective-permute-start.3 = (bf16[2,48,2048]{2,1,0:T(8,128)(2,1)}, bf16[2,48,2048]{2,1,0:T(8,128)(2,1)S(1)}, u32[]{:S(2)}, u32[]{:S(2)}) collective-permute-start(bf16[2,48,2048]{2,1,0:T(8,128)(2,1)} %get-tuple-element.25), channel_id=1, source_target_pairs={{0,4},{4,0},{8,12},{12,8},{1,5},{5,1},{9,13},{13,9},{2,6},{6,2},{1... | collective-permute-start | bytes 1179656 | tf_op jit(solution)/shard_map/ppermute | solution.py:571
  5.9 2.6 %collective-permute-start = (bf16[2048,128]{1,0:T(8,128)(2,1)}, bf16[2048,128]{1,0:T(8,128)(2,1)}, u32[]{:S(2)}, u32[]{:S(2)}) collective-permute-start(bf16[2048,128]{1,0:T(8,128)(2,1)} %get-tuple-element.22), channel_id=1, source_target_pairs={{0,8},{4,12},{8,0},{12,4},{1,9},{5,13},{9,1},{13,5},{2,10},{6,14},... | collective-permute-start | bytes 1572872 | tf_op jit(solution)/shard_map/ppermute | solution.py:571
  8.5 15.0 %collective-permute-done.3.rest_0_ = bf16[2,48,2048]{2,1,0:T(8,128)(2,1)S(1)} collective-permute-done((bf16[2,48,2048]{2,1,0:T(8,128)(2,1)}, bf16[2,48,2048]{2,1,0:T(8,128)(2,1)S(1)}, u32[]{:S(2)}, u32[]{:S(2)}) %collective-permute-start.3) | collective-permute-done | bytes 393248 | tf_op jit(solution)/shard_map/ppermute | solution.py:571
  23.6 1.7 %collective-permute-start.5 = (bf16[2,48,2048]{2,1,0:T(8,128)(2,1)S(1)}, bf16[2,48,2048]{2,1,0:T(8,128)(2,1)}, u32[]{:S(2)}, u32[]{:S(2)}) collective-permute-start(bf16[2,48,2048]{2,1,0:T(8,128)(2,1)S(1)} %collective-permute-done.3.rest_0_), channel_id=1, source_target_pairs={{0,2},{1,3},{2,0},{3,1},{4,6},{5,7},{6,4},{7,5},{8,10},{9,11},{10,... | collective-permute-start | bytes 1179656 | tf_op jit(solution)/shard_map/ppermute | solution.py:571
  25.2 3.2 %pick_docs.1 = (bf16[4,2,128,128]{3,2,1,0:T(8,128)(2,1)}, bf16[4,2,128,128]{3,2,1,0:T(8,128)(2,1)}, bf16[4,2,128,128]{3,2,1,0:T(8,128)(2,1)}) custom-call(s32[4,16]{1,0:T(4,128)} %request_docs.5, bf16[8,128,128]{2,1,0:T(8,128)(2,1)} %rest_0_.1, bf16[8,128,128]{2,1,0:T(8,128)(2,1)} %rest_1_.1), custom_call_target="tpu_custom_call" | custom-call | tf_op jit(solution)/shard_map/pick_docs/pallas_call | solution.py:153
  28.4 0.1 collective-permute-start.2
  28.5 0.1 collective-permute-start.4
  28.5 3.4 %collective-permute-done.refs_2_ = bf16[2048,128]{1,0:T(8,128)(2,1)} collective-permute-done((bf16[2048,128]{1,0:T(8,128)(2,1)}, bf16[2048,128]{1,0:T(8,128)(2,1)}, u32[]{:S(2)}, u32[]{:S(2)}) %collective-permute-start) | collective-permute-done | bytes 524320 | tf_op jit(solution)/shard_map/ppermute | solution.py:571
  31.9 1.6 %collective-permute-start.1 = (bf16[2048,128]{1,0:T(8,128)(2,1)}, bf16[2048,128]{1,0:T(8,128)(2,1)S(1)}, u32[]{:S(2)}, u32[]{:S(2)}) collective-permute-start(bf16[2048,128]{1,0:T(8,128)(2,1)} %get-tuple-element.23.w_far), channel_id=1, source_target_pairs={{0,16},{16,0},{1,17},{17,1},{2,18},{18,2},{3,19},{19,3},{4,20},{20... | collective-permute-start | bytes 1572872 | tf_op jit(solution)/shard_map/ppermute | solution.py:571
  33.5 4.8 %collective-permute-done.2._.rest_4_ = bf16[4,2,128,128]{3,2,1,0:T(8,128)(2,1)S(1)} collective-permute-done((bf16[4,2,128,128]{3,2,1,0:T(8,128)(2,1)}, bf16[4,2,128,128]{3,2,1,0:T(8,128)(2,1)S(1)}, u32[]{:S(2)}, u32[]{:S(2)}) %collective-permute-start.2) | collective-permute-done | bytes 262176 | tf_op jit(solution)/shard_map/ppermute | solution.py:571
  38.3 1.6 %collective-permute-start.9 = (bf16[4,2,128,128]{3,2,1,0:T(8,128)(2,1)}, bf16[4,2,128,128]{3,2,1,0:T(8,128)(2,1)}, u32[]{:S(2)}, u32[]{:S(2)}) collective-permute-start(bf16[4,2,128,128]{3,2,1,0:T(8,128)(2,1)} %get-tuple-element.36), channel_id=1, source_target_pairs={{0,12},{4,8},{8,4},{12,0},{1,13},{5,9},{9,5},{13,1},{2,14},{6,10},... | collective-permute-start | bytes 786440 | tf_op jit(solution)/shard_map/ppermute | solution.py:571
  39.9 1.6 %project_near.1.near = f32[192,256]{1,0:T(8,128)S(1)} custom-call(bf16[1,192,8192]{2,1,0:T(8,128)(2,1)S(1)} %copy-done, bf16[2048,128]{1,0:T(8,128)(2,1)} %w_key.5, bf16[2048,128]{1,0:T(8,128)(2,1)} %w_value.5, bf16[4,2,128,128]{3,2,1,0:T(8,128)(2,1)S(1)} %collective-permute-done.2._.rest_4_), custom_call_target="tpu_custom_call" | custom-call | flops 10000000000 | bytes 1 | tf_op jit(solution)/shard_map/project_near/pallas_call | solution.py:239
  41.5 0.3 collective-permute-done.6.rest_3_
  41.8 1.9 %project_neighbour.1.neighbour = f32[192,256]{1,0:T(8,128)S(1)} custom-call(bf16[2048,128]{1,0:T(8,128)(2,1)} %w_key.5, bf16[2048,128]{1,0:T(8,128)(2,1)} %w_value.5, bf16[2,48,2048]{2,1,0:T(8,128)(2,1)S(1)} %collective-permute-done.3.rest_0_, bf16[2,48,2048]{2,1,0:T(8,128)(2,1)S(1)} %collective-permute-done.4.rest_1_, ...), custom_call_target="tpu_custom_call" | custom-call | flops 1 | bytes 1 | tf_op jit(solution)/shard_map/project_neighbour/pallas_call | solution.py:249
  43.8 0.7 %collective-permute-done.1.w_swapped = bf16[2048,128]{1,0:T(8,128)(2,1)S(1)} collective-permute-done((bf16[2048,128]{1,0:T(8,128)(2,1)}, bf16[2048,128]{1,0:T(8,128)(2,1)S(1)}, u32[]{:S(2)}, u32[]{:S(2)}) %collective-permute-start.1) | collective-permute-done | bytes 524320 | tf_op jit(solution)/shard_map/ppermute | solution.py:571
  44.5 3.1 %project_far.1 = (f32[192,256]{1,0:T(8,128)S(1)}, bf16[192,256]{1,0:T(8,128)(2,1)S(1)}) custom-call(bf16[1,192,8192]{2,1,0:T(8,128)(2,1)S(1)} %copy-done, bf16[2048,128]{1,0:T(8,128)(2,1)} %get-tuple-element.23.w_far, bf16[2048,128]{1,0:T(8,128)(2,1)S(1)} %collective-permute-done.1.w_swapped, f32[192,256]{1,0:T(8,128)S(1)} %project_near.1.near, ...), custom_call_target="tpu_custom_call" | custom-call | flops 1 | bytes 1 | tf_op jit(solution)/shard_map/project_far/pallas_call | solution.py:263
  47.6 0.6 collective-permute-start.7
  48.2 1.2 %plan.1 = (bf16[2048,128]{1,0:T(8,128)(2,1)S(1)}, bf16[16,2048]{1,0:T(8,128)(2,1)S(1)}, f32[1,2048]{1,0:T(1,128)S(1)}, s32[192,1]{1,0:T(8,128)S(1)}, s32[1,192]{1,0:T(1,128)S(1)}, /*index=5*/s32[1,192]{1,0:T(1,128)S(1)}) custom-call(s32[4,16]{1,0:T(4,128)S(1)} %copy-done.2, s32[32]{0:T(128)S(1)} %copy-done.4, s32[12,1,16]{2,1,0:T(1,128)S(1)} %bitcast.2), custom_call_target="tpu_custom_call" | custom-call | tf_op jit(solution)/shard_map/plan/pallas_call | solution.py:355
  49.4 5.0 %collective-permute-done.7.arrived = bf16[192,256]{1,0:T(8,128)(2,1)S(1)} collective-permute-done((bf16[192,256]{1,0:T(8,128)(2,1)S(1)}, bf16[192,256]{1,0:T(8,128)(2,1)S(1)}, u32[]{:S(2)}, u32[]{:S(2)}) %collective-permute-start.7) | collective-permute-done | bytes 98336 | tf_op jit(solution)/shard_map/ppermute | solution.py:571
  54.4 1.1 %finish.1 = (bf16[192,256]{1,0:T(8,128)(2,1)S(1)}, bf16[192,256]{1,0:T(8,128)(2,1)}) custom-call(f32[192,256]{1,0:T(8,128)S(1)} %get-tuple-element.26.own, bf16[192,256]{1,0:T(8,128)(2,1)S(1)} %collective-permute-done.7.arrived, s32[1,192]{1,0:T(1,128)S(1)} %get-tuple-element.28.slot_row), custom_call_target="tpu_custom_call" | custom-call | tf_op jit(solution)/shard_map/finish/pallas_call | solution.py:379
  55.5 3.7 %all-to-all-start = ((bf16[4,48,256]{2,1,0:T(8,128)(2,1)}), bf16[4,48,256]{2,1,0:T(8,128)(2,1)S(1)}, u32[]{:S(2)}, u32[]{:S(2)}) async-start(bf16[4,48,256]{2,1,0:T(8,128)(2,1)} %bitcast.1), calls=%async_computation | async-start | bytes 196608 | tf_op jit(solution)/shard_map/all_to_all | solution.py:614
  59.2 7.0 %attend.1 = bf16[1,192,1024]{2,1,0:T(8,128)(2,1)} custom-call(s32[4,16]{1,0:T(4,128)S(1)} %copy-done.2, bf16[1,192,1024]{2,1,0:T(8,128)(2,1)} %queries.1, bf16[192,256]{1,0:T(8,128)(2,1)S(1)} %get-tuple-element.29.fresh, bf16[2048,128]{1,0:T(8,128)(2,1)S(1)} %get-tuple-element.30.held, bf16[16,2048]{1,0:T(8,128)(2,1)S(1)} %get-tuple-element.31.spare, ...), custom_call_target="tpu_custom_call" | custom-call | tf_op jit(solution)/shard_map/attend/pallas_call | solution.py:522
  66.2 0.7 %broadcast_in_dim_reshape.3 = bf16[1,4,4,12,2,128]{5,4,3,2,1,0:T(2,128)(2,1)} reshape(bf16[4,48,256]{2,1,0:T(8,128)(2,1)S(1)} %all-to-all-done) | data formatting | bytes 196608 | tf_op jit(solution)/shard_map/broadcast_in_dim;reshape | solution.py:616
  (18 shorter events, 0.0 us)
Async XLA Ops:
  0.6 39.3 %copy-start = (bf16[1,192,8192]{2,1,0:T(8,128)(2,1)S(1)}, bf16[1,192,8192]{2,1,0:T(8,128)(2,1)}, u32[]{:S(2)}) copy-start(bf16[1,192,8192]{2,1,0:T(8,128)(2,1)} %hidden.5) | copy-start | bytes 9437188
  2.8 20.7 %collective-permute-start.3 = (bf16[2,48,2048]{2,1,0:T(8,128)(2,1)}, bf16[2,48,2048]{2,1,0:T(8,128)(2,1)S(1)}, u32[]{:S(2)}, u32[]{:S(2)}) collective-permute-start(bf16[2,48,2048]{2,1,0:T(8,128)(2,1)} %get-tuple-element.25), channel_id=1, source_target_pairs={{0,4},{4,0},{8,12},{12,8},{1,5},{5,1},{9,13},{13,9},{2,6},{6,2},{1... | collective-permute-start | bytes 1179656 | tf_op jit(solution)/shard_map/ppermute | solution.py:571
  5.9 26.0 %collective-permute-start = (bf16[2048,128]{1,0:T(8,128)(2,1)}, bf16[2048,128]{1,0:T(8,128)(2,1)}, u32[]{:S(2)}, u32[]{:S(2)}) collective-permute-start(bf16[2048,128]{1,0:T(8,128)(2,1)} %get-tuple-element.22), channel_id=1, source_target_pairs={{0,8},{4,12},{8,0},{12,4},{1,9},{5,13},{9,1},{13,5},{2,10},{6,14},... | collective-permute-start | bytes 1572872 | tf_op jit(solution)/shard_map/ppermute | solution.py:571
  23.6 16.3 %collective-permute-start.5 = (bf16[2,48,2048]{2,1,0:T(8,128)(2,1)S(1)}, bf16[2,48,2048]{2,1,0:T(8,128)(2,1)}, u32[]{:S(2)}, u32[]{:S(2)}) collective-permute-start(bf16[2,48,2048]{2,1,0:T(8,128)(2,1)S(1)} %collective-permute-done.3.rest_0_), channel_id=1, source_target_pairs={{0,2},{1,3},{2,0},{3,1},{4,6},{5,7},{6,4},{7,5},{8,10},{9,11},{10,... | collective-permute-start | bytes 1179656 | tf_op jit(solution)/shard_map/ppermute | solution.py:571
  28.4 9.9 %collective-permute-start.2 = (bf16[4,2,128,128]{3,2,1,0:T(8,128)(2,1)}, bf16[4,2,128,128]{3,2,1,0:T(8,128)(2,1)S(1)}, u32[]{:S(2)}, u32[]{:S(2)}) collective-permute-start(bf16[4,2,128,128]{3,2,1,0:T(8,128)(2,1)} %get-tuple-element.24), channel_id=1, source_target_pairs={{0,4},{4,0},{8,12},{12,8},{1,5},{5,1},{9,13},{13,9},{2,6},{6,2},{1... | collective-permute-start | bytes 786440 | tf_op jit(solution)/shard_map/ppermute | solution.py:571
  28.5 13.1 %collective-permute-start.4 = (bf16[2,48,2048]{2,1,0:T(8,128)(2,1)S(1)}, bf16[2,48,2048]{2,1,0:T(8,128)(2,1)S(1)}, u32[]{:S(2)}, u32[]{:S(2)}) collective-permute-start(bf16[2,48,2048]{2,1,0:T(8,128)(2,1)S(1)} %collective-permute-done.3.rest_0_), channel_id=1, source_target_pairs={{0,1},{1,0},{2,3},{3,2},{4,5},{5,4},{6,7},{7,6},{8,9},{9,8},{10,11... | collective-permute-start | bytes 1179656 | tf_op jit(solution)/shard_map/ppermute | solution.py:571
  31.9 12.6 %collective-permute-start.1 = (bf16[2048,128]{1,0:T(8,128)(2,1)}, bf16[2048,128]{1,0:T(8,128)(2,1)S(1)}, u32[]{:S(2)}, u32[]{:S(2)}) collective-permute-start(bf16[2048,128]{1,0:T(8,128)(2,1)} %get-tuple-element.23.w_far), channel_id=1, source_target_pairs={{0,16},{16,0},{1,17},{17,1},{2,18},{18,2},{3,19},{19,3},{4,20},{20... | collective-permute-start | bytes 1572872 | tf_op jit(solution)/shard_map/ppermute | solution.py:571
  33.5 25.7 %collective-permute-start.8 = (bf16[4,2,128,128]{3,2,1,0:T(8,128)(2,1)}, bf16[4,2,128,128]{3,2,1,0:T(8,128)(2,1)}, u32[]{:S(2)}, u32[]{:S(2)}) collective-permute-start(bf16[4,2,128,128]{3,2,1,0:T(8,128)(2,1)} %get-tuple-element.35), channel_id=1, source_target_pairs={{0,8},{4,12},{8,0},{12,4},{1,9},{5,13},{9,1},{13,5},{2,10},{6,14},... | collective-permute-start | bytes 786440 | tf_op jit(solution)/shard_map/ppermute | solution.py:571
  38.3 3.2 %copy-start.1 = (bf16[4,2,128,128]{3,2,1,0:T(8,128)(2,1)}, bf16[4,2,128,128]{3,2,1,0:T(8,128)(2,1)S(1)}, u32[]{:S(2)}) copy-start(bf16[4,2,128,128]{3,2,1,0:T(8,128)(2,1)S(1)} %collective-permute-done.2._.rest_4_) | copy-start | bytes 786436
  38.3 20.9 %collective-permute-start.9 = (bf16[4,2,128,128]{3,2,1,0:T(8,128)(2,1)}, bf16[4,2,128,128]{3,2,1,0:T(8,128)(2,1)}, u32[]{:S(2)}, u32[]{:S(2)}) collective-permute-start(bf16[4,2,128,128]{3,2,1,0:T(8,128)(2,1)} %get-tuple-element.36), channel_id=1, source_target_pairs={{0,12},{4,8},{8,4},{12,0},{1,13},{5,9},{9,5},{13,1},{2,14},{6,10},... | collective-permute-start | bytes 786440 | tf_op jit(solution)/shard_map/ppermute | solution.py:571
  39.9 1.9 %collective-permute-start.6 = (bf16[2,48,2048]{2,1,0:T(8,128)(2,1)}, bf16[2,48,2048]{2,1,0:T(8,128)(2,1)S(1)}, u32[]{:S(2)}, u32[]{:S(2)}) collective-permute-start(bf16[2,48,2048]{2,1,0:T(8,128)(2,1)} %collective-permute-done.5.rest_2_), channel_id=1, source_target_pairs={{0,1},{1,0},{2,3},{3,2},{4,5},{5,4},{6,7},{7,6},{8,9},{9,8},{10,11... | collective-permute-start | bytes 1179656 | tf_op jit(solution)/shard_map/ppermute | solution.py:571
  43.8 4.4 %copy-start.2 = (s32[4,16]{1,0:T(4,128)S(1)}, s32[4,16]{1,0:T(4,128)}, u32[]{:S(2)}) copy-start(s32[4,16]{1,0:T(4,128)} %request_docs.5) | copy-start | bytes 772
  43.8 4.4 %copy-start.3 = (s32[1,16,12]{1,0,2:T(1,128)S(1)}, s32[1,16,12]{1,0,2:T(1,128)}, u32[]{:S(2)}) copy-start(s32[1,16,12]{1,0,2:T(1,128)} %param.17) | copy-start | bytes 2308
  43.8 4.4 %copy-start.4 = (s32[32]{0:T(128)S(1)}, s32[32]{0:T(128)}, u32[]{:S(2)}) copy-start(s32[32]{0:T(128)} %doc_lengths.1) | copy-start | bytes 388
  47.6 6.8 %collective-permute-start.7 = (bf16[192,256]{1,0:T(8,128)(2,1)S(1)}, bf16[192,256]{1,0:T(8,128)(2,1)S(1)}, u32[]{:S(2)}, u32[]{:S(2)}) collective-permute-start(bf16[192,256]{1,0:T(8,128)(2,1)S(1)} %get-tuple-element.27), channel_id=1, source_target_pairs={{0,4},{4,0},{8,12},{12,8},{1,5},{5,1},{9,13},{13,9},{2,6},{6,2},{1... | collective-permute-start | bytes 294920 | tf_op jit(solution)/shard_map/ppermute | solution.py:571
  55.5 10.7 %all-to-all-start = ((bf16[4,48,256]{2,1,0:T(8,128)(2,1)}), bf16[4,48,256]{2,1,0:T(8,128)(2,1)S(1)}, u32[]{:S(2)}, u32[]{:S(2)}) async-start(bf16[4,48,256]{2,1,0:T(8,128)(2,1)} %bitcast.1), calls=%async_computation | async-start | bytes 196608 | tf_op jit(solution)/shard_map/all_to_all | solution.py:614

commit v11 on v10

--- a/solution.py
+++ b/solution.py
@@ -87,7 +87,7 @@
     pass
 
 
-def gate(arrays, first=()):
+def gate(arrays, first=(), pinned=0):
     return pl.pallas_call(
         gate_kernel,
         out_shape=tuple(jax.ShapeDtypeStruct(one.shape, one.dtype) for one in arrays),
@@ -95,8 +95,9 @@
         out_specs=(ANY,) * len(arrays),
         input_output_aliases={i: i for i in range(len(arrays))},
         compiler_params=pltpu.CompilerParams(vmem_limit_bytes=1024 * 1024),
+        cost_estimate=pl.CostEstimate(flops=8000000000, bytes_accessed=1, transcendentals=0),
         name="gate",
-    )(*(in_hbm(one) for one in arrays), *first)
+    )(*(in_hbm(one) for one in arrays[:pinned]), *arrays[pinned:], *first)
 
 
 def docs_kernel(by_owner, request_docs, store_keys, store_values, *rest):
@@ -203,7 +204,7 @@
 
 
 def far_kernel(hidden, w_far, w_swapped, near, neighbour, *rest):
-    *quarters, own, part, w, h, n, sems, held_own, own_sem = rest
+    *quarters, own, part, w, h, n, sems = rest
     group = lax.axis_index("groups")
     depth, width = w_far.shape
     copies = []
@@ -219,12 +220,9 @@
     lay_quarters(quarters, 1, n, copy)
     for one in copies:
         one.wait()
-    held_own[...] = near[...] + jnp.dot(h[...], w[...], preferred_element_type=jnp.float32)
-    store = pltpu.make_async_copy(held_own, own, own_sem)
-    store.start()
+    own[...] = near[...] + jnp.dot(h[...], w[...], preferred_element_type=jnp.float32)
     total = neighbour[...] + jnp.dot(n[...], w[...], preferred_element_type=jnp.float32)
     part[...] = total.astype(part.dtype)
-    store.wait()
 
 
 def project(hidden, w_key, w_value, w_far, w_swapped, quarters, first):
@@ -264,14 +262,12 @@
         far_kernel,
         out_shape=(sums, jax.ShapeDtypeStruct((rows, 2 * width), jnp.bfloat16)),
         in_specs=[ANY] * 3 + [VMEM] * 2 + [ANY] * len(quarters),
-        out_specs=(ANY, VMEM),
+        out_specs=(VMEM, VMEM),
         scratch_shapes=[
             w_scratch,
             h_scratch,
             h_scratch,
             pltpu.SemaphoreType.DMA((3 + len(quarters),)),
-            pltpu.VMEM((rows, 2 * width), jnp.float32),
-            pltpu.SemaphoreType.DMA,
         ],
         compiler_params=limit,
         cost_estimate=cheap,
@@ -363,11 +359,8 @@
     )(request_docs, doc_lengths, jnp.transpose(recompute_rows, (2, 0, 1)))
 
 
-def finish_kernel(own, arrived, slot_row, fresh, outgoing, held, sem):
-    fetch = pltpu.make_async_copy(own, held, sem)
-    fetch.start()
-    fetch.wait()
-    total = (held[...] + arrived[...].astype(jnp.float32)).astype(jnp.bfloat16)
+def finish_kernel(own, arrived, slot_row, fresh, outgoing):
+    total = (own[...] + arrived[...].astype(jnp.float32)).astype(jnp.bfloat16)
     fresh[...] = total
     slots = lax.broadcasted_iota(jnp.int32, (outgoing.shape[0], 1), 0)
     pick = (slots == slot_row[...]).astype(jnp.bfloat16)
@@ -379,9 +372,8 @@
     return pl.pallas_call(
         finish_kernel,
         out_shape=tuple(jax.ShapeDtypeStruct(one, jnp.bfloat16) for one in shapes),
-        in_specs=[ANY, VMEM, VMEM],
+        in_specs=[VMEM] * 3,
         out_specs=(VMEM, VMEM),
-        scratch_shapes=[pltpu.VMEM(own.shape, jnp.float32), pltpu.SemaphoreType.DMA],
         compiler_params=pltpu.CompilerParams(vmem_limit_bytes=16 * 1024 * 1024),
         name="finish",
     )(own, arrived, slot_row)
@@ -530,7 +522,7 @@
             pltpu.VMEM((context, 2 * head_dim), jnp.bfloat16),
             pltpu.VMEM((context, 2 * head_dim), jnp.bfloat16),
             pltpu.SMEM((request_docs.shape[0],), jnp.int32),
-            pltpu.SemaphoreType.DMA((2, 4)),
+            pltpu.SemaphoreType.DMA((2, request_docs.shape[1] // 2)),
             pltpu.SemaphoreType.DMA,
         ],
         compiler_params=pltpu.CompilerParams(vmem_limit_bytes=32 * 1024 * 1024),
@@ -544,7 +536,8 @@
         key_bias,
         row_place,
         key_place,
-        *(in_hbm(one) for one in sources),
+        *(in_hbm(one) for one in sources[:2]),
+        *sources[2:],
     )
 
 
@@ -574,9 +567,10 @@
         w_far = swap(w_send, "seq", 2)
         h_mine = swap(h_send, "seq", 1)
         doc_1, doc_2, doc_3 = pick_docs(request_docs, store_keys, store_values, False)
+        (h_mine,) = gate((h_mine,), (in_hbm(doc_1),))
+        h_chip = swap(h_mine, "tp", 2)
         h_core = swap(h_mine, "tp", 1)
-        h_chip = swap(h_mine, "tp", 2)
-        doc_2, doc_3, w_far = gate((doc_2, doc_3, w_far))
+        doc_2, doc_3, w_far = gate((doc_2, doc_3, w_far), pinned=2)
         w_swapped = swap(w_far, "groups", 1)
         doc_1 = swap(doc_1, "seq", 1)
         docs = (swap(doc_2, "seq", 2), swap(doc_3, "seq", 3), doc_1)

time: 67.3 us -> 67.2 us (level)
  Pallas kernels: 21.2 us -> 20.2 us
  starting transfers between devices: 14.9 us -> 15.6 us
    pallas_call x1, Pallas kernels: 3.08 us -> 1.94 us  [project(): pl.pallas_call(far_kernel, out_shape=(sums, jax.ShapeDtypeStruct((rows, 2...]
    ppermute x10, starting transfers between devices: 11.2 us -> 12.3 us  [swap(): return lax.ppermute(array, axis, [(i, i ^ apart) for i in range(count)])]
    pallas_call x1, Pallas kernels: 6.96 us -> 7.8 us  [attend(): pl.pallas_call(functools.partial(attend_kernel, by_owner), out_shape=jax....]
  transfers between devices with their start and end apart: 11 -> 11, of which waited for: 6 -> 6; matrix products, arithmetic and copies ran while one was open for 0% -> 0% of each run, Pallas kernels for 28% -> 27%
where the time goes in v11:
time: 67.2 us; the launch traced here: 66.7 us
  waiting for transfers between devices  29.4 us (44%)
  Pallas kernels  20.2 us (30%)
  starting transfers between devices  15.6 us (23%)
  between operations  0.79 us (1%)
  local copies, waits for them, and re-layouts  0.69 us (1%)
    ppermute x10, waiting for transfers between devices, swap(): return lax.ppermute(array, axis, [(i, i ^ apart) for i in range(count)])  29.4 us
    ppermute x10, starting transfers between devices, swap(): return lax.ppermute(array, axis, [(i, i ^ apart) for i in range(count)])  12.3 us
    pallas_call x1, Pallas kernels, attend(): pl.pallas_call(functools.partial(attend_kernel, by_owner), out_shape=jax....  7.8 us
    all_to_all x1, starting transfers between devices, shards(): lax.all_to_all(outgoing, 'seq', split_axis=0, concat_axis=0, tiled=True)  3.3 us
    pallas_call x1, Pallas kernels, pick_docs(): pl.pallas_call(functools.partial(docs_kernel, by_owner), out_shape=tuple(...  3.13 us
    pallas_call x1, Pallas kernels, pick_sent(): pl.pallas_call(send_kernel, out_shape=(jax.ShapeDtypeStruct(w_key.shape,...  2.05 us
    pallas_call x1, Pallas kernels, project(): pl.pallas_call(far_kernel, out_shape=(sums, jax.ShapeDtypeStruct((rows, 2...  1.94 us
    pallas_call x1, Pallas kernels, project(): pl.pallas_call(neighbour_kernel, out_shape=sums, in_specs=[ANY] * (2 + le...  1.64 us
  transfers between devices with their start and end apart: 11, of which 6 were waited for; matrix products, arithmetic and copies ran while one was open for 0% of the time, Pallas kernels for 27%

profile of v11, /device:TPU:0, one launch (start us, length us, event | category | flops | bytes accessed | tf_op | source)
XLA Modules:
  0.0 66.7 jit_solution(12961290083890860431)
XLA Ops:
  0.6 2.0 %pick_sent.1 = (bf16[2048,128]{1,0:T(8,128)(2,1)}, bf16[2,48,2048]{2,1,0:T(8,128)(2,1)}) custom-call(bf16[1,192,8192]{2,1,0:T(8,128)(2,1)} %hidden.5, bf16[2048,128]{1,0:T(8,128)(2,1)} %w_key.5, bf16[2048,128]{1,0:T(8,128)(2,1)} %w_value.5), custom_call_target="tpu_custom_call" | custom-call | tf_op jit(solution)/shard_map/pick_sent/pallas_call | solution.py:68
  2.7 3.1 %collective-permute-start.3 = (bf16[2,48,2048]{2,1,0:T(8,128)(2,1)}, bf16[2,48,2048]{2,1,0:T(8,128)(2,1)S(1)}, u32[]{:S(2)}, u32[]{:S(2)}) collective-permute-start(bf16[2,48,2048]{2,1,0:T(8,128)(2,1)} %get-tuple-element.25), channel_id=1, source_target_pairs={{0,4},{4,0},{8,12},{12,8},{1,5},{5,1},{9,13},{13,9},{2,6},{6,2},{1... | collective-permute-start | bytes 1179656 | tf_op jit(solution)/shard_map/ppermute | solution.py:564
  5.8 2.6 %collective-permute-start = (bf16[2048,128]{1,0:T(8,128)(2,1)}, bf16[2048,128]{1,0:T(8,128)(2,1)S(1)}, u32[]{:S(2)}, u32[]{:S(2)}) collective-permute-start(bf16[2048,128]{1,0:T(8,128)(2,1)} %get-tuple-element.22), channel_id=1, source_target_pairs={{0,8},{4,12},{8,0},{12,4},{1,9},{5,13},{9,1},{13,5},{2,10},{6,14},... | collective-permute-start | bytes 1572872 | tf_op jit(solution)/shard_map/ppermute | solution.py:564
  8.4 3.1 %pick_docs.1 = (bf16[4,2,128,128]{3,2,1,0:T(8,128)(2,1)}, bf16[4,2,128,128]{3,2,1,0:T(8,128)(2,1)}, bf16[4,2,128,128]{3,2,1,0:T(8,128)(2,1)}) custom-call(s32[4,16]{1,0:T(4,128)} %request_docs.5, bf16[8,128,128]{2,1,0:T(8,128)(2,1)} %rest_0_.1, bf16[8,128,128]{2,1,0:T(8,128)(2,1)} %rest_1_.1), custom_call_target="tpu_custom_call" | custom-call | tf_op jit(solution)/shard_map/pick_docs/pallas_call | solution.py:154
  11.5 0.5 collective-permute-start.2
  12.0 12.2 %collective-permute-done.3.refs_0_ = bf16[2,48,2048]{2,1,0:T(8,128)(2,1)S(1)} collective-permute-done((bf16[2,48,2048]{2,1,0:T(8,128)(2,1)}, bf16[2,48,2048]{2,1,0:T(8,128)(2,1)S(1)}, u32[]{:S(2)}, u32[]{:S(2)}) %collective-permute-start.3) | collective-permute-done | bytes 393248 | tf_op jit(solution)/shard_map/ppermute | solution.py:564
  24.2 2.0 %collective-permute-start.5 = (bf16[2,48,2048]{2,1,0:T(8,128)(2,1)S(1)}, bf16[2,48,2048]{2,1,0:T(8,128)(2,1)S(1)}, u32[]{:S(2)}, u32[]{:S(2)}) collective-permute-start(bf16[2,48,2048]{2,1,0:T(8,128)(2,1)S(1)} %gate.3.rest_0_), channel_id=1, source_target_pairs={{0,2},{1,3},{2,0},{3,1},{4,6},{5,7},{6,4},{7,5},{8,10},{9,11},{10,... | collective-permute-start | bytes 1179656 | tf_op jit(solution)/shard_map/ppermute | solution.py:564
  26.2 5.4 %collective-permute-done.refs_2_ = bf16[2048,128]{1,0:T(8,128)(2,1)S(1)} collective-permute-done((bf16[2048,128]{1,0:T(8,128)(2,1)}, bf16[2048,128]{1,0:T(8,128)(2,1)S(1)}, u32[]{:S(2)}, u32[]{:S(2)}) %collective-permute-start) | collective-permute-done | bytes 524320 | tf_op jit(solution)/shard_map/ppermute | solution.py:564
  31.7 1.6 %collective-permute-start.1 = (bf16[2048,128]{1,0:T(8,128)(2,1)S(1)}, bf16[2048,128]{1,0:T(8,128)(2,1)S(1)}, u32[]{:S(2)}, u32[]{:S(2)}) collective-permute-start(bf16[2048,128]{1,0:T(8,128)(2,1)S(1)} %get-tuple-element.23.w_far), channel_id=1, source_target_pairs={{0,16},{16,0},{1,17},{17,1},{2,18},{18,2},{3,19},{19,3},{4,20},{20... | collective-permute-start | bytes 1572872 | tf_op jit(solution)/shard_map/ppermute | solution.py:564
  33.2 2.5 %collective-permute-start.9 = (bf16[4,2,128,128]{3,2,1,0:T(8,128)(2,1)}, bf16[4,2,128,128]{3,2,1,0:T(8,128)(2,1)S(1)}, u32[]{:S(2)}, u32[]{:S(2)}) collective-permute-start(bf16[4,2,128,128]{3,2,1,0:T(8,128)(2,1)} %get-tuple-element.36), channel_id=1, source_target_pairs={{0,12},{4,8},{8,4},{12,0},{1,13},{5,9},{9,5},{13,1},{2,14},{6,10},... | collective-permute-start | bytes 786440 | tf_op jit(solution)/shard_map/ppermute | solution.py:564
  35.7 0.3 collective-permute-done.5.rest_2_
  36.0 1.6 %project_near.1.near = f32[192,256]{1,0:T(8,128)S(1)} custom-call(bf16[1,192,8192]{2,1,0:T(8,128)(2,1)S(1)} %copy-done, bf16[2048,128]{1,0:T(8,128)(2,1)} %w_key.5, bf16[2048,128]{1,0:T(8,128)(2,1)} %w_value.5, bf16[4,2,128,128]{3,2,1,0:T(8,128)(2,1)S(1)} %collective-permute-done.2._.rest_4_), custom_call_target="tpu_custom_call" | custom-call | flops 10000000000 | bytes 1 | tf_op jit(solution)/shard_map/project_near/pallas_call | solution.py:237
  37.6 0.1 collective-permute-done.6.rest_3_
  37.7 1.6 %project_neighbour.1.neighbour = f32[192,256]{1,0:T(8,128)S(1)} custom-call(bf16[2048,128]{1,0:T(8,128)(2,1)} %w_key.5, bf16[2048,128]{1,0:T(8,128)(2,1)} %w_value.5, bf16[2,48,2048]{2,1,0:T(8,128)(2,1)S(1)} %gate.3.rest_0_, bf16[2,48,2048]{2,1,0:T(8,128)(2,1)S(1)} %collective-permute-done.4.rest_1_, ...), custom_call_target="tpu_custom_call" | custom-call | flops 1 | bytes 1 | tf_op jit(solution)/shard_map/project_neighbour/pallas_call | solution.py:247
  39.4 0.0 copy-start.1
  39.4 4.7 %collective-permute-done.1.w_swapped = bf16[2048,128]{1,0:T(8,128)(2,1)S(1)} collective-permute-done((bf16[2048,128]{1,0:T(8,128)(2,1)S(1)}, bf16[2048,128]{1,0:T(8,128)(2,1)S(1)}, u32[]{:S(2)}, u32[]{:S(2)}) %collective-permute-start.1) | collective-permute-done | bytes 524320 | tf_op jit(solution)/shard_map/ppermute | solution.py:564
  44.1 1.9 %project_far.1 = (f32[192,256]{1,0:T(8,128)S(1)}, bf16[192,256]{1,0:T(8,128)(2,1)S(1)}) custom-call(bf16[1,192,8192]{2,1,0:T(8,128)(2,1)S(1)} %copy-done, bf16[2048,128]{1,0:T(8,128)(2,1)S(1)} %get-tuple-element.23.w_far, bf16[2048,128]{1,0:T(8,128)(2,1)S(1)} %collective-permute-done.1.w_swapped, f32[192,256]{1,0:T(8,128)S(1)} %project_near.1.near, ...), custom_call_target="tpu_custom_call" | custom-call | flops 1 | bytes 1 | tf_op jit(solution)/shard_map/project_far/pallas_call | solution.py:261
  46.0 0.1 collective-permute-start.7
  46.1 1.2 %plan.1 = (bf16[2048,128]{1,0:T(8,128)(2,1)S(1)}, bf16[16,2048]{1,0:T(8,128)(2,1)S(1)}, f32[1,2048]{1,0:T(1,128)S(1)}, s32[192,1]{1,0:T(8,128)S(1)}, s32[1,192]{1,0:T(1,128)S(1)}, /*index=5*/s32[1,192]{1,0:T(1,128)S(1)}) custom-call(s32[4,16]{1,0:T(4,128)S(1)} %copy-done.1, s32[32]{0:T(128)S(1)} %copy-done.3, s32[12,1,16]{2,1,0:T(1,128)S(1)} %bitcast.2), custom_call_target="tpu_custom_call" | custom-call | tf_op jit(solution)/shard_map/plan/pallas_call | solution.py:351
  47.4 6.7 %collective-permute-done.7.arrived = bf16[192,256]{1,0:T(8,128)(2,1)S(1)} collective-permute-done((bf16[192,256]{1,0:T(8,128)(2,1)S(1)}, bf16[192,256]{1,0:T(8,128)(2,1)S(1)}, u32[]{:S(2)}, u32[]{:S(2)}) %collective-permute-start.7) | collective-permute-done | bytes 98336 | tf_op jit(solution)/shard_map/ppermute | solution.py:564
  54.1 0.8 %finish.1 = (bf16[192,256]{1,0:T(8,128)(2,1)S(1)}, bf16[192,256]{1,0:T(8,128)(2,1)}) custom-call(f32[192,256]{1,0:T(8,128)S(1)} %get-tuple-element.26.own, bf16[192,256]{1,0:T(8,128)(2,1)S(1)} %collective-permute-done.7.arrived, s32[1,192]{1,0:T(1,128)S(1)} %get-tuple-element.28.slot_row), custom_call_target="tpu_custom_call" | custom-call | tf_op jit(solution)/shard_map/finish/pallas_call | solution.py:372
  54.9 3.3 %all-to-all-start = ((bf16[4,48,256]{2,1,0:T(8,128)(2,1)}), bf16[4,48,256]{2,1,0:T(8,128)(2,1)S(1)}, u32[]{:S(2)}, u32[]{:S(2)}) async-start(bf16[4,48,256]{2,1,0:T(8,128)(2,1)} %bitcast.1), calls=%async_computation | async-start | bytes 196608 | tf_op jit(solution)/shard_map/all_to_all | solution.py:608
  58.2 7.8 %attend.1 = bf16[1,192,1024]{2,1,0:T(8,128)(2,1)} custom-call(s32[4,16]{1,0:T(4,128)S(1)} %copy-done.1, bf16[1,192,1024]{2,1,0:T(8,128)(2,1)} %queries.1, bf16[192,256]{1,0:T(8,128)(2,1)S(1)} %get-tuple-element.29.fresh, bf16[2048,128]{1,0:T(8,128)(2,1)S(1)} %get-tuple-element.30.held, bf16[16,2048]{1,0:T(8,128)(2,1)S(1)} %get-tuple-element.31.spare, ...), custom_call_target="tpu_custom_call" | custom-call | tf_op jit(solution)/shard_map/attend/pallas_call | solution.py:514
  66.0 0.7 %broadcast_in_dim_reshape.3 = bf16[1,4,4,12,2,128]{5,4,3,2,1,0:T(2,128)(2,1)} reshape(bf16[4,48,256]{2,1,0:T(8,128)(2,1)S(1)} %all-to-all-done) | data formatting | bytes 196608 | tf_op jit(solution)/shard_map/broadcast_in_dim;reshape | solution.py:610
  (17 shorter events, 0.0 us)
Async XLA Ops:
  2.7 21.6 %collective-permute-start.3 = (bf16[2,48,2048]{2,1,0:T(8,128)(2,1)}, bf16[2,48,2048]{2,1,0:T(8,128)(2,1)S(1)}, u32[]{:S(2)}, u32[]{:S(2)}) collective-permute-start(bf16[2,48,2048]{2,1,0:T(8,128)(2,1)} %get-tuple-element.25), channel_id=1, source_target_pairs={{0,4},{4,0},{8,12},{12,8},{1,5},{5,1},{9,13},{13,9},{2,6},{6,2},{1... | collective-permute-start | bytes 1179656 | tf_op jit(solution)/shard_map/ppermute | solution.py:564
  5.8 25.9 %collective-permute-start = (bf16[2048,128]{1,0:T(8,128)(2,1)}, bf16[2048,128]{1,0:T(8,128)(2,1)S(1)}, u32[]{:S(2)}, u32[]{:S(2)}) collective-permute-start(bf16[2048,128]{1,0:T(8,128)(2,1)} %get-tuple-element.22), channel_id=1, source_target_pairs={{0,8},{4,12},{8,0},{12,4},{1,9},{5,13},{9,1},{13,5},{2,10},{6,14},... | collective-permute-start | bytes 1572872 | tf_op jit(solution)/shard_map/ppermute | solution.py:564
  11.5 21.7 %collective-permute-start.2 = (bf16[4,2,128,128]{3,2,1,0:T(8,128)(2,1)}, bf16[4,2,128,128]{3,2,1,0:T(8,128)(2,1)S(1)}, u32[]{:S(2)}, u32[]{:S(2)}) collective-permute-start(bf16[4,2,128,128]{3,2,1,0:T(8,128)(2,1)} %get-tuple-element.24.refs_1_), channel_id=1, source_target_pairs={{0,4},{4,0},{8,12},{12,8},{1,5},{5,1},{9,13},{13,9},{2,6},{6,2},{1... | collective-permute-start | bytes 786440 | tf_op jit(solution)/shard_map/ppermute | solution.py:564
  24.2 13.4 %collective-permute-start.4 = (bf16[2,48,2048]{2,1,0:T(8,128)(2,1)S(1)}, bf16[2,48,2048]{2,1,0:T(8,128)(2,1)S(1)}, u32[]{:S(2)}, u32[]{:S(2)}) collective-permute-start(bf16[2,48,2048]{2,1,0:T(8,128)(2,1)S(1)} %gate.3.rest_0_), channel_id=1, source_target_pairs={{0,1},{1,0},{2,3},{3,2},{4,5},{5,4},{6,7},{7,6},{8,9},{9,8},{10,11... | collective-permute-start | bytes 1179656 | tf_op jit(solution)/shard_map/ppermute | solution.py:564
  24.2 11.8 %collective-permute-start.5 = (bf16[2,48,2048]{2,1,0:T(8,128)(2,1)S(1)}, bf16[2,48,2048]{2,1,0:T(8,128)(2,1)S(1)}, u32[]{:S(2)}, u32[]{:S(2)}) collective-permute-start(bf16[2,48,2048]{2,1,0:T(8,128)(2,1)S(1)} %gate.3.rest_0_), channel_id=1, source_target_pairs={{0,2},{1,3},{2,0},{3,1},{4,6},{5,7},{6,4},{7,5},{8,10},{9,11},{10,... | collective-permute-start | bytes 1179656 | tf_op jit(solution)/shard_map/ppermute | solution.py:564
  31.7 4.4 %copy-start = (bf16[1,192,8192]{2,1,0:T(8,128)(2,1)S(1)}, bf16[1,192,8192]{2,1,0:T(8,128)(2,1)}, u32[]{:S(2)}) copy-start(bf16[1,192,8192]{2,1,0:T(8,128)(2,1)} %hidden.5) | copy-start | bytes 9437188
  31.7 12.4 %collective-permute-start.1 = (bf16[2048,128]{1,0:T(8,128)(2,1)S(1)}, bf16[2048,128]{1,0:T(8,128)(2,1)S(1)}, u32[]{:S(2)}, u32[]{:S(2)}) collective-permute-start(bf16[2048,128]{1,0:T(8,128)(2,1)S(1)} %get-tuple-element.23.w_far), channel_id=1, source_target_pairs={{0,16},{16,0},{1,17},{17,1},{2,18},{18,2},{3,19},{19,3},{4,20},{20... | collective-permute-start | bytes 1572872 | tf_op jit(solution)/shard_map/ppermute | solution.py:564
  33.2 25.0 %collective-permute-start.8 = (bf16[4,2,128,128]{3,2,1,0:T(8,128)(2,1)}, bf16[4,2,128,128]{3,2,1,0:T(8,128)(2,1)S(1)}, u32[]{:S(2)}, u32[]{:S(2)}) collective-permute-start(bf16[4,2,128,128]{3,2,1,0:T(8,128)(2,1)} %get-tuple-element.35), channel_id=1, source_target_pairs={{0,8},{4,12},{8,0},{12,4},{1,9},{5,13},{9,1},{13,5},{2,10},{6,14},... | collective-permute-start | bytes 786440 | tf_op jit(solution)/shard_map/ppermute | solution.py:564
  33.2 25.0 %collective-permute-start.9 = (bf16[4,2,128,128]{3,2,1,0:T(8,128)(2,1)}, bf16[4,2,128,128]{3,2,1,0:T(8,128)(2,1)S(1)}, u32[]{:S(2)}, u32[]{:S(2)}) collective-permute-start(bf16[4,2,128,128]{3,2,1,0:T(8,128)(2,1)} %get-tuple-element.36), channel_id=1, source_target_pairs={{0,12},{4,8},{8,4},{12,0},{1,13},{5,9},{9,5},{13,1},{2,14},{6,10},... | collective-permute-start | bytes 786440 | tf_op jit(solution)/shard_map/ppermute | solution.py:564
  36.0 1.7 %collective-permute-start.6 = (bf16[2,48,2048]{2,1,0:T(8,128)(2,1)S(1)}, bf16[2,48,2048]{2,1,0:T(8,128)(2,1)S(1)}, u32[]{:S(2)}, u32[]{:S(2)}) collective-permute-start(bf16[2,48,2048]{2,1,0:T(8,128)(2,1)S(1)} %collective-permute-done.5.rest_2_), channel_id=1, source_target_pairs={{0,1},{1,0},{2,3},{3,2},{4,5},{5,4},{6,7},{7,6},{8,9},{9,8},{10,11... | collective-permute-start | bytes 1179656 | tf_op jit(solution)/shard_map/ppermute | solution.py:564
  39.4 6.7 %copy-start.1 = (s32[4,16]{1,0:T(4,128)S(1)}, s32[4,16]{1,0:T(4,128)}, u32[]{:S(2)}) copy-start(s32[4,16]{1,0:T(4,128)} %request_docs.5) | copy-start | bytes 772
  39.4 6.7 %copy-start.2 = (s32[1,16,12]{1,0,2:T(1,128)S(1)}, s32[1,16,12]{1,0,2:T(1,128)}, u32[]{:S(2)}) copy-start(s32[1,16,12]{1,0,2:T(1,128)} %param.17) | copy-start | bytes 2308
  39.4 6.7 %copy-start.3 = (s32[32]{0:T(128)S(1)}, s32[32]{0:T(128)}, u32[]{:S(2)}) copy-start(s32[32]{0:T(128)} %doc_lengths.1) | copy-start | bytes 388
  46.0 8.0 %collective-permute-start.7 = (bf16[192,256]{1,0:T(8,128)(2,1)S(1)}, bf16[192,256]{1,0:T(8,128)(2,1)S(1)}, u32[]{:S(2)}, u32[]{:S(2)}) collective-permute-start(bf16[192,256]{1,0:T(8,128)(2,1)S(1)} %get-tuple-element.27), channel_id=1, source_target_pairs={{0,4},{4,0},{8,12},{12,8},{1,5},{5,1},{9,13},{13,9},{2,6},{6,2},{1... | collective-permute-start | bytes 294920 | tf_op jit(solution)/shard_map/ppermute | solution.py:564
  54.9 11.1 %all-to-all-start = ((bf16[4,48,256]{2,1,0:T(8,128)(2,1)}), bf16[4,48,256]{2,1,0:T(8,128)(2,1)S(1)}, u32[]{:S(2)}, u32[]{:S(2)}) async-start(bf16[4,48,256]{2,1,0:T(8,128)(2,1)} %bitcast.1), calls=%async_computation | async-start | bytes 196608 | tf_op jit(solution)/shard_map/all_to_all | solution.py:608

commit v12 on v11

--- a/solution.py
+++ b/solution.py
@@ -19,16 +19,13 @@
     return pltpu.with_memory_space_constraint(array, pltpu.HBM)
 
 
-def send_kernel(hidden, w_key, w_value, w_out, h_out, w_held, h_held, w_sems, h_sems):
+def pick_weights_kernel(w_key, w_value, w_out, held, sems):
     group = lax.axis_index("groups")
-    me = lax.axis_index("seq")
-    quarter = lax.axis_index("tp")
-    pieces, piece = w_held.shape[:2]
-    rows, depth = h_out.shape[1:]
+    pieces, piece = held.shape[:2]
 
     def fetch(i, weight):
         source = weight.at[pl.ds(i * piece, piece)]
-        return pltpu.make_async_copy(source, w_held.at[i], w_sems.at[0, i])
+        return pltpu.make_async_copy(source, held.at[i], sems.at[0, i])
 
     for chosen, weight in ((0, w_key), (1, w_value)):
 
@@ -37,57 +34,70 @@
             for i in range(pieces):
                 fetch(i, weight).start()
 
+    stores = []
+    for i in range(pieces):
+        fetch(i, w_key).wait()
+        target = w_out.at[pl.ds(i * piece, piece)]
+        stores.append(pltpu.make_async_copy(held.at[i], target, sems.at[1, i]))
+        stores[-1].start()
+    for store in stores:
+        store.wait()
+
+
+def pick_weights(w_key, w_value):
+    depth, width = w_key.shape
+    pieces = 4
+    return pl.pallas_call(
+        pick_weights_kernel,
+        out_shape=jax.ShapeDtypeStruct(w_key.shape, jnp.bfloat16),
+        in_specs=[ANY] * 2,
+        out_specs=ANY,
+        scratch_shapes=[
+            pltpu.VMEM((pieces, depth // pieces, width), jnp.bfloat16),
+            pltpu.SemaphoreType.DMA((2, pieces)),
+        ],
+        name="pick_weights",
+    )(w_key, w_value)
+
+
+def pick_hidden_kernel(hidden, _, out, held, sems):
+    me = lax.axis_index("seq")
+    rows, depth = out.shape[1:]
     first = me + 1 - 2 * lax.rem(me, 2)
-    stores = []
-    h_fetches = []
+    fetches, stores = [], []
     for i, block in enumerate((first, lax.rem(first + 2, 4))):
         source = hidden.at[
             0,
-            pl.ds(pl.multiple_of(quarter * rows, rows), rows),
+            pl.ds(pl.multiple_of(lax.axis_index("tp") * rows, rows), rows),
             pl.ds(pl.multiple_of(block * depth, depth), depth),
         ]
-        h_fetches.append(pltpu.make_async_copy(source, h_held.at[i], h_sems.at[0, i]))
-        h_fetches[-1].start()
-    for i in range(pieces):
-        fetch(i, w_key).wait()
-        target = w_out.at[pl.ds(i * piece, piece)]
-        stores.append(pltpu.make_async_copy(w_held.at[i], target, w_sems.at[1, i]))
-        stores[-1].start()
-    for i, one in enumerate(h_fetches):
-        one.wait()
-        stores.append(pltpu.make_async_copy(h_held.at[i], h_out.at[i], h_sems.at[1, i]))
-        stores[-1].start()
+        fetches.append(pltpu.make_async_copy(source, held.at[i], sems.at[0, i]))
+        fetches[-1].start()
+        stores.append(pltpu.make_async_copy(held.at[i], out.at[i], sems.at[1, i]))
+    for fetch, store in zip(fetches, stores):
+        fetch.wait()
+        store.start()
     for store in stores:
         store.wait()
 
 
-def pick_sent(hidden, w_key, w_value):
-    depth, width = w_key.shape
-    pieces = 4
-    h_shape = (2, hidden.shape[1] // 4, depth)
-    return pl.pallas_call(
-        send_kernel,
-        out_shape=(
-            jax.ShapeDtypeStruct(w_key.shape, jnp.bfloat16),
-            jax.ShapeDtypeStruct(h_shape, jnp.bfloat16),
-        ),
-        in_specs=[ANY] * 3,
-        out_specs=(ANY, ANY),
-        scratch_shapes=[
-            pltpu.VMEM((pieces, depth // pieces, width), jnp.bfloat16),
-            pltpu.VMEM(h_shape, jnp.bfloat16),
-            pltpu.SemaphoreType.DMA((2, pieces)),
-            pltpu.SemaphoreType.DMA((2, 2)),
-        ],
-        name="pick_sent",
-    )(hidden, w_key, w_value)
+def pick_hidden(hidden, depth, after):
+    shape = (2, hidden.shape[1] // 4, depth)
+    return pl.pallas_call(
+        pick_hidden_kernel,
+        out_shape=jax.ShapeDtypeStruct(shape, jnp.bfloat16),
+        in_specs=[ANY] * 2,
+        out_specs=ANY,
+        scratch_shapes=[pltpu.VMEM(shape, jnp.bfloat16), pltpu.SemaphoreType.DMA((2, 2))],
+        name="pick_hidden",
+    )(hidden, after)
 
 
 def gate_kernel(*refs):
     pass
 
 
-def gate(arrays, first=(), pinned=0):
+def gate(arrays, first=(), pinned=0, cost=1):
     return pl.pallas_call(
         gate_kernel,
         out_shape=tuple(jax.ShapeDtypeStruct(one.shape, one.dtype) for one in arrays),
@@ -95,7 +105,7 @@
         out_specs=(ANY,) * len(arrays),
         input_output_aliases={i: i for i in range(len(arrays))},
         compiler_params=pltpu.CompilerParams(vmem_limit_bytes=1024 * 1024),
-        cost_estimate=pl.CostEstimate(flops=8000000000, bytes_accessed=1, transcendentals=0),
+        cost_estimate=pl.CostEstimate(flops=cost, bytes_accessed=1, transcendentals=0),
         name="gate",
     )(*(in_hbm(one) for one in arrays[:pinned]), *arrays[pinned:], *first)
 
@@ -204,7 +214,7 @@
 
 
 def far_kernel(hidden, w_far, w_swapped, near, neighbour, *rest):
-    *quarters, own, part, w, h, n, sems = rest
+    *quarters, own, part_k, part_v, w, h, n, sems = rest
     group = lax.axis_index("groups")
     depth, width = w_far.shape
     copies = []
@@ -222,7 +232,8 @@
         one.wait()
     own[...] = near[...] + jnp.dot(h[...], w[...], preferred_element_type=jnp.float32)
     total = neighbour[...] + jnp.dot(n[...], w[...], preferred_element_type=jnp.float32)
-    part[...] = total.astype(part.dtype)
+    part_k[...] = total[:, :width].astype(part_k.dtype)
+    part_v[...] = total[:, width:].astype(part_v.dtype)
 
 
 def project(hidden, w_key, w_value, w_far, w_swapped, quarters, first):
@@ -260,9 +271,9 @@
     )(w_key, w_value, *quarters)
     return pl.pallas_call(
         far_kernel,
-        out_shape=(sums, jax.ShapeDtypeStruct((rows, 2 * width), jnp.bfloat16)),
+        out_shape=(sums,) + (jax.ShapeDtypeStruct((rows, width), jnp.bfloat16),) * 2,
         in_specs=[ANY] * 3 + [VMEM] * 2 + [ANY] * len(quarters),
-        out_specs=(VMEM, VMEM),
+        out_specs=(VMEM,) * 3,
         scratch_shapes=[
             w_scratch,
             h_scratch,
@@ -359,8 +370,9 @@
     )(request_docs, doc_lengths, jnp.transpose(recompute_rows, (2, 0, 1)))
 
 
-def finish_kernel(own, arrived, slot_row, fresh, outgoing):
-    total = (own[...] + arrived[...].astype(jnp.float32)).astype(jnp.bfloat16)
+def finish_kernel(own, arrived_k, arrived_v, slot_row, fresh, outgoing):
+    arrived = jnp.concatenate([arrived_k[...], arrived_v[...]], axis=1)
+    total = (own[...] + arrived.astype(jnp.float32)).astype(jnp.bfloat16)
     fresh[...] = total
     slots = lax.broadcasted_iota(jnp.int32, (outgoing.shape[0], 1), 0)
     pick = (slots == slot_row[...]).astype(jnp.bfloat16)
@@ -372,11 +384,11 @@
     return pl.pallas_call(
         finish_kernel,
         out_shape=tuple(jax.ShapeDtypeStruct(one, jnp.bfloat16) for one in shapes),
-        in_specs=[VMEM] * 3,
+        in_specs=[VMEM] * 4,
         out_specs=(VMEM, VMEM),
         compiler_params=pltpu.CompilerParams(vmem_limit_bytes=16 * 1024 * 1024),
         name="finish",
-    )(own, arrived, slot_row)
+    )(own, *arrived, slot_row)
 
 
 def attend_kernel(
@@ -522,7 +534,7 @@
             pltpu.VMEM((context, 2 * head_dim), jnp.bfloat16),
             pltpu.VMEM((context, 2 * head_dim), jnp.bfloat16),
             pltpu.SMEM((request_docs.shape[0],), jnp.int32),
-            pltpu.SemaphoreType.DMA((2, request_docs.shape[1] // 2)),
+            pltpu.SemaphoreType.DMA((2, 4)),
             pltpu.SemaphoreType.DMA,
         ],
         compiler_params=pltpu.CompilerParams(vmem_limit_bytes=32 * 1024 * 1024),
@@ -563,20 +575,20 @@
             count = lax.axis_size(axis)
             return lax.ppermute(array, axis, [(i, i ^ apart) for i in range(count)])
 
-        w_send, h_send = pick_sent(hidden, w_key, w_value)
+        w_send = pick_weights(w_key, w_value)
         w_far = swap(w_send, "seq", 2)
-        h_mine = swap(h_send, "seq", 1)
+        h_mine = swap(pick_hidden(hidden, w_key.shape[0], w_send), "seq", 1)
         doc_1, doc_2, doc_3 = pick_docs(request_docs, store_keys, store_values, False)
-        (h_mine,) = gate((h_mine,), (in_hbm(doc_1),))
+        (h_mine,) = gate((h_mine,), (in_hbm(doc_1),), cost=1)
         h_chip = swap(h_mine, "tp", 2)
         h_core = swap(h_mine, "tp", 1)
-        doc_2, doc_3, w_far = gate((doc_2, doc_3, w_far), pinned=2)
+        doc_2, doc_3, w_far = gate((doc_2, doc_3, w_far), pinned=2, cost=8000000000)
         w_swapped = swap(w_far, "groups", 1)
         doc_1 = swap(doc_1, "seq", 1)
         docs = (swap(doc_2, "seq", 2), swap(doc_3, "seq", 3), doc_1)
         quarters = (h_mine, h_core, h_chip, swap(h_chip, "tp", 1))
-        own, part = project(hidden, w_key, w_value, w_far, w_swapped, quarters, doc_1)
-        arrived = swap(part, "seq", 1)
+        own, *parts = project(hidden, w_key, w_value, w_far, w_swapped, quarters, doc_1)
+        arrived = [swap(one, "seq", 1) for one in parts]
         sources = (store_keys, store_values, *docs)
     else:
         (docs,) = pick_docs(request_docs, store_keys, store_values, True)
@@ -585,7 +597,7 @@
             jnp.concatenate([w_key, w_value], axis=1), "seq", axis=0, tiled=True
         )
         own = jnp.dot(hidden[0], weights, preferred_element_type=jnp.float32)
-        arrived = jnp.zeros(own.shape, jnp.bfloat16)
+        arrived = [jnp.zeros((own.shape[0], head_dim), jnp.bfloat16)] * 2
 
     held, spare, key_bias, row_place, key_place, slot_row = plan(
         request_docs, doc_lengths, recompute_rows, slot_count, head_dim, doc_len

time: 67.2 us -> 67.8 us (level)
  waiting for transfers between devices: 29.4 us -> 27.6 us
  starting transfers between devices: 15.6 us -> 17.2 us
  Pallas kernels: 20.2 us -> 21.1 us
    ppermute x10 -> x11, waiting for transfers between devices: 29.4 us -> 27.6 us  [swap(): return lax.ppermute(array, axis, [(i, i ^ apart) for i in range(count)])]
    pallas_call x2 -> x3, Pallas kernels: 3.99 us -> 5.49 us  [the longest x1 1.94 us: project(): pl.pallas_call(far_kernel, out_shape=(sums,) + (jax.ShapeDtypeStruct((row...]
    ppermute x10 -> x11, starting transfers between devices: 12.3 us -> 13.8 us  [swap(): return lax.ppermute(array, axis, [(i, i ^ apart) for i in range(count)])]
  transfers between devices with their start and end apart: 11 -> 12, of which waited for: 6 -> 7; matrix products, arithmetic and copies ran while one was open for 0% -> 0% of each run, Pallas kernels for 27% -> 29%
where the time goes in v12:
time: 67.8 us; the launch traced here: 67.4 us
  waiting for transfers between devices  27.6 us (41%)
  Pallas kernels  21.1 us (31%)
  starting transfers between devices  17.2 us (25%)
  between operations  0.76 us (1%)
  local copies, waits for them, and re-layouts  0.69 us (1%)
    ppermute x11, waiting for transfers between devices, swap(): return lax.ppermute(array, axis, [(i, i ^ apart) for i in range(count)])  27.6 us
    ppermute x11, starting transfers between devices, swap(): return lax.ppermute(array, axis, [(i, i ^ apart) for i in range(count)])  13.8 us
    pallas_call x1, Pallas kernels, attend(): pl.pallas_call(functools.partial(attend_kernel, by_owner), out_shape=jax....  7.14 us
    all_to_all x1, starting transfers between devices, shards(): lax.all_to_all(outgoing, 'seq', split_axis=0, concat_axis=0, tiled=True)  3.39 us
    pallas_call x1, Pallas kernels, pick_docs(): pl.pallas_call(functools.partial(docs_kernel, by_owner), out_shape=tuple(...  3.19 us
    pallas_call x1, Pallas kernels, project(): pl.pallas_call(far_kernel, out_shape=(sums,) + (jax.ShapeDtypeStruct((row...  1.94 us
    pallas_call x1, Pallas kernels, pick_weights(): pl.pallas_call(pick_weights_kernel, out_shape=jax.ShapeDtypeStruct(w_key....  1.82 us
    pallas_call x1, Pallas kernels, pick_hidden(): pl.pallas_call(pick_hidden_kernel, out_shape=jax.ShapeDtypeStruct(shape,...  1.73 us
  transfers between devices with their start and end apart: 12, of which 7 were waited for; matrix products, arithmetic and copies ran while one was open for 0% of the time, Pallas kernels for 29%

profile of v12, /device:TPU:0, one launch (start us, length us, event | category | flops | bytes accessed | tf_op | source)
XLA Modules:
  0.0 67.4 jit_solution(2013800474839677561)
XLA Ops:
  0.6 1.8 %pick_weights.1._ = bf16[2048,128]{1,0:T(8,128)(2,1)} custom-call(bf16[2048,128]{1,0:T(8,128)(2,1)} %w_key.5, bf16[2048,128]{1,0:T(8,128)(2,1)} %w_value.5), custom_call_target="tpu_custom_call" | custom-call | tf_op jit(solution)/shard_map/pick_weights/pallas_call | solution.py:50
  2.5 4.1 %collective-permute-start = (bf16[2048,128]{1,0:T(8,128)(2,1)}, bf16[2048,128]{1,0:T(8,128)(2,1)S(1)}, u32[]{:S(2)}, u32[]{:S(2)}) collective-permute-start(bf16[2048,128]{1,0:T(8,128)(2,1)} %pick_weights.1._), channel_id=1, source_target_pairs={{0,8},{4,12},{8,0},{12,4},{1,9},{5,13},{9,1},{13,5},{2,10},{6,14},... | collective-permute-start | bytes 1572872 | tf_op jit(solution)/shard_map/ppermute | solution.py:576
  6.6 1.7 %pick_hidden.1 = bf16[2,48,2048]{2,1,0:T(8,128)(2,1)} custom-call(bf16[1,192,8192]{2,1,0:T(8,128)(2,1)} %hidden.5, bf16[2048,128]{1,0:T(8,128)(2,1)} %pick_weights.1._), custom_call_target="tpu_custom_call" | custom-call | tf_op jit(solution)/shard_map/pick_hidden/pallas_call | solution.py:86
  8.3 1.6 %collective-permute-start.3 = (bf16[2,48,2048]{2,1,0:T(8,128)(2,1)}, bf16[2,48,2048]{2,1,0:T(8,128)(2,1)S(1)}, u32[]{:S(2)}, u32[]{:S(2)}) collective-permute-start(bf16[2,48,2048]{2,1,0:T(8,128)(2,1)} %pick_hidden.1), channel_id=1, source_target_pairs={{0,4},{4,0},{8,12},{12,8},{1,5},{5,1},{9,13},{13,9},{2,6},{6,2},{1... | collective-permute-start | bytes 1179656 | tf_op jit(solution)/shard_map/ppermute | solution.py:576
  9.9 3.2 %pick_docs.1 = (bf16[4,2,128,128]{3,2,1,0:T(8,128)(2,1)}, bf16[4,2,128,128]{3,2,1,0:T(8,128)(2,1)}, bf16[4,2,128,128]{3,2,1,0:T(8,128)(2,1)}) custom-call(s32[4,16]{1,0:T(4,128)} %request_docs.5, bf16[8,128,128]{2,1,0:T(8,128)(2,1)} %rest_0_.1, bf16[8,128,128]{2,1,0:T(8,128)(2,1)} %rest_1_.1), custom_call_target="tpu_custom_call" | custom-call | tf_op jit(solution)/shard_map/pick_docs/pallas_call | solution.py:164
  13.1 0.5 collective-permute-start.2
  13.6 17.1 %collective-permute-done.3.refs_0_ = bf16[2,48,2048]{2,1,0:T(8,128)(2,1)S(1)} collective-permute-done((bf16[2,48,2048]{2,1,0:T(8,128)(2,1)}, bf16[2,48,2048]{2,1,0:T(8,128)(2,1)S(1)}, u32[]{:S(2)}, u32[]{:S(2)}) %collective-permute-start.3) | collective-permute-done | bytes 393248 | tf_op jit(solution)/shard_map/ppermute | solution.py:576
  30.7 1.5 %collective-permute-start.5 = (bf16[2,48,2048]{2,1,0:T(8,128)(2,1)S(1)}, bf16[2,48,2048]{2,1,0:T(8,128)(2,1)S(1)}, u32[]{:S(2)}, u32[]{:S(2)}) collective-permute-start(bf16[2,48,2048]{2,1,0:T(8,128)(2,1)S(1)} %gate.3.rest_0_), channel_id=1, source_target_pairs={{0,2},{1,3},{2,0},{3,1},{4,6},{5,7},{6,4},{7,5},{8,10},{9,11},{10,... | collective-permute-start | bytes 1179656 | tf_op jit(solution)/shard_map/ppermute | solution.py:576
  32.2 1.5 %collective-permute-start.1 = (bf16[2048,128]{1,0:T(8,128)(2,1)S(1)}, bf16[2048,128]{1,0:T(8,128)(2,1)S(1)}, u32[]{:S(2)}, u32[]{:S(2)}) collective-permute-start(bf16[2048,128]{1,0:T(8,128)(2,1)S(1)} %get-tuple-element.21.w_far), channel_id=1, source_target_pairs={{0,16},{16,0},{1,17},{17,1},{2,18},{18,2},{3,19},{19,3},{4,20},{20... | collective-permute-start | bytes 1572872 | tf_op jit(solution)/shard_map/ppermute | solution.py:576
  33.8 1.1 %collective-permute-done.2._.rest_4_ = bf16[4,2,128,128]{3,2,1,0:T(8,128)(2,1)S(1)} collective-permute-done((bf16[4,2,128,128]{3,2,1,0:T(8,128)(2,1)}, bf16[4,2,128,128]{3,2,1,0:T(8,128)(2,1)S(1)}, u32[]{:S(2)}, u32[]{:S(2)}) %collective-permute-start.2) | collective-permute-done | bytes 262176 | tf_op jit(solution)/shard_map/ppermute | solution.py:576
  34.8 2.4 %collective-permute-start.10 = (bf16[4,2,128,128]{3,2,1,0:T(8,128)(2,1)}, bf16[4,2,128,128]{3,2,1,0:T(8,128)(2,1)S(1)}, u32[]{:S(2)}, u32[]{:S(2)}) collective-permute-start(bf16[4,2,128,128]{3,2,1,0:T(8,128)(2,1)} %get-tuple-element.34), channel_id=1, source_target_pairs={{0,12},{4,8},{8,4},{12,0},{1,13},{5,9},{9,5},{13,1},{2,14},{6,10},... | collective-permute-start | bytes 786440 | tf_op jit(solution)/shard_map/ppermute | solution.py:576
  37.3 5.0 %collective-permute-done.5.rest_2_ = bf16[2,48,2048]{2,1,0:T(8,128)(2,1)S(1)} collective-permute-done((bf16[2,48,2048]{2,1,0:T(8,128)(2,1)S(1)}, bf16[2,48,2048]{2,1,0:T(8,128)(2,1)S(1)}, u32[]{:S(2)}, u32[]{:S(2)}) %collective-permute-start.5) | collective-permute-done | bytes 393248 | tf_op jit(solution)/shard_map/ppermute | solution.py:576
  42.2 1.6 %project_near.1.near = f32[192,256]{1,0:T(8,128)S(1)} custom-call(bf16[1,192,8192]{2,1,0:T(8,128)(2,1)S(1)} %copy-done, bf16[2048,128]{1,0:T(8,128)(2,1)} %w_key.5, bf16[2048,128]{1,0:T(8,128)(2,1)} %w_value.5, bf16[4,2,128,128]{3,2,1,0:T(8,128)(2,1)S(1)} %collective-permute-done.2._.rest_4_), custom_call_target="tpu_custom_call" | custom-call | flops 10000000000 | bytes 1 | tf_op jit(solution)/shard_map/project_near/pallas_call | solution.py:248
  43.9 1.6 %project_neighbour.1.neighbour = f32[192,256]{1,0:T(8,128)S(1)} custom-call(bf16[2048,128]{1,0:T(8,128)(2,1)} %w_key.5, bf16[2048,128]{1,0:T(8,128)(2,1)} %w_value.5, bf16[2,48,2048]{2,1,0:T(8,128)(2,1)S(1)} %gate.3.rest_0_, bf16[2,48,2048]{2,1,0:T(8,128)(2,1)S(1)} %collective-permute-done.4.rest_1_, ...), custom_call_target="tpu_custom_call" | custom-call | flops 1 | bytes 1 | tf_op jit(solution)/shard_map/project_neighbour/pallas_call | solution.py:258
  45.6 0.7 collective-permute-done.1.w_swapped
  46.3 1.9 %project_far.1 = (f32[192,256]{1,0:T(8,128)S(1)}, bf16[192,128]{1,0:T(8,128)(2,1)S(1)}, bf16[192,128]{1,0:T(8,128)(2,1)S(1)}) custom-call(bf16[1,192,8192]{2,1,0:T(8,128)(2,1)S(1)} %copy-done, bf16[2048,128]{1,0:T(8,128)(2,1)S(1)} %get-tuple-element.21.w_far, bf16[2048,128]{1,0:T(8,128)(2,1)S(1)} %collective-permute-done.1.w_swapped, ...), custom_call_target="tpu_custom_call" | custom-call | flops 1 | bytes 1 | tf_op jit(solution)/shard_map/project_far/pallas_call | solution.py:272
  48.3 2.0 %collective-permute-start.8 = (bf16[192,128]{1,0:T(8,128)(2,1)S(1)}, bf16[192,128]{1,0:T(8,128)(2,1)S(1)}, u32[]{:S(2)}, u32[]{:S(2)}) collective-permute-start(bf16[192,128]{1,0:T(8,128)(2,1)S(1)} %get-tuple-element.25), channel_id=1, source_target_pairs={{0,4},{4,0},{8,12},{12,8},{1,5},{5,1},{9,13},{13,9},{2,6},{6,2},{1... | collective-permute-start | bytes 147464 | tf_op jit(solution)/shard_map/ppermute | solution.py:576
  50.3 1.2 %plan.1 = (bf16[2048,128]{1,0:T(8,128)(2,1)S(1)}, bf16[16,2048]{1,0:T(8,128)(2,1)S(1)}, f32[1,2048]{1,0:T(1,128)S(1)}, s32[192,1]{1,0:T(8,128)S(1)}, s32[1,192]{1,0:T(1,128)S(1)}, /*index=5*/s32[1,192]{1,0:T(1,128)S(1)}) custom-call(s32[4,16]{1,0:T(4,128)S(1)} %copy-done.1, s32[32]{0:T(128)S(1)} %copy-done.3, s32[12,1,16]{2,1,0:T(1,128)S(1)} %bitcast.2), custom_call_target="tpu_custom_call" | custom-call | tf_op jit(solution)/shard_map/plan/pallas_call | solution.py:362
  51.6 2.8 %collective-permute-done.7.arrived_k = bf16[192,128]{1,0:T(8,128)(2,1)S(1)} collective-permute-done((bf16[192,128]{1,0:T(8,128)(2,1)S(1)}, bf16[192,128]{1,0:T(8,128)(2,1)S(1)}, u32[]{:S(2)}, u32[]{:S(2)}) %collective-permute-start.7) | collective-permute-done | bytes 49184 | tf_op jit(solution)/shard_map/ppermute | solution.py:576
  54.3 1.0 %collective-permute-done.8.arrived_v = bf16[192,128]{1,0:T(8,128)(2,1)S(1)} collective-permute-done((bf16[192,128]{1,0:T(8,128)(2,1)S(1)}, bf16[192,128]{1,0:T(8,128)(2,1)S(1)}, u32[]{:S(2)}, u32[]{:S(2)}) %collective-permute-start.8) | collective-permute-done | bytes 49184 | tf_op jit(solution)/shard_map/ppermute | solution.py:576
  55.3 0.8 %finish.1 = (bf16[192,256]{1,0:T(8,128)(2,1)S(1)}, bf16[192,256]{1,0:T(8,128)(2,1)}) custom-call(f32[192,256]{1,0:T(8,128)S(1)} %get-tuple-element.23.own, bf16[192,128]{1,0:T(8,128)(2,1)S(1)} %collective-permute-done.7.arrived_k, bf16[192,128]{1,0:T(8,128)(2,1)S(1)} %collective-permute-done.8.arrived_v, s32[1,192]{1,0:T(1,128)S(1)} %get-tuple-element.26.slot_row), custom_call_target="tpu_custom_call" | custom-call | tf_op jit(solution)/shard_map/finish/pallas_call | solution.py:384
  56.1 3.4 %all-to-all-start = ((bf16[4,48,256]{2,1,0:T(8,128)(2,1)}), bf16[4,48,256]{2,1,0:T(8,128)(2,1)S(1)}, u32[]{:S(2)}, u32[]{:S(2)}) async-start(bf16[4,48,256]{2,1,0:T(8,128)(2,1)} %bitcast.1), calls=%async_computation | async-start | bytes 196608 | tf_op jit(solution)/shard_map/all_to_all | solution.py:620
  59.5 7.1 %attend.1 = bf16[1,192,1024]{2,1,0:T(8,128)(2,1)} custom-call(s32[4,16]{1,0:T(4,128)S(1)} %copy-done.1, bf16[1,192,1024]{2,1,0:T(8,128)(2,1)} %queries.1, bf16[192,256]{1,0:T(8,128)(2,1)S(1)} %get-tuple-element.27.fresh, bf16[2048,128]{1,0:T(8,128)(2,1)S(1)} %get-tuple-element.28.held, bf16[16,2048]{1,0:T(8,128)(2,1)S(1)} %get-tuple-element.29.spare, ...), custom_call_target="tpu_custom_call" | custom-call | tf_op jit(solution)/shard_map/attend/pallas_call | solution.py:526
  66.7 0.7 broadcast_in_dim_reshape.3
  (20 shorter events, 0.2 us)
Async XLA Ops:
  2.5 29.8 %collective-permute-start = (bf16[2048,128]{1,0:T(8,128)(2,1)}, bf16[2048,128]{1,0:T(8,128)(2,1)S(1)}, u32[]{:S(2)}, u32[]{:S(2)}) collective-permute-start(bf16[2048,128]{1,0:T(8,128)(2,1)} %pick_weights.1._), channel_id=1, source_target_pairs={{0,8},{4,12},{8,0},{12,4},{1,9},{5,13},{9,1},{13,5},{2,10},{6,14},... | collective-permute-start | bytes 1572872 | tf_op jit(solution)/shard_map/ppermute | solution.py:576
  8.3 22.4 %collective-permute-start.3 = (bf16[2,48,2048]{2,1,0:T(8,128)(2,1)}, bf16[2,48,2048]{2,1,0:T(8,128)(2,1)S(1)}, u32[]{:S(2)}, u32[]{:S(2)}) collective-permute-start(bf16[2,48,2048]{2,1,0:T(8,128)(2,1)} %pick_hidden.1), channel_id=1, source_target_pairs={{0,4},{4,0},{8,12},{12,8},{1,5},{5,1},{9,13},{13,9},{2,6},{6,2},{1... | collective-permute-start | bytes 1179656 | tf_op jit(solution)/shard_map/ppermute | solution.py:576
  13.1 21.7 %collective-permute-start.2 = (bf16[4,2,128,128]{3,2,1,0:T(8,128)(2,1)}, bf16[4,2,128,128]{3,2,1,0:T(8,128)(2,1)S(1)}, u32[]{:S(2)}, u32[]{:S(2)}) collective-permute-start(bf16[4,2,128,128]{3,2,1,0:T(8,128)(2,1)} %get-tuple-element.22.refs_1_), channel_id=1, source_target_pairs={{0,4},{4,0},{8,12},{12,8},{1,5},{5,1},{9,13},{13,9},{2,6},{6,2},{1... | collective-permute-start | bytes 786440 | tf_op jit(solution)/shard_map/ppermute | solution.py:576
  30.7 13.2 %collective-permute-start.4 = (bf16[2,48,2048]{2,1,0:T(8,128)(2,1)S(1)}, bf16[2,48,2048]{2,1,0:T(8,128)(2,1)S(1)}, u32[]{:S(2)}, u32[]{:S(2)}) collective-permute-start(bf16[2,48,2048]{2,1,0:T(8,128)(2,1)S(1)} %gate.3.rest_0_), channel_id=1, source_target_pairs={{0,1},{1,0},{2,3},{3,2},{4,5},{5,4},{6,7},{7,6},{8,9},{9,8},{10,11... | collective-permute-start | bytes 1179656 | tf_op jit(solution)/shard_map/ppermute | solution.py:576
  30.7 11.5 %collective-permute-start.5 = (bf16[2,48,2048]{2,1,0:T(8,128)(2,1)S(1)}, bf16[2,48,2048]{2,1,0:T(8,128)(2,1)S(1)}, u32[]{:S(2)}, u32[]{:S(2)}) collective-permute-start(bf16[2,48,2048]{2,1,0:T(8,128)(2,1)S(1)} %gate.3.rest_0_), channel_id=1, source_target_pairs={{0,2},{1,3},{2,0},{3,1},{4,6},{5,7},{6,4},{7,5},{8,10},{9,11},{10,... | collective-permute-start | bytes 1179656 | tf_op jit(solution)/shard_map/ppermute | solution.py:576
  32.2 10.0 %copy-start = (bf16[1,192,8192]{2,1,0:T(8,128)(2,1)S(1)}, bf16[1,192,8192]{2,1,0:T(8,128)(2,1)}, u32[]{:S(2)}) copy-start(bf16[1,192,8192]{2,1,0:T(8,128)(2,1)} %hidden.5) | copy-start | bytes 9437188
  32.2 14.1 %collective-permute-start.1 = (bf16[2048,128]{1,0:T(8,128)(2,1)S(1)}, bf16[2048,128]{1,0:T(8,128)(2,1)S(1)}, u32[]{:S(2)}, u32[]{:S(2)}) collective-permute-start(bf16[2048,128]{1,0:T(8,128)(2,1)S(1)} %get-tuple-element.21.w_far), channel_id=1, source_target_pairs={{0,16},{16,0},{1,17},{17,1},{2,18},{18,2},{3,19},{19,3},{4,20},{20... | collective-permute-start | bytes 1572872 | tf_op jit(solution)/shard_map/ppermute | solution.py:576
  33.8 25.8 %collective-permute-start.9 = (bf16[4,2,128,128]{3,2,1,0:T(8,128)(2,1)}, bf16[4,2,128,128]{3,2,1,0:T(8,128)(2,1)S(1)}, u32[]{:S(2)}, u32[]{:S(2)}) collective-permute-start(bf16[4,2,128,128]{3,2,1,0:T(8,128)(2,1)} %get-tuple-element.33), channel_id=1, source_target_pairs={{0,8},{4,12},{8,0},{12,4},{1,9},{5,13},{9,1},{13,5},{2,10},{6,14},... | collective-permute-start | bytes 786440 | tf_op jit(solution)/shard_map/ppermute | solution.py:576
  34.8 24.7 %collective-permute-start.10 = (bf16[4,2,128,128]{3,2,1,0:T(8,128)(2,1)}, bf16[4,2,128,128]{3,2,1,0:T(8,128)(2,1)S(1)}, u32[]{:S(2)}, u32[]{:S(2)}) collective-permute-start(bf16[4,2,128,128]{3,2,1,0:T(8,128)(2,1)} %get-tuple-element.34), channel_id=1, source_target_pairs={{0,12},{4,8},{8,4},{12,0},{1,13},{5,9},{9,5},{13,1},{2,14},{6,10},... | collective-permute-start | bytes 786440 | tf_op jit(solution)/shard_map/ppermute | solution.py:576
  42.2 1.7 %collective-permute-start.6 = (bf16[2,48,2048]{2,1,0:T(8,128)(2,1)S(1)}, bf16[2,48,2048]{2,1,0:T(8,128)(2,1)S(1)}, u32[]{:S(2)}, u32[]{:S(2)}) collective-permute-start(bf16[2,48,2048]{2,1,0:T(8,128)(2,1)S(1)} %collective-permute-done.5.rest_2_), channel_id=1, source_target_pairs={{0,1},{1,0},{2,3},{3,2},{4,5},{5,4},{6,7},{7,6},{8,9},{9,8},{10,11... | collective-permute-start | bytes 1179656 | tf_op jit(solution)/shard_map/ppermute | solution.py:576
  45.6 4.8 %copy-start.1 = (s32[4,16]{1,0:T(4,128)S(1)}, s32[4,16]{1,0:T(4,128)}, u32[]{:S(2)}) copy-start(s32[4,16]{1,0:T(4,128)} %request_docs.5) | copy-start | bytes 772
  45.6 4.7 %copy-start.2 = (s32[1,16,12]{1,0,2:T(1,128)S(1)}, s32[1,16,12]{1,0,2:T(1,128)}, u32[]{:S(2)}) copy-start(s32[1,16,12]{1,0,2:T(1,128)} %param.17) | copy-start | bytes 2308
  45.6 4.7 %copy-start.3 = (s32[32]{0:T(128)S(1)}, s32[32]{0:T(128)}, u32[]{:S(2)}) copy-start(s32[32]{0:T(128)} %doc_lengths.1) | copy-start | bytes 388
  48.2 6.1 %collective-permute-start.7 = (bf16[192,128]{1,0:T(8,128)(2,1)S(1)}, bf16[192,128]{1,0:T(8,128)(2,1)S(1)}, u32[]{:S(2)}, u32[]{:S(2)}) collective-permute-start(bf16[192,128]{1,0:T(8,128)(2,1)S(1)} %get-tuple-element.24), channel_id=1, source_target_pairs={{0,4},{4,0},{8,12},{12,8},{1,5},{5,1},{9,13},{13,9},{2,6},{6,2},{1... | collective-permute-start | bytes 147464 | tf_op jit(solution)/shard_map/ppermute | solution.py:576
  48.3 7.0 %collective-permute-start.8 = (bf16[192,128]{1,0:T(8,128)(2,1)S(1)}, bf16[192,128]{1,0:T(8,128)(2,1)S(1)}, u32[]{:S(2)}, u32[]{:S(2)}) collective-permute-start(bf16[192,128]{1,0:T(8,128)(2,1)S(1)} %get-tuple-element.25), channel_id=1, source_target_pairs={{0,4},{4,0},{8,12},{12,8},{1,5},{5,1},{9,13},{13,9},{2,6},{6,2},{1... | collective-permute-start | bytes 147464 | tf_op jit(solution)/shard_map/ppermute | solution.py:576
  56.1 10.6 %all-to-all-start = ((bf16[4,48,256]{2,1,0:T(8,128)(2,1)}), bf16[4,48,256]{2,1,0:T(8,128)(2,1)S(1)}, u32[]{:S(2)}, u32[]{:S(2)}) async-start(bf16[4,48,256]{2,1,0:T(8,128)(2,1)} %bitcast.1), calls=%async_computation | async-start | bytes 196608 | tf_op jit(solution)/shard_map/all_to_all | solution.py:620

commit v13 on v12

--- a/solution.py
+++ b/solution.py
@@ -19,78 +19,45 @@
     return pltpu.with_memory_space_constraint(array, pltpu.HBM)
 
 
-def pick_weights_kernel(w_key, w_value, w_out, held, sems):
+def send_kernel(hidden, w_key, w_value, w_out, h_out, sems):
     group = lax.axis_index("groups")
-    pieces, piece = held.shape[:2]
-
-    def fetch(i, weight):
-        source = weight.at[pl.ds(i * piece, piece)]
-        return pltpu.make_async_copy(source, held.at[i], sems.at[0, i])
-
+    me = lax.axis_index("seq")
+    rows, depth = h_out.shape[1:]
     for chosen, weight in ((0, w_key), (1, w_value)):
 
         @pl.when(group == chosen)
         def _():
-            for i in range(pieces):
-                fetch(i, weight).start()
-
-    stores = []
-    for i in range(pieces):
-        fetch(i, w_key).wait()
-        target = w_out.at[pl.ds(i * piece, piece)]
-        stores.append(pltpu.make_async_copy(held.at[i], target, sems.at[1, i]))
-        stores[-1].start()
-    for store in stores:
-        store.wait()
-
-
-def pick_weights(w_key, w_value):
-    depth, width = w_key.shape
-    pieces = 4
-    return pl.pallas_call(
-        pick_weights_kernel,
-        out_shape=jax.ShapeDtypeStruct(w_key.shape, jnp.bfloat16),
-        in_specs=[ANY] * 2,
-        out_specs=ANY,
-        scratch_shapes=[
-            pltpu.VMEM((pieces, depth // pieces, width), jnp.bfloat16),
-            pltpu.SemaphoreType.DMA((2, pieces)),
-        ],
-        name="pick_weights",
-    )(w_key, w_value)
-
-
-def pick_hidden_kernel(hidden, _, out, held, sems):
-    me = lax.axis_index("seq")
-    rows, depth = out.shape[1:]
+            pltpu.make_async_copy(weight, w_out, sems.at[0]).start()
+
     first = me + 1 - 2 * lax.rem(me, 2)
-    fetches, stores = [], []
+    copies = []
     for i, block in enumerate((first, lax.rem(first + 2, 4))):
         source = hidden.at[
             0,
             pl.ds(pl.multiple_of(lax.axis_index("tp") * rows, rows), rows),
             pl.ds(pl.multiple_of(block * depth, depth), depth),
         ]
-        fetches.append(pltpu.make_async_copy(source, held.at[i], sems.at[0, i]))
-        fetches[-1].start()
-        stores.append(pltpu.make_async_copy(held.at[i], out.at[i], sems.at[1, i]))
-    for fetch, store in zip(fetches, stores):
-        fetch.wait()
-        store.start()
-    for store in stores:
-        store.wait()
-
-
-def pick_hidden(hidden, depth, after):
-    shape = (2, hidden.shape[1] // 4, depth)
+        copies.append(pltpu.make_async_copy(source, h_out.at[i], sems.at[1 + i]))
+        copies[-1].start()
+    pltpu.make_async_copy(w_key, w_out, sems.at[0]).wait()
+    for copy in copies:
+        copy.wait()
+
+
+def pick_sent(hidden, w_key, w_value):
+    h_shape = (2, hidden.shape[1] // 4, w_key.shape[0])
     return pl.pallas_call(
-        pick_hidden_kernel,
-        out_shape=jax.ShapeDtypeStruct(shape, jnp.bfloat16),
-        in_specs=[ANY] * 2,
-        out_specs=ANY,
-        scratch_shapes=[pltpu.VMEM(shape, jnp.bfloat16), pltpu.SemaphoreType.DMA((2, 2))],
-        name="pick_hidden",
-    )(hidden, after)
+        send_kernel,
+        out_shape=(
+            jax.ShapeDtypeStruct(w_key.shape, jnp.bfloat16),
+            jax.ShapeDtypeStruct(h_shape, jnp.bfloat16),
+        ),
+        in_specs=[ANY] * 3,
+        out_specs=(VMEM, VMEM),
+        scratch_shapes=[pltpu.SemaphoreType.DMA((3,))],
+        compiler_params=pltpu.CompilerParams(vmem_limit_bytes=16 * 1024 * 1024),
+        name="pick_sent",
+    )(in_hbm(hidden), in_hbm(w_key), in_hbm(w_value))
 
 
 def gate_kernel(*refs):
@@ -170,8 +137,9 @@
             pltpu.SMEM((requests, capacity), jnp.int32),
             pltpu.SemaphoreType.DMA((len(shapes),)),
         ],
+        compiler_params=pltpu.CompilerParams(vmem_limit_bytes=16 * 1024 * 1024),
         name="pick_docs",
-    )(request_docs, store_keys, store_values)
+    )(request_docs, in_hbm(store_keys), in_hbm(store_values))
 
 
 def near_kernel(hidden, w_key, w_value, _, total, w, h, sems):
@@ -575,14 +543,14 @@
             count = lax.axis_size(axis)
             return lax.ppermute(array, axis, [(i, i ^ apart) for i in range(count)])
 
-        w_send = pick_weights(w_key, w_value)
+        w_send, h_send = pick_sent(hidden, w_key, w_value)
         w_far = swap(w_send, "seq", 2)
-        h_mine = swap(pick_hidden(hidden, w_key.shape[0], w_send), "seq", 1)
+        h_mine = swap(h_send, "seq", 1)
         doc_1, doc_2, doc_3 = pick_docs(request_docs, store_keys, store_values, False)
-        (h_mine,) = gate((h_mine,), (in_hbm(doc_1),), cost=1)
+        (h_mine,) = gate((h_mine,), (doc_1,), cost=8000000000)
         h_chip = swap(h_mine, "tp", 2)
         h_core = swap(h_mine, "tp", 1)
-        doc_2, doc_3, w_far = gate((doc_2, doc_3, w_far), pinned=2, cost=8000000000)
+        doc_2, doc_3, w_far = gate((doc_2, doc_3, w_far), cost=8000000000)
         w_swapped = swap(w_far, "groups", 1)
         doc_1 = swap(doc_1, "seq", 1)
         docs = (swap(doc_2, "seq", 2), swap(doc_3, "seq", 3), doc_1)

time: 67.8 us -> 65.1 us (0.960)
  Pallas kernels: 21.1 us -> 17.7 us
    pallas_call x2 -> x1, Pallas kernels: 3.55 us -> 1.18 us  [pick_sent(): pl.pallas_call(send_kernel, out_shape=(jax.ShapeDtypeStruct(w_key.shape,...]
    pallas_call x1, Pallas kernels: 3.19 us -> 2.17 us  [pick_docs(): pl.pallas_call(functools.partial(docs_kernel, by_owner), out_shape=tuple(...]
  transfers between devices with their start and end apart: 12 -> 12, of which waited for: 7 -> 7; matrix products, arithmetic and copies ran while one was open for 0% -> 0% of each run, Pallas kernels for 29% -> 25%
where the time goes in v13:
time: 65.1 us; the launch traced here: 64.7 us
  waiting for transfers between devices  27.9 us (43%)
  Pallas kernels  17.7 us (27%)
  starting transfers between devices  17.7 us (27%)
  between operations  0.77 us (1%)
  local copies, waits for them, and re-layouts  0.69 us (1%)
    ppermute x11, waiting for transfers between devices, swap(): return lax.ppermute(array, axis, [(i, i ^ apart) for i in range(count)])  27.9 us
    ppermute x11, starting transfers between devices, swap(): return lax.ppermute(array, axis, [(i, i ^ apart) for i in range(count)])  14.4 us
    pallas_call x1, Pallas kernels, attend(): pl.pallas_call(functools.partial(attend_kernel, by_owner), out_shape=jax....  7.1 us
    all_to_all x1, starting transfers between devices, shards(): lax.all_to_all(outgoing, 'seq', split_axis=0, concat_axis=0, tiled=True)  3.3 us
    pallas_call x1, Pallas kernels, pick_docs(): pl.pallas_call(functools.partial(docs_kernel, by_owner), out_shape=tuple(...  2.17 us
    pallas_call x1, Pallas kernels, project(): pl.pallas_call(far_kernel, out_shape=(sums,) + (jax.ShapeDtypeStruct((row...  1.94 us
    pallas_call x1, Pallas kernels, project(): pl.pallas_call(neighbour_kernel, out_shape=sums, in_specs=[ANY] * (2 + le...  1.64 us
    pallas_call x1, Pallas kernels, project(): pl.pallas_call(near_kernel, out_shape=sums, in_specs=[ANY] * 4, out_specs...  1.6 us
  transfers between devices with their start and end apart: 12, of which 7 were waited for; matrix products, arithmetic and copies ran while one was open for 0% of the time, Pallas kernels for 25%

profile of v13, /device:TPU:0, one launch (start us, length us, event | category | flops | bytes accessed | tf_op | source)
XLA Modules:
  0.0 64.7 jit_solution(3310674214184165343)
XLA Ops:
  0.6 1.2 %pick_sent.1 = (bf16[2048,128]{1,0:T(8,128)(2,1)S(1)}, bf16[2,48,2048]{2,1,0:T(8,128)(2,1)S(1)}) custom-call(bf16[1,192,8192]{2,1,0:T(8,128)(2,1)} %hidden.5, bf16[2048,128]{1,0:T(8,128)(2,1)} %w_key.5, bf16[2048,128]{1,0:T(8,128)(2,1)} %w_value.5), custom_call_target="tpu_custom_call" | custom-call | tf_op jit(solution)/shard_map/pick_sent/pallas_call | solution.py:49
  1.8 3.1 %collective-permute-start.3 = (bf16[2,48,2048]{2,1,0:T(8,128)(2,1)S(1)}, bf16[2,48,2048]{2,1,0:T(8,128)(2,1)S(1)}, u32[]{:S(2)}, u32[]{:S(2)}) collective-permute-start(bf16[2,48,2048]{2,1,0:T(8,128)(2,1)S(1)} %get-tuple-element.26), channel_id=1, source_target_pairs={{0,4},{4,0},{8,12},{12,8},{1,5},{5,1},{9,13},{13,9},{2,6},{6,2},{1... | collective-permute-start | bytes 1179656 | tf_op jit(solution)/shard_map/ppermute | solution.py:544
  4.9 2.6 %collective-permute-start = (bf16[2048,128]{1,0:T(8,128)(2,1)S(1)}, bf16[2048,128]{1,0:T(8,128)(2,1)S(1)}, u32[]{:S(2)}, u32[]{:S(2)}) collective-permute-start(bf16[2048,128]{1,0:T(8,128)(2,1)S(1)} %get-tuple-element.23), channel_id=1, source_target_pairs={{0,8},{4,12},{8,0},{12,4},{1,9},{5,13},{9,1},{13,5},{2,10},{6,14},... | collective-permute-start | bytes 1572872 | tf_op jit(solution)/shard_map/ppermute | solution.py:544
  7.5 2.2 %pick_docs.1 = (bf16[4,2,128,128]{3,2,1,0:T(8,128)(2,1)S(1)}, bf16[4,2,128,128]{3,2,1,0:T(8,128)(2,1)S(1)}, bf16[4,2,128,128]{3,2,1,0:T(8,128)(2,1)S(1)}) custom-call(s32[4,16]{1,0:T(4,128)S(1)} %copy-done.1, bf16[8,128,128]{2,1,0:T(8,128)(2,1)} %rest_0_.1, bf16[8,128,128]{2,1,0:T(8,128)(2,1)} %rest_1_.1), custom_call_target="tpu_custom_call" | custom-call | tf_op jit(solution)/shard_map/pick_docs/pallas_call | solution.py:131
  9.7 0.6 collective-permute-start.2
  10.3 12.9 %collective-permute-done.3.refs_0_ = bf16[2,48,2048]{2,1,0:T(8,128)(2,1)S(1)} collective-permute-done((bf16[2,48,2048]{2,1,0:T(8,128)(2,1)S(1)}, bf16[2,48,2048]{2,1,0:T(8,128)(2,1)S(1)}, u32[]{:S(2)}, u32[]{:S(2)}) %collective-permute-start.3) | collective-permute-done | bytes 393248 | tf_op jit(solution)/shard_map/ppermute | solution.py:544
  23.2 2.0 %collective-permute-start.5 = (bf16[2,48,2048]{2,1,0:T(8,128)(2,1)S(1)}, bf16[2,48,2048]{2,1,0:T(8,128)(2,1)S(1)}, u32[]{:S(2)}, u32[]{:S(2)}) collective-permute-start(bf16[2,48,2048]{2,1,0:T(8,128)(2,1)S(1)} %gate.3.rest_0_), channel_id=1, source_target_pairs={{0,2},{1,3},{2,0},{3,1},{4,6},{5,7},{6,4},{7,5},{8,10},{9,11},{10,... | collective-permute-start | bytes 1179656 | tf_op jit(solution)/shard_map/ppermute | solution.py:544
  25.2 5.4 %collective-permute-done.refs_2_ = bf16[2048,128]{1,0:T(8,128)(2,1)S(1)} collective-permute-done((bf16[2048,128]{1,0:T(8,128)(2,1)S(1)}, bf16[2048,128]{1,0:T(8,128)(2,1)S(1)}, u32[]{:S(2)}, u32[]{:S(2)}) %collective-permute-start) | collective-permute-done | bytes 524320 | tf_op jit(solution)/shard_map/ppermute | solution.py:544
  30.6 1.5 %collective-permute-start.1 = (bf16[2048,128]{1,0:T(8,128)(2,1)S(1)}, bf16[2048,128]{1,0:T(8,128)(2,1)S(1)}, u32[]{:S(2)}, u32[]{:S(2)}) collective-permute-start(bf16[2048,128]{1,0:T(8,128)(2,1)S(1)} %get-tuple-element.24.w_far), channel_id=1, source_target_pairs={{0,16},{16,0},{1,17},{17,1},{2,18},{18,2},{3,19},{19,3},{4,20},{20... | collective-permute-start | bytes 1572872 | tf_op jit(solution)/shard_map/ppermute | solution.py:544
  32.1 2.5 %collective-permute-start.10 = (bf16[4,2,128,128]{3,2,1,0:T(8,128)(2,1)S(1)}, bf16[4,2,128,128]{3,2,1,0:T(8,128)(2,1)S(1)}, u32[]{:S(2)}, u32[]{:S(2)}) collective-permute-start(bf16[4,2,128,128]{3,2,1,0:T(8,128)(2,1)S(1)} %get-tuple-element.38), channel_id=1, source_target_pairs={{0,12},{4,8},{8,4},{12,0},{1,13},{5,9},{9,5},{13,1},{2,14},{6,10},... | collective-permute-start | bytes 786440 | tf_op jit(solution)/shard_map/ppermute | solution.py:544
  34.7 0.3 collective-permute-done.5.rest_2_
  34.9 1.6 %project_near.1.near = f32[192,256]{1,0:T(8,128)S(1)} custom-call(bf16[1,192,8192]{2,1,0:T(8,128)(2,1)S(1)} %copy-done, bf16[2048,128]{1,0:T(8,128)(2,1)} %w_key.5, bf16[2048,128]{1,0:T(8,128)(2,1)} %w_value.5, bf16[4,2,128,128]{3,2,1,0:T(8,128)(2,1)S(1)} %collective-permute-done.2._.rest_4_), custom_call_target="tpu_custom_call" | custom-call | flops 10000000000 | bytes 1 | tf_op jit(solution)/shard_map/project_near/pallas_call | solution.py:216
  36.6 0.1 collective-permute-done.6.rest_3_
  36.7 1.6 %project_neighbour.1.neighbour = f32[192,256]{1,0:T(8,128)S(1)} custom-call(bf16[2048,128]{1,0:T(8,128)(2,1)} %w_key.5, bf16[2048,128]{1,0:T(8,128)(2,1)} %w_value.5, bf16[2,48,2048]{2,1,0:T(8,128)(2,1)S(1)} %gate.3.rest_0_, bf16[2,48,2048]{2,1,0:T(8,128)(2,1)S(1)} %collective-permute-done.4.rest_1_, ...), custom_call_target="tpu_custom_call" | custom-call | flops 1 | bytes 1 | tf_op jit(solution)/shard_map/project_neighbour/pallas_call | solution.py:226
  38.3 4.7 %collective-permute-done.1.w_swapped = bf16[2048,128]{1,0:T(8,128)(2,1)S(1)} collective-permute-done((bf16[2048,128]{1,0:T(8,128)(2,1)S(1)}, bf16[2048,128]{1,0:T(8,128)(2,1)S(1)}, u32[]{:S(2)}, u32[]{:S(2)}) %collective-permute-start.1) | collective-permute-done | bytes 524320 | tf_op jit(solution)/shard_map/ppermute | solution.py:544
  43.0 1.9 %project_far.1 = (f32[192,256]{1,0:T(8,128)S(1)}, bf16[192,128]{1,0:T(8,128)(2,1)S(1)}, bf16[192,128]{1,0:T(8,128)(2,1)S(1)}) custom-call(bf16[1,192,8192]{2,1,0:T(8,128)(2,1)S(1)} %copy-done, bf16[2048,128]{1,0:T(8,128)(2,1)S(1)} %get-tuple-element.24.w_far, bf16[2048,128]{1,0:T(8,128)(2,1)S(1)} %collective-permute-done.1.w_swapped, ...), custom_call_target="tpu_custom_call" | custom-call | flops 1 | bytes 1 | tf_op jit(solution)/shard_map/project_far/pallas_call | solution.py:240
  45.0 2.0 %collective-permute-start.8 = (bf16[192,128]{1,0:T(8,128)(2,1)S(1)}, bf16[192,128]{1,0:T(8,128)(2,1)S(1)}, u32[]{:S(2)}, u32[]{:S(2)}) collective-permute-start(bf16[192,128]{1,0:T(8,128)(2,1)S(1)} %get-tuple-element.29), channel_id=1, source_target_pairs={{0,4},{4,0},{8,12},{12,8},{1,5},{5,1},{9,13},{13,9},{2,6},{6,2},{1... | collective-permute-start | bytes 147464 | tf_op jit(solution)/shard_map/ppermute | solution.py:544
  47.1 1.2 %plan.1 = (bf16[2048,128]{1,0:T(8,128)(2,1)S(1)}, bf16[16,2048]{1,0:T(8,128)(2,1)S(1)}, f32[1,2048]{1,0:T(1,128)S(1)}, s32[192,1]{1,0:T(8,128)S(1)}, s32[1,192]{1,0:T(1,128)S(1)}, /*index=5*/s32[1,192]{1,0:T(1,128)S(1)}) custom-call(s32[4,16]{1,0:T(4,128)S(1)} %copy-done.1, s32[32]{0:T(128)S(1)} %copy-done.3, s32[12,1,16]{2,1,0:T(1,128)S(1)} %bitcast.2), custom_call_target="tpu_custom_call" | custom-call | tf_op jit(solution)/shard_map/plan/pallas_call | solution.py:330
  48.3 3.5 %collective-permute-done.7.arrived_k = bf16[192,128]{1,0:T(8,128)(2,1)S(1)} collective-permute-done((bf16[192,128]{1,0:T(8,128)(2,1)S(1)}, bf16[192,128]{1,0:T(8,128)(2,1)S(1)}, u32[]{:S(2)}, u32[]{:S(2)}) %collective-permute-start.7) | collective-permute-done | bytes 49184 | tf_op jit(solution)/shard_map/ppermute | solution.py:544
  51.8 1.0 %collective-permute-done.8.arrived_v = bf16[192,128]{1,0:T(8,128)(2,1)S(1)} collective-permute-done((bf16[192,128]{1,0:T(8,128)(2,1)S(1)}, bf16[192,128]{1,0:T(8,128)(2,1)S(1)}, u32[]{:S(2)}, u32[]{:S(2)}) %collective-permute-start.8) | collective-permute-done | bytes 49184 | tf_op jit(solution)/shard_map/ppermute | solution.py:544
  52.7 0.8 %finish.1 = (bf16[192,256]{1,0:T(8,128)(2,1)S(1)}, bf16[192,256]{1,0:T(8,128)(2,1)}) custom-call(f32[192,256]{1,0:T(8,128)S(1)} %get-tuple-element.27.own, bf16[192,128]{1,0:T(8,128)(2,1)S(1)} %collective-permute-done.7.arrived_k, bf16[192,128]{1,0:T(8,128)(2,1)S(1)} %collective-permute-done.8.arrived_v, s32[1,192]{1,0:T(1,128)S(1)} %get-tuple-element.30.slot_row), custom_call_target="tpu_custom_call" | custom-call | tf_op jit(solution)/shard_map/finish/pallas_call | solution.py:352
  53.6 3.3 %all-to-all-start = ((bf16[4,48,256]{2,1,0:T(8,128)(2,1)}), bf16[4,48,256]{2,1,0:T(8,128)(2,1)S(1)}, u32[]{:S(2)}, u32[]{:S(2)}) async-start(bf16[4,48,256]{2,1,0:T(8,128)(2,1)} %bitcast.1), calls=%async_computation | async-start | bytes 196608 | tf_op jit(solution)/shard_map/all_to_all | solution.py:588
  56.9 7.1 %attend.1 = bf16[1,192,1024]{2,1,0:T(8,128)(2,1)} custom-call(s32[4,16]{1,0:T(4,128)S(1)} %copy-done.1, bf16[1,192,1024]{2,1,0:T(8,128)(2,1)} %queries.1, bf16[192,256]{1,0:T(8,128)(2,1)S(1)} %get-tuple-element.31.fresh, bf16[2048,128]{1,0:T(8,128)(2,1)S(1)} %get-tuple-element.32.held, bf16[16,2048]{1,0:T(8,128)(2,1)S(1)} %get-tuple-element.33.spare, ...), custom_call_target="tpu_custom_call" | custom-call | tf_op jit(solution)/shard_map/attend/pallas_call | solution.py:494
  64.0 0.7 %broadcast_in_dim_reshape.3 = bf16[1,4,4,12,2,128]{5,4,3,2,1,0:T(2,128)(2,1)} reshape(bf16[4,48,256]{2,1,0:T(8,128)(2,1)S(1)} %all-to-all-done) | data formatting | bytes 196608 | tf_op jit(solution)/shard_map/broadcast_in_dim;reshape | solution.py:590
  (19 shorter events, 0.1 us)
Async XLA Ops:
  0.6 6.9 %copy-start.1 = (s32[4,16]{1,0:T(4,128)S(1)}, s32[4,16]{1,0:T(4,128)}, u32[]{:S(2)}) copy-start(s32[4,16]{1,0:T(4,128)} %request_docs.5) | copy-start | bytes 772
  1.8 21.3 %collective-permute-start.3 = (bf16[2,48,2048]{2,1,0:T(8,128)(2,1)S(1)}, bf16[2,48,2048]{2,1,0:T(8,128)(2,1)S(1)}, u32[]{:S(2)}, u32[]{:S(2)}) collective-permute-start(bf16[2,48,2048]{2,1,0:T(8,128)(2,1)S(1)} %get-tuple-element.26), channel_id=1, source_target_pairs={{0,4},{4,0},{8,12},{12,8},{1,5},{5,1},{9,13},{13,9},{2,6},{6,2},{1... | collective-permute-start | bytes 1179656 | tf_op jit(solution)/shard_map/ppermute | solution.py:544
  4.9 25.7 %collective-permute-start = (bf16[2048,128]{1,0:T(8,128)(2,1)S(1)}, bf16[2048,128]{1,0:T(8,128)(2,1)S(1)}, u32[]{:S(2)}, u32[]{:S(2)}) collective-permute-start(bf16[2048,128]{1,0:T(8,128)(2,1)S(1)} %get-tuple-element.23), channel_id=1, source_target_pairs={{0,8},{4,12},{8,0},{12,4},{1,9},{5,13},{9,1},{13,5},{2,10},{6,14},... | collective-permute-start | bytes 1572872 | tf_op jit(solution)/shard_map/ppermute | solution.py:544
  9.7 22.4 %collective-permute-start.2 = (bf16[4,2,128,128]{3,2,1,0:T(8,128)(2,1)S(1)}, bf16[4,2,128,128]{3,2,1,0:T(8,128)(2,1)S(1)}, u32[]{:S(2)}, u32[]{:S(2)}) collective-permute-start(bf16[4,2,128,128]{3,2,1,0:T(8,128)(2,1)S(1)} %get-tuple-element.25.refs_1_), channel_id=1, source_target_pairs={{0,4},{4,0},{8,12},{12,8},{1,5},{5,1},{9,13},{13,9},{2,6},{6,2},{1... | collective-permute-start | bytes 786440 | tf_op jit(solution)/shard_map/ppermute | solution.py:544
  23.2 13.4 %collective-permute-start.4 = (bf16[2,48,2048]{2,1,0:T(8,128)(2,1)S(1)}, bf16[2,48,2048]{2,1,0:T(8,128)(2,1)S(1)}, u32[]{:S(2)}, u32[]{:S(2)}) collective-permute-start(bf16[2,48,2048]{2,1,0:T(8,128)(2,1)S(1)} %gate.3.rest_0_), channel_id=1, source_target_pairs={{0,1},{1,0},{2,3},{3,2},{4,5},{5,4},{6,7},{7,6},{8,9},{9,8},{10,11... | collective-permute-start | bytes 1179656 | tf_op jit(solution)/shard_map/ppermute | solution.py:544
  23.2 11.8 %collective-permute-start.5 = (bf16[2,48,2048]{2,1,0:T(8,128)(2,1)S(1)}, bf16[2,48,2048]{2,1,0:T(8,128)(2,1)S(1)}, u32[]{:S(2)}, u32[]{:S(2)}) collective-permute-start(bf16[2,48,2048]{2,1,0:T(8,128)(2,1)S(1)} %gate.3.rest_0_), channel_id=1, source_target_pairs={{0,2},{1,3},{2,0},{3,1},{4,6},{5,7},{6,4},{7,5},{8,10},{9,11},{10,... | collective-permute-start | bytes 1179656 | tf_op jit(solution)/shard_map/ppermute | solution.py:544
  30.6 4.3 %copy-start = (bf16[1,192,8192]{2,1,0:T(8,128)(2,1)S(1)}, bf16[1,192,8192]{2,1,0:T(8,128)(2,1)}, u32[]{:S(2)}) copy-start(bf16[1,192,8192]{2,1,0:T(8,128)(2,1)} %hidden.5) | copy-start | bytes 9437188
  30.6 12.4 %collective-permute-start.1 = (bf16[2048,128]{1,0:T(8,128)(2,1)S(1)}, bf16[2048,128]{1,0:T(8,128)(2,1)S(1)}, u32[]{:S(2)}, u32[]{:S(2)}) collective-permute-start(bf16[2048,128]{1,0:T(8,128)(2,1)S(1)} %get-tuple-element.24.w_far), channel_id=1, source_target_pairs={{0,16},{16,0},{1,17},{17,1},{2,18},{18,2},{3,19},{19,3},{4,20},{20... | collective-permute-start | bytes 1572872 | tf_op jit(solution)/shard_map/ppermute | solution.py:544
  32.1 24.8 %collective-permute-start.9 = (bf16[4,2,128,128]{3,2,1,0:T(8,128)(2,1)S(1)}, bf16[4,2,128,128]{3,2,1,0:T(8,128)(2,1)S(1)}, u32[]{:S(2)}, u32[]{:S(2)}) collective-permute-start(bf16[4,2,128,128]{3,2,1,0:T(8,128)(2,1)S(1)} %get-tuple-element.37), channel_id=1, source_target_pairs={{0,8},{4,12},{8,0},{12,4},{1,9},{5,13},{9,1},{13,5},{2,10},{6,14},... | collective-permute-start | bytes 786440 | tf_op jit(solution)/shard_map/ppermute | solution.py:544
  32.1 24.8 %collective-permute-start.10 = (bf16[4,2,128,128]{3,2,1,0:T(8,128)(2,1)S(1)}, bf16[4,2,128,128]{3,2,1,0:T(8,128)(2,1)S(1)}, u32[]{:S(2)}, u32[]{:S(2)}) collective-permute-start(bf16[4,2,128,128]{3,2,1,0:T(8,128)(2,1)S(1)} %get-tuple-element.38), channel_id=1, source_target_pairs={{0,12},{4,8},{8,4},{12,0},{1,13},{5,9},{9,5},{13,1},{2,14},{6,10},... | collective-permute-start | bytes 786440 | tf_op jit(solution)/shard_map/ppermute | solution.py:544
  34.9 1.7 %collective-permute-start.6 = (bf16[2,48,2048]{2,1,0:T(8,128)(2,1)S(1)}, bf16[2,48,2048]{2,1,0:T(8,128)(2,1)S(1)}, u32[]{:S(2)}, u32[]{:S(2)}) collective-permute-start(bf16[2,48,2048]{2,1,0:T(8,128)(2,1)S(1)} %collective-permute-done.5.rest_2_), channel_id=1, source_target_pairs={{0,1},{1,0},{2,3},{3,2},{4,5},{5,4},{6,7},{7,6},{8,9},{9,8},{10,11... | collective-permute-start | bytes 1179656 | tf_op jit(solution)/shard_map/ppermute | solution.py:544
  38.3 8.7 %copy-start.2 = (s32[1,16,12]{1,0,2:T(1,128)S(1)}, s32[1,16,12]{1,0,2:T(1,128)}, u32[]{:S(2)}) copy-start(s32[1,16,12]{1,0,2:T(1,128)} %param.17) | copy-start | bytes 2308
  38.3 8.7 %copy-start.3 = (s32[32]{0:T(128)S(1)}, s32[32]{0:T(128)}, u32[]{:S(2)}) copy-start(s32[32]{0:T(128)} %doc_lengths.1) | copy-start | bytes 388
  45.0 6.8 %collective-permute-start.7 = (bf16[192,128]{1,0:T(8,128)(2,1)S(1)}, bf16[192,128]{1,0:T(8,128)(2,1)S(1)}, u32[]{:S(2)}, u32[]{:S(2)}) collective-permute-start(bf16[192,128]{1,0:T(8,128)(2,1)S(1)} %get-tuple-element.28), channel_id=1, source_target_pairs={{0,4},{4,0},{8,12},{12,8},{1,5},{5,1},{9,13},{13,9},{2,6},{6,2},{1... | collective-permute-start | bytes 147464 | tf_op jit(solution)/shard_map/ppermute | solution.py:544
  45.0 7.7 %collective-permute-start.8 = (bf16[192,128]{1,0:T(8,128)(2,1)S(1)}, bf16[192,128]{1,0:T(8,128)(2,1)S(1)}, u32[]{:S(2)}, u32[]{:S(2)}) collective-permute-start(bf16[192,128]{1,0:T(8,128)(2,1)S(1)} %get-tuple-element.29), channel_id=1, source_target_pairs={{0,4},{4,0},{8,12},{12,8},{1,5},{5,1},{9,13},{13,9},{2,6},{6,2},{1... | collective-permute-start | bytes 147464 | tf_op jit(solution)/shard_map/ppermute | solution.py:544
  53.6 10.4 %all-to-all-start = ((bf16[4,48,256]{2,1,0:T(8,128)(2,1)}), bf16[4,48,256]{2,1,0:T(8,128)(2,1)S(1)}, u32[]{:S(2)}, u32[]{:S(2)}) async-start(bf16[4,48,256]{2,1,0:T(8,128)(2,1)} %bitcast.1), calls=%async_computation | async-start | bytes 196608 | tf_op jit(solution)/shard_map/all_to_all | solution.py:588

commit v14 on v13

--- a/solution.py
+++ b/solution.py
@@ -255,8 +255,21 @@
 
 
 def plan_kernel(
-    capacity, slots, request_docs, doc_lengths, rows, held, spare, key_bias, row_place, key_place, slot_row, counts
+    capacity, slots, request_docs, doc_lengths, rows, queries, q, held, spare, key_bias, row_place, key_place,
+    slot_row, counts
 ):
+    head_dim = q.shape[1] // 2
+    heads = queries.shape[2] // head_dim
+    block_rows = 4 * rows.shape[0]
+    scale = math.log2(math.e) / math.sqrt(head_dim)
+    for b in range(queries.shape[1] // block_rows):
+        for h in range(heads):
+            here = queries[0, b * block_rows : (b + 1) * block_rows, h * head_dim : (h + 1) * head_dim]
+            here = here.astype(jnp.float32) * scale
+            high = here.astype(jnp.bfloat16)
+            place = slice((b * heads + h) * block_rows, (b * heads + h + 1) * block_rows)
+            q[place, :head_dim] = high
+            q[place, head_dim:] = (here - high.astype(jnp.float32)).astype(jnp.bfloat16)
     me = lax.axis_index("seq")
     per_doc, _, doc_count = rows.shape
     doc_len = held.shape[0] // doc_count
@@ -315,11 +328,12 @@
     slot_row[...] = jnp.sum(jnp.where(same, goes, 0), axis=0, keepdims=True)
 
 
-def plan(request_docs, doc_lengths, recompute_rows, slots, head_dim, doc_len):
+def plan(request_docs, doc_lengths, recompute_rows, queries, slots, head_dim, doc_len):
     _, doc_count, per_doc = recompute_rows.shape
     rows = doc_count * per_doc
     context = doc_count * doc_len
     shapes = (
+        ((rows * queries.shape[2] // head_dim, 2 * head_dim), jnp.bfloat16),
         ((context, head_dim), jnp.bfloat16),
         ((doc_count, context), jnp.bfloat16),
         ((1, context), jnp.float32),
@@ -330,12 +344,12 @@
     return pl.pallas_call(
         functools.partial(plan_kernel, slots // 2, slots),
         out_shape=tuple(jax.ShapeDtypeStruct(*one) for one in shapes),
-        in_specs=[SMEM, SMEM, VMEM],
+        in_specs=[SMEM, SMEM, VMEM, VMEM],
         out_specs=(VMEM,) * len(shapes),
         scratch_shapes=[pltpu.SMEM((request_docs.shape[0],), jnp.int32)],
         compiler_params=pltpu.CompilerParams(vmem_limit_bytes=16 * 1024 * 1024),
         name="plan",
-    )(request_docs, doc_lengths, jnp.transpose(recompute_rows, (2, 0, 1)))
+    )(request_docs, doc_lengths, jnp.transpose(recompute_rows, (2, 0, 1)), queries)
 
 
 def finish_kernel(own, arrived_k, arrived_v, slot_row, fresh, outgoing):
@@ -360,9 +374,9 @@
 
 
 def attend_kernel(
-    by_owner, request_docs, queries, fresh, held, spare, key_bias, row_place, key_place, *rest
+    by_owner, request_docs, q, fresh, held, spare, key_bias, row_place, key_place, *rest
 ):
-    sources, (mixed, raw, q, keys, values, counts, sems, q_sem) = rest[:-8], rest[-8:]
+    sources, (mixed, keys, values, counts, sems) = rest[:-5], rest[-5:]
     me = lax.axis_index("seq")
     doc_count = request_docs.shape[1]
     head_dim = keys.shape[1] // 2
@@ -376,8 +390,6 @@
     heads = mixed.shape[2] // head_dim
     left = pl.ds(0, head_dim)
 
-    fetch_queries = pltpu.make_async_copy(queries, raw, q_sem)
-    fetch_queries.start()
     for o in range(owners):
         counts[o] = 0
 
@@ -411,26 +423,14 @@
 
         return carry
 
-    lax.fori_loop(0, doc_count, one_doc, 0)
-
-    fetch_queries.wait()
-    scale = math.log2(math.e) / math.sqrt(head_dim)
-    for b in range(blocks):
-        for h in range(heads):
-            here = raw[0, b * block_rows : (b + 1) * block_rows, h * head_dim : (h + 1) * head_dim]
-            here = here.astype(jnp.float32) * scale
-            high = here.astype(jnp.bfloat16)
-            place = slice((b * heads + h) * block_rows, (b * heads + h + 1) * block_rows)
-            q[place, :head_dim] = high
-            q[place, head_dim:] = (here - high.astype(jnp.float32)).astype(jnp.bfloat16)
-
-    for b in range(blocks):
+    lax.fori_loop(0, doc_count, one_doc, 0, unroll=True)
+
+    def assemble(b):
         block = pl.ds(b * block_keys, block_keys)
         for i, context in enumerate((keys, values)):
             pltpu.make_async_copy(
                 context.at[block, left], context.at[block, left], sems.at[i, b]
             ).wait()
-    for b in range(blocks):
         block = slice(b * block_keys, (b + 1) * block_keys)
         spares = jnp.dot(
             spare[:, block], keys[block, :head_dim], preferred_element_type=jnp.float32
@@ -448,7 +448,10 @@
     fresh_v = jnp.concatenate([fresh[:, head_dim:], jnp.ones_like(fresh[:, head_dim:])], axis=1)
     slot_place = lax.broadcasted_iota(jnp.int32, (1, block_keys), 1)
     contract_last = (((1,), (1,)), ((), ()))
+    assemble(0)
     for b in range(blocks):
+        if b + 1 < blocks:
+            assemble(b + 1)
         rows = slice(b * block_rows, (b + 1) * block_rows)
         q_here = q[b * heads * block_rows : (b + 1) * heads * block_rows, :]
         own_place = row_place[rows, :]
@@ -488,28 +491,26 @@
             ]
 
 
-def attend(request_docs, queries, fresh, held, spare, key_bias, row_place, key_place, sources, by_owner):
+def attend(
+    shape, request_docs, q, fresh, held, spare, key_bias, row_place, key_place, sources, by_owner
+):
     context, head_dim = held.shape
-    rows = queries.shape[1] * queries.shape[2] // head_dim
     return pl.pallas_call(
         functools.partial(attend_kernel, by_owner),
-        out_shape=jax.ShapeDtypeStruct(queries.shape, jnp.bfloat16),
-        in_specs=[SMEM, ANY] + [VMEM] * 6 + [ANY] * len(sources),
+        out_shape=jax.ShapeDtypeStruct(shape, jnp.bfloat16),
+        in_specs=[SMEM] + [VMEM] * 7 + [ANY] * len(sources),
         out_specs=VMEM,
         scratch_shapes=[
-            pltpu.VMEM(queries.shape, jnp.bfloat16),
-            pltpu.VMEM((rows, 2 * head_dim), jnp.bfloat16),
             pltpu.VMEM((context, 2 * head_dim), jnp.bfloat16),
             pltpu.VMEM((context, 2 * head_dim), jnp.bfloat16),
             pltpu.SMEM((request_docs.shape[0],), jnp.int32),
             pltpu.SemaphoreType.DMA((2, 4)),
-            pltpu.SemaphoreType.DMA,
         ],
         compiler_params=pltpu.CompilerParams(vmem_limit_bytes=32 * 1024 * 1024),
         name="attend",
     )(
         request_docs,
-        in_hbm(queries),
+        q,
         fresh,
         held,
         spare,
@@ -567,13 +568,14 @@
         own = jnp.dot(hidden[0], weights, preferred_element_type=jnp.float32)
         arrived = [jnp.zeros((own.shape[0], head_dim), jnp.bfloat16)] * 2
 
-    held, spare, key_bias, row_place, key_place, slot_row = plan(
-        request_docs, doc_lengths, recompute_rows, slot_count, head_dim, doc_len
+    q, held, spare, key_bias, row_place, key_place, slot_row = plan(
+        request_docs, doc_lengths, recompute_rows, queries, slot_count, head_dim, doc_len
     )
     fresh, outgoing = finish(own, arrived, slot_row, seq_count * capacity * per_doc)
     mixed = attend(
+        queries.shape,
         request_docs,
-        queries,
+        q,
         fresh,
         held,
         spare,

time: 65.1 us -> 68.1 us (1.046)
  starting transfers between devices: 17.7 us -> 22.8 us
  waiting for transfers between devices: 27.9 us -> 25.2 us
    all_to_all x1, starting transfers between devices: 3.3 us -> 7.95 us  [shards(): lax.all_to_all(outgoing, 'seq', split_axis=0, concat_axis=0, tiled=True)]
    ppermute x11, waiting for transfers between devices: 27.9 us -> 25.2 us  [swap(): return lax.ppermute(array, axis, [(i, i ^ apart) for i in range(count)])]
  transfers between devices with their start and end apart: 12 -> 12, of which waited for: 7 -> 6; matrix products, arithmetic and copies ran while one was open for 0% -> 0% of each run, Pallas kernels for 25% -> 25%
where the time goes in v14:
time: 68.1 us; the launch traced here: 67.6 us
  waiting for transfers between devices  25.2 us (37%)
  starting transfers between devices  22.8 us (33%)
  Pallas kernels  18.2 us (27%)
  between operations  0.77 us (1%)
  local copies, waits for them, and re-layouts  0.7 us (1%)
    ppermute x11, waiting for transfers between devices, swap(): return lax.ppermute(array, axis, [(i, i ^ apart) for i in range(count)])  25.2 us
    ppermute x11, starting transfers between devices, swap(): return lax.ppermute(array, axis, [(i, i ^ apart) for i in range(count)])  14.9 us
    all_to_all x1, starting transfers between devices, shards(): lax.all_to_all(outgoing, 'seq', split_axis=0, concat_axis=0, tiled=True)  7.95 us
    pallas_call x1, Pallas kernels, attend(): pl.pallas_call(functools.partial(attend_kernel, by_owner), out_shape=jax....  7.47 us
    pallas_call x1, Pallas kernels, pick_docs(): pl.pallas_call(functools.partial(docs_kernel, by_owner), out_shape=tuple(...  2.12 us
    pallas_call x1, Pallas kernels, project(): pl.pallas_call(far_kernel, out_shape=(sums,) + (jax.ShapeDtypeStruct((row...  1.94 us
    pallas_call x1, Pallas kernels, project(): pl.pallas_call(neighbour_kernel, out_shape=sums, in_specs=[ANY] * (2 + le...  1.63 us
    pallas_call x1, Pallas kernels, project(): pl.pallas_call(near_kernel, out_shape=sums, in_specs=[ANY] * 4, out_specs...  1.61 us
  transfers between devices with their start and end apart: 12, of which 6 were waited for; matrix products, arithmetic and copies ran while one was open for 0% of the time, Pallas kernels for 25%

profile of v14, /device:TPU:0, one launch (start us, length us, event | category | flops | bytes accessed | tf_op | source)
XLA Modules:
  0.0 67.6 jit_solution(11574409361399978464)
XLA Ops:
  0.6 1.2 %pick_sent.1 = (bf16[2048,128]{1,0:T(8,128)(2,1)S(1)}, bf16[2,48,2048]{2,1,0:T(8,128)(2,1)S(1)}) custom-call(bf16[1,192,8192]{2,1,0:T(8,128)(2,1)} %hidden.5, bf16[2048,128]{1,0:T(8,128)(2,1)} %w_key.5, bf16[2048,128]{1,0:T(8,128)(2,1)} %w_value.5), custom_call_target="tpu_custom_call" | custom-call | tf_op jit(solution)/shard_map/pick_sent/pallas_call | solution.py:49
  1.8 3.1 %collective-permute-start.3 = (bf16[2,48,2048]{2,1,0:T(8,128)(2,1)S(1)}, bf16[2,48,2048]{2,1,0:T(8,128)(2,1)S(1)}, u32[]{:S(2)}, u32[]{:S(2)}) collective-permute-start(bf16[2,48,2048]{2,1,0:T(8,128)(2,1)S(1)} %get-tuple-element.28), channel_id=1, source_target_pairs={{0,4},{4,0},{8,12},{12,8},{1,5},{5,1},{9,13},{13,9},{2,6},{6,2},{1... | collective-permute-start | bytes 1179656 | tf_op jit(solution)/shard_map/ppermute | solution.py:545
  4.9 2.6 %collective-permute-start = (bf16[2048,128]{1,0:T(8,128)(2,1)S(1)}, bf16[2048,128]{1,0:T(8,128)(2,1)S(1)}, u32[]{:S(2)}, u32[]{:S(2)}) collective-permute-start(bf16[2048,128]{1,0:T(8,128)(2,1)S(1)} %get-tuple-element.25), channel_id=1, source_target_pairs={{0,8},{4,12},{8,0},{12,4},{1,9},{5,13},{9,1},{13,5},{2,10},{6,14},... | collective-permute-start | bytes 1572872 | tf_op jit(solution)/shard_map/ppermute | solution.py:545
  7.5 2.1 %pick_docs.1 = (bf16[4,2,128,128]{3,2,1,0:T(8,128)(2,1)S(1)}, bf16[4,2,128,128]{3,2,1,0:T(8,128)(2,1)S(1)}, bf16[4,2,128,128]{3,2,1,0:T(8,128)(2,1)S(1)}) custom-call(s32[4,16]{1,0:T(4,128)S(1)} %copy-done.2, bf16[8,128,128]{2,1,0:T(8,128)(2,1)} %rest_0_.1, bf16[8,128,128]{2,1,0:T(8,128)(2,1)} %rest_1_.1), custom_call_target="tpu_custom_call" | custom-call | tf_op jit(solution)/shard_map/pick_docs/pallas_call | solution.py:131
  9.6 0.5 collective-permute-start.2
  10.2 13.0 %collective-permute-done.3.refs_0_ = bf16[2,48,2048]{2,1,0:T(8,128)(2,1)S(1)} collective-permute-done((bf16[2,48,2048]{2,1,0:T(8,128)(2,1)S(1)}, bf16[2,48,2048]{2,1,0:T(8,128)(2,1)S(1)}, u32[]{:S(2)}, u32[]{:S(2)}) %collective-permute-start.3) | collective-permute-done | bytes 393248 | tf_op jit(solution)/shard_map/ppermute | solution.py:545
  23.2 2.0 %collective-permute-start.5 = (bf16[2,48,2048]{2,1,0:T(8,128)(2,1)S(1)}, bf16[2,48,2048]{2,1,0:T(8,128)(2,1)S(1)}, u32[]{:S(2)}, u32[]{:S(2)}) collective-permute-start(bf16[2,48,2048]{2,1,0:T(8,128)(2,1)S(1)} %gate.3.rest_0_), channel_id=1, source_target_pairs={{0,2},{1,3},{2,0},{3,1},{4,6},{5,7},{6,4},{7,5},{8,10},{9,11},{10,... | collective-permute-start | bytes 1179656 | tf_op jit(solution)/shard_map/ppermute | solution.py:545
  25.2 5.4 %collective-permute-done.refs_2_ = bf16[2048,128]{1,0:T(8,128)(2,1)S(1)} collective-permute-done((bf16[2048,128]{1,0:T(8,128)(2,1)S(1)}, bf16[2048,128]{1,0:T(8,128)(2,1)S(1)}, u32[]{:S(2)}, u32[]{:S(2)}) %collective-permute-start) | collective-permute-done | bytes 524320 | tf_op jit(solution)/shard_map/ppermute | solution.py:545
  30.6 1.5 %collective-permute-start.1 = (bf16[2048,128]{1,0:T(8,128)(2,1)S(1)}, bf16[2048,128]{1,0:T(8,128)(2,1)S(1)}, u32[]{:S(2)}, u32[]{:S(2)}) collective-permute-start(bf16[2048,128]{1,0:T(8,128)(2,1)S(1)} %get-tuple-element.26.w_far), channel_id=1, source_target_pairs={{0,16},{16,0},{1,17},{17,1},{2,18},{18,2},{3,19},{19,3},{4,20},{20... | collective-permute-start | bytes 1572872 | tf_op jit(solution)/shard_map/ppermute | solution.py:545
  32.1 3.0 %collective-permute-start.10 = (bf16[4,2,128,128]{3,2,1,0:T(8,128)(2,1)S(1)}, bf16[4,2,128,128]{3,2,1,0:T(8,128)(2,1)S(1)}, u32[]{:S(2)}, u32[]{:S(2)}) collective-permute-start(bf16[4,2,128,128]{3,2,1,0:T(8,128)(2,1)S(1)} %get-tuple-element.40), channel_id=1, source_target_pairs={{0,12},{4,8},{8,4},{12,0},{1,13},{5,9},{9,5},{13,1},{2,14},{6,10},... | collective-permute-start | bytes 786440 | tf_op jit(solution)/shard_map/ppermute | solution.py:545
  35.2 0.1 collective-permute-start.6
  35.2 1.6 %project_near.1.near = f32[192,256]{1,0:T(8,128)S(1)} custom-call(bf16[1,192,8192]{2,1,0:T(8,128)(2,1)S(1)} %copy-done, bf16[2048,128]{1,0:T(8,128)(2,1)} %w_key.5, bf16[2048,128]{1,0:T(8,128)(2,1)} %w_value.5, bf16[4,2,128,128]{3,2,1,0:T(8,128)(2,1)S(1)} %collective-permute-done.2._.rest_4_), custom_call_target="tpu_custom_call" | custom-call | flops 10000000000 | bytes 1 | tf_op jit(solution)/shard_map/project_near/pallas_call | solution.py:216
  36.9 0.1 collective-permute-done.6.rest_3_
  36.9 1.6 %project_neighbour.1.neighbour = f32[192,256]{1,0:T(8,128)S(1)} custom-call(bf16[2048,128]{1,0:T(8,128)(2,1)} %w_key.5, bf16[2048,128]{1,0:T(8,128)(2,1)} %w_value.5, bf16[2,48,2048]{2,1,0:T(8,128)(2,1)S(1)} %gate.3.rest_0_, bf16[2,48,2048]{2,1,0:T(8,128)(2,1)S(1)} %collective-permute-done.4.rest_1_, ...), custom_call_target="tpu_custom_call" | custom-call | flops 1 | bytes 1 | tf_op jit(solution)/shard_map/project_neighbour/pallas_call | solution.py:226
  38.6 4.4 %collective-permute-done.1.w_swapped = bf16[2048,128]{1,0:T(8,128)(2,1)S(1)} collective-permute-done((bf16[2048,128]{1,0:T(8,128)(2,1)S(1)}, bf16[2048,128]{1,0:T(8,128)(2,1)S(1)}, u32[]{:S(2)}, u32[]{:S(2)}) %collective-permute-start.1) | collective-permute-done | bytes 524320 | tf_op jit(solution)/shard_map/ppermute | solution.py:545
  43.0 1.9 %project_far.1 = (f32[192,256]{1,0:T(8,128)S(1)}, bf16[192,128]{1,0:T(8,128)(2,1)S(1)}, bf16[192,128]{1,0:T(8,128)(2,1)S(1)}) custom-call(bf16[1,192,8192]{2,1,0:T(8,128)(2,1)S(1)} %copy-done, bf16[2048,128]{1,0:T(8,128)(2,1)S(1)} %get-tuple-element.26.w_far, bf16[2048,128]{1,0:T(8,128)(2,1)S(1)} %collective-permute-done.1.w_swapped, ...), custom_call_target="tpu_custom_call" | custom-call | flops 1 | bytes 1 | tf_op jit(solution)/shard_map/project_far/pallas_call | solution.py:240
  45.0 2.0 %collective-permute-start.8 = (bf16[192,128]{1,0:T(8,128)(2,1)S(1)}, bf16[192,128]{1,0:T(8,128)(2,1)S(1)}, u32[]{:S(2)}, u32[]{:S(2)}) collective-permute-start(bf16[192,128]{1,0:T(8,128)(2,1)S(1)} %get-tuple-element.31), channel_id=1, source_target_pairs={{0,4},{4,0},{8,12},{12,8},{1,5},{5,1},{9,13},{13,9},{2,6},{6,2},{1... | collective-permute-start | bytes 147464 | tf_op jit(solution)/shard_map/ppermute | solution.py:545
  47.1 1.4 %plan.1 = (bf16[1536,256]{1,0:T(8,128)(2,1)S(1)}, bf16[2048,128]{1,0:T(8,128)(2,1)S(1)}, bf16[16,2048]{1,0:T(8,128)(2,1)S(1)}, f32[1,2048]{1,0:T(1,128)S(1)}, s3...) custom-call(s32[4,16]{1,0:T(4,128)S(1)} %copy-done.2, s32[32]{0:T(128)S(1)} %copy-done.4, ...), custom_call_target="tpu_custom_call" | custom-call | tf_op jit(solution)/shard_map/plan/pallas_call | solution.py:344
  48.4 1.2 %collective-permute-done.7.arrived_k = bf16[192,128]{1,0:T(8,128)(2,1)S(1)} collective-permute-done((bf16[192,128]{1,0:T(8,128)(2,1)S(1)}, bf16[192,128]{1,0:T(8,128)(2,1)S(1)}, u32[]{:S(2)}, u32[]{:S(2)}) %collective-permute-start.7) | collective-permute-done | bytes 49184 | tf_op jit(solution)/shard_map/ppermute | solution.py:545
  49.6 1.1 %collective-permute-done.8.arrived_v = bf16[192,128]{1,0:T(8,128)(2,1)S(1)} collective-permute-done((bf16[192,128]{1,0:T(8,128)(2,1)S(1)}, bf16[192,128]{1,0:T(8,128)(2,1)S(1)}, u32[]{:S(2)}, u32[]{:S(2)}) %collective-permute-start.8) | collective-permute-done | bytes 49184 | tf_op jit(solution)/shard_map/ppermute | solution.py:545
  50.7 0.8 %finish.1 = (bf16[192,256]{1,0:T(8,128)(2,1)S(1)}, bf16[192,256]{1,0:T(8,128)(2,1)}) custom-call(f32[192,256]{1,0:T(8,128)S(1)} %get-tuple-element.29.own, bf16[192,128]{1,0:T(8,128)(2,1)S(1)} %collective-permute-done.7.arrived_k, bf16[192,128]{1,0:T(8,128)(2,1)S(1)} %collective-permute-done.8.arrived_v, s32[1,192]{1,0:T(1,128)S(1)} %get-tuple-element.32.slot_row), custom_call_target="tpu_custom_call" | custom-call | tf_op jit(solution)/shard_map/finish/pallas_call | solution.py:366
  51.5 7.9 %all-to-all-start = ((bf16[4,48,256]{2,1,0:T(8,128)(2,1)}), bf16[4,48,256]{2,1,0:T(8,128)(2,1)S(1)}, u32[]{:S(2)}, u32[]{:S(2)}) async-start(bf16[4,48,256]{2,1,0:T(8,128)(2,1)} %bitcast.1), calls=%async_computation | async-start | bytes 196608 | tf_op jit(solution)/shard_map/all_to_all | solution.py:590
  59.5 7.5 %attend.1 = bf16[1,192,1024]{2,1,0:T(8,128)(2,1)} custom-call(s32[4,16]{1,0:T(4,128)S(1)} %copy-done.2, bf16[1536,256]{1,0:T(8,128)(2,1)S(1)} %get-tuple-element.22.q, bf16[192,256]{1,0:T(8,128)(2,1)S(1)} %get-tuple-element.33.fresh, bf16[2048,128]{1,0:T(8,128)(2,1)S(1)} %get-tuple-element.34.held, bf16[16,2048]{1,0:T(8,128)(2,1)S(1)} %get-tuple-element.35.spare, ...), custom_call_target="tpu_custom_call" | custom-call | tf_op jit(solution)/shard_map/attend/pallas_call | solution.py:498
  67.0 0.7 broadcast_in_dim_reshape.3
  (21 shorter events, 0.1 us)
Async XLA Ops:
  0.6 6.9 %copy-start.2 = (s32[4,16]{1,0:T(4,128)S(1)}, s32[4,16]{1,0:T(4,128)}, u32[]{:S(2)}) copy-start(s32[4,16]{1,0:T(4,128)} %request_docs.5) | copy-start | bytes 772
  1.8 21.3 %collective-permute-start.3 = (bf16[2,48,2048]{2,1,0:T(8,128)(2,1)S(1)}, bf16[2,48,2048]{2,1,0:T(8,128)(2,1)S(1)}, u32[]{:S(2)}, u32[]{:S(2)}) collective-permute-start(bf16[2,48,2048]{2,1,0:T(8,128)(2,1)S(1)} %get-tuple-element.28), channel_id=1, source_target_pairs={{0,4},{4,0},{8,12},{12,8},{1,5},{5,1},{9,13},{13,9},{2,6},{6,2},{1... | collective-permute-start | bytes 1179656 | tf_op jit(solution)/shard_map/ppermute | solution.py:545
  4.9 25.7 %collective-permute-start = (bf16[2048,128]{1,0:T(8,128)(2,1)S(1)}, bf16[2048,128]{1,0:T(8,128)(2,1)S(1)}, u32[]{:S(2)}, u32[]{:S(2)}) collective-permute-start(bf16[2048,128]{1,0:T(8,128)(2,1)S(1)} %get-tuple-element.25), channel_id=1, source_target_pairs={{0,8},{4,12},{8,0},{12,4},{1,9},{5,13},{9,1},{13,5},{2,10},{6,14},... | collective-permute-start | bytes 1572872 | tf_op jit(solution)/shard_map/ppermute | solution.py:545
  9.6 25.5 %collective-permute-start.2 = (bf16[4,2,128,128]{3,2,1,0:T(8,128)(2,1)S(1)}, bf16[4,2,128,128]{3,2,1,0:T(8,128)(2,1)S(1)}, u32[]{:S(2)}, u32[]{:S(2)}) collective-permute-start(bf16[4,2,128,128]{3,2,1,0:T(8,128)(2,1)S(1)} %get-tuple-element.27.refs_1_), channel_id=1, source_target_pairs={{0,4},{4,0},{8,12},{12,8},{1,5},{5,1},{9,13},{13,9},{2,6},{6,2},{1... | collective-permute-start | bytes 786440 | tf_op jit(solution)/shard_map/ppermute | solution.py:545
  23.2 12.0 %collective-permute-start.5 = (bf16[2,48,2048]{2,1,0:T(8,128)(2,1)S(1)}, bf16[2,48,2048]{2,1,0:T(8,128)(2,1)S(1)}, u32[]{:S(2)}, u32[]{:S(2)}) collective-permute-start(bf16[2,48,2048]{2,1,0:T(8,128)(2,1)S(1)} %gate.3.rest_0_), channel_id=1, source_target_pairs={{0,2},{1,3},{2,0},{3,1},{4,6},{5,7},{6,4},{7,5},{8,10},{9,11},{10,... | collective-permute-start | bytes 1179656 | tf_op jit(solution)/shard_map/ppermute | solution.py:545
  25.1 11.7 %collective-permute-start.4 = (bf16[2,48,2048]{2,1,0:T(8,128)(2,1)S(1)}, bf16[2,48,2048]{2,1,0:T(8,128)(2,1)S(1)}, u32[]{:S(2)}, u32[]{:S(2)}) collective-permute-start(bf16[2,48,2048]{2,1,0:T(8,128)(2,1)S(1)} %gate.3.rest_0_), channel_id=1, source_target_pairs={{0,1},{1,0},{2,3},{3,2},{4,5},{5,4},{6,7},{7,6},{8,9},{9,8},{10,11... | collective-permute-start | bytes 1179656 | tf_op jit(solution)/shard_map/ppermute | solution.py:545
  30.6 4.6 %copy-start = (bf16[1,192,8192]{2,1,0:T(8,128)(2,1)S(1)}, bf16[1,192,8192]{2,1,0:T(8,128)(2,1)}, u32[]{:S(2)}) copy-start(bf16[1,192,8192]{2,1,0:T(8,128)(2,1)} %hidden.5) | copy-start | bytes 9437188
  30.6 12.4 %collective-permute-start.1 = (bf16[2048,128]{1,0:T(8,128)(2,1)S(1)}, bf16[2048,128]{1,0:T(8,128)(2,1)S(1)}, u32[]{:S(2)}, u32[]{:S(2)}) collective-permute-start(bf16[2048,128]{1,0:T(8,128)(2,1)S(1)} %get-tuple-element.26.w_far), channel_id=1, source_target_pairs={{0,16},{16,0},{1,17},{17,1},{2,18},{18,2},{3,19},{19,3},{4,20},{20... | collective-permute-start | bytes 1572872 | tf_op jit(solution)/shard_map/ppermute | solution.py:545
  32.1 27.3 %collective-permute-start.10 = (bf16[4,2,128,128]{3,2,1,0:T(8,128)(2,1)S(1)}, bf16[4,2,128,128]{3,2,1,0:T(8,128)(2,1)S(1)}, u32[]{:S(2)}, u32[]{:S(2)}) collective-permute-start(bf16[4,2,128,128]{3,2,1,0:T(8,128)(2,1)S(1)} %get-tuple-element.40), channel_id=1, source_target_pairs={{0,12},{4,8},{8,4},{12,0},{1,13},{5,9},{9,5},{13,1},{2,14},{6,10},... | collective-permute-start | bytes 786440 | tf_op jit(solution)/shard_map/ppermute | solution.py:545
  35.1 24.3 %collective-permute-start.9 = (bf16[4,2,128,128]{3,2,1,0:T(8,128)(2,1)S(1)}, bf16[4,2,128,128]{3,2,1,0:T(8,128)(2,1)S(1)}, u32[]{:S(2)}, u32[]{:S(2)}) collective-permute-start(bf16[4,2,128,128]{3,2,1,0:T(8,128)(2,1)S(1)} %get-tuple-element.39), channel_id=1, source_target_pairs={{0,8},{4,12},{8,0},{12,4},{1,9},{5,13},{9,1},{13,5},{2,10},{6,14},... | collective-permute-start | bytes 786440 | tf_op jit(solution)/shard_map/ppermute | solution.py:545
  35.2 1.8 %collective-permute-start.6 = (bf16[2,48,2048]{2,1,0:T(8,128)(2,1)S(1)}, bf16[2,48,2048]{2,1,0:T(8,128)(2,1)S(1)}, u32[]{:S(2)}, u32[]{:S(2)}) collective-permute-start(bf16[2,48,2048]{2,1,0:T(8,128)(2,1)S(1)} %collective-permute-done.5.rest_2_), channel_id=1, source_target_pairs={{0,1},{1,0},{2,3},{3,2},{4,5},{5,4},{6,7},{7,6},{8,9},{9,8},{10,11... | collective-permute-start | bytes 1179656 | tf_op jit(solution)/shard_map/ppermute | solution.py:545
  38.6 8.5 %copy-start.1 = (bf16[1,192,1024]{2,1,0:T(8,128)(2,1)S(1)}, bf16[1,192,1024]{2,1,0:T(8,128)(2,1)}, u32[]{:S(2)}) copy-start(bf16[1,192,1024]{2,1,0:T(8,128)(2,1)} %queries.1) | copy-start | bytes 1179652
  38.6 8.5 %copy-start.3 = (s32[1,16,12]{1,0,2:T(1,128)S(1)}, s32[1,16,12]{1,0,2:T(1,128)}, u32[]{:S(2)}) copy-start(s32[1,16,12]{1,0,2:T(1,128)} %param.17) | copy-start | bytes 2308
  38.6 8.4 %copy-start.4 = (s32[32]{0:T(128)S(1)}, s32[32]{0:T(128)}, u32[]{:S(2)}) copy-start(s32[32]{0:T(128)} %doc_lengths.1) | copy-start | bytes 388
  45.0 4.7 %collective-permute-start.7 = (bf16[192,128]{1,0:T(8,128)(2,1)S(1)}, bf16[192,128]{1,0:T(8,128)(2,1)S(1)}, u32[]{:S(2)}, u32[]{:S(2)}) collective-permute-start(bf16[192,128]{1,0:T(8,128)(2,1)S(1)} %get-tuple-element.30), channel_id=1, source_target_pairs={{0,4},{4,0},{8,12},{12,8},{1,5},{5,1},{9,13},{13,9},{2,6},{6,2},{1... | collective-permute-start | bytes 147464 | tf_op jit(solution)/shard_map/ppermute | solution.py:545
  45.0 5.7 %collective-permute-start.8 = (bf16[192,128]{1,0:T(8,128)(2,1)S(1)}, bf16[192,128]{1,0:T(8,128)(2,1)S(1)}, u32[]{:S(2)}, u32[]{:S(2)}) collective-permute-start(bf16[192,128]{1,0:T(8,128)(2,1)S(1)} %get-tuple-element.31), channel_id=1, source_target_pairs={{0,4},{4,0},{8,12},{12,8},{1,5},{5,1},{9,13},{13,9},{2,6},{6,2},{1... | collective-permute-start | bytes 147464 | tf_op jit(solution)/shard_map/ppermute | solution.py:545
  51.5 15.4 %all-to-all-start = ((bf16[4,48,256]{2,1,0:T(8,128)(2,1)}), bf16[4,48,256]{2,1,0:T(8,128)(2,1)S(1)}, u32[]{:S(2)}, u32[]{:S(2)}) async-start(bf16[4,48,256]{2,1,0:T(8,128)(2,1)} %bitcast.1), calls=%async_computation | async-start | bytes 196608 | tf_op jit(solution)/shard_map/all_to_all | solution.py:590

commit v15 on v14

--- a/solution.py
+++ b/solution.py
@@ -19,7 +19,7 @@
     return pltpu.with_memory_space_constraint(array, pltpu.HBM)
 
 
-def send_kernel(hidden, w_key, w_value, w_out, h_out, sems):
+def send_kernel(hidden, w_key, w_value, w_first, w_second, h_out, sems):
     group = lax.axis_index("groups")
     me = lax.axis_index("seq")
     rows, depth = h_out.shape[1:]
@@ -27,7 +27,9 @@
 
         @pl.when(group == chosen)
         def _():
-            pltpu.make_async_copy(weight, w_out, sems.at[0]).start()
+            for i, out in enumerate((w_first, w_second)):
+                half = weight.at[pl.ds(i * out.shape[0], out.shape[0])]
+                pltpu.make_async_copy(half, out, sems.at[i]).start()
 
     first = me + 1 - 2 * lax.rem(me, 2)
     copies = []
@@ -37,24 +39,27 @@
             pl.ds(pl.multiple_of(lax.axis_index("tp") * rows, rows), rows),
             pl.ds(pl.multiple_of(block * depth, depth), depth),
         ]
-        copies.append(pltpu.make_async_copy(source, h_out.at[i], sems.at[1 + i]))
+        copies.append(pltpu.make_async_copy(source, h_out.at[i], sems.at[2 + i]))
         copies[-1].start()
-    pltpu.make_async_copy(w_key, w_out, sems.at[0]).wait()
+    for i, out in enumerate((w_first, w_second)):
+        pltpu.make_async_copy(w_key.at[pl.ds(0, out.shape[0])], out, sems.at[i]).wait()
     for copy in copies:
         copy.wait()
 
 
 def pick_sent(hidden, w_key, w_value):
     h_shape = (2, hidden.shape[1] // 4, w_key.shape[0])
+    half = jax.ShapeDtypeStruct((w_key.shape[0] // 2, w_key.shape[1]), jnp.bfloat16)
     return pl.pallas_call(
         send_kernel,
         out_shape=(
-            jax.ShapeDtypeStruct(w_key.shape, jnp.bfloat16),
+            half,
+            half,
             jax.ShapeDtypeStruct(h_shape, jnp.bfloat16),
         ),
         in_specs=[ANY] * 3,
-        out_specs=(VMEM, VMEM),
-        scratch_shapes=[pltpu.SemaphoreType.DMA((3,))],
+        out_specs=(VMEM,) * 3,
+        scratch_shapes=[pltpu.SemaphoreType.DMA((4,))],
         compiler_params=pltpu.CompilerParams(vmem_limit_bytes=16 * 1024 * 1024),
         name="pick_sent",
     )(in_hbm(hidden), in_hbm(w_key), in_hbm(w_value))
@@ -181,18 +186,22 @@
     total[...] = jnp.dot(n[...], w[...], preferred_element_type=jnp.float32)
 
 
-def far_kernel(hidden, w_far, w_swapped, near, neighbour, *rest):
+def far_kernel(hidden, w_far_0, w_far_1, w_swapped_0, w_swapped_1, near, neighbour, *rest):
     *quarters, own, part_k, part_v, w, h, n, sems = rest
     group = lax.axis_index("groups")
-    depth, width = w_far.shape
+    half, width = w_far_0.shape
+    depth = 2 * half
     copies = []
 
     def copy(source, target):
         copies.append(pltpu.make_async_copy(source, target, sems.at[len(copies)]))
         copies[-1].start()
 
-    for held, place in ((w_far, group), (w_swapped, 1 - group)):
-        copy(held, w.at[:, pl.ds(pl.multiple_of(place * width, width), width)])
+    halves = ((w_far_0, w_far_1, group), (w_swapped_0, w_swapped_1, 1 - group))
+    for first, second, place in halves:
+        columns = pl.ds(pl.multiple_of(place * width, width), width)
+        copy(first, w.at[pl.ds(0, half), columns])
+        copy(second, w.at[pl.ds(half, half), columns])
     start = pl.multiple_of(lax.rem(lax.axis_index("seq") + 2, 4) * depth, depth)
     copy(hidden.at[0, :, pl.ds(start, depth)], h)
     lay_quarters(quarters, 1, n, copy)
@@ -240,18 +249,18 @@
     return pl.pallas_call(
         far_kernel,
         out_shape=(sums,) + (jax.ShapeDtypeStruct((rows, width), jnp.bfloat16),) * 2,
-        in_specs=[ANY] * 3 + [VMEM] * 2 + [ANY] * len(quarters),
+        in_specs=[ANY] * 5 + [VMEM] * 2 + [ANY] * len(quarters),
         out_specs=(VMEM,) * 3,
         scratch_shapes=[
             w_scratch,
             h_scratch,
             h_scratch,
-            pltpu.SemaphoreType.DMA((3 + len(quarters),)),
+            pltpu.SemaphoreType.DMA((5 + len(quarters),)),
         ],
         compiler_params=limit,
         cost_estimate=cheap,
         name="project_far",
-    )(hidden, w_far, w_swapped, near, neighbour, *quarters)
+    )(hidden, *w_far, *w_swapped, near, neighbour, *quarters)
 
 
 def plan_kernel(
@@ -544,15 +553,18 @@
             count = lax.axis_size(axis)
             return lax.ppermute(array, axis, [(i, i ^ apart) for i in range(count)])
 
-        w_send, h_send = pick_sent(hidden, w_key, w_value)
-        w_far = swap(w_send, "seq", 2)
+        *w_send, h_send = pick_sent(hidden, w_key, w_value)
+        w_far = [swap(half, "seq", 2) for half in w_send]
         h_mine = swap(h_send, "seq", 1)
         doc_1, doc_2, doc_3 = pick_docs(request_docs, store_keys, store_values, False)
         (h_mine,) = gate((h_mine,), (doc_1,), cost=8000000000)
         h_chip = swap(h_mine, "tp", 2)
         h_core = swap(h_mine, "tp", 1)
-        doc_2, doc_3, w_far = gate((doc_2, doc_3, w_far), cost=8000000000)
-        w_swapped = swap(w_far, "groups", 1)
+        w_swapped = [swap(w_far[0], "groups", 1)]
+        doc_2, doc_3, w_far[1] = gate(
+            (doc_2, doc_3, w_far[1]), (w_swapped[0],), cost=8 * 10**9
+        )
+        w_swapped.append(swap(w_far[1], "groups", 1))
         doc_1 = swap(doc_1, "seq", 1)
         docs = (swap(doc_2, "seq", 2), swap(doc_3, "seq", 3), doc_1)
         quarters = (h_mine, h_core, h_chip, swap(h_chip, "tp", 1))

time: 68.1 us -> 65.5 us (0.962)
  waiting for transfers between devices: 25.2 us -> 22.5 us
    ppermute x11 -> x13, starting transfers between devices: 14.9 us -> 19.1 us  [swap(): return lax.ppermute(array, axis, [(i, i ^ apart) for i in range(count)])]
    all_to_all x1, starting transfers between devices: 7.95 us -> 3.75 us  [shards(): lax.all_to_all(outgoing, 'seq', split_axis=0, concat_axis=0, tiled=True)]
    ppermute x11 -> x13, waiting for transfers between devices: 25.2 us -> 22.5 us  [swap(): return lax.ppermute(array, axis, [(i, i ^ apart) for i in range(count)])]
  transfers between devices with their start and end apart: 12 -> 14, of which waited for: 6 -> 7; matrix products, arithmetic and copies ran while one was open for 0% -> 0% of each run, Pallas kernels for 25% -> 26%
where the time goes in v15:
time: 65.5 us; the launch traced here: 65 us
  starting transfers between devices  22.8 us (35%)
  waiting for transfers between devices  22.5 us (34%)
  Pallas kernels  18.2 us (28%)
  between operations  0.76 us (1%)
  local copies, waits for them, and re-layouts  0.7 us (1%)
    ppermute x13, waiting for transfers between devices, swap(): return lax.ppermute(array, axis, [(i, i ^ apart) for i in range(count)])  22.5 us
    ppermute x13, starting transfers between devices, swap(): return lax.ppermute(array, axis, [(i, i ^ apart) for i in range(count)])  19.1 us
    pallas_call x1, Pallas kernels, attend(): pl.pallas_call(functools.partial(attend_kernel, by_owner), out_shape=jax....  7.4 us
    all_to_all x1, starting transfers between devices, shards(): lax.all_to_all(outgoing, 'seq', split_axis=0, concat_axis=0, tiled=True)  3.75 us
    pallas_call x1, Pallas kernels, pick_docs(): pl.pallas_call(functools.partial(docs_kernel, by_owner), out_shape=tuple(...  2.21 us
    pallas_call x1, Pallas kernels, project(): pl.pallas_call(far_kernel, out_shape=(sums,) + (jax.ShapeDtypeStruct((row...  1.96 us
    pallas_call x1, Pallas kernels, project(): pl.pallas_call(neighbour_kernel, out_shape=sums, in_specs=[ANY] * (2 + le...  1.64 us
    pallas_call x1, Pallas kernels, project(): pl.pallas_call(near_kernel, out_shape=sums, in_specs=[ANY] * 4, out_specs...  1.61 us
  transfers between devices with their start and end apart: 14, of which 7 were waited for; matrix products, arithmetic and copies ran while one was open for 0% of the time, Pallas kernels for 26%

profile of v15, /device:TPU:0, one launch (start us, length us, event | category | flops | bytes accessed | tf_op | source)
XLA Modules:
  0.0 65.0 jit_solution(6990200718872522223)
XLA Ops:
  0.6 1.2 %pick_sent.1 = (bf16[1024,128]{1,0:T(8,128)(2,1)S(1)}, bf16[1024,128]{1,0:T(8,128)(2,1)S(1)}, bf16[2,48,2048]{2,1,0:T(8,128)(2,1)S(1)}) custom-call(bf16[1,192,8192]{2,1,0:T(8,128)(2,1)} %hidden.5, bf16[2048,128]{1,0:T(8,128)(2,1)} %w_key.5, bf16[2048,128]{1,0:T(8,128)(2,1)} %w_value.5), custom_call_target="tpu_custom_call" | custom-call | tf_op jit(solution)/shard_map/pick_sent/pallas_call | solution.py:53
  1.8 3.1 %collective-permute-start.5 = (bf16[2,48,2048]{2,1,0:T(8,128)(2,1)S(1)}, bf16[2,48,2048]{2,1,0:T(8,128)(2,1)S(1)}, u32[]{:S(2)}, u32[]{:S(2)}) collective-permute-start(bf16[2,48,2048]{2,1,0:T(8,128)(2,1)S(1)} %get-tuple-element.30), channel_id=1, source_target_pairs={{0,4},{4,0},{8,12},{12,8},{1,5},{5,1},{9,13},{13,9},{2,6},{6,2},{1... | collective-permute-start | bytes 1179656 | tf_op jit(solution)/shard_map/ppermute | solution.py:554
  4.9 2.6 %collective-permute-start = (bf16[1024,128]{1,0:T(8,128)(2,1)S(1)}, bf16[1024,128]{1,0:T(8,128)(2,1)S(1)}, u32[]{:S(2)}, u32[]{:S(2)}) collective-permute-start(bf16[1024,128]{1,0:T(8,128)(2,1)S(1)} %get-tuple-element.24), channel_id=1, source_target_pairs={{0,8},{4,12},{8,0},{12,4},{1,9},{5,13},{9,1},{13,5},{2,10},{6,14},... | collective-permute-start | bytes 786440 | tf_op jit(solution)/shard_map/ppermute | solution.py:554
  7.5 2.2 %pick_docs.1 = (bf16[4,2,128,128]{3,2,1,0:T(8,128)(2,1)S(1)}, bf16[4,2,128,128]{3,2,1,0:T(8,128)(2,1)S(1)}, bf16[4,2,128,128]{3,2,1,0:T(8,128)(2,1)S(1)}) custom-call(s32[4,16]{1,0:T(4,128)S(1)} %copy-done.2, bf16[8,128,128]{2,1,0:T(8,128)(2,1)} %rest_0_.1, bf16[8,128,128]{2,1,0:T(8,128)(2,1)} %rest_1_.1), custom_call_target="tpu_custom_call" | custom-call | tf_op jit(solution)/shard_map/pick_docs/pallas_call | solution.py:136
  10.2 9.9 %collective-permute-done.w_far_0 = bf16[1024,128]{1,0:T(8,128)(2,1)S(1)} collective-permute-done((bf16[1024,128]{1,0:T(8,128)(2,1)S(1)}, bf16[1024,128]{1,0:T(8,128)(2,1)S(1)}, u32[]{:S(2)}, u32[]{:S(2)}) %collective-permute-start) | collective-permute-done | bytes 262176 | tf_op jit(solution)/shard_map/ppermute | solution.py:554
  20.1 1.5 %collective-permute-start.2 = (bf16[1024,128]{1,0:T(8,128)(2,1)S(1)}, bf16[1024,128]{1,0:T(8,128)(2,1)S(1)}, u32[]{:S(2)}, u32[]{:S(2)}) collective-permute-start(bf16[1024,128]{1,0:T(8,128)(2,1)S(1)} %collective-permute-done.w_far_0), channel_id=1, source_target_pairs={{0,16},{16,0},{1,17},{17,1},{2,18},{18,2},{3,19},{19,3},{4,20},{20... | collective-permute-start | bytes 786440 | tf_op jit(solution)/shard_map/ppermute | solution.py:554
  21.6 4.5 %collective-permute-done.5.refs_0_ = bf16[2,48,2048]{2,1,0:T(8,128)(2,1)S(1)} collective-permute-done((bf16[2,48,2048]{2,1,0:T(8,128)(2,1)S(1)}, bf16[2,48,2048]{2,1,0:T(8,128)(2,1)S(1)}, u32[]{:S(2)}, u32[]{:S(2)}) %collective-permute-start.5) | collective-permute-done | bytes 393248 | tf_op jit(solution)/shard_map/ppermute | solution.py:554
  26.1 2.0 %collective-permute-start.7 = (bf16[2,48,2048]{2,1,0:T(8,128)(2,1)S(1)}, bf16[2,48,2048]{2,1,0:T(8,128)(2,1)S(1)}, u32[]{:S(2)}, u32[]{:S(2)}) collective-permute-start(bf16[2,48,2048]{2,1,0:T(8,128)(2,1)S(1)} %gate.3.rest_0_), channel_id=1, source_target_pairs={{0,2},{1,3},{2,0},{3,1},{4,6},{5,7},{6,4},{7,5},{8,10},{9,11},{10,... | collective-permute-start | bytes 1179656 | tf_op jit(solution)/shard_map/ppermute | solution.py:554
  28.1 2.1 %collective-permute-done.1.refs_2_ = bf16[1024,128]{1,0:T(8,128)(2,1)S(1)} collective-permute-done((bf16[1024,128]{1,0:T(8,128)(2,1)S(1)}, bf16[1024,128]{1,0:T(8,128)(2,1)S(1)}, u32[]{:S(2)}, u32[]{:S(2)}) %collective-permute-start.1) | collective-permute-done | bytes 262176 | tf_op jit(solution)/shard_map/ppermute | solution.py:554
  30.2 3.4 %collective-permute-start.11 = (bf16[4,2,128,128]{3,2,1,0:T(8,128)(2,1)S(1)}, bf16[4,2,128,128]{3,2,1,0:T(8,128)(2,1)S(1)}, u32[]{:S(2)}, u32[]{:S(2)}) collective-permute-start(bf16[4,2,128,128]{3,2,1,0:T(8,128)(2,1)S(1)} %get-tuple-element.41), channel_id=1, source_target_pairs={{0,8},{4,12},{8,0},{12,4},{1,9},{5,13},{9,1},{13,5},{2,10},{6,14},... | collective-permute-start | bytes 786440 | tf_op jit(solution)/shard_map/ppermute | solution.py:554
  33.6 2.5 %collective-permute-start.12 = (bf16[4,2,128,128]{3,2,1,0:T(8,128)(2,1)S(1)}, bf16[4,2,128,128]{3,2,1,0:T(8,128)(2,1)S(1)}, u32[]{:S(2)}, u32[]{:S(2)}) collective-permute-start(bf16[4,2,128,128]{3,2,1,0:T(8,128)(2,1)S(1)} %get-tuple-element.42), channel_id=1, source_target_pairs={{0,12},{4,8},{8,4},{12,0},{1,13},{5,9},{9,5},{13,1},{2,14},{6,10},... | collective-permute-start | bytes 786440 | tf_op jit(solution)/shard_map/ppermute | solution.py:554
  36.1 1.5 %collective-permute-start.3 = (bf16[1024,128]{1,0:T(8,128)(2,1)S(1)}, bf16[1024,128]{1,0:T(8,128)(2,1)S(1)}, u32[]{:S(2)}, u32[]{:S(2)}) collective-permute-start(bf16[1024,128]{1,0:T(8,128)(2,1)S(1)} %get-tuple-element.28.w_far_1), channel_id=1, source_target_pairs={{0,16},{16,0},{1,17},{17,1},{2,18},{18,2},{3,19},{19,3},{4,20},{20... | collective-permute-start | bytes 786440 | tf_op jit(solution)/shard_map/ppermute | solution.py:554
  37.6 1.6 %project_near.1.near = f32[192,256]{1,0:T(8,128)S(1)} custom-call(bf16[1,192,8192]{2,1,0:T(8,128)(2,1)S(1)} %copy-done, bf16[2048,128]{1,0:T(8,128)(2,1)} %w_key.5, bf16[2048,128]{1,0:T(8,128)(2,1)} %w_value.5, bf16[4,2,128,128]{3,2,1,0:T(8,128)(2,1)S(1)} %collective-permute-done.4._.rest_4_), custom_call_target="tpu_custom_call" | custom-call | flops 10000000000 | bytes 1 | tf_op jit(solution)/shard_map/project_near/pallas_call | solution.py:225
  39.3 1.6 %project_neighbour.1.neighbour = f32[192,256]{1,0:T(8,128)S(1)} custom-call(bf16[2048,128]{1,0:T(8,128)(2,1)} %w_key.5, bf16[2048,128]{1,0:T(8,128)(2,1)} %w_value.5, bf16[2,48,2048]{2,1,0:T(8,128)(2,1)S(1)} %gate.3.rest_0_, bf16[2,48,2048]{2,1,0:T(8,128)(2,1)S(1)} %collective-permute-done.6.rest_1_, ...), custom_call_target="tpu_custom_call" | custom-call | flops 1 | bytes 1 | tf_op jit(solution)/shard_map/project_neighbour/pallas_call | solution.py:235
  41.0 1.7 %collective-permute-done.3.w_swapped_1 = bf16[1024,128]{1,0:T(8,128)(2,1)S(1)} collective-permute-done((bf16[1024,128]{1,0:T(8,128)(2,1)S(1)}, bf16[1024,128]{1,0:T(8,128)(2,1)S(1)}, u32[]{:S(2)}, u32[]{:S(2)}) %collective-permute-start.3) | collective-permute-done | bytes 262176 | tf_op jit(solution)/shard_map/ppermute | solution.py:554
  42.7 2.0 %project_far.1 = (f32[192,256]{1,0:T(8,128)S(1)}, bf16[192,128]{1,0:T(8,128)(2,1)S(1)}, bf16[192,128]{1,0:T(8,128)(2,1)S(1)}) custom-call(bf16[1,192,8192]{2,1,0:T(8,128)(2,1)S(1)} %copy-done, bf16[1024,128]{1,0:T(8,128)(2,1)S(1)} %collective-permute-done.w_far_0, bf16[1024,128]{1,0:T(8,128)(2,1)S(1)} %get-tuple-element.28.w_far_1, ...), custom_call_target="tpu_custom_call" | custom-call | flops 1 | bytes 1 | tf_op jit(solution)/shard_map/project_far/pallas_call | solution.py:249
  44.7 2.0 %collective-permute-start.10 = (bf16[192,128]{1,0:T(8,128)(2,1)S(1)}, bf16[192,128]{1,0:T(8,128)(2,1)S(1)}, u32[]{:S(2)}, u32[]{:S(2)}) collective-permute-start(bf16[192,128]{1,0:T(8,128)(2,1)S(1)} %get-tuple-element.33), channel_id=1, source_target_pairs={{0,4},{4,0},{8,12},{12,8},{1,5},{5,1},{9,13},{13,9},{2,6},{6,2},{1... | collective-permute-start | bytes 147464 | tf_op jit(solution)/shard_map/ppermute | solution.py:554
  46.8 1.4 %plan.1 = (bf16[1536,256]{1,0:T(8,128)(2,1)S(1)}, bf16[2048,128]{1,0:T(8,128)(2,1)S(1)}, bf16[16,2048]{1,0:T(8,128)(2,1)S(1)}, f32[1,2048]{1,0:T(1,128)S(1)}, s3...) custom-call(s32[4,16]{1,0:T(4,128)S(1)} %copy-done.2, s32[32]{0:T(128)S(1)} %copy-done.4, ...), custom_call_target="tpu_custom_call" | custom-call | tf_op jit(solution)/shard_map/plan/pallas_call | solution.py:353
  48.1 2.6 %collective-permute-done.9.arrived_k = bf16[192,128]{1,0:T(8,128)(2,1)S(1)} collective-permute-done((bf16[192,128]{1,0:T(8,128)(2,1)S(1)}, bf16[192,128]{1,0:T(8,128)(2,1)S(1)}, u32[]{:S(2)}, u32[]{:S(2)}) %collective-permute-start.9) | collective-permute-done | bytes 49184 | tf_op jit(solution)/shard_map/ppermute | solution.py:554
  50.7 1.7 %collective-permute-done.10.arrived_v = bf16[192,128]{1,0:T(8,128)(2,1)S(1)} collective-permute-done((bf16[192,128]{1,0:T(8,128)(2,1)S(1)}, bf16[192,128]{1,0:T(8,128)(2,1)S(1)}, u32[]{:S(2)}, u32[]{:S(2)}) %collective-permute-start.10) | collective-permute-done | bytes 49184 | tf_op jit(solution)/shard_map/ppermute | solution.py:554
  52.4 0.8 %finish.1 = (bf16[192,256]{1,0:T(8,128)(2,1)S(1)}, bf16[192,256]{1,0:T(8,128)(2,1)}) custom-call(f32[192,256]{1,0:T(8,128)S(1)} %get-tuple-element.31.own, bf16[192,128]{1,0:T(8,128)(2,1)S(1)} %collective-permute-done.9.arrived_k, bf16[192,128]{1,0:T(8,128)(2,1)S(1)} %collective-permute-done.10.arrived_v, s32[1,192]{1,0:T(1,128)S(1)} %get-tuple-element.34.slot_row), custom_call_target="tpu_custom_call" | custom-call | tf_op jit(solution)/shard_map/finish/pallas_call | solution.py:375
  53.2 3.7 %all-to-all-start = ((bf16[4,48,256]{2,1,0:T(8,128)(2,1)}), bf16[4,48,256]{2,1,0:T(8,128)(2,1)S(1)}, u32[]{:S(2)}, u32[]{:S(2)}) async-start(bf16[4,48,256]{2,1,0:T(8,128)(2,1)} %bitcast.1), calls=%async_computation | async-start | bytes 196608 | tf_op jit(solution)/shard_map/all_to_all | solution.py:602
  56.9 7.4 %attend.1 = bf16[1,192,1024]{2,1,0:T(8,128)(2,1)} custom-call(s32[4,16]{1,0:T(4,128)S(1)} %copy-done.2, bf16[1536,256]{1,0:T(8,128)(2,1)S(1)} %get-tuple-element.23.q, bf16[192,256]{1,0:T(8,128)(2,1)S(1)} %get-tuple-element.35.fresh, bf16[2048,128]{1,0:T(8,128)(2,1)S(1)} %get-tuple-element.36.held, bf16[16,2048]{1,0:T(8,128)(2,1)S(1)} %get-tuple-element.37.spare, ...), custom_call_target="tpu_custom_call" | custom-call | tf_op jit(solution)/shard_map/attend/pallas_call | solution.py:507
  64.4 0.7 %broadcast_in_dim_reshape.3 = bf16[1,4,4,12,2,128]{5,4,3,2,1,0:T(2,128)(2,1)} reshape(bf16[4,48,256]{2,1,0:T(8,128)(2,1)S(1)} %all-to-all-done) | data formatting | bytes 196608 | tf_op jit(solution)/shard_map/broadcast_in_dim;reshape | solution.py:604
  (25 shorter events, 0.7 us)
Async XLA Ops:
  0.6 6.9 %copy-start.2 = (s32[4,16]{1,0:T(4,128)S(1)}, s32[4,16]{1,0:T(4,128)}, u32[]{:S(2)}) copy-start(s32[4,16]{1,0:T(4,128)} %request_docs.5) | copy-start | bytes 772
  1.8 24.3 %collective-permute-start.5 = (bf16[2,48,2048]{2,1,0:T(8,128)(2,1)S(1)}, bf16[2,48,2048]{2,1,0:T(8,128)(2,1)S(1)}, u32[]{:S(2)}, u32[]{:S(2)}) collective-permute-start(bf16[2,48,2048]{2,1,0:T(8,128)(2,1)S(1)} %get-tuple-element.30), channel_id=1, source_target_pairs={{0,4},{4,0},{8,12},{12,8},{1,5},{5,1},{9,13},{13,9},{2,6},{6,2},{1... | collective-permute-start | bytes 1179656 | tf_op jit(solution)/shard_map/ppermute | solution.py:554
  4.9 15.2 %collective-permute-start = (bf16[1024,128]{1,0:T(8,128)(2,1)S(1)}, bf16[1024,128]{1,0:T(8,128)(2,1)S(1)}, u32[]{:S(2)}, u32[]{:S(2)}) collective-permute-start(bf16[1024,128]{1,0:T(8,128)(2,1)S(1)} %get-tuple-element.24), channel_id=1, source_target_pairs={{0,8},{4,12},{8,0},{12,4},{1,9},{5,13},{9,1},{13,5},{2,10},{6,14},... | collective-permute-start | bytes 786440 | tf_op jit(solution)/shard_map/ppermute | solution.py:554
  9.7 26.3 %collective-permute-start.4 = (bf16[4,2,128,128]{3,2,1,0:T(8,128)(2,1)S(1)}, bf16[4,2,128,128]{3,2,1,0:T(8,128)(2,1)S(1)}, u32[]{:S(2)}, u32[]{:S(2)}) collective-permute-start(bf16[4,2,128,128]{3,2,1,0:T(8,128)(2,1)S(1)} %get-tuple-element.29.refs_1_), channel_id=1, source_target_pairs={{0,4},{4,0},{8,12},{12,8},{1,5},{5,1},{9,13},{13,9},{2,6},{6,2},{1... | collective-permute-start | bytes 786440 | tf_op jit(solution)/shard_map/ppermute | solution.py:554
  10.2 20.0 %collective-permute-start.1 = (bf16[1024,128]{1,0:T(8,128)(2,1)S(1)}, bf16[1024,128]{1,0:T(8,128)(2,1)S(1)}, u32[]{:S(2)}, u32[]{:S(2)}) collective-permute-start(bf16[1024,128]{1,0:T(8,128)(2,1)S(1)} %get-tuple-element.27), channel_id=1, source_target_pairs={{0,8},{4,12},{8,0},{12,4},{1,9},{5,13},{9,1},{13,5},{2,10},{6,14},... | collective-permute-start | bytes 786440 | tf_op jit(solution)/shard_map/ppermute | solution.py:554
  20.1 10.1 %collective-permute-start.2 = (bf16[1024,128]{1,0:T(8,128)(2,1)S(1)}, bf16[1024,128]{1,0:T(8,128)(2,1)S(1)}, u32[]{:S(2)}, u32[]{:S(2)}) collective-permute-start(bf16[1024,128]{1,0:T(8,128)(2,1)S(1)} %collective-permute-done.w_far_0), channel_id=1, source_target_pairs={{0,16},{16,0},{1,17},{17,1},{2,18},{18,2},{3,19},{19,3},{4,20},{20... | collective-permute-start | bytes 786440 | tf_op jit(solution)/shard_map/ppermute | solution.py:554
  26.1 11.5 %collective-permute-start.7 = (bf16[2,48,2048]{2,1,0:T(8,128)(2,1)S(1)}, bf16[2,48,2048]{2,1,0:T(8,128)(2,1)S(1)}, u32[]{:S(2)}, u32[]{:S(2)}) collective-permute-start(bf16[2,48,2048]{2,1,0:T(8,128)(2,1)S(1)} %gate.3.rest_0_), channel_id=1, source_target_pairs={{0,2},{1,3},{2,0},{3,1},{4,6},{5,7},{6,4},{7,5},{8,10},{9,11},{10,... | collective-permute-start | bytes 1179656 | tf_op jit(solution)/shard_map/ppermute | solution.py:554
  28.1 11.1 %collective-permute-start.6 = (bf16[2,48,2048]{2,1,0:T(8,128)(2,1)S(1)}, bf16[2,48,2048]{2,1,0:T(8,128)(2,1)S(1)}, u32[]{:S(2)}, u32[]{:S(2)}) collective-permute-start(bf16[2,48,2048]{2,1,0:T(8,128)(2,1)S(1)} %gate.3.rest_0_), channel_id=1, source_target_pairs={{0,1},{1,0},{2,3},{3,2},{4,5},{5,4},{6,7},{7,6},{8,9},{9,8},{10,11... | collective-permute-start | bytes 1179656 | tf_op jit(solution)/shard_map/ppermute | solution.py:554
  30.2 7.4 %copy-start = (bf16[1,192,8192]{2,1,0:T(8,128)(2,1)S(1)}, bf16[1,192,8192]{2,1,0:T(8,128)(2,1)}, u32[]{:S(2)}) copy-start(bf16[1,192,8192]{2,1,0:T(8,128)(2,1)} %hidden.5) | copy-start | bytes 9437188
  30.2 26.7 %collective-permute-start.11 = (bf16[4,2,128,128]{3,2,1,0:T(8,128)(2,1)S(1)}, bf16[4,2,128,128]{3,2,1,0:T(8,128)(2,1)S(1)}, u32[]{:S(2)}, u32[]{:S(2)}) collective-permute-start(bf16[4,2,128,128]{3,2,1,0:T(8,128)(2,1)S(1)} %get-tuple-element.41), channel_id=1, source_target_pairs={{0,8},{4,12},{8,0},{12,4},{1,9},{5,13},{9,1},{13,5},{2,10},{6,14},... | collective-permute-start | bytes 786440 | tf_op jit(solution)/shard_map/ppermute | solution.py:554
  33.6 23.4 %collective-permute-start.12 = (bf16[4,2,128,128]{3,2,1,0:T(8,128)(2,1)S(1)}, bf16[4,2,128,128]{3,2,1,0:T(8,128)(2,1)S(1)}, u32[]{:S(2)}, u32[]{:S(2)}) collective-permute-start(bf16[4,2,128,128]{3,2,1,0:T(8,128)(2,1)S(1)} %get-tuple-element.42), channel_id=1, source_target_pairs={{0,12},{4,8},{8,4},{12,0},{1,13},{5,9},{9,5},{13,1},{2,14},{6,10},... | collective-permute-start | bytes 786440 | tf_op jit(solution)/shard_map/ppermute | solution.py:554
  36.1 6.6 %collective-permute-start.3 = (bf16[1024,128]{1,0:T(8,128)(2,1)S(1)}, bf16[1024,128]{1,0:T(8,128)(2,1)S(1)}, u32[]{:S(2)}, u32[]{:S(2)}) collective-permute-start(bf16[1024,128]{1,0:T(8,128)(2,1)S(1)} %get-tuple-element.28.w_far_1), channel_id=1, source_target_pairs={{0,16},{16,0},{1,17},{17,1},{2,18},{18,2},{3,19},{19,3},{4,20},{20... | collective-permute-start | bytes 786440 | tf_op jit(solution)/shard_map/ppermute | solution.py:554
  37.6 1.7 %collective-permute-start.8 = (bf16[2,48,2048]{2,1,0:T(8,128)(2,1)S(1)}, bf16[2,48,2048]{2,1,0:T(8,128)(2,1)S(1)}, u32[]{:S(2)}, u32[]{:S(2)}) collective-permute-start(bf16[2,48,2048]{2,1,0:T(8,128)(2,1)S(1)} %collective-permute-done.7.rest_2_), channel_id=1, source_target_pairs={{0,1},{1,0},{2,3},{3,2},{4,5},{5,4},{6,7},{7,6},{8,9},{9,8},{10,11... | collective-permute-start | bytes 1179656 | tf_op jit(solution)/shard_map/ppermute | solution.py:554
  41.0 5.8 %copy-start.1 = (bf16[1,192,1024]{2,1,0:T(8,128)(2,1)S(1)}, bf16[1,192,1024]{2,1,0:T(8,128)(2,1)}, u32[]{:S(2)}) copy-start(bf16[1,192,1024]{2,1,0:T(8,128)(2,1)} %queries.1) | copy-start | bytes 1179652
  41.0 5.8 %copy-start.3 = (s32[1,16,12]{1,0,2:T(1,128)S(1)}, s32[1,16,12]{1,0,2:T(1,128)}, u32[]{:S(2)}) copy-start(s32[1,16,12]{1,0,2:T(1,128)} %param.17) | copy-start | bytes 2308
  41.0 5.8 %copy-start.4 = (s32[32]{0:T(128)S(1)}, s32[32]{0:T(128)}, u32[]{:S(2)}) copy-start(s32[32]{0:T(128)} %doc_lengths.1) | copy-start | bytes 388
  44.7 6.1 %collective-permute-start.9 = (bf16[192,128]{1,0:T(8,128)(2,1)S(1)}, bf16[192,128]{1,0:T(8,128)(2,1)S(1)}, u32[]{:S(2)}, u32[]{:S(2)}) collective-permute-start(bf16[192,128]{1,0:T(8,128)(2,1)S(1)} %get-tuple-element.32), channel_id=1, source_target_pairs={{0,4},{4,0},{8,12},{12,8},{1,5},{5,1},{9,13},{13,9},{2,6},{6,2},{1... | collective-permute-start | bytes 147464 | tf_op jit(solution)/shard_map/ppermute | solution.py:554
  44.7 7.6 %collective-permute-start.10 = (bf16[192,128]{1,0:T(8,128)(2,1)S(1)}, bf16[192,128]{1,0:T(8,128)(2,1)S(1)}, u32[]{:S(2)}, u32[]{:S(2)}) collective-permute-start(bf16[192,128]{1,0:T(8,128)(2,1)S(1)} %get-tuple-element.33), channel_id=1, source_target_pairs={{0,4},{4,0},{8,12},{12,8},{1,5},{5,1},{9,13},{13,9},{2,6},{6,2},{1... | collective-permute-start | bytes 147464 | tf_op jit(solution)/shard_map/ppermute | solution.py:554
  53.2 11.2 %all-to-all-start = ((bf16[4,48,256]{2,1,0:T(8,128)(2,1)}), bf16[4,48,256]{2,1,0:T(8,128)(2,1)S(1)}, u32[]{:S(2)}, u32[]{:S(2)}) async-start(bf16[4,48,256]{2,1,0:T(8,128)(2,1)} %bitcast.1), calls=%async_computation | async-start | bytes 196608 | tf_op jit(solution)/shard_map/all_to_all | solution.py:602

commit v16 on v14

--- a/solution.py
+++ b/solution.py
@@ -324,7 +324,8 @@
     row_place[...] = column
     square = (row_count, row_count)
     same = lax.broadcasted_iota(jnp.int32, square, 0) == lax.broadcasted_iota(jnp.int32, square, 1)
-    key_place[...] = jnp.sum(jnp.where(same, column, 0), axis=0, keepdims=True)
+    key_place[...] = jnp.full(key_place.shape, held.shape[0], jnp.int32)
+    key_place[:, :row_count] = jnp.sum(jnp.where(same, column, 0), axis=0, keepdims=True)
     slot_row[...] = jnp.sum(jnp.where(same, goes, 0), axis=0, keepdims=True)
 
 
@@ -338,7 +339,7 @@
         ((doc_count, context), jnp.bfloat16),
         ((1, context), jnp.float32),
         ((rows, 1), jnp.int32),
-        ((1, rows), jnp.int32),
+        ((1, rows + -rows % 128), jnp.int32),
         ((1, rows), jnp.int32),
     )
     return pl.pallas_call(
@@ -415,7 +416,7 @@
                 slot = lax.rem(doc, slots)
                 fetch(sources[0].at[slot], sources[1].at[slot])
 
-            for k, source in zip((2, 3, 1), sources[2:]):
+            for k, source in zip((3, 2, 1), sources[2:]):
 
                 @pl.when(away == k)
                 def _():
@@ -423,7 +424,7 @@
 
         return carry
 
-    lax.fori_loop(0, doc_count, one_doc, 0, unroll=True)
+    lax.fori_loop(0, doc_count, one_doc, 0)
 
     def assemble(b):
         block = pl.ds(b * block_keys, block_keys)
@@ -444,14 +445,17 @@
             values[place, :head_dim] = values[place, :head_dim] * used
             values[place, head_dim:] = used
 
+    fresh_count = fresh.shape[0]
+    spare_rows = jnp.zeros((-fresh_count % 128, 2 * head_dim), fresh.dtype)
     fresh_k = jnp.concatenate([fresh[:, :head_dim]] * 2, axis=1)
+    fresh_k = jnp.concatenate([fresh_k, spare_rows], axis=0)
     fresh_v = jnp.concatenate([fresh[:, head_dim:], jnp.ones_like(fresh[:, head_dim:])], axis=1)
+    fresh_v = jnp.concatenate([fresh_v, spare_rows], axis=0)
     slot_place = lax.broadcasted_iota(jnp.int32, (1, block_keys), 1)
     contract_last = (((1,), (1,)), ((), ()))
-    assemble(0)
     for b in range(blocks):
-        if b + 1 < blocks:
-            assemble(b + 1)
+        assemble(b)
+    for b in range(blocks):
         rows = slice(b * block_rows, (b + 1) * block_rows)
         q_here = q[b * heads * block_rows : (b + 1) * heads * block_rows, :]
         own_place = row_place[rows, :]
@@ -477,9 +481,11 @@
         sides.append(values[part, :])
         chunks.append(masked(fresh_k, key_place[...] <= own_place))
         sides.append(fresh_v)
-        row_max = functools.reduce(
-            jnp.maximum, [jnp.max(one, axis=1, keepdims=True) for one in chunks]
+        lane_max = functools.reduce(
+            jnp.maximum,
+            [one[:, i : i + 128] for one in chunks for i in range(0, one.shape[1], 128)],
         )
+        row_max = jnp.max(lane_max, axis=1, keepdims=True)
         total = jnp.zeros((heads * block_rows, 2 * head_dim), jnp.float32)
         for one, side in zip(chunks, sides):
             powers = jnp.exp2(one - row_max).astype(jnp.bfloat16)
@@ -554,7 +560,7 @@
         doc_2, doc_3, w_far = gate((doc_2, doc_3, w_far), cost=8000000000)
         w_swapped = swap(w_far, "groups", 1)
         doc_1 = swap(doc_1, "seq", 1)
-        docs = (swap(doc_2, "seq", 2), swap(doc_3, "seq", 3), doc_1)
+        docs = (swap(doc_3, "seq", 3), swap(doc_2, "seq", 2), doc_1)
         quarters = (h_mine, h_core, h_chip, swap(h_chip, "tp", 1))
         own, *parts = project(hidden, w_key, w_value, w_far, w_swapped, quarters, doc_1)
         arrived = [swap(one, "seq", 1) for one in parts]

time: 68.1 us -> 65 us (0.954)
  starting transfers between devices: 22.8 us -> 17.6 us
  waiting for transfers between devices: 25.2 us -> 27.8 us
    all_to_all x1, starting transfers between devices: 7.95 us -> 3.3 us  [shards(): lax.all_to_all(outgoing, 'seq', split_axis=0, concat_axis=0, tiled=True)]
    ppermute x11, waiting for transfers between devices: 25.2 us -> 27.8 us  [swap(): return lax.ppermute(array, axis, [(i, i ^ apart) for i in range(count)])]
  transfers between devices with their start and end apart: 12 -> 12, of which waited for: 6 -> 6; matrix products, arithmetic and copies ran while one was open for 0% -> 0% of each run, Pallas kernels for 25% -> 26%
where the time goes in v16:
time: 65 us; the launch traced here: 64.5 us
  waiting for transfers between devices  27.8 us (43%)
  Pallas kernels  17.7 us (27%)
  starting transfers between devices  17.6 us (27%)
  between operations  0.78 us (1%)
  local copies, waits for them, and re-layouts  0.7 us (1%)
    ppermute x11, waiting for transfers between devices, swap(): return lax.ppermute(array, axis, [(i, i ^ apart) for i in range(count)])  27.8 us
    ppermute x11, starting transfers between devices, swap(): return lax.ppermute(array, axis, [(i, i ^ apart) for i in range(count)])  14.3 us
    pallas_call x1, Pallas kernels, attend(): pl.pallas_call(functools.partial(attend_kernel, by_owner), out_shape=jax....  6.96 us
    all_to_all x1, starting transfers between devices, shards(): lax.all_to_all(outgoing, 'seq', split_axis=0, concat_axis=0, tiled=True)  3.3 us
    pallas_call x1, Pallas kernels, pick_docs(): pl.pallas_call(functools.partial(docs_kernel, by_owner), out_shape=tuple(...  2.12 us
    pallas_call x1, Pallas kernels, project(): pl.pallas_call(far_kernel, out_shape=(sums,) + (jax.ShapeDtypeStruct((row...  1.94 us
    pallas_call x1, Pallas kernels, project(): pl.pallas_call(neighbour_kernel, out_shape=sums, in_specs=[ANY] * (2 + le...  1.64 us
    pallas_call x1, Pallas kernels, project(): pl.pallas_call(near_kernel, out_shape=sums, in_specs=[ANY] * 4, out_specs...  1.61 us
  transfers between devices with their start and end apart: 12, of which 6 were waited for; matrix products, arithmetic and copies ran while one was open for 0% of the time, Pallas kernels for 26%

profile of v16, /device:TPU:0, one launch (start us, length us, event | category | flops | bytes accessed | tf_op | source)
XLA Modules:
  0.0 64.5 jit_solution(11457373281976508944)
XLA Ops:
  0.6 1.2 %pick_sent.1 = (bf16[2048,128]{1,0:T(8,128)(2,1)S(1)}, bf16[2,48,2048]{2,1,0:T(8,128)(2,1)S(1)}) custom-call(bf16[1,192,8192]{2,1,0:T(8,128)(2,1)} %hidden.5, bf16[2048,128]{1,0:T(8,128)(2,1)} %w_key.5, bf16[2048,128]{1,0:T(8,128)(2,1)} %w_value.5), custom_call_target="tpu_custom_call" | custom-call | tf_op jit(solution)/shard_map/pick_sent/pallas_call | solution.py:49
  1.8 3.1 %collective-permute-start.3 = (bf16[2,48,2048]{2,1,0:T(8,128)(2,1)S(1)}, bf16[2,48,2048]{2,1,0:T(8,128)(2,1)S(1)}, u32[]{:S(2)}, u32[]{:S(2)}) collective-permute-start(bf16[2,48,2048]{2,1,0:T(8,128)(2,1)S(1)} %get-tuple-element.28), channel_id=1, source_target_pairs={{0,4},{4,0},{8,12},{12,8},{1,5},{5,1},{9,13},{13,9},{2,6},{6,2},{1... | collective-permute-start | bytes 1179656 | tf_op jit(solution)/shard_map/ppermute | solution.py:551
  4.9 2.6 %collective-permute-start = (bf16[2048,128]{1,0:T(8,128)(2,1)S(1)}, bf16[2048,128]{1,0:T(8,128)(2,1)S(1)}, u32[]{:S(2)}, u32[]{:S(2)}) collective-permute-start(bf16[2048,128]{1,0:T(8,128)(2,1)S(1)} %get-tuple-element.25), channel_id=1, source_target_pairs={{0,8},{4,12},{8,0},{12,4},{1,9},{5,13},{9,1},{13,5},{2,10},{6,14},... | collective-permute-start | bytes 1572872 | tf_op jit(solution)/shard_map/ppermute | solution.py:551
  7.5 2.1 %pick_docs.1 = (bf16[4,2,128,128]{3,2,1,0:T(8,128)(2,1)S(1)}, bf16[4,2,128,128]{3,2,1,0:T(8,128)(2,1)S(1)}, bf16[4,2,128,128]{3,2,1,0:T(8,128)(2,1)S(1)}) custom-call(s32[4,16]{1,0:T(4,128)S(1)} %copy-done.2, bf16[8,128,128]{2,1,0:T(8,128)(2,1)} %rest_0_.1, bf16[8,128,128]{2,1,0:T(8,128)(2,1)} %rest_1_.1), custom_call_target="tpu_custom_call" | custom-call | tf_op jit(solution)/shard_map/pick_docs/pallas_call | solution.py:131
  9.6 0.5 collective-permute-start.2
  10.2 13.0 %collective-permute-done.3.refs_0_ = bf16[2,48,2048]{2,1,0:T(8,128)(2,1)S(1)} collective-permute-done((bf16[2,48,2048]{2,1,0:T(8,128)(2,1)S(1)}, bf16[2,48,2048]{2,1,0:T(8,128)(2,1)S(1)}, u32[]{:S(2)}, u32[]{:S(2)}) %collective-permute-start.3) | collective-permute-done | bytes 393248 | tf_op jit(solution)/shard_map/ppermute | solution.py:551
  23.2 2.0 %collective-permute-start.5 = (bf16[2,48,2048]{2,1,0:T(8,128)(2,1)S(1)}, bf16[2,48,2048]{2,1,0:T(8,128)(2,1)S(1)}, u32[]{:S(2)}, u32[]{:S(2)}) collective-permute-start(bf16[2,48,2048]{2,1,0:T(8,128)(2,1)S(1)} %gate.3.rest_0_), channel_id=1, source_target_pairs={{0,2},{1,3},{2,0},{3,1},{4,6},{5,7},{6,4},{7,5},{8,10},{9,11},{10,... | collective-permute-start | bytes 1179656 | tf_op jit(solution)/shard_map/ppermute | solution.py:551
  25.2 5.4 %collective-permute-done.refs_2_ = bf16[2048,128]{1,0:T(8,128)(2,1)S(1)} collective-permute-done((bf16[2048,128]{1,0:T(8,128)(2,1)S(1)}, bf16[2048,128]{1,0:T(8,128)(2,1)S(1)}, u32[]{:S(2)}, u32[]{:S(2)}) %collective-permute-start) | collective-permute-done | bytes 524320 | tf_op jit(solution)/shard_map/ppermute | solution.py:551
  30.6 1.5 %collective-permute-start.1 = (bf16[2048,128]{1,0:T(8,128)(2,1)S(1)}, bf16[2048,128]{1,0:T(8,128)(2,1)S(1)}, u32[]{:S(2)}, u32[]{:S(2)}) collective-permute-start(bf16[2048,128]{1,0:T(8,128)(2,1)S(1)} %get-tuple-element.26.w_far), channel_id=1, source_target_pairs={{0,16},{16,0},{1,17},{17,1},{2,18},{18,2},{3,19},{19,3},{4,20},{20... | collective-permute-start | bytes 1572872 | tf_op jit(solution)/shard_map/ppermute | solution.py:551
  32.1 2.5 %collective-permute-start.9 = (bf16[4,2,128,128]{3,2,1,0:T(8,128)(2,1)S(1)}, bf16[4,2,128,128]{3,2,1,0:T(8,128)(2,1)S(1)}, u32[]{:S(2)}, u32[]{:S(2)}) collective-permute-start(bf16[4,2,128,128]{3,2,1,0:T(8,128)(2,1)S(1)} %get-tuple-element.39), channel_id=1, source_target_pairs={{0,12},{4,8},{8,4},{12,0},{1,13},{5,9},{9,5},{13,1},{2,14},{6,10},... | collective-permute-start | bytes 786440 | tf_op jit(solution)/shard_map/ppermute | solution.py:551
  34.7 1.6 %project_near.1.near = f32[192,256]{1,0:T(8,128)S(1)} custom-call(bf16[1,192,8192]{2,1,0:T(8,128)(2,1)S(1)} %copy-done, bf16[2048,128]{1,0:T(8,128)(2,1)} %w_key.5, bf16[2048,128]{1,0:T(8,128)(2,1)} %w_value.5, bf16[4,2,128,128]{3,2,1,0:T(8,128)(2,1)S(1)} %collective-permute-done.2._.rest_4_), custom_call_target="tpu_custom_call" | custom-call | flops 10000000000 | bytes 1 | tf_op jit(solution)/shard_map/project_near/pallas_call | solution.py:216
  36.3 0.1 collective-permute-done.6.rest_3_
  36.4 1.6 %project_neighbour.1.neighbour = f32[192,256]{1,0:T(8,128)S(1)} custom-call(bf16[2048,128]{1,0:T(8,128)(2,1)} %w_key.5, bf16[2048,128]{1,0:T(8,128)(2,1)} %w_value.5, bf16[2,48,2048]{2,1,0:T(8,128)(2,1)S(1)} %gate.3.rest_0_, bf16[2,48,2048]{2,1,0:T(8,128)(2,1)S(1)} %collective-permute-done.4.rest_1_, ...), custom_call_target="tpu_custom_call" | custom-call | flops 1 | bytes 1 | tf_op jit(solution)/shard_map/project_neighbour/pallas_call | solution.py:226
  38.1 4.9 %collective-permute-done.1.w_swapped = bf16[2048,128]{1,0:T(8,128)(2,1)S(1)} collective-permute-done((bf16[2048,128]{1,0:T(8,128)(2,1)S(1)}, bf16[2048,128]{1,0:T(8,128)(2,1)S(1)}, u32[]{:S(2)}, u32[]{:S(2)}) %collective-permute-start.1) | collective-permute-done | bytes 524320 | tf_op jit(solution)/shard_map/ppermute | solution.py:551
  43.0 1.9 %project_far.1 = (f32[192,256]{1,0:T(8,128)S(1)}, bf16[192,128]{1,0:T(8,128)(2,1)S(1)}, bf16[192,128]{1,0:T(8,128)(2,1)S(1)}) custom-call(bf16[1,192,8192]{2,1,0:T(8,128)(2,1)S(1)} %copy-done, bf16[2048,128]{1,0:T(8,128)(2,1)S(1)} %get-tuple-element.26.w_far, bf16[2048,128]{1,0:T(8,128)(2,1)S(1)} %collective-permute-done.1.w_swapped, ...), custom_call_target="tpu_custom_call" | custom-call | flops 1 | bytes 1 | tf_op jit(solution)/shard_map/project_far/pallas_call | solution.py:240
  45.0 0.1 collective-permute-start.7
  45.0 2.0 %collective-permute-start.8 = (bf16[192,128]{1,0:T(8,128)(2,1)S(1)}, bf16[192,128]{1,0:T(8,128)(2,1)S(1)}, u32[]{:S(2)}, u32[]{:S(2)}) collective-permute-start(bf16[192,128]{1,0:T(8,128)(2,1)S(1)} %get-tuple-element.31), channel_id=1, source_target_pairs={{0,4},{4,0},{8,12},{12,8},{1,5},{5,1},{9,13},{13,9},{2,6},{6,2},{1... | collective-permute-start | bytes 147464 | tf_op jit(solution)/shard_map/ppermute | solution.py:551
  47.1 1.4 %plan.1 = (bf16[1536,256]{1,0:T(8,128)(2,1)S(1)}, bf16[2048,128]{1,0:T(8,128)(2,1)S(1)}, bf16[16,2048]{1,0:T(8,128)(2,1)S(1)}, f32[1,2048]{1,0:T(1,128)S(1)}, s3...) custom-call(s32[4,16]{1,0:T(4,128)S(1)} %copy-done.2, s32[32]{0:T(128)S(1)} %copy-done.4, ...), custom_call_target="tpu_custom_call" | custom-call | tf_op jit(solution)/shard_map/plan/pallas_call | solution.py:345
  48.4 3.3 %collective-permute-done.7.arrived_k = bf16[192,128]{1,0:T(8,128)(2,1)S(1)} collective-permute-done((bf16[192,128]{1,0:T(8,128)(2,1)S(1)}, bf16[192,128]{1,0:T(8,128)(2,1)S(1)}, u32[]{:S(2)}, u32[]{:S(2)}) %collective-permute-start.7) | collective-permute-done | bytes 49184 | tf_op jit(solution)/shard_map/ppermute | solution.py:551
  51.8 1.0 %collective-permute-done.8.arrived_v = bf16[192,128]{1,0:T(8,128)(2,1)S(1)} collective-permute-done((bf16[192,128]{1,0:T(8,128)(2,1)S(1)}, bf16[192,128]{1,0:T(8,128)(2,1)S(1)}, u32[]{:S(2)}, u32[]{:S(2)}) %collective-permute-start.8) | collective-permute-done | bytes 49184 | tf_op jit(solution)/shard_map/ppermute | solution.py:551
  52.7 0.8 %finish.1 = (bf16[192,256]{1,0:T(8,128)(2,1)S(1)}, bf16[192,256]{1,0:T(8,128)(2,1)}) custom-call(f32[192,256]{1,0:T(8,128)S(1)} %get-tuple-element.29.own, bf16[192,128]{1,0:T(8,128)(2,1)S(1)} %collective-permute-done.7.arrived_k, bf16[192,128]{1,0:T(8,128)(2,1)S(1)} %collective-permute-done.8.arrived_v, s32[1,192]{1,0:T(1,128)S(1)} %get-tuple-element.32.slot_row), custom_call_target="tpu_custom_call" | custom-call | tf_op jit(solution)/shard_map/finish/pallas_call | solution.py:367
  53.6 3.3 %all-to-all-start = ((bf16[4,48,256]{2,1,0:T(8,128)(2,1)}), bf16[4,48,256]{2,1,0:T(8,128)(2,1)S(1)}, u32[]{:S(2)}, u32[]{:S(2)}) async-start(bf16[4,48,256]{2,1,0:T(8,128)(2,1)} %bitcast.1), calls=%async_computation | async-start | bytes 196608 | tf_op jit(solution)/shard_map/all_to_all | solution.py:596
  56.9 7.0 %attend.1 = bf16[1,192,1024]{2,1,0:T(8,128)(2,1)} custom-call(s32[4,16]{1,0:T(4,128)S(1)} %copy-done.2, bf16[1536,256]{1,0:T(8,128)(2,1)S(1)} %get-tuple-element.22.q, bf16[192,256]{1,0:T(8,128)(2,1)S(1)} %get-tuple-element.33.fresh, bf16[2048,128]{1,0:T(8,128)(2,1)S(1)} %get-tuple-element.34.held, bf16[16,2048]{1,0:T(8,128)(2,1)S(1)} %get-tuple-element.35.spare, ...), custom_call_target="tpu_custom_call" | custom-call | tf_op jit(solution)/shard_map/attend/pallas_call | solution.py:504
  63.9 0.7 %broadcast_in_dim_reshape.3 = bf16[1,4,4,12,2,128]{5,4,3,2,1,0:T(2,128)(2,1)} reshape(bf16[4,48,256]{2,1,0:T(8,128)(2,1)S(1)} %all-to-all-done) | data formatting | bytes 196608 | tf_op jit(solution)/shard_map/broadcast_in_dim;reshape | solution.py:598
  (21 shorter events, 0.1 us)
Async XLA Ops:
  0.6 6.9 %copy-start.2 = (s32[4,16]{1,0:T(4,128)S(1)}, s32[4,16]{1,0:T(4,128)}, u32[]{:S(2)}) copy-start(s32[4,16]{1,0:T(4,128)} %request_docs.5) | copy-start | bytes 772
  1.8 21.3 %collective-permute-start.3 = (bf16[2,48,2048]{2,1,0:T(8,128)(2,1)S(1)}, bf16[2,48,2048]{2,1,0:T(8,128)(2,1)S(1)}, u32[]{:S(2)}, u32[]{:S(2)}) collective-permute-start(bf16[2,48,2048]{2,1,0:T(8,128)(2,1)S(1)} %get-tuple-element.28), channel_id=1, source_target_pairs={{0,4},{4,0},{8,12},{12,8},{1,5},{5,1},{9,13},{13,9},{2,6},{6,2},{1... | collective-permute-start | bytes 1179656 | tf_op jit(solution)/shard_map/ppermute | solution.py:551
  4.9 25.7 %collective-permute-start = (bf16[2048,128]{1,0:T(8,128)(2,1)S(1)}, bf16[2048,128]{1,0:T(8,128)(2,1)S(1)}, u32[]{:S(2)}, u32[]{:S(2)}) collective-permute-start(bf16[2048,128]{1,0:T(8,128)(2,1)S(1)} %get-tuple-element.25), channel_id=1, source_target_pairs={{0,8},{4,12},{8,0},{12,4},{1,9},{5,13},{9,1},{13,5},{2,10},{6,14},... | collective-permute-start | bytes 1572872 | tf_op jit(solution)/shard_map/ppermute | solution.py:551
  9.6 22.5 %collective-permute-start.2 = (bf16[4,2,128,128]{3,2,1,0:T(8,128)(2,1)S(1)}, bf16[4,2,128,128]{3,2,1,0:T(8,128)(2,1)S(1)}, u32[]{:S(2)}, u32[]{:S(2)}) collective-permute-start(bf16[4,2,128,128]{3,2,1,0:T(8,128)(2,1)S(1)} %get-tuple-element.27.refs_1_), channel_id=1, source_target_pairs={{0,4},{4,0},{8,12},{12,8},{1,5},{5,1},{9,13},{13,9},{2,6},{6,2},{1... | collective-permute-start | bytes 786440 | tf_op jit(solution)/shard_map/ppermute | solution.py:551
  23.2 11.5 %collective-permute-start.5 = (bf16[2,48,2048]{2,1,0:T(8,128)(2,1)S(1)}, bf16[2,48,2048]{2,1,0:T(8,128)(2,1)S(1)}, u32[]{:S(2)}, u32[]{:S(2)}) collective-permute-start(bf16[2,48,2048]{2,1,0:T(8,128)(2,1)S(1)} %gate.3.rest_0_), channel_id=1, source_target_pairs={{0,2},{1,3},{2,0},{3,1},{4,6},{5,7},{6,4},{7,5},{8,10},{9,11},{10,... | collective-permute-start | bytes 1179656 | tf_op jit(solution)/shard_map/ppermute | solution.py:551
  25.1 11.1 %collective-permute-start.4 = (bf16[2,48,2048]{2,1,0:T(8,128)(2,1)S(1)}, bf16[2,48,2048]{2,1,0:T(8,128)(2,1)S(1)}, u32[]{:S(2)}, u32[]{:S(2)}) collective-permute-start(bf16[2,48,2048]{2,1,0:T(8,128)(2,1)S(1)} %gate.3.rest_0_), channel_id=1, source_target_pairs={{0,1},{1,0},{2,3},{3,2},{4,5},{5,4},{6,7},{7,6},{8,9},{9,8},{10,11... | collective-permute-start | bytes 1179656 | tf_op jit(solution)/shard_map/ppermute | solution.py:551
  30.6 4.1 %copy-start = (bf16[1,192,8192]{2,1,0:T(8,128)(2,1)S(1)}, bf16[1,192,8192]{2,1,0:T(8,128)(2,1)}, u32[]{:S(2)}) copy-start(bf16[1,192,8192]{2,1,0:T(8,128)(2,1)} %hidden.5) | copy-start | bytes 9437188
  30.6 12.4 %collective-permute-start.1 = (bf16[2048,128]{1,0:T(8,128)(2,1)S(1)}, bf16[2048,128]{1,0:T(8,128)(2,1)S(1)}, u32[]{:S(2)}, u32[]{:S(2)}) collective-permute-start(bf16[2048,128]{1,0:T(8,128)(2,1)S(1)} %get-tuple-element.26.w_far), channel_id=1, source_target_pairs={{0,16},{16,0},{1,17},{17,1},{2,18},{18,2},{3,19},{19,3},{4,20},{20... | collective-permute-start | bytes 1572872 | tf_op jit(solution)/shard_map/ppermute | solution.py:551
  32.1 24.8 %collective-permute-start.10 = (bf16[4,2,128,128]{3,2,1,0:T(8,128)(2,1)S(1)}, bf16[4,2,128,128]{3,2,1,0:T(8,128)(2,1)S(1)}, u32[]{:S(2)}, u32[]{:S(2)}) collective-permute-start(bf16[4,2,128,128]{3,2,1,0:T(8,128)(2,1)S(1)} %get-tuple-element.40), channel_id=1, source_target_pairs={{0,8},{4,12},{8,0},{12,4},{1,9},{5,13},{9,1},{13,5},{2,10},{6,14},... | collective-permute-start | bytes 786440 | tf_op jit(solution)/shard_map/ppermute | solution.py:551
  32.1 24.8 %collective-permute-start.9 = (bf16[4,2,128,128]{3,2,1,0:T(8,128)(2,1)S(1)}, bf16[4,2,128,128]{3,2,1,0:T(8,128)(2,1)S(1)}, u32[]{:S(2)}, u32[]{:S(2)}) collective-permute-start(bf16[4,2,128,128]{3,2,1,0:T(8,128)(2,1)S(1)} %get-tuple-element.39), channel_id=1, source_target_pairs={{0,12},{4,8},{8,4},{12,0},{1,13},{5,9},{9,5},{13,1},{2,14},{6,10},... | collective-permute-start | bytes 786440 | tf_op jit(solution)/shard_map/ppermute | solution.py:551
  34.7 1.7 %collective-permute-start.6 = (bf16[2,48,2048]{2,1,0:T(8,128)(2,1)S(1)}, bf16[2,48,2048]{2,1,0:T(8,128)(2,1)S(1)}, u32[]{:S(2)}, u32[]{:S(2)}) collective-permute-start(bf16[2,48,2048]{2,1,0:T(8,128)(2,1)S(1)} %collective-permute-done.5.rest_2_), channel_id=1, source_target_pairs={{0,1},{1,0},{2,3},{3,2},{4,5},{5,4},{6,7},{7,6},{8,9},{9,8},{10,11... | collective-permute-start | bytes 1179656 | tf_op jit(solution)/shard_map/ppermute | solution.py:551
  38.0 9.0 %copy-start.1 = (bf16[1,192,1024]{2,1,0:T(8,128)(2,1)S(1)}, bf16[1,192,1024]{2,1,0:T(8,128)(2,1)}, u32[]{:S(2)}) copy-start(bf16[1,192,1024]{2,1,0:T(8,128)(2,1)} %queries.1) | copy-start | bytes 1179652
  38.0 9.0 %copy-start.3 = (s32[1,16,12]{1,0,2:T(1,128)S(1)}, s32[1,16,12]{1,0,2:T(1,128)}, u32[]{:S(2)}) copy-start(s32[1,16,12]{1,0,2:T(1,128)} %param.17) | copy-start | bytes 2308
  38.0 9.0 %copy-start.4 = (s32[32]{0:T(128)S(1)}, s32[32]{0:T(128)}, u32[]{:S(2)}) copy-start(s32[32]{0:T(128)} %doc_lengths.1) | copy-start | bytes 388
  45.0 6.8 %collective-permute-start.7 = (bf16[192,128]{1,0:T(8,128)(2,1)S(1)}, bf16[192,128]{1,0:T(8,128)(2,1)S(1)}, u32[]{:S(2)}, u32[]{:S(2)}) collective-permute-start(bf16[192,128]{1,0:T(8,128)(2,1)S(1)} %get-tuple-element.30), channel_id=1, source_target_pairs={{0,4},{4,0},{8,12},{12,8},{1,5},{5,1},{9,13},{13,9},{2,6},{6,2},{1... | collective-permute-start | bytes 147464 | tf_op jit(solution)/shard_map/ppermute | solution.py:551
  45.0 7.7 %collective-permute-start.8 = (bf16[192,128]{1,0:T(8,128)(2,1)S(1)}, bf16[192,128]{1,0:T(8,128)(2,1)S(1)}, u32[]{:S(2)}, u32[]{:S(2)}) collective-permute-start(bf16[192,128]{1,0:T(8,128)(2,1)S(1)} %get-tuple-element.31), channel_id=1, source_target_pairs={{0,4},{4,0},{8,12},{12,8},{1,5},{5,1},{9,13},{13,9},{2,6},{6,2},{1... | collective-permute-start | bytes 147464 | tf_op jit(solution)/shard_map/ppermute | solution.py:551
  53.6 10.3 %all-to-all-start = ((bf16[4,48,256]{2,1,0:T(8,128)(2,1)}), bf16[4,48,256]{2,1,0:T(8,128)(2,1)S(1)}, u32[]{:S(2)}, u32[]{:S(2)}) async-start(bf16[4,48,256]{2,1,0:T(8,128)(2,1)} %bitcast.1), calls=%async_computation | async-start | bytes 196608 | tf_op jit(solution)/shard_map/all_to_all | solution.py:596

commit v17 on v16

--- a/solution.py
+++ b/solution.py
@@ -255,7 +255,7 @@
 
 
 def plan_kernel(
-    capacity, slots, request_docs, doc_lengths, rows, queries, q, held, spare, key_bias, row_place, key_place,
+    pairs, capacity, slots, request_docs, doc_lengths, rows, queries, q, held, spare, key_bias, row_place, key_place,
     slot_row, counts
 ):
     head_dim = q.shape[1] // 2
@@ -285,7 +285,8 @@
         rank = counts[owner]
         counts[owner] = rank + 1
         lengths = jnp.where(docs == j, doc_lengths[doc], lengths)
-        places = jnp.where(docs == j, owner * capacity + rank, places)
+        target = lax.bitwise_xor(owner, me) if pairs else owner
+        places = jnp.where(docs == j, target * capacity + rank, places)
     slot = lax.broadcasted_iota(jnp.int32, (doc_len, doc_count), 0)
     used = slot < lengths
     for i in range(per_doc):
@@ -329,7 +330,7 @@
     slot_row[...] = jnp.sum(jnp.where(same, goes, 0), axis=0, keepdims=True)
 
 
-def plan(request_docs, doc_lengths, recompute_rows, queries, slots, head_dim, doc_len):
+def plan(pairs, request_docs, doc_lengths, recompute_rows, queries, slots, head_dim, doc_len):
     _, doc_count, per_doc = recompute_rows.shape
     rows = doc_count * per_doc
     context = doc_count * doc_len
@@ -343,7 +344,7 @@
         ((1, rows), jnp.int32),
     )
     return pl.pallas_call(
-        functools.partial(plan_kernel, slots // 2, slots),
+        functools.partial(plan_kernel, pairs, slots // 2, slots),
         out_shape=tuple(jax.ShapeDtypeStruct(*one) for one in shapes),
         in_specs=[SMEM, SMEM, VMEM, VMEM],
         out_specs=(VMEM,) * len(shapes),
@@ -353,22 +354,24 @@
     )(request_docs, doc_lengths, jnp.transpose(recompute_rows, (2, 0, 1)), queries)
 
 
-def finish_kernel(own, arrived_k, arrived_v, slot_row, fresh, outgoing):
+def finish_kernel(own, arrived_k, arrived_v, slot_row, fresh, *outgoing):
     arrived = jnp.concatenate([arrived_k[...], arrived_v[...]], axis=1)
     total = (own[...] + arrived.astype(jnp.float32)).astype(jnp.bfloat16)
     fresh[...] = total
-    slots = lax.broadcasted_iota(jnp.int32, (outgoing.shape[0], 1), 0)
-    pick = (slots == slot_row[...]).astype(jnp.bfloat16)
-    outgoing[...] = jnp.dot(pick, total, preferred_element_type=jnp.float32).astype(jnp.bfloat16)
-
-
-def finish(own, arrived, slot_row, slots):
-    shapes = (own.shape, (slots, own.shape[1]))
+    for i, out in enumerate(outgoing):
+        count = out.shape[0]
+        slots = i * count + lax.broadcasted_iota(jnp.int32, (count, 1), 0)
+        pick = (slots == slot_row[...]).astype(jnp.bfloat16)
+        out[...] = jnp.dot(pick, total, preferred_element_type=jnp.float32).astype(jnp.bfloat16)
+
+
+def finish(own, arrived, slot_row, slots, parts):
+    shapes = (own.shape,) + ((slots // parts, own.shape[1]),) * parts
     return pl.pallas_call(
         finish_kernel,
         out_shape=tuple(jax.ShapeDtypeStruct(one, jnp.bfloat16) for one in shapes),
         in_specs=[VMEM] * 4,
-        out_specs=(VMEM, VMEM),
+        out_specs=(VMEM,) * len(shapes),
         compiler_params=pltpu.CompilerParams(vmem_limit_bytes=16 * 1024 * 1024),
         name="finish",
     )(own, *arrived, slot_row)
@@ -377,7 +380,10 @@
 def attend_kernel(
     by_owner, request_docs, q, fresh, held, spare, key_bias, row_place, key_place, *rest
 ):
-    sources, (mixed, keys, values, counts, sems) = rest[:-5], rest[-5:]
+    *sources, mixed, keys, values, counts, sems = rest
+    if not by_owner:
+        *sources, returned = sources
+        sources, back = sources[:-4], sources[-4:]
     me = lax.axis_index("seq")
     doc_count = request_docs.shape[1]
     head_dim = keys.shape[1] // 2
@@ -391,6 +397,11 @@
     heads = mixed.shape[2] // head_dim
     left = pl.ds(0, head_dim)
 
+    if not by_owner:
+        for k, rows in enumerate(back):
+            count = rows.shape[0]
+            start = pl.multiple_of(lax.bitwise_xor(me, k) * count, count)
+            returned[pl.ds(start, count), :] = rows[...]
     for o in range(owners):
         counts[o] = 0
 
@@ -498,14 +509,18 @@
 
 
 def attend(
-    shape, request_docs, q, fresh, held, spare, key_bias, row_place, key_place, sources, by_owner
+    shape, request_docs, q, fresh, held, spare, key_bias, row_place, key_place, sources, back
 ):
     context, head_dim = held.shape
+    outs = [jax.ShapeDtypeStruct(shape, jnp.bfloat16)]
+    if back:
+        count, width = back[0].shape
+        outs.insert(0, jax.ShapeDtypeStruct((len(back) * count, width), jnp.bfloat16))
     return pl.pallas_call(
-        functools.partial(attend_kernel, by_owner),
-        out_shape=jax.ShapeDtypeStruct(shape, jnp.bfloat16),
-        in_specs=[SMEM] + [VMEM] * 7 + [ANY] * len(sources),
-        out_specs=VMEM,
+        functools.partial(attend_kernel, not back),
+        out_shape=outs,
+        in_specs=[SMEM] + [VMEM] * 7 + [ANY] * len(sources) + [VMEM] * len(back),
+        out_specs=[VMEM] * len(outs),
         scratch_shapes=[
             pltpu.VMEM((context, 2 * head_dim), jnp.bfloat16),
             pltpu.VMEM((context, 2 * head_dim), jnp.bfloat16),
@@ -525,6 +540,7 @@
         key_place,
         *(in_hbm(one) for one in sources[:2]),
         *sources[2:],
+        *back,
     )
 
 
@@ -575,10 +591,18 @@
         arrived = [jnp.zeros((own.shape[0], head_dim), jnp.bfloat16)] * 2
 
     q, held, spare, key_bias, row_place, key_place, slot_row = plan(
-        request_docs, doc_lengths, recompute_rows, queries, slot_count, head_dim, doc_len
+        pairs, request_docs, doc_lengths, recompute_rows, queries, slot_count, head_dim, doc_len
     )
-    fresh, outgoing = finish(own, arrived, slot_row, seq_count * capacity * per_doc)
-    mixed = attend(
+    fresh, *outgoing = finish(
+        own, arrived, slot_row, seq_count * capacity * per_doc, seq_count if pairs else 1
+    )
+    if pairs:
+        back = outgoing[:1] + [swap(outgoing[k], "seq", k) for k in range(1, seq_count)]
+    else:
+        back = ()
+        outgoing = outgoing[0].reshape(seq_count, capacity * per_doc, 2 * head_dim)
+        returned = lax.all_to_all(outgoing, "seq", split_axis=0, concat_axis=0, tiled=True)
+    *placed, mixed = attend(
         queries.shape,
         request_docs,
         q,
@@ -589,11 +613,11 @@
         row_place,
         key_place,
         sources,
-        not pairs,
+        back,
     )
-
-    outgoing = outgoing.reshape(seq_count, capacity * per_doc, 2 * head_dim)
-    returned = lax.all_to_all(outgoing, "seq", split_axis=0, concat_axis=0, tiled=True)
+    if pairs:
+        (returned,) = placed
+
     returned = returned.reshape(seq_count, capacity, per_doc, 2, head_dim)
     return (mixed, returned[None])
 

time: 65 us -> 68.6 us (1.055)
  waiting for transfers between devices: 27.8 us -> 30.9 us
  starting transfers between devices: 17.6 us -> 18.7 us
    ppermute x11 -> x14, starting transfers between devices: 14.3 us -> 18.7 us  [swap(): return lax.ppermute(array, axis, [(i, i ^ apart) for i in range(count)])]
    all_to_all x1 -> x0, starting transfers between devices: 3.3 us -> none  [shards(): lax.all_to_all(outgoing, 'seq', split_axis=0, concat_axis=0, tiled=True)]
    ppermute x11 -> x14, waiting for transfers between devices: 27.8 us -> 30.9 us  [swap(): return lax.ppermute(array, axis, [(i, i ^ apart) for i in range(count)])]
  transfers between devices with their start and end apart: 12 -> 14, of which waited for: 6 -> 8; matrix products, arithmetic and copies ran while one was open for 0% -> 0% of each run, Pallas kernels for 26% -> 13%
where the time goes in v17:
time: 68.6 us; the launch traced here: 68.2 us
  waiting for transfers between devices  30.9 us (45%)
  starting transfers between devices  18.7 us (27%)
  Pallas kernels  17.1 us (25%)
  between operations  0.77 us (1%)
  local copies, waits for them, and re-layouts  0.7 us (1%)
    ppermute x14, waiting for transfers between devices, swap(): return lax.ppermute(array, axis, [(i, i ^ apart) for i in range(count)])  30.9 us
    ppermute x14, starting transfers between devices, swap(): return lax.ppermute(array, axis, [(i, i ^ apart) for i in range(count)])  18.7 us
    pallas_call x1, Pallas kernels, attend(): pl.pallas_call(functools.partial(attend_kernel, not back), out_shape=outs...  7.04 us
    pallas_call x1, Pallas kernels, pick_docs(): pl.pallas_call(functools.partial(docs_kernel, by_owner), out_shape=tuple(...  2.17 us
    pallas_call x1, Pallas kernels, project(): pl.pallas_call(far_kernel, out_shape=(sums,) + (jax.ShapeDtypeStruct((row...  1.94 us
    pallas_call x1, Pallas kernels, project(): pl.pallas_call(neighbour_kernel, out_shape=sums, in_specs=[ANY] * (2 + le...  1.64 us
    pallas_call x1, Pallas kernels, project(): pl.pallas_call(near_kernel, out_shape=sums, in_specs=[ANY] * 4, out_specs...  1.61 us
    pallas_call x1, Pallas kernels, plan(): pl.pallas_call(functools.partial(plan_kernel, pairs, slots // 2, slots),...  1.39 us
  transfers between devices with their start and end apart: 14, of which 8 were waited for; matrix products, arithmetic and copies ran while one was open for 0% of the time, Pallas kernels for 13%

profile of v17, /device:TPU:0, one launch (start us, length us, event | category | flops | bytes accessed | tf_op | source)
XLA Modules:
  0.0 68.2 jit_solution(3747460409417402496)
XLA Ops:
  0.6 1.2 %pick_sent.1 = (bf16[2048,128]{1,0:T(8,128)(2,1)S(1)}, bf16[2,48,2048]{2,1,0:T(8,128)(2,1)S(1)}) custom-call(bf16[1,192,8192]{2,1,0:T(8,128)(2,1)} %hidden.5, bf16[2048,128]{1,0:T(8,128)(2,1)} %w_key.5, bf16[2048,128]{1,0:T(8,128)(2,1)} %w_value.5), custom_call_target="tpu_custom_call" | custom-call | tf_op jit(solution)/shard_map/pick_sent/pallas_call | solution.py:49
  1.8 3.1 %collective-permute-start.3 = (bf16[2,48,2048]{2,1,0:T(8,128)(2,1)S(1)}, bf16[2,48,2048]{2,1,0:T(8,128)(2,1)S(1)}, u32[]{:S(2)}, u32[]{:S(2)}) collective-permute-start(bf16[2,48,2048]{2,1,0:T(8,128)(2,1)S(1)} %get-tuple-element.33), channel_id=1, source_target_pairs={{0,4},{4,0},{8,12},{12,8},{1,5},{5,1},{9,13},{13,9},{2,6},{6,2},{1... | collective-permute-start | bytes 1179656 | tf_op jit(solution)/shard_map/ppermute | solution.py:567
  4.9 2.6 %collective-permute-start = (bf16[2048,128]{1,0:T(8,128)(2,1)S(1)}, bf16[2048,128]{1,0:T(8,128)(2,1)S(1)}, u32[]{:S(2)}, u32[]{:S(2)}) collective-permute-start(bf16[2048,128]{1,0:T(8,128)(2,1)S(1)} %get-tuple-element.30), channel_id=1, source_target_pairs={{0,8},{4,12},{8,0},{12,4},{1,9},{5,13},{9,1},{13,5},{2,10},{6,14},... | collective-permute-start | bytes 1572872 | tf_op jit(solution)/shard_map/ppermute | solution.py:567
  7.5 2.2 %pick_docs.1 = (bf16[4,2,128,128]{3,2,1,0:T(8,128)(2,1)S(1)}, bf16[4,2,128,128]{3,2,1,0:T(8,128)(2,1)S(1)}, bf16[4,2,128,128]{3,2,1,0:T(8,128)(2,1)S(1)}) custom-call(s32[4,16]{1,0:T(4,128)S(1)} %copy-done.2, bf16[8,128,128]{2,1,0:T(8,128)(2,1)} %rest_0_.1, bf16[8,128,128]{2,1,0:T(8,128)(2,1)} %rest_1_.1), custom_call_target="tpu_custom_call" | custom-call | tf_op jit(solution)/shard_map/pick_docs/pallas_call | solution.py:131
  9.7 0.5 collective-permute-start.2
  10.2 13.0 %collective-permute-done.3.refs_0_ = bf16[2,48,2048]{2,1,0:T(8,128)(2,1)S(1)} collective-permute-done((bf16[2,48,2048]{2,1,0:T(8,128)(2,1)S(1)}, bf16[2,48,2048]{2,1,0:T(8,128)(2,1)S(1)}, u32[]{:S(2)}, u32[]{:S(2)}) %collective-permute-start.3) | collective-permute-done | bytes 393248 | tf_op jit(solution)/shard_map/ppermute | solution.py:567
  23.2 2.0 %collective-permute-start.5 = (bf16[2,48,2048]{2,1,0:T(8,128)(2,1)S(1)}, bf16[2,48,2048]{2,1,0:T(8,128)(2,1)S(1)}, u32[]{:S(2)}, u32[]{:S(2)}) collective-permute-start(bf16[2,48,2048]{2,1,0:T(8,128)(2,1)S(1)} %gate.3.rest_0_), channel_id=1, source_target_pairs={{0,2},{1,3},{2,0},{3,1},{4,6},{5,7},{6,4},{7,5},{8,10},{9,11},{10,... | collective-permute-start | bytes 1179656 | tf_op jit(solution)/shard_map/ppermute | solution.py:567
  25.2 5.4 %collective-permute-done.refs_2_ = bf16[2048,128]{1,0:T(8,128)(2,1)S(1)} collective-permute-done((bf16[2048,128]{1,0:T(8,128)(2,1)S(1)}, bf16[2048,128]{1,0:T(8,128)(2,1)S(1)}, u32[]{:S(2)}, u32[]{:S(2)}) %collective-permute-start) | collective-permute-done | bytes 524320 | tf_op jit(solution)/shard_map/ppermute | solution.py:567
  30.6 1.5 %collective-permute-start.1 = (bf16[2048,128]{1,0:T(8,128)(2,1)S(1)}, bf16[2048,128]{1,0:T(8,128)(2,1)S(1)}, u32[]{:S(2)}, u32[]{:S(2)}) collective-permute-start(bf16[2048,128]{1,0:T(8,128)(2,1)S(1)} %get-tuple-element.31.w_far), channel_id=1, source_target_pairs={{0,16},{16,0},{1,17},{17,1},{2,18},{18,2},{3,19},{19,3},{4,20},{20... | collective-permute-start | bytes 1572872 | tf_op jit(solution)/shard_map/ppermute | solution.py:567
  32.1 2.5 %collective-permute-start.9 = (bf16[4,2,128,128]{3,2,1,0:T(8,128)(2,1)S(1)}, bf16[4,2,128,128]{3,2,1,0:T(8,128)(2,1)S(1)}, u32[]{:S(2)}, u32[]{:S(2)}) collective-permute-start(bf16[4,2,128,128]{3,2,1,0:T(8,128)(2,1)S(1)} %get-tuple-element.44), channel_id=1, source_target_pairs={{0,12},{4,8},{8,4},{12,0},{1,13},{5,9},{9,5},{13,1},{2,14},{6,10},... | collective-permute-start | bytes 786440 | tf_op jit(solution)/shard_map/ppermute | solution.py:567
  34.7 1.6 %project_near.1.near = f32[192,256]{1,0:T(8,128)S(1)} custom-call(bf16[1,192,8192]{2,1,0:T(8,128)(2,1)S(1)} %copy-done, bf16[2048,128]{1,0:T(8,128)(2,1)} %w_key.5, bf16[2048,128]{1,0:T(8,128)(2,1)} %w_value.5, bf16[4,2,128,128]{3,2,1,0:T(8,128)(2,1)S(1)} %collective-permute-done.2._.rest_4_), custom_call_target="tpu_custom_call" | custom-call | flops 10000000000 | bytes 1 | tf_op jit(solution)/shard_map/project_near/pallas_call | solution.py:216
  36.4 1.6 %project_neighbour.1.neighbour = f32[192,256]{1,0:T(8,128)S(1)} custom-call(bf16[2048,128]{1,0:T(8,128)(2,1)} %w_key.5, bf16[2048,128]{1,0:T(8,128)(2,1)} %w_value.5, bf16[2,48,2048]{2,1,0:T(8,128)(2,1)S(1)} %gate.3.rest_0_, bf16[2,48,2048]{2,1,0:T(8,128)(2,1)S(1)} %collective-permute-done.4.rest_1_, ...), custom_call_target="tpu_custom_call" | custom-call | flops 1 | bytes 1 | tf_op jit(solution)/shard_map/project_neighbour/pallas_call | solution.py:226
  38.1 4.9 %collective-permute-done.1.w_swapped = bf16[2048,128]{1,0:T(8,128)(2,1)S(1)} collective-permute-done((bf16[2048,128]{1,0:T(8,128)(2,1)S(1)}, bf16[2048,128]{1,0:T(8,128)(2,1)S(1)}, u32[]{:S(2)}, u32[]{:S(2)}) %collective-permute-start.1) | collective-permute-done | bytes 524320 | tf_op jit(solution)/shard_map/ppermute | solution.py:567
  43.0 1.9 %project_far.1 = (f32[192,256]{1,0:T(8,128)S(1)}, bf16[192,128]{1,0:T(8,128)(2,1)S(1)}, bf16[192,128]{1,0:T(8,128)(2,1)S(1)}) custom-call(bf16[1,192,8192]{2,1,0:T(8,128)(2,1)S(1)} %copy-done, bf16[2048,128]{1,0:T(8,128)(2,1)S(1)} %get-tuple-element.31.w_far, bf16[2048,128]{1,0:T(8,128)(2,1)S(1)} %collective-permute-done.1.w_swapped, ...), custom_call_target="tpu_custom_call" | custom-call | flops 1 | bytes 1 | tf_op jit(solution)/shard_map/project_far/pallas_call | solution.py:240
  45.0 2.0 %collective-permute-start.8 = (bf16[192,128]{1,0:T(8,128)(2,1)S(1)}, bf16[192,128]{1,0:T(8,128)(2,1)S(1)}, u32[]{:S(2)}, u32[]{:S(2)}) collective-permute-start(bf16[192,128]{1,0:T(8,128)(2,1)S(1)} %get-tuple-element.36), channel_id=1, source_target_pairs={{0,4},{4,0},{8,12},{12,8},{1,5},{5,1},{9,13},{13,9},{2,6},{6,2},{1... | collective-permute-start | bytes 147464 | tf_op jit(solution)/shard_map/ppermute | solution.py:567
  47.1 1.4 %plan.1 = (bf16[1536,256]{1,0:T(8,128)(2,1)S(1)}, bf16[2048,128]{1,0:T(8,128)(2,1)S(1)}, bf16[16,2048]{1,0:T(8,128)(2,1)S(1)}, f32[1,2048]{1,0:T(1,128)S(1)}, s3...) custom-call(s32[4,16]{1,0:T(4,128)S(1)} %copy-done.2, s32[32]{0:T(128)S(1)} %copy-done.4, ...), custom_call_target="tpu_custom_call" | custom-call | tf_op jit(solution)/shard_map/plan/pallas_call | solution.py:346
  48.4 3.3 %collective-permute-done.7.arrived_k = bf16[192,128]{1,0:T(8,128)(2,1)S(1)} collective-permute-done((bf16[192,128]{1,0:T(8,128)(2,1)S(1)}, bf16[192,128]{1,0:T(8,128)(2,1)S(1)}, u32[]{:S(2)}, u32[]{:S(2)}) %collective-permute-start.7) | collective-permute-done | bytes 49184 | tf_op jit(solution)/shard_map/ppermute | solution.py:567
  51.8 1.0 %collective-permute-done.8.arrived_v = bf16[192,128]{1,0:T(8,128)(2,1)S(1)} collective-permute-done((bf16[192,128]{1,0:T(8,128)(2,1)S(1)}, bf16[192,128]{1,0:T(8,128)(2,1)S(1)}, u32[]{:S(2)}, u32[]{:S(2)}) %collective-permute-start.8) | collective-permute-done | bytes 49184 | tf_op jit(solution)/shard_map/ppermute | solution.py:567
  53.0 1.9 %collective-permute-start.12 = (bf16[48,256]{1,0:T(8,128)(2,1)S(1)}, bf16[48,256]{1,0:T(8,128)(2,1)S(1)}, u32[]{:S(2)}, u32[]{:S(2)}) collective-permute-start(bf16[48,256]{1,0:T(8,128)(2,1)S(1)} %get-tuple-element.48), channel_id=1, source_target_pairs={{0,8},{4,12},{8,0},{12,4},{1,9},{5,13},{9,1},{13,5},{2,10},{6,14},... | collective-permute-start | bytes 73736 | tf_op jit(solution)/shard_map/ppermute | solution.py:567
  54.9 2.5 %collective-permute-start.13 = (bf16[48,256]{1,0:T(8,128)(2,1)S(1)}, bf16[48,256]{1,0:T(8,128)(2,1)S(1)}, u32[]{:S(2)}, u32[]{:S(2)}) collective-permute-start(bf16[48,256]{1,0:T(8,128)(2,1)S(1)} %get-tuple-element.49), channel_id=1, source_target_pairs={{0,12},{4,8},{8,4},{12,0},{1,13},{5,9},{9,5},{13,1},{2,14},{6,10},... | collective-permute-start | bytes 73736 | tf_op jit(solution)/shard_map/ppermute | solution.py:567
  57.4 0.7 collective-permute-done.12.rest_7_
  58.1 2.4 %collective-permute-done.13.rest_8_ = bf16[48,256]{1,0:T(8,128)(2,1)S(1)} collective-permute-done((bf16[48,256]{1,0:T(8,128)(2,1)S(1)}, bf16[48,256]{1,0:T(8,128)(2,1)S(1)}, u32[]{:S(2)}, u32[]{:S(2)}) %collective-permute-start.13) | collective-permute-done | bytes 24608 | tf_op jit(solution)/shard_map/ppermute | solution.py:567
  60.5 7.0 %attend.1 = (bf16[192,256]{1,0:T(8,128)(2,1)S(1)}, bf16[1,192,1024]{2,1,0:T(8,128)(2,1)}) custom-call(s32[4,16]{1,0:T(4,128)S(1)} %copy-done.2, bf16[1536,256]{1,0:T(8,128)(2,1)S(1)} %get-tuple-element.27.q, bf16[192,256]{1,0:T(8,128)(2,1)S(1)} %get-tuple-element.38.fresh, bf16[2048,128]{1,0:T(8,128)(2,1)S(1)} %get-tuple-element.39.held, ...), custom_call_target="tpu_custom_call" | custom-call | tf_op jit(solution)/shard_map/attend/pallas_call | solution.py:519
  67.5 0.7 broadcast_in_dim_reshape.3
  (25 shorter events, 0.5 us)
Async XLA Ops:
  0.6 6.9 %copy-start.2 = (s32[4,16]{1,0:T(4,128)S(1)}, s32[4,16]{1,0:T(4,128)}, u32[]{:S(2)}) copy-start(s32[4,16]{1,0:T(4,128)} %request_docs.5) | copy-start | bytes 772
  1.8 21.3 %collective-permute-start.3 = (bf16[2,48,2048]{2,1,0:T(8,128)(2,1)S(1)}, bf16[2,48,2048]{2,1,0:T(8,128)(2,1)S(1)}, u32[]{:S(2)}, u32[]{:S(2)}) collective-permute-start(bf16[2,48,2048]{2,1,0:T(8,128)(2,1)S(1)} %get-tuple-element.33), channel_id=1, source_target_pairs={{0,4},{4,0},{8,12},{12,8},{1,5},{5,1},{9,13},{13,9},{2,6},{6,2},{1... | collective-permute-start | bytes 1179656 | tf_op jit(solution)/shard_map/ppermute | solution.py:567
  4.9 25.7 %collective-permute-start = (bf16[2048,128]{1,0:T(8,128)(2,1)S(1)}, bf16[2048,128]{1,0:T(8,128)(2,1)S(1)}, u32[]{:S(2)}, u32[]{:S(2)}) collective-permute-start(bf16[2048,128]{1,0:T(8,128)(2,1)S(1)} %get-tuple-element.30), channel_id=1, source_target_pairs={{0,8},{4,12},{8,0},{12,4},{1,9},{5,13},{9,1},{13,5},{2,10},{6,14},... | collective-permute-start | bytes 1572872 | tf_op jit(solution)/shard_map/ppermute | solution.py:567
  9.7 22.4 %collective-permute-start.2 = (bf16[4,2,128,128]{3,2,1,0:T(8,128)(2,1)S(1)}, bf16[4,2,128,128]{3,2,1,0:T(8,128)(2,1)S(1)}, u32[]{:S(2)}, u32[]{:S(2)}) collective-permute-start(bf16[4,2,128,128]{3,2,1,0:T(8,128)(2,1)S(1)} %get-tuple-element.32.refs_1_), channel_id=1, source_target_pairs={{0,4},{4,0},{8,12},{12,8},{1,5},{5,1},{9,13},{13,9},{2,6},{6,2},{1... | collective-permute-start | bytes 786440 | tf_op jit(solution)/shard_map/ppermute | solution.py:567
  23.2 11.5 %collective-permute-start.5 = (bf16[2,48,2048]{2,1,0:T(8,128)(2,1)S(1)}, bf16[2,48,2048]{2,1,0:T(8,128)(2,1)S(1)}, u32[]{:S(2)}, u32[]{:S(2)}) collective-permute-start(bf16[2,48,2048]{2,1,0:T(8,128)(2,1)S(1)} %gate.3.rest_0_), channel_id=1, source_target_pairs={{0,2},{1,3},{2,0},{3,1},{4,6},{5,7},{6,4},{7,5},{8,10},{9,11},{10,... | collective-permute-start | bytes 1179656 | tf_op jit(solution)/shard_map/ppermute | solution.py:567
  25.1 11.1 %collective-permute-start.4 = (bf16[2,48,2048]{2,1,0:T(8,128)(2,1)S(1)}, bf16[2,48,2048]{2,1,0:T(8,128)(2,1)S(1)}, u32[]{:S(2)}, u32[]{:S(2)}) collective-permute-start(bf16[2,48,2048]{2,1,0:T(8,128)(2,1)S(1)} %gate.3.rest_0_), channel_id=1, source_target_pairs={{0,1},{1,0},{2,3},{3,2},{4,5},{5,4},{6,7},{7,6},{8,9},{9,8},{10,11... | collective-permute-start | bytes 1179656 | tf_op jit(solution)/shard_map/ppermute | solution.py:567
  30.6 4.1 %copy-start = (bf16[1,192,8192]{2,1,0:T(8,128)(2,1)S(1)}, bf16[1,192,8192]{2,1,0:T(8,128)(2,1)}, u32[]{:S(2)}) copy-start(bf16[1,192,8192]{2,1,0:T(8,128)(2,1)} %hidden.5) | copy-start | bytes 9437188
  30.6 12.4 %collective-permute-start.1 = (bf16[2048,128]{1,0:T(8,128)(2,1)S(1)}, bf16[2048,128]{1,0:T(8,128)(2,1)S(1)}, u32[]{:S(2)}, u32[]{:S(2)}) collective-permute-start(bf16[2048,128]{1,0:T(8,128)(2,1)S(1)} %get-tuple-element.31.w_far), channel_id=1, source_target_pairs={{0,16},{16,0},{1,17},{17,1},{2,18},{18,2},{3,19},{19,3},{4,20},{20... | collective-permute-start | bytes 1572872 | tf_op jit(solution)/shard_map/ppermute | solution.py:567
  32.1 25.3 %collective-permute-start.10 = (bf16[4,2,128,128]{3,2,1,0:T(8,128)(2,1)S(1)}, bf16[4,2,128,128]{3,2,1,0:T(8,128)(2,1)S(1)}, u32[]{:S(2)}, u32[]{:S(2)}) collective-permute-start(bf16[4,2,128,128]{3,2,1,0:T(8,128)(2,1)S(1)} %get-tuple-element.45), channel_id=1, source_target_pairs={{0,8},{4,12},{8,0},{12,4},{1,9},{5,13},{9,1},{13,5},{2,10},{6,14},... | collective-permute-start | bytes 786440 | tf_op jit(solution)/shard_map/ppermute | solution.py:567
  32.1 25.3 %collective-permute-start.9 = (bf16[4,2,128,128]{3,2,1,0:T(8,128)(2,1)S(1)}, bf16[4,2,128,128]{3,2,1,0:T(8,128)(2,1)S(1)}, u32[]{:S(2)}, u32[]{:S(2)}) collective-permute-start(bf16[4,2,128,128]{3,2,1,0:T(8,128)(2,1)S(1)} %get-tuple-element.44), channel_id=1, source_target_pairs={{0,12},{4,8},{8,4},{12,0},{1,13},{5,9},{9,5},{13,1},{2,14},{6,10},... | collective-permute-start | bytes 786440 | tf_op jit(solution)/shard_map/ppermute | solution.py:567
  34.7 1.7 %collective-permute-start.6 = (bf16[2,48,2048]{2,1,0:T(8,128)(2,1)S(1)}, bf16[2,48,2048]{2,1,0:T(8,128)(2,1)S(1)}, u32[]{:S(2)}, u32[]{:S(2)}) collective-permute-start(bf16[2,48,2048]{2,1,0:T(8,128)(2,1)S(1)} %collective-permute-done.5.rest_2_), channel_id=1, source_target_pairs={{0,1},{1,0},{2,3},{3,2},{4,5},{5,4},{6,7},{7,6},{8,9},{9,8},{10,11... | collective-permute-start | bytes 1179656 | tf_op jit(solution)/shard_map/ppermute | solution.py:567
  38.0 9.0 %copy-start.1 = (bf16[1,192,1024]{2,1,0:T(8,128)(2,1)S(1)}, bf16[1,192,1024]{2,1,0:T(8,128)(2,1)}, u32[]{:S(2)}) copy-start(bf16[1,192,1024]{2,1,0:T(8,128)(2,1)} %queries.1) | copy-start | bytes 1179652
  38.0 9.0 %copy-start.3 = (s32[1,16,12]{1,0,2:T(1,128)S(1)}, s32[1,16,12]{1,0,2:T(1,128)}, u32[]{:S(2)}) copy-start(s32[1,16,12]{1,0,2:T(1,128)} %param.17) | copy-start | bytes 2308
  38.0 9.0 %copy-start.4 = (s32[32]{0:T(128)S(1)}, s32[32]{0:T(128)}, u32[]{:S(2)}) copy-start(s32[32]{0:T(128)} %doc_lengths.1) | copy-start | bytes 388
  45.0 6.8 %collective-permute-start.7 = (bf16[192,128]{1,0:T(8,128)(2,1)S(1)}, bf16[192,128]{1,0:T(8,128)(2,1)S(1)}, u32[]{:S(2)}, u32[]{:S(2)}) collective-permute-start(bf16[192,128]{1,0:T(8,128)(2,1)S(1)} %get-tuple-element.35), channel_id=1, source_target_pairs={{0,4},{4,0},{8,12},{12,8},{1,5},{5,1},{9,13},{13,9},{2,6},{6,2},{1... | collective-permute-start | bytes 147464 | tf_op jit(solution)/shard_map/ppermute | solution.py:567
  45.0 7.7 %collective-permute-start.8 = (bf16[192,128]{1,0:T(8,128)(2,1)S(1)}, bf16[192,128]{1,0:T(8,128)(2,1)S(1)}, u32[]{:S(2)}, u32[]{:S(2)}) collective-permute-start(bf16[192,128]{1,0:T(8,128)(2,1)S(1)} %get-tuple-element.36), channel_id=1, source_target_pairs={{0,4},{4,0},{8,12},{12,8},{1,5},{5,1},{9,13},{13,9},{2,6},{6,2},{1... | collective-permute-start | bytes 147464 | tf_op jit(solution)/shard_map/ppermute | solution.py:567
  52.9 4.5 %collective-permute-start.11 = (bf16[48,256]{1,0:T(8,128)(2,1)S(1)}, bf16[48,256]{1,0:T(8,128)(2,1)S(1)}, u32[]{:S(2)}, u32[]{:S(2)}) collective-permute-start(bf16[48,256]{1,0:T(8,128)(2,1)S(1)} %get-tuple-element.47), channel_id=1, source_target_pairs={{0,4},{4,0},{8,12},{12,8},{1,5},{5,1},{9,13},{13,9},{2,6},{6,2},{1... | collective-permute-start | bytes 73736 | tf_op jit(solution)/shard_map/ppermute | solution.py:567
  53.0 5.1 %collective-permute-start.12 = (bf16[48,256]{1,0:T(8,128)(2,1)S(1)}, bf16[48,256]{1,0:T(8,128)(2,1)S(1)}, u32[]{:S(2)}, u32[]{:S(2)}) collective-permute-start(bf16[48,256]{1,0:T(8,128)(2,1)S(1)} %get-tuple-element.48), channel_id=1, source_target_pairs={{0,8},{4,12},{8,0},{12,4},{1,9},{5,13},{9,1},{13,5},{2,10},{6,14},... | collective-permute-start | bytes 73736 | tf_op jit(solution)/shard_map/ppermute | solution.py:567
  54.9 5.6 %collective-permute-start.13 = (bf16[48,256]{1,0:T(8,128)(2,1)S(1)}, bf16[48,256]{1,0:T(8,128)(2,1)S(1)}, u32[]{:S(2)}, u32[]{:S(2)}) collective-permute-start(bf16[48,256]{1,0:T(8,128)(2,1)S(1)} %get-tuple-element.49), channel_id=1, source_target_pairs={{0,12},{4,8},{8,4},{12,0},{1,13},{5,9},{9,5},{13,1},{2,14},{6,10},... | collective-permute-start | bytes 73736 | tf_op jit(solution)/shard_map/ppermute | solution.py:567

commit v18 on v15

--- a/solution.py
+++ b/solution.py
@@ -28,8 +28,8 @@
         @pl.when(group == chosen)
         def _():
             for i, out in enumerate((w_first, w_second)):
-                half = weight.at[pl.ds(i * out.shape[0], out.shape[0])]
-                pltpu.make_async_copy(half, out, sems.at[i]).start()
+                part = weight.at[pl.ds(i * w_first.shape[0], out.shape[0])]
+                pltpu.make_async_copy(part, out, sems.at[i]).start()
 
     first = me + 1 - 2 * lax.rem(me, 2)
     copies = []
@@ -48,13 +48,14 @@
 
 
 def pick_sent(hidden, w_key, w_value):
-    h_shape = (2, hidden.shape[1] // 4, w_key.shape[0])
-    half = jax.ShapeDtypeStruct((w_key.shape[0] // 2, w_key.shape[1]), jnp.bfloat16)
+    depth, width = w_key.shape
+    h_shape = (2, hidden.shape[1] // 4, depth)
+    first = depth * 7 // 32
     return pl.pallas_call(
         send_kernel,
         out_shape=(
-            half,
-            half,
+            jax.ShapeDtypeStruct((first, width), jnp.bfloat16),
+            jax.ShapeDtypeStruct((depth - first, width), jnp.bfloat16),
             jax.ShapeDtypeStruct(h_shape, jnp.bfloat16),
         ),
         in_specs=[ANY] * 3,
@@ -189,19 +190,19 @@
 def far_kernel(hidden, w_far_0, w_far_1, w_swapped_0, w_swapped_1, near, neighbour, *rest):
     *quarters, own, part_k, part_v, w, h, n, sems = rest
     group = lax.axis_index("groups")
-    half, width = w_far_0.shape
-    depth = 2 * half
+    start, width = w_far_0.shape
+    depth = start + w_far_1.shape[0]
     copies = []
 
     def copy(source, target):
         copies.append(pltpu.make_async_copy(source, target, sems.at[len(copies)]))
         copies[-1].start()
 
-    halves = ((w_far_0, w_far_1, group), (w_swapped_0, w_swapped_1, 1 - group))
-    for first, second, place in halves:
+    pairs = ((w_far_0, w_far_1, group), (w_swapped_0, w_swapped_1, 1 - group))
+    for first, second, place in pairs:
         columns = pl.ds(pl.multiple_of(place * width, width), width)
-        copy(first, w.at[pl.ds(0, half), columns])
-        copy(second, w.at[pl.ds(half, half), columns])
+        copy(first, w.at[pl.ds(0, start), columns])
+        copy(second, w.at[pl.ds(start, depth - start), columns])
     start = pl.multiple_of(lax.rem(lax.axis_index("seq") + 2, 4) * depth, depth)
     copy(hidden.at[0, :, pl.ds(start, depth)], h)
     lay_quarters(quarters, 1, n, copy)
@@ -333,7 +334,8 @@
     row_place[...] = column
     square = (row_count, row_count)
     same = lax.broadcasted_iota(jnp.int32, square, 0) == lax.broadcasted_iota(jnp.int32, square, 1)
-    key_place[...] = jnp.sum(jnp.where(same, column, 0), axis=0, keepdims=True)
+    key_place[...] = jnp.full(key_place.shape, held.shape[0], jnp.int32)
+    key_place[:, :row_count] = jnp.sum(jnp.where(same, column, 0), axis=0, keepdims=True)
     slot_row[...] = jnp.sum(jnp.where(same, goes, 0), axis=0, keepdims=True)
 
 
@@ -347,7 +349,7 @@
         ((doc_count, context), jnp.bfloat16),
         ((1, context), jnp.float32),
         ((rows, 1), jnp.int32),
-        ((1, rows), jnp.int32),
+        ((1, rows + -rows % 128), jnp.int32),
         ((1, rows), jnp.int32),
     )
     return pl.pallas_call(
@@ -365,13 +367,18 @@
     arrived = jnp.concatenate([arrived_k[...], arrived_v[...]], axis=1)
     total = (own[...] + arrived.astype(jnp.float32)).astype(jnp.bfloat16)
     fresh[...] = total
+    width = outgoing.shape[1]
     slots = lax.broadcasted_iota(jnp.int32, (outgoing.shape[0], 1), 0)
-    pick = (slots == slot_row[...]).astype(jnp.bfloat16)
-    outgoing[...] = jnp.dot(pick, total, preferred_element_type=jnp.float32).astype(jnp.bfloat16)
+    placed = jnp.zeros(outgoing.shape, jnp.float32)
+    for i in range(2):
+        pick = (slots == 2 * slot_row[...] + i).astype(jnp.bfloat16)
+        part = total[:, i * width : (i + 1) * width]
+        placed += jnp.dot(pick, part, preferred_element_type=jnp.float32)
+    outgoing[...] = placed.astype(jnp.bfloat16)
 
 
 def finish(own, arrived, slot_row, slots):
-    shapes = (own.shape, (slots, own.shape[1]))
+    shapes = (own.shape, (2 * slots, own.shape[1] // 2))
     return pl.pallas_call(
         finish_kernel,
         out_shape=tuple(jax.ShapeDtypeStruct(one, jnp.bfloat16) for one in shapes),
@@ -432,7 +439,7 @@
 
         return carry
 
-    lax.fori_loop(0, doc_count, one_doc, 0, unroll=True)
+    lax.fori_loop(0, doc_count, one_doc, 0)
 
     def assemble(b):
         block = pl.ds(b * block_keys, block_keys)
@@ -453,14 +460,17 @@
             values[place, :head_dim] = values[place, :head_dim] * used
             values[place, head_dim:] = used
 
+    fresh_count = fresh.shape[0]
+    spare_rows = jnp.zeros((-fresh_count % 128, 2 * head_dim), fresh.dtype)
     fresh_k = jnp.concatenate([fresh[:, :head_dim]] * 2, axis=1)
+    fresh_k = jnp.concatenate([fresh_k, spare_rows], axis=0)
     fresh_v = jnp.concatenate([fresh[:, head_dim:], jnp.ones_like(fresh[:, head_dim:])], axis=1)
+    fresh_v = jnp.concatenate([fresh_v, spare_rows], axis=0)
     slot_place = lax.broadcasted_iota(jnp.int32, (1, block_keys), 1)
     contract_last = (((1,), (1,)), ((), ()))
-    assemble(0)
     for b in range(blocks):
-        if b + 1 < blocks:
-            assemble(b + 1)
+        assemble(b)
+    for b in range(blocks):
         rows = slice(b * block_rows, (b + 1) * block_rows)
         q_here = q[b * heads * block_rows : (b + 1) * heads * block_rows, :]
         own_place = row_place[rows, :]
@@ -486,9 +496,11 @@
         sides.append(values[part, :])
         chunks.append(masked(fresh_k, key_place[...] <= own_place))
         sides.append(fresh_v)
-        row_max = functools.reduce(
-            jnp.maximum, [jnp.max(one, axis=1, keepdims=True) for one in chunks]
+        lane_max = functools.reduce(
+            jnp.maximum,
+            [one[:, i : i + 128] for one in chunks for i in range(0, one.shape[1], 128)],
         )
+        row_max = jnp.max(lane_max, axis=1, keepdims=True)
         total = jnp.zeros((heads * block_rows, 2 * head_dim), jnp.float32)
         for one, side in zip(chunks, sides):
             powers = jnp.exp2(one - row_max).astype(jnp.bfloat16)
@@ -554,7 +566,7 @@
             return lax.ppermute(array, axis, [(i, i ^ apart) for i in range(count)])
 
         *w_send, h_send = pick_sent(hidden, w_key, w_value)
-        w_far = [swap(half, "seq", 2) for half in w_send]
+        w_far = [swap(part, "seq", 2) for part in w_send]
         h_mine = swap(h_send, "seq", 1)
         doc_1, doc_2, doc_3 = pick_docs(request_docs, store_keys, store_values, False)
         (h_mine,) = gate((h_mine,), (doc_1,), cost=8000000000)
@@ -598,7 +610,7 @@
         not pairs,
     )
 
-    outgoing = outgoing.reshape(seq_count, capacity * per_doc, 2 * head_dim)
+    outgoing = outgoing.reshape(seq_count, capacity * per_doc * 2, head_dim)
     returned = lax.all_to_all(outgoing, "seq", split_axis=0, concat_axis=0, tiled=True)
     returned = returned.reshape(seq_count, capacity, per_doc, 2, head_dim)
     return (mixed, returned[None])

time: 65.5 us -> 65.1 us (level)
  waiting for transfers between devices: 22.5 us -> 26.4 us
  starting transfers between devices: 22.8 us -> 19 us
    ppermute x13, waiting for transfers between devices: 22.5 us -> 26.4 us  [swap(): return lax.ppermute(array, axis, [(i, i ^ apart) for i in range(count)])]
    ppermute x13, starting transfers between devices: 19.1 us -> 15.7 us  [swap(): return lax.ppermute(array, axis, [(i, i ^ apart) for i in range(count)])]
    another operation x1 -> x0, local copies, waits for them, and re-layouts: 0.67 us -> none  [shards(): return (mixed, returned[None])]
where the time goes in v18:
time: 65.1 us; the launch traced here: 64.6 us
  waiting for transfers between devices  26.4 us (41%)
  starting transfers between devices  19 us (29%)
  Pallas kernels  17.8 us (27%)
  between operations  0.78 us (1%)
  local copies, waits for them, and re-layouts  0.67 us (1%)
    ppermute x13, waiting for transfers between devices, swap(): return lax.ppermute(array, axis, [(i, i ^ apart) for i in range(count)])  26.4 us
    ppermute x13, starting transfers between devices, swap(): return lax.ppermute(array, axis, [(i, i ^ apart) for i in range(count)])  15.7 us
    pallas_call x1, Pallas kernels, attend(): pl.pallas_call(functools.partial(attend_kernel, by_owner), out_shape=jax....  6.92 us
    all_to_all x1, starting transfers between devices, shards(): lax.all_to_all(outgoing, 'seq', split_axis=0, concat_axis=0, tiled=True)  3.3 us
    pallas_call x1, Pallas kernels, pick_docs(): pl.pallas_call(functools.partial(docs_kernel, by_owner), out_shape=tuple(...  2.14 us
    pallas_call x1, Pallas kernels, project(): pl.pallas_call(far_kernel, out_shape=(sums,) + (jax.ShapeDtypeStruct((row...  1.97 us
    pallas_call x1, Pallas kernels, project(): pl.pallas_call(neighbour_kernel, out_shape=sums, in_specs=[ANY] * (2 + le...  1.63 us
    pallas_call x1, Pallas kernels, project(): pl.pallas_call(near_kernel, out_shape=sums, in_specs=[ANY] * 4, out_specs...  1.61 us
  transfers between devices with their start and end apart: 14, of which 7 were waited for; matrix products, arithmetic and copies ran while one was open for 0% of the time, Pallas kernels for 26%

profile of v18, /device:TPU:0, one launch (start us, length us, event | category | flops | bytes accessed | tf_op | source)
XLA Modules:
  0.0 64.6 jit_solution(17409380407336051550)
XLA Ops:
  0.6 1.2 %pick_sent.1 = (bf16[448,128]{1,0:T(8,128)(2,1)S(1)}, bf16[1600,128]{1,0:T(8,128)(2,1)S(1)}, bf16[2,48,2048]{2,1,0:T(8,128)(2,1)S(1)}) custom-call(bf16[1,192,8192]{2,1,0:T(8,128)(2,1)} %hidden.5, bf16[2048,128]{1,0:T(8,128)(2,1)} %w_key.5, bf16[2048,128]{1,0:T(8,128)(2,1)} %w_value.5), custom_call_target="tpu_custom_call" | custom-call | tf_op jit(solution)/shard_map/pick_sent/pallas_call | solution.py:54
  1.9 3.1 %collective-permute-start.5 = (bf16[2,48,2048]{2,1,0:T(8,128)(2,1)S(1)}, bf16[2,48,2048]{2,1,0:T(8,128)(2,1)S(1)}, u32[]{:S(2)}, u32[]{:S(2)}) collective-permute-start(bf16[2,48,2048]{2,1,0:T(8,128)(2,1)S(1)} %get-tuple-element.30), channel_id=1, source_target_pairs={{0,4},{4,0},{8,12},{12,8},{1,5},{5,1},{9,13},{13,9},{2,6},{6,2},{1... | collective-permute-start | bytes 1179656 | tf_op jit(solution)/shard_map/ppermute | solution.py:566
  5.0 2.6 %collective-permute-start = (bf16[448,128]{1,0:T(8,128)(2,1)S(1)}, bf16[448,128]{1,0:T(8,128)(2,1)S(1)}, u32[]{:S(2)}, u32[]{:S(2)}) collective-permute-start(bf16[448,128]{1,0:T(8,128)(2,1)S(1)} %get-tuple-element.24), channel_id=1, source_target_pairs={{0,8},{4,12},{8,0},{12,4},{1,9},{5,13},{9,1},{13,5},{2,10},{6,14},... | collective-permute-start | bytes 344072 | tf_op jit(solution)/shard_map/ppermute | solution.py:566
  7.5 0.3 collective-permute-start.1
  7.9 2.1 %pick_docs.1 = (bf16[4,2,128,128]{3,2,1,0:T(8,128)(2,1)S(1)}, bf16[4,2,128,128]{3,2,1,0:T(8,128)(2,1)S(1)}, bf16[4,2,128,128]{3,2,1,0:T(8,128)(2,1)S(1)}) custom-call(s32[4,16]{1,0:T(4,128)S(1)} %copy-done.2, bf16[8,128,128]{2,1,0:T(8,128)(2,1)} %rest_0_.1, bf16[8,128,128]{2,1,0:T(8,128)(2,1)} %rest_1_.1), custom_call_target="tpu_custom_call" | custom-call | tf_op jit(solution)/shard_map/pick_docs/pallas_call | solution.py:137
  10.2 6.8 %collective-permute-done.w_far_0 = bf16[448,128]{1,0:T(8,128)(2,1)S(1)} collective-permute-done((bf16[448,128]{1,0:T(8,128)(2,1)S(1)}, bf16[448,128]{1,0:T(8,128)(2,1)S(1)}, u32[]{:S(2)}, u32[]{:S(2)}) %collective-permute-start) | collective-permute-done | bytes 114720 | tf_op jit(solution)/shard_map/ppermute | solution.py:566
  17.0 1.5 %collective-permute-start.2 = (bf16[448,128]{1,0:T(8,128)(2,1)S(1)}, bf16[448,128]{1,0:T(8,128)(2,1)S(1)}, u32[]{:S(2)}, u32[]{:S(2)}) collective-permute-start(bf16[448,128]{1,0:T(8,128)(2,1)S(1)} %collective-permute-done.w_far_0), channel_id=1, source_target_pairs={{0,16},{16,0},{1,17},{17,1},{2,18},{18,2},{3,19},{19,3},{4,20},{20... | collective-permute-start | bytes 344072 | tf_op jit(solution)/shard_map/ppermute | solution.py:566
  18.5 4.6 %collective-permute-done.5.refs_0_ = bf16[2,48,2048]{2,1,0:T(8,128)(2,1)S(1)} collective-permute-done((bf16[2,48,2048]{2,1,0:T(8,128)(2,1)S(1)}, bf16[2,48,2048]{2,1,0:T(8,128)(2,1)S(1)}, u32[]{:S(2)}, u32[]{:S(2)}) %collective-permute-start.5) | collective-permute-done | bytes 393248 | tf_op jit(solution)/shard_map/ppermute | solution.py:566
  23.1 2.0 %collective-permute-start.7 = (bf16[2,48,2048]{2,1,0:T(8,128)(2,1)S(1)}, bf16[2,48,2048]{2,1,0:T(8,128)(2,1)S(1)}, u32[]{:S(2)}, u32[]{:S(2)}) collective-permute-start(bf16[2,48,2048]{2,1,0:T(8,128)(2,1)S(1)} %gate.3.rest_0_), channel_id=1, source_target_pairs={{0,2},{1,3},{2,0},{3,1},{4,6},{5,7},{6,4},{7,5},{8,10},{9,11},{10,... | collective-permute-start | bytes 1179656 | tf_op jit(solution)/shard_map/ppermute | solution.py:566
  25.1 5.7 %collective-permute-done.1.refs_2_ = bf16[1600,128]{1,0:T(8,128)(2,1)S(1)} collective-permute-done((bf16[1600,128]{1,0:T(8,128)(2,1)S(1)}, bf16[1600,128]{1,0:T(8,128)(2,1)S(1)}, u32[]{:S(2)}, u32[]{:S(2)}) %collective-permute-start.1) | collective-permute-done | bytes 409632 | tf_op jit(solution)/shard_map/ppermute | solution.py:566
  30.8 1.5 %collective-permute-start.3 = (bf16[1600,128]{1,0:T(8,128)(2,1)S(1)}, bf16[1600,128]{1,0:T(8,128)(2,1)S(1)}, u32[]{:S(2)}, u32[]{:S(2)}) collective-permute-start(bf16[1600,128]{1,0:T(8,128)(2,1)S(1)} %get-tuple-element.28.w_far_1), channel_id=1, source_target_pairs={{0,16},{16,0},{1,17},{17,1},{2,18},{18,2},{3,19},{19,3},{4,20},{20... | collective-permute-start | bytes 1228808 | tf_op jit(solution)/shard_map/ppermute | solution.py:566
  32.3 2.4 %collective-permute-start.12 = (bf16[4,2,128,128]{3,2,1,0:T(8,128)(2,1)S(1)}, bf16[4,2,128,128]{3,2,1,0:T(8,128)(2,1)S(1)}, u32[]{:S(2)}, u32[]{:S(2)}) collective-permute-start(bf16[4,2,128,128]{3,2,1,0:T(8,128)(2,1)S(1)} %get-tuple-element.42), channel_id=1, source_target_pairs={{0,12},{4,8},{8,4},{12,0},{1,13},{5,9},{9,5},{13,1},{2,14},{6,10},... | collective-permute-start | bytes 786440 | tf_op jit(solution)/shard_map/ppermute | solution.py:566
  34.7 1.6 %project_near.1.near = f32[192,256]{1,0:T(8,128)S(1)} custom-call(bf16[1,192,8192]{2,1,0:T(8,128)(2,1)S(1)} %copy-done, bf16[2048,128]{1,0:T(8,128)(2,1)} %w_key.5, bf16[2048,128]{1,0:T(8,128)(2,1)} %w_value.5, bf16[4,2,128,128]{3,2,1,0:T(8,128)(2,1)S(1)} %collective-permute-done.4._.rest_4_), custom_call_target="tpu_custom_call" | custom-call | flops 10000000000 | bytes 1 | tf_op jit(solution)/shard_map/project_near/pallas_call | solution.py:226
  36.4 1.6 %project_neighbour.1.neighbour = f32[192,256]{1,0:T(8,128)S(1)} custom-call(bf16[2048,128]{1,0:T(8,128)(2,1)} %w_key.5, bf16[2048,128]{1,0:T(8,128)(2,1)} %w_value.5, bf16[2,48,2048]{2,1,0:T(8,128)(2,1)S(1)} %gate.3.rest_0_, bf16[2,48,2048]{2,1,0:T(8,128)(2,1)S(1)} %collective-permute-done.6.rest_1_, ...), custom_call_target="tpu_custom_call" | custom-call | flops 1 | bytes 1 | tf_op jit(solution)/shard_map/project_neighbour/pallas_call | solution.py:236
  38.1 2.6 %collective-permute-done.3.w_swapped_1 = bf16[1600,128]{1,0:T(8,128)(2,1)S(1)} collective-permute-done((bf16[1600,128]{1,0:T(8,128)(2,1)S(1)}, bf16[1600,128]{1,0:T(8,128)(2,1)S(1)}, u32[]{:S(2)}, u32[]{:S(2)}) %collective-permute-start.3) | collective-permute-done | bytes 409632 | tf_op jit(solution)/shard_map/ppermute | solution.py:566
  40.7 2.0 %project_far.1 = (f32[192,256]{1,0:T(8,128)S(1)}, bf16[192,128]{1,0:T(8,128)(2,1)S(1)}, bf16[192,128]{1,0:T(8,128)(2,1)S(1)}) custom-call(bf16[1,192,8192]{2,1,0:T(8,128)(2,1)S(1)} %copy-done, bf16[448,128]{1,0:T(8,128)(2,1)S(1)} %collective-permute-done.w_far_0, bf16[1600,128]{1,0:T(8,128)(2,1)S(1)} %get-tuple-element.28.w_far_1, ...), custom_call_target="tpu_custom_call" | custom-call | flops 1 | bytes 1 | tf_op jit(solution)/shard_map/project_far/pallas_call | solution.py:250
  42.8 2.0 %collective-permute-start.9 = (bf16[192,128]{1,0:T(8,128)(2,1)S(1)}, bf16[192,128]{1,0:T(8,128)(2,1)S(1)}, u32[]{:S(2)}, u32[]{:S(2)}) collective-permute-start(bf16[192,128]{1,0:T(8,128)(2,1)S(1)} %get-tuple-element.32), channel_id=1, source_target_pairs={{0,4},{4,0},{8,12},{12,8},{1,5},{5,1},{9,13},{13,9},{2,6},{6,2},{1... | collective-permute-start | bytes 147464 | tf_op jit(solution)/shard_map/ppermute | solution.py:566
  44.8 1.4 %plan.1 = (bf16[1536,256]{1,0:T(8,128)(2,1)S(1)}, bf16[2048,128]{1,0:T(8,128)(2,1)S(1)}, bf16[16,2048]{1,0:T(8,128)(2,1)S(1)}, f32[1,2048]{1,0:T(1,128)S(1)}, s3...) custom-call(s32[4,16]{1,0:T(4,128)S(1)} %copy-done.2, s32[32]{0:T(128)S(1)} %copy-done.4, ...), custom_call_target="tpu_custom_call" | custom-call | tf_op jit(solution)/shard_map/plan/pallas_call | solution.py:355
  46.2 5.6 %collective-permute-done.10.arrived_v = bf16[192,128]{1,0:T(8,128)(2,1)S(1)} collective-permute-done((bf16[192,128]{1,0:T(8,128)(2,1)S(1)}, bf16[192,128]{1,0:T(8,128)(2,1)S(1)}, u32[]{:S(2)}, u32[]{:S(2)}) %collective-permute-start.10) | collective-permute-done | bytes 49184 | tf_op jit(solution)/shard_map/ppermute | solution.py:566
  51.8 1.0 %collective-permute-done.9.arrived_k = bf16[192,128]{1,0:T(8,128)(2,1)S(1)} collective-permute-done((bf16[192,128]{1,0:T(8,128)(2,1)S(1)}, bf16[192,128]{1,0:T(8,128)(2,1)S(1)}, u32[]{:S(2)}, u32[]{:S(2)}) %collective-permute-start.9) | collective-permute-done | bytes 49184 | tf_op jit(solution)/shard_map/ppermute | solution.py:566
  52.8 0.9 %finish.1 = (bf16[192,256]{1,0:T(8,128)(2,1)S(1)}, bf16[384,128]{1,0:T(8,128)(2,1)}) custom-call(f32[192,256]{1,0:T(8,128)S(1)} %get-tuple-element.31.own, bf16[192,128]{1,0:T(8,128)(2,1)S(1)} %collective-permute-done.9.arrived_k, bf16[192,128]{1,0:T(8,128)(2,1)S(1)} %collective-permute-done.10.arrived_v, s32[1,192]{1,0:T(1,128)S(1)} %get-tuple-element.34.slot_row), custom_call_target="tpu_custom_call" | custom-call | tf_op jit(solution)/shard_map/finish/pallas_call | solution.py:382
  53.7 3.3 %all-to-all-start = ((bf16[4,96,128]{2,1,0:T(8,128)(2,1)}), bf16[4,96,128]{2,1,0:T(8,128)(2,1)S(1)}, u32[]{:S(2)}, u32[]{:S(2)}) async-start(bf16[4,96,128]{2,1,0:T(8,128)(2,1)} %bitcast.1), calls=%async_computation | async-start | bytes 196608 | tf_op jit(solution)/shard_map/all_to_all | solution.py:614
  57.0 6.9 %attend.1 = bf16[1,192,1024]{2,1,0:T(8,128)(2,1)} custom-call(s32[4,16]{1,0:T(4,128)S(1)} %copy-done.2, bf16[1536,256]{1,0:T(8,128)(2,1)S(1)} %get-tuple-element.23.q, bf16[192,256]{1,0:T(8,128)(2,1)S(1)} %get-tuple-element.35.fresh, bf16[2048,128]{1,0:T(8,128)(2,1)S(1)} %get-tuple-element.36.held, bf16[16,2048]{1,0:T(8,128)(2,1)S(1)} %get-tuple-element.37.spare, ...), custom_call_target="tpu_custom_call" | custom-call | tf_op jit(solution)/shard_map/attend/pallas_call | solution.py:519
  64.0 0.6 copy.20
  (25 shorter events, 0.4 us)
Async XLA Ops:
  0.6 7.3 %copy-start.2 = (s32[4,16]{1,0:T(4,128)S(1)}, s32[4,16]{1,0:T(4,128)}, u32[]{:S(2)}) copy-start(s32[4,16]{1,0:T(4,128)} %request_docs.5) | copy-start | bytes 772
  1.9 21.2 %collective-permute-start.5 = (bf16[2,48,2048]{2,1,0:T(8,128)(2,1)S(1)}, bf16[2,48,2048]{2,1,0:T(8,128)(2,1)S(1)}, u32[]{:S(2)}, u32[]{:S(2)}) collective-permute-start(bf16[2,48,2048]{2,1,0:T(8,128)(2,1)S(1)} %get-tuple-element.30), channel_id=1, source_target_pairs={{0,4},{4,0},{8,12},{12,8},{1,5},{5,1},{9,13},{13,9},{2,6},{6,2},{1... | collective-permute-start | bytes 1179656 | tf_op jit(solution)/shard_map/ppermute | solution.py:566
  5.0 12.0 %collective-permute-start = (bf16[448,128]{1,0:T(8,128)(2,1)S(1)}, bf16[448,128]{1,0:T(8,128)(2,1)S(1)}, u32[]{:S(2)}, u32[]{:S(2)}) collective-permute-start(bf16[448,128]{1,0:T(8,128)(2,1)S(1)} %get-tuple-element.24), channel_id=1, source_target_pairs={{0,8},{4,12},{8,0},{12,4},{1,9},{5,13},{9,1},{13,5},{2,10},{6,14},... | collective-permute-start | bytes 344072 | tf_op jit(solution)/shard_map/ppermute | solution.py:566
  7.5 23.2 %collective-permute-start.1 = (bf16[1600,128]{1,0:T(8,128)(2,1)S(1)}, bf16[1600,128]{1,0:T(8,128)(2,1)S(1)}, u32[]{:S(2)}, u32[]{:S(2)}) collective-permute-start(bf16[1600,128]{1,0:T(8,128)(2,1)S(1)} %get-tuple-element.27), channel_id=1, source_target_pairs={{0,8},{4,12},{8,0},{12,4},{1,9},{5,13},{9,1},{13,5},{2,10},{6,14},... | collective-permute-start | bytes 1228808 | tf_op jit(solution)/shard_map/ppermute | solution.py:566
  10.0 22.3 %collective-permute-start.4 = (bf16[4,2,128,128]{3,2,1,0:T(8,128)(2,1)S(1)}, bf16[4,2,128,128]{3,2,1,0:T(8,128)(2,1)S(1)}, u32[]{:S(2)}, u32[]{:S(2)}) collective-permute-start(bf16[4,2,128,128]{3,2,1,0:T(8,128)(2,1)S(1)} %get-tuple-element.29.refs_1_), channel_id=1, source_target_pairs={{0,4},{4,0},{8,12},{12,8},{1,5},{5,1},{9,13},{13,9},{2,6},{6,2},{1... | collective-permute-start | bytes 786440 | tf_op jit(solution)/shard_map/ppermute | solution.py:566
  17.0 8.1 %collective-permute-start.2 = (bf16[448,128]{1,0:T(8,128)(2,1)S(1)}, bf16[448,128]{1,0:T(8,128)(2,1)S(1)}, u32[]{:S(2)}, u32[]{:S(2)}) collective-permute-start(bf16[448,128]{1,0:T(8,128)(2,1)S(1)} %collective-permute-done.w_far_0), channel_id=1, source_target_pairs={{0,16},{16,0},{1,17},{17,1},{2,18},{18,2},{3,19},{19,3},{4,20},{20... | collective-permute-start | bytes 344072 | tf_op jit(solution)/shard_map/ppermute | solution.py:566
  23.1 11.6 %collective-permute-start.7 = (bf16[2,48,2048]{2,1,0:T(8,128)(2,1)S(1)}, bf16[2,48,2048]{2,1,0:T(8,128)(2,1)S(1)}, u32[]{:S(2)}, u32[]{:S(2)}) collective-permute-start(bf16[2,48,2048]{2,1,0:T(8,128)(2,1)S(1)} %gate.3.rest_0_), channel_id=1, source_target_pairs={{0,2},{1,3},{2,0},{3,1},{4,6},{5,7},{6,4},{7,5},{8,10},{9,11},{10,... | collective-permute-start | bytes 1179656 | tf_op jit(solution)/shard_map/ppermute | solution.py:566
  25.0 11.3 %collective-permute-start.6 = (bf16[2,48,2048]{2,1,0:T(8,128)(2,1)S(1)}, bf16[2,48,2048]{2,1,0:T(8,128)(2,1)S(1)}, u32[]{:S(2)}, u32[]{:S(2)}) collective-permute-start(bf16[2,48,2048]{2,1,0:T(8,128)(2,1)S(1)} %gate.3.rest_0_), channel_id=1, source_target_pairs={{0,1},{1,0},{2,3},{3,2},{4,5},{5,4},{6,7},{7,6},{8,9},{9,8},{10,11... | collective-permute-start | bytes 1179656 | tf_op jit(solution)/shard_map/ppermute | solution.py:566
  30.8 3.9 %copy-start = (bf16[1,192,8192]{2,1,0:T(8,128)(2,1)S(1)}, bf16[1,192,8192]{2,1,0:T(8,128)(2,1)}, u32[]{:S(2)}) copy-start(bf16[1,192,8192]{2,1,0:T(8,128)(2,1)} %hidden.5) | copy-start | bytes 9437188
  30.8 9.9 %collective-permute-start.3 = (bf16[1600,128]{1,0:T(8,128)(2,1)S(1)}, bf16[1600,128]{1,0:T(8,128)(2,1)S(1)}, u32[]{:S(2)}, u32[]{:S(2)}) collective-permute-start(bf16[1600,128]{1,0:T(8,128)(2,1)S(1)} %get-tuple-element.28.w_far_1), channel_id=1, source_target_pairs={{0,16},{16,0},{1,17},{17,1},{2,18},{18,2},{3,19},{19,3},{4,20},{20... | collective-permute-start | bytes 1228808 | tf_op jit(solution)/shard_map/ppermute | solution.py:566
  32.3 24.7 %collective-permute-start.11 = (bf16[4,2,128,128]{3,2,1,0:T(8,128)(2,1)S(1)}, bf16[4,2,128,128]{3,2,1,0:T(8,128)(2,1)S(1)}, u32[]{:S(2)}, u32[]{:S(2)}) collective-permute-start(bf16[4,2,128,128]{3,2,1,0:T(8,128)(2,1)S(1)} %get-tuple-element.41), channel_id=1, source_target_pairs={{0,8},{4,12},{8,0},{12,4},{1,9},{5,13},{9,1},{13,5},{2,10},{6,14},... | collective-permute-start | bytes 786440 | tf_op jit(solution)/shard_map/ppermute | solution.py:566
  32.3 24.7 %collective-permute-start.12 = (bf16[4,2,128,128]{3,2,1,0:T(8,128)(2,1)S(1)}, bf16[4,2,128,128]{3,2,1,0:T(8,128)(2,1)S(1)}, u32[]{:S(2)}, u32[]{:S(2)}) collective-permute-start(bf16[4,2,128,128]{3,2,1,0:T(8,128)(2,1)S(1)} %get-tuple-element.42), channel_id=1, source_target_pairs={{0,12},{4,8},{8,4},{12,0},{1,13},{5,9},{9,5},{13,1},{2,14},{6,10},... | collective-permute-start | bytes 786440 | tf_op jit(solution)/shard_map/ppermute | solution.py:566
  34.7 1.7 %collective-permute-start.8 = (bf16[2,48,2048]{2,1,0:T(8,128)(2,1)S(1)}, bf16[2,48,2048]{2,1,0:T(8,128)(2,1)S(1)}, u32[]{:S(2)}, u32[]{:S(2)}) collective-permute-start(bf16[2,48,2048]{2,1,0:T(8,128)(2,1)S(1)} %collective-permute-done.7.rest_2_), channel_id=1, source_target_pairs={{0,1},{1,0},{2,3},{3,2},{4,5},{5,4},{6,7},{7,6},{8,9},{9,8},{10,11... | collective-permute-start | bytes 1179656 | tf_op jit(solution)/shard_map/ppermute | solution.py:566
  38.1 6.7 %copy-start.1 = (bf16[1,192,1024]{2,1,0:T(8,128)(2,1)S(1)}, bf16[1,192,1024]{2,1,0:T(8,128)(2,1)}, u32[]{:S(2)}) copy-start(bf16[1,192,1024]{2,1,0:T(8,128)(2,1)} %queries.1) | copy-start | bytes 1179652
  38.1 6.7 %copy-start.3 = (s32[1,16,12]{1,0,2:T(1,128)S(1)}, s32[1,16,12]{1,0,2:T(1,128)}, u32[]{:S(2)}) copy-start(s32[1,16,12]{1,0,2:T(1,128)} %param.17) | copy-start | bytes 2308
  38.1 6.7 %copy-start.4 = (s32[32]{0:T(128)S(1)}, s32[32]{0:T(128)}, u32[]{:S(2)}) copy-start(s32[32]{0:T(128)} %doc_lengths.1) | copy-start | bytes 388
  42.7 9.1 %collective-permute-start.10 = (bf16[192,128]{1,0:T(8,128)(2,1)S(1)}, bf16[192,128]{1,0:T(8,128)(2,1)S(1)}, u32[]{:S(2)}, u32[]{:S(2)}) collective-permute-start(bf16[192,128]{1,0:T(8,128)(2,1)S(1)} %get-tuple-element.33), channel_id=1, source_target_pairs={{0,4},{4,0},{8,12},{12,8},{1,5},{5,1},{9,13},{13,9},{2,6},{6,2},{1... | collective-permute-start | bytes 147464 | tf_op jit(solution)/shard_map/ppermute | solution.py:566
  42.8 10.0 %collective-permute-start.9 = (bf16[192,128]{1,0:T(8,128)(2,1)S(1)}, bf16[192,128]{1,0:T(8,128)(2,1)S(1)}, u32[]{:S(2)}, u32[]{:S(2)}) collective-permute-start(bf16[192,128]{1,0:T(8,128)(2,1)S(1)} %get-tuple-element.32), channel_id=1, source_target_pairs={{0,4},{4,0},{8,12},{12,8},{1,5},{5,1},{9,13},{13,9},{2,6},{6,2},{1... | collective-permute-start | bytes 147464 | tf_op jit(solution)/shard_map/ppermute | solution.py:566
  53.7 10.3 %all-to-all-start = ((bf16[4,96,128]{2,1,0:T(8,128)(2,1)}), bf16[4,96,128]{2,1,0:T(8,128)(2,1)S(1)}, u32[]{:S(2)}, u32[]{:S(2)}) async-start(bf16[4,96,128]{2,1,0:T(8,128)(2,1)} %bitcast.1), calls=%async_computation | async-start | bytes 196608 | tf_op jit(solution)/shard_map/all_to_all | solution.py:614

commit v19 on v18

--- a/solution.py
+++ b/solution.py
@@ -188,7 +188,7 @@
 
 
 def far_kernel(hidden, w_far_0, w_far_1, w_swapped_0, w_swapped_1, near, neighbour, *rest):
-    *quarters, own, part_k, part_v, w, h, n, sems = rest
+    *quarters, own, part_0, part_1, part_2, w, h, n, sems = rest
     group = lax.axis_index("groups")
     start, width = w_far_0.shape
     depth = start + w_far_1.shape[0]
@@ -210,8 +210,9 @@
         one.wait()
     own[...] = near[...] + jnp.dot(h[...], w[...], preferred_element_type=jnp.float32)
     total = neighbour[...] + jnp.dot(n[...], w[...], preferred_element_type=jnp.float32)
-    part_k[...] = total[:, :width].astype(part_k.dtype)
-    part_v[...] = total[:, width:].astype(part_v.dtype)
+    for i, part in enumerate((part_0, part_1, part_2)):
+        count = part.shape[0]
+        part[...] = total[i * count : (i + 1) * count].astype(part.dtype)
 
 
 def project(hidden, w_key, w_value, w_far, w_swapped, quarters, first):
@@ -249,9 +250,9 @@
     )(w_key, w_value, *quarters)
     return pl.pallas_call(
         far_kernel,
-        out_shape=(sums,) + (jax.ShapeDtypeStruct((rows, width), jnp.bfloat16),) * 2,
+        out_shape=(sums,) + (jax.ShapeDtypeStruct((rows // 3, 2 * width), jnp.bfloat16),) * 3,
         in_specs=[ANY] * 5 + [VMEM] * 2 + [ANY] * len(quarters),
-        out_specs=(VMEM,) * 3,
+        out_specs=(VMEM,) * 4,
         scratch_shapes=[
             w_scratch,
             h_scratch,
@@ -363,8 +364,8 @@
     )(request_docs, doc_lengths, jnp.transpose(recompute_rows, (2, 0, 1)), queries)
 
 
-def finish_kernel(own, arrived_k, arrived_v, slot_row, fresh, outgoing):
-    arrived = jnp.concatenate([arrived_k[...], arrived_v[...]], axis=1)
+def finish_kernel(own, arrived_0, arrived_1, arrived_2, slot_row, fresh, outgoing):
+    arrived = jnp.concatenate([arrived_0[...], arrived_1[...], arrived_2[...]], axis=0)
     total = (own[...] + arrived.astype(jnp.float32)).astype(jnp.bfloat16)
     fresh[...] = total
     width = outgoing.shape[1]
@@ -382,7 +383,7 @@
     return pl.pallas_call(
         finish_kernel,
         out_shape=tuple(jax.ShapeDtypeStruct(one, jnp.bfloat16) for one in shapes),
-        in_specs=[VMEM] * 4,
+        in_specs=[VMEM] * 5,
         out_specs=(VMEM, VMEM),
         compiler_params=pltpu.CompilerParams(vmem_limit_bytes=16 * 1024 * 1024),
         name="finish",
@@ -590,7 +591,7 @@
             jnp.concatenate([w_key, w_value], axis=1), "seq", axis=0, tiled=True
         )
         own = jnp.dot(hidden[0], weights, preferred_element_type=jnp.float32)
-        arrived = [jnp.zeros((own.shape[0], head_dim), jnp.bfloat16)] * 2
+        arrived = [jnp.zeros((own.shape[0] // 3, 2 * head_dim), jnp.bfloat16)] * 3
 
     q, held, spare, key_bias, row_place, key_place, slot_row = plan(
         request_docs, doc_lengths, recompute_rows, queries, slot_count, head_dim, doc_len

time: 65.1 us -> 65.1 us (level)
    ppermute x13 -> x14, starting transfers between devices: 15.7 us -> 15.8 us  [swap(): return lax.ppermute(array, axis, [(i, i ^ apart) for i in range(count)])]
    ppermute x13 -> x14, waiting for transfers between devices: 26.4 us -> 26.3 us  [swap(): return lax.ppermute(array, axis, [(i, i ^ apart) for i in range(count)])]
  transfers between devices with their start and end apart: 14 -> 15, of which waited for: 7 -> 8; matrix products, arithmetic and copies ran while one was open for 0% -> 0% of each run, Pallas kernels for 26% -> 26%
where the time goes in v19:
time: 65.1 us; the launch traced here: 64.6 us
  waiting for transfers between devices  26.3 us (40%)
  starting transfers between devices  19.1 us (29%)
  Pallas kernels  17.8 us (27%)
  between operations  0.78 us (1%)
  local copies, waits for them, and re-layouts  0.67 us (1%)
    ppermute x14, waiting for transfers between devices, swap(): return lax.ppermute(array, axis, [(i, i ^ apart) for i in range(count)])  26.3 us
    ppermute x14, starting transfers between devices, swap(): return lax.ppermute(array, axis, [(i, i ^ apart) for i in range(count)])  15.8 us
    pallas_call x1, Pallas kernels, attend(): pl.pallas_call(functools.partial(attend_kernel, by_owner), out_shape=jax....  6.96 us
    all_to_all x1, starting transfers between devices, shards(): lax.all_to_all(outgoing, 'seq', split_axis=0, concat_axis=0, tiled=True)  3.3 us
    pallas_call x1, Pallas kernels, pick_docs(): pl.pallas_call(functools.partial(docs_kernel, by_owner), out_shape=tuple(...  2.12 us
    pallas_call x1, Pallas kernels, project(): pl.pallas_call(far_kernel, out_shape=(sums,) + (jax.ShapeDtypeStruct((row...  1.97 us
    pallas_call x1, Pallas kernels, project(): pl.pallas_call(neighbour_kernel, out_shape=sums, in_specs=[ANY] * (2 + le...  1.63 us
    pallas_call x1, Pallas kernels, project(): pl.pallas_call(near_kernel, out_shape=sums, in_specs=[ANY] * 4, out_specs...  1.61 us
  transfers between devices with their start and end apart: 15, of which 8 were waited for; matrix products, arithmetic and copies ran while one was open for 0% of the time, Pallas kernels for 26%

profile of v19, /device:TPU:0, one launch (start us, length us, event | category | flops | bytes accessed | tf_op | source)
XLA Modules:
  0.0 64.6 jit_solution(5098251813868728508)
XLA Ops:
  0.6 1.2 %pick_sent.1 = (bf16[448,128]{1,0:T(8,128)(2,1)S(1)}, bf16[1600,128]{1,0:T(8,128)(2,1)S(1)}, bf16[2,48,2048]{2,1,0:T(8,128)(2,1)S(1)}) custom-call(bf16[1,192,8192]{2,1,0:T(8,128)(2,1)} %hidden.5, bf16[2048,128]{1,0:T(8,128)(2,1)} %w_key.5, bf16[2048,128]{1,0:T(8,128)(2,1)} %w_value.5), custom_call_target="tpu_custom_call" | custom-call | tf_op jit(solution)/shard_map/pick_sent/pallas_call | solution.py:54
  1.9 3.1 %collective-permute-start.5 = (bf16[2,48,2048]{2,1,0:T(8,128)(2,1)S(1)}, bf16[2,48,2048]{2,1,0:T(8,128)(2,1)S(1)}, u32[]{:S(2)}, u32[]{:S(2)}) collective-permute-start(bf16[2,48,2048]{2,1,0:T(8,128)(2,1)S(1)} %get-tuple-element.31), channel_id=1, source_target_pairs={{0,4},{4,0},{8,12},{12,8},{1,5},{5,1},{9,13},{13,9},{2,6},{6,2},{1... | collective-permute-start | bytes 1179656 | tf_op jit(solution)/shard_map/ppermute | solution.py:567
  5.0 2.6 %collective-permute-start = (bf16[448,128]{1,0:T(8,128)(2,1)S(1)}, bf16[448,128]{1,0:T(8,128)(2,1)S(1)}, u32[]{:S(2)}, u32[]{:S(2)}) collective-permute-start(bf16[448,128]{1,0:T(8,128)(2,1)S(1)} %get-tuple-element.25), channel_id=1, source_target_pairs={{0,8},{4,12},{8,0},{12,4},{1,9},{5,13},{9,1},{13,5},{2,10},{6,14},... | collective-permute-start | bytes 344072 | tf_op jit(solution)/shard_map/ppermute | solution.py:567
  7.9 2.1 %pick_docs.1 = (bf16[4,2,128,128]{3,2,1,0:T(8,128)(2,1)S(1)}, bf16[4,2,128,128]{3,2,1,0:T(8,128)(2,1)S(1)}, bf16[4,2,128,128]{3,2,1,0:T(8,128)(2,1)S(1)}) custom-call(s32[4,16]{1,0:T(4,128)S(1)} %copy-done.2, bf16[8,128,128]{2,1,0:T(8,128)(2,1)} %rest_0_.1, bf16[8,128,128]{2,1,0:T(8,128)(2,1)} %rest_1_.1), custom_call_target="tpu_custom_call" | custom-call | tf_op jit(solution)/shard_map/pick_docs/pallas_call | solution.py:137
  10.2 6.8 %collective-permute-done.w_far_0 = bf16[448,128]{1,0:T(8,128)(2,1)S(1)} collective-permute-done((bf16[448,128]{1,0:T(8,128)(2,1)S(1)}, bf16[448,128]{1,0:T(8,128)(2,1)S(1)}, u32[]{:S(2)}, u32[]{:S(2)}) %collective-permute-start) | collective-permute-done | bytes 114720 | tf_op jit(solution)/shard_map/ppermute | solution.py:567
  17.0 1.5 %collective-permute-start.2 = (bf16[448,128]{1,0:T(8,128)(2,1)S(1)}, bf16[448,128]{1,0:T(8,128)(2,1)S(1)}, u32[]{:S(2)}, u32[]{:S(2)}) collective-permute-start(bf16[448,128]{1,0:T(8,128)(2,1)S(1)} %collective-permute-done.w_far_0), channel_id=1, source_target_pairs={{0,16},{16,0},{1,17},{17,1},{2,18},{18,2},{3,19},{19,3},{4,20},{20... | collective-permute-start | bytes 344072 | tf_op jit(solution)/shard_map/ppermute | solution.py:567
  18.5 4.6 %collective-permute-done.5.refs_0_ = bf16[2,48,2048]{2,1,0:T(8,128)(2,1)S(1)} collective-permute-done((bf16[2,48,2048]{2,1,0:T(8,128)(2,1)S(1)}, bf16[2,48,2048]{2,1,0:T(8,128)(2,1)S(1)}, u32[]{:S(2)}, u32[]{:S(2)}) %collective-permute-start.5) | collective-permute-done | bytes 393248 | tf_op jit(solution)/shard_map/ppermute | solution.py:567
  23.1 2.0 %collective-permute-start.7 = (bf16[2,48,2048]{2,1,0:T(8,128)(2,1)S(1)}, bf16[2,48,2048]{2,1,0:T(8,128)(2,1)S(1)}, u32[]{:S(2)}, u32[]{:S(2)}) collective-permute-start(bf16[2,48,2048]{2,1,0:T(8,128)(2,1)S(1)} %gate.3.rest_0_), channel_id=1, source_target_pairs={{0,2},{1,3},{2,0},{3,1},{4,6},{5,7},{6,4},{7,5},{8,10},{9,11},{10,... | collective-permute-start | bytes 1179656 | tf_op jit(solution)/shard_map/ppermute | solution.py:567
  25.1 5.7 %collective-permute-done.1.refs_2_ = bf16[1600,128]{1,0:T(8,128)(2,1)S(1)} collective-permute-done((bf16[1600,128]{1,0:T(8,128)(2,1)S(1)}, bf16[1600,128]{1,0:T(8,128)(2,1)S(1)}, u32[]{:S(2)}, u32[]{:S(2)}) %collective-permute-start.1) | collective-permute-done | bytes 409632 | tf_op jit(solution)/shard_map/ppermute | solution.py:567
  30.8 1.5 %collective-permute-start.3 = (bf16[1600,128]{1,0:T(8,128)(2,1)S(1)}, bf16[1600,128]{1,0:T(8,128)(2,1)S(1)}, u32[]{:S(2)}, u32[]{:S(2)}) collective-permute-start(bf16[1600,128]{1,0:T(8,128)(2,1)S(1)} %get-tuple-element.29.w_far_1), channel_id=1, source_target_pairs={{0,16},{16,0},{1,17},{17,1},{2,18},{18,2},{3,19},{19,3},{4,20},{20... | collective-permute-start | bytes 1228808 | tf_op jit(solution)/shard_map/ppermute | solution.py:567
  32.3 2.4 %collective-permute-start.13 = (bf16[4,2,128,128]{3,2,1,0:T(8,128)(2,1)S(1)}, bf16[4,2,128,128]{3,2,1,0:T(8,128)(2,1)S(1)}, u32[]{:S(2)}, u32[]{:S(2)}) collective-permute-start(bf16[4,2,128,128]{3,2,1,0:T(8,128)(2,1)S(1)} %get-tuple-element.44), channel_id=1, source_target_pairs={{0,12},{4,8},{8,4},{12,0},{1,13},{5,9},{9,5},{13,1},{2,14},{6,10},... | collective-permute-start | bytes 786440 | tf_op jit(solution)/shard_map/ppermute | solution.py:567
  34.7 1.6 %project_near.1.near = f32[192,256]{1,0:T(8,128)S(1)} custom-call(bf16[1,192,8192]{2,1,0:T(8,128)(2,1)S(1)} %copy-done, bf16[2048,128]{1,0:T(8,128)(2,1)} %w_key.5, bf16[2048,128]{1,0:T(8,128)(2,1)} %w_value.5, bf16[4,2,128,128]{3,2,1,0:T(8,128)(2,1)S(1)} %collective-permute-done.4._.rest_4_), custom_call_target="tpu_custom_call" | custom-call | flops 10000000000 | bytes 1 | tf_op jit(solution)/shard_map/project_near/pallas_call | solution.py:227
  36.4 1.6 %project_neighbour.1.neighbour = f32[192,256]{1,0:T(8,128)S(1)} custom-call(bf16[2048,128]{1,0:T(8,128)(2,1)} %w_key.5, bf16[2048,128]{1,0:T(8,128)(2,1)} %w_value.5, bf16[2,48,2048]{2,1,0:T(8,128)(2,1)S(1)} %gate.3.rest_0_, bf16[2,48,2048]{2,1,0:T(8,128)(2,1)S(1)} %collective-permute-done.6.rest_1_, ...), custom_call_target="tpu_custom_call" | custom-call | flops 1 | bytes 1 | tf_op jit(solution)/shard_map/project_neighbour/pallas_call | solution.py:237
  38.1 2.6 %collective-permute-done.3.w_swapped_1 = bf16[1600,128]{1,0:T(8,128)(2,1)S(1)} collective-permute-done((bf16[1600,128]{1,0:T(8,128)(2,1)S(1)}, bf16[1600,128]{1,0:T(8,128)(2,1)S(1)}, u32[]{:S(2)}, u32[]{:S(2)}) %collective-permute-start.3) | collective-permute-done | bytes 409632 | tf_op jit(solution)/shard_map/ppermute | solution.py:567
  40.7 2.0 %project_far.1 = (f32[192,256]{1,0:T(8,128)S(1)}, bf16[64,256]{1,0:T(8,128)(2,1)S(1)}, bf16[64,256]{1,0:T(8,128)(2,1)S(1)}, bf16[64,256]{1,0:T(8,128)(2,1)S(1)}) custom-call(bf16[1,192,8192]{2,1,0:T(8,128)(2,1)S(1)} %copy-done, bf16[448,128]{1,0:T(8,128)(2,1)S(1)} %collective-permute-done.w_far_0, bf16[1600,128]{1,0:T(8,128)(2,1)S(1)} %get-tuple-element.29.w_far_1, ...), custom_call_target="tpu_custom_call" | custom-call | flops 1 | bytes 1 | tf_op jit(solution)/shard_map/project_far/pallas_call | solution.py:251
  42.8 2.0 %collective-permute-start.11 = (bf16[64,256]{1,0:T(8,128)(2,1)S(1)}, bf16[64,256]{1,0:T(8,128)(2,1)S(1)}, u32[]{:S(2)}, u32[]{:S(2)}) collective-permute-start(bf16[64,256]{1,0:T(8,128)(2,1)S(1)} %get-tuple-element.35), channel_id=1, source_target_pairs={{0,4},{4,0},{8,12},{12,8},{1,5},{5,1},{9,13},{13,9},{2,6},{6,2},{1... | collective-permute-start | bytes 98312 | tf_op jit(solution)/shard_map/ppermute | solution.py:567
  44.9 1.4 %plan.1 = (bf16[1536,256]{1,0:T(8,128)(2,1)S(1)}, bf16[2048,128]{1,0:T(8,128)(2,1)S(1)}, bf16[16,2048]{1,0:T(8,128)(2,1)S(1)}, f32[1,2048]{1,0:T(1,128)S(1)}, s3...) custom-call(s32[4,16]{1,0:T(4,128)S(1)} %copy-done.2, s32[32]{0:T(128)S(1)} %copy-done.4, ...), custom_call_target="tpu_custom_call" | custom-call | tf_op jit(solution)/shard_map/plan/pallas_call | solution.py:356
  46.3 5.2 %collective-permute-done.10.arrived_1 = bf16[64,256]{1,0:T(8,128)(2,1)S(1)} collective-permute-done((bf16[64,256]{1,0:T(8,128)(2,1)S(1)}, bf16[64,256]{1,0:T(8,128)(2,1)S(1)}, u32[]{:S(2)}, u32[]{:S(2)}) %collective-permute-start.10) | collective-permute-done | bytes 32800 | tf_op jit(solution)/shard_map/ppermute | solution.py:567
  51.5 0.7 %collective-permute-done.11.arrived_2 = bf16[64,256]{1,0:T(8,128)(2,1)S(1)} collective-permute-done((bf16[64,256]{1,0:T(8,128)(2,1)S(1)}, bf16[64,256]{1,0:T(8,128)(2,1)S(1)}, u32[]{:S(2)}, u32[]{:S(2)}) %collective-permute-start.11) | collective-permute-done | bytes 32800 | tf_op jit(solution)/shard_map/ppermute | solution.py:567
  52.2 0.6 collective-permute-done.9.arrived_0
  52.8 0.9 %finish.1 = (bf16[192,256]{1,0:T(8,128)(2,1)S(1)}, bf16[384,128]{1,0:T(8,128)(2,1)}) custom-call(f32[192,256]{1,0:T(8,128)S(1)} %get-tuple-element.32.own, bf16[64,256]{1,0:T(8,128)(2,1)S(1)} %collective-permute-done.9.arrived_0, bf16[64,256]{1,0:T(8,128)(2,1)S(1)} %collective-permute-done.10.arrived_1, ...), custom_call_target="tpu_custom_call" | custom-call | tf_op jit(solution)/shard_map/finish/pallas_call | solution.py:383
  53.7 3.3 %all-to-all-start = ((bf16[4,96,128]{2,1,0:T(8,128)(2,1)}), bf16[4,96,128]{2,1,0:T(8,128)(2,1)S(1)}, u32[]{:S(2)}, u32[]{:S(2)}) async-start(bf16[4,96,128]{2,1,0:T(8,128)(2,1)} %bitcast.1), calls=%async_computation | async-start | bytes 196608 | tf_op jit(solution)/shard_map/all_to_all | solution.py:615
  57.0 7.0 %attend.1 = bf16[1,192,1024]{2,1,0:T(8,128)(2,1)} custom-call(s32[4,16]{1,0:T(4,128)S(1)} %copy-done.2, bf16[1536,256]{1,0:T(8,128)(2,1)S(1)} %get-tuple-element.24.q, bf16[192,256]{1,0:T(8,128)(2,1)S(1)} %get-tuple-element.37.fresh, bf16[2048,128]{1,0:T(8,128)(2,1)S(1)} %get-tuple-element.38.held, bf16[16,2048]{1,0:T(8,128)(2,1)S(1)} %get-tuple-element.39.spare, ...), custom_call_target="tpu_custom_call" | custom-call | tf_op jit(solution)/shard_map/attend/pallas_call | solution.py:520
  64.0 0.6 copy.20
  (27 shorter events, 0.8 us)
Async XLA Ops:
  0.6 7.3 %copy-start.2 = (s32[4,16]{1,0:T(4,128)S(1)}, s32[4,16]{1,0:T(4,128)}, u32[]{:S(2)}) copy-start(s32[4,16]{1,0:T(4,128)} %request_docs.5) | copy-start | bytes 772
  1.9 21.2 %collective-permute-start.5 = (bf16[2,48,2048]{2,1,0:T(8,128)(2,1)S(1)}, bf16[2,48,2048]{2,1,0:T(8,128)(2,1)S(1)}, u32[]{:S(2)}, u32[]{:S(2)}) collective-permute-start(bf16[2,48,2048]{2,1,0:T(8,128)(2,1)S(1)} %get-tuple-element.31), channel_id=1, source_target_pairs={{0,4},{4,0},{8,12},{12,8},{1,5},{5,1},{9,13},{13,9},{2,6},{6,2},{1... | collective-permute-start | bytes 1179656 | tf_op jit(solution)/shard_map/ppermute | solution.py:567
  5.0 12.0 %collective-permute-start = (bf16[448,128]{1,0:T(8,128)(2,1)S(1)}, bf16[448,128]{1,0:T(8,128)(2,1)S(1)}, u32[]{:S(2)}, u32[]{:S(2)}) collective-permute-start(bf16[448,128]{1,0:T(8,128)(2,1)S(1)} %get-tuple-element.25), channel_id=1, source_target_pairs={{0,8},{4,12},{8,0},{12,4},{1,9},{5,13},{9,1},{13,5},{2,10},{6,14},... | collective-permute-start | bytes 344072 | tf_op jit(solution)/shard_map/ppermute | solution.py:567
  7.5 23.2 %collective-permute-start.1 = (bf16[1600,128]{1,0:T(8,128)(2,1)S(1)}, bf16[1600,128]{1,0:T(8,128)(2,1)S(1)}, u32[]{:S(2)}, u32[]{:S(2)}) collective-permute-start(bf16[1600,128]{1,0:T(8,128)(2,1)S(1)} %get-tuple-element.28), channel_id=1, source_target_pairs={{0,8},{4,12},{8,0},{12,4},{1,9},{5,13},{9,1},{13,5},{2,10},{6,14},... | collective-permute-start | bytes 1228808 | tf_op jit(solution)/shard_map/ppermute | solution.py:567
  10.0 22.3 %collective-permute-start.4 = (bf16[4,2,128,128]{3,2,1,0:T(8,128)(2,1)S(1)}, bf16[4,2,128,128]{3,2,1,0:T(8,128)(2,1)S(1)}, u32[]{:S(2)}, u32[]{:S(2)}) collective-permute-start(bf16[4,2,128,128]{3,2,1,0:T(8,128)(2,1)S(1)} %get-tuple-element.30.refs_1_), channel_id=1, source_target_pairs={{0,4},{4,0},{8,12},{12,8},{1,5},{5,1},{9,13},{13,9},{2,6},{6,2},{1... | collective-permute-start | bytes 786440 | tf_op jit(solution)/shard_map/ppermute | solution.py:567
  17.0 8.1 %collective-permute-start.2 = (bf16[448,128]{1,0:T(8,128)(2,1)S(1)}, bf16[448,128]{1,0:T(8,128)(2,1)S(1)}, u32[]{:S(2)}, u32[]{:S(2)}) collective-permute-start(bf16[448,128]{1,0:T(8,128)(2,1)S(1)} %collective-permute-done.w_far_0), channel_id=1, source_target_pairs={{0,16},{16,0},{1,17},{17,1},{2,18},{18,2},{3,19},{19,3},{4,20},{20... | collective-permute-start | bytes 344072 | tf_op jit(solution)/shard_map/ppermute | solution.py:567
  23.1 11.6 %collective-permute-start.7 = (bf16[2,48,2048]{2,1,0:T(8,128)(2,1)S(1)}, bf16[2,48,2048]{2,1,0:T(8,128)(2,1)S(1)}, u32[]{:S(2)}, u32[]{:S(2)}) collective-permute-start(bf16[2,48,2048]{2,1,0:T(8,128)(2,1)S(1)} %gate.3.rest_0_), channel_id=1, source_target_pairs={{0,2},{1,3},{2,0},{3,1},{4,6},{5,7},{6,4},{7,5},{8,10},{9,11},{10,... | collective-permute-start | bytes 1179656 | tf_op jit(solution)/shard_map/ppermute | solution.py:567
  25.0 11.3 %collective-permute-start.6 = (bf16[2,48,2048]{2,1,0:T(8,128)(2,1)S(1)}, bf16[2,48,2048]{2,1,0:T(8,128)(2,1)S(1)}, u32[]{:S(2)}, u32[]{:S(2)}) collective-permute-start(bf16[2,48,2048]{2,1,0:T(8,128)(2,1)S(1)} %gate.3.rest_0_), channel_id=1, source_target_pairs={{0,1},{1,0},{2,3},{3,2},{4,5},{5,4},{6,7},{7,6},{8,9},{9,8},{10,11... | collective-permute-start | bytes 1179656 | tf_op jit(solution)/shard_map/ppermute | solution.py:567
  30.8 3.9 %copy-start = (bf16[1,192,8192]{2,1,0:T(8,128)(2,1)S(1)}, bf16[1,192,8192]{2,1,0:T(8,128)(2,1)}, u32[]{:S(2)}) copy-start(bf16[1,192,8192]{2,1,0:T(8,128)(2,1)} %hidden.5) | copy-start | bytes 9437188
  30.8 9.9 %collective-permute-start.3 = (bf16[1600,128]{1,0:T(8,128)(2,1)S(1)}, bf16[1600,128]{1,0:T(8,128)(2,1)S(1)}, u32[]{:S(2)}, u32[]{:S(2)}) collective-permute-start(bf16[1600,128]{1,0:T(8,128)(2,1)S(1)} %get-tuple-element.29.w_far_1), channel_id=1, source_target_pairs={{0,16},{16,0},{1,17},{17,1},{2,18},{18,2},{3,19},{19,3},{4,20},{20... | collective-permute-start | bytes 1228808 | tf_op jit(solution)/shard_map/ppermute | solution.py:567
  32.3 24.7 %collective-permute-start.12 = (bf16[4,2,128,128]{3,2,1,0:T(8,128)(2,1)S(1)}, bf16[4,2,128,128]{3,2,1,0:T(8,128)(2,1)S(1)}, u32[]{:S(2)}, u32[]{:S(2)}) collective-permute-start(bf16[4,2,128,128]{3,2,1,0:T(8,128)(2,1)S(1)} %get-tuple-element.43), channel_id=1, source_target_pairs={{0,8},{4,12},{8,0},{12,4},{1,9},{5,13},{9,1},{13,5},{2,10},{6,14},... | collective-permute-start | bytes 786440 | tf_op jit(solution)/shard_map/ppermute | solution.py:567
  32.3 24.7 %collective-permute-start.13 = (bf16[4,2,128,128]{3,2,1,0:T(8,128)(2,1)S(1)}, bf16[4,2,128,128]{3,2,1,0:T(8,128)(2,1)S(1)}, u32[]{:S(2)}, u32[]{:S(2)}) collective-permute-start(bf16[4,2,128,128]{3,2,1,0:T(8,128)(2,1)S(1)} %get-tuple-element.44), channel_id=1, source_target_pairs={{0,12},{4,8},{8,4},{12,0},{1,13},{5,9},{9,5},{13,1},{2,14},{6,10},... | collective-permute-start | bytes 786440 | tf_op jit(solution)/shard_map/ppermute | solution.py:567
  34.7 1.7 %collective-permute-start.8 = (bf16[2,48,2048]{2,1,0:T(8,128)(2,1)S(1)}, bf16[2,48,2048]{2,1,0:T(8,128)(2,1)S(1)}, u32[]{:S(2)}, u32[]{:S(2)}) collective-permute-start(bf16[2,48,2048]{2,1,0:T(8,128)(2,1)S(1)} %collective-permute-done.7.rest_2_), channel_id=1, source_target_pairs={{0,1},{1,0},{2,3},{3,2},{4,5},{5,4},{6,7},{7,6},{8,9},{9,8},{10,11... | collective-permute-start | bytes 1179656 | tf_op jit(solution)/shard_map/ppermute | solution.py:567
  38.1 6.8 %copy-start.1 = (bf16[1,192,1024]{2,1,0:T(8,128)(2,1)S(1)}, bf16[1,192,1024]{2,1,0:T(8,128)(2,1)}, u32[]{:S(2)}) copy-start(bf16[1,192,1024]{2,1,0:T(8,128)(2,1)} %queries.1) | copy-start | bytes 1179652
  38.1 6.8 %copy-start.3 = (s32[1,16,12]{1,0,2:T(1,128)S(1)}, s32[1,16,12]{1,0,2:T(1,128)}, u32[]{:S(2)}) copy-start(s32[1,16,12]{1,0,2:T(1,128)} %param.17) | copy-start | bytes 2308
  38.1 6.8 %copy-start.4 = (s32[32]{0:T(128)S(1)}, s32[32]{0:T(128)}, u32[]{:S(2)}) copy-start(s32[32]{0:T(128)} %doc_lengths.1) | copy-start | bytes 388
  42.7 8.8 %collective-permute-start.10 = (bf16[64,256]{1,0:T(8,128)(2,1)S(1)}, bf16[64,256]{1,0:T(8,128)(2,1)S(1)}, u32[]{:S(2)}, u32[]{:S(2)}) collective-permute-start(bf16[64,256]{1,0:T(8,128)(2,1)S(1)} %get-tuple-element.34), channel_id=1, source_target_pairs={{0,4},{4,0},{8,12},{12,8},{1,5},{5,1},{9,13},{13,9},{2,6},{6,2},{1... | collective-permute-start | bytes 98312 | tf_op jit(solution)/shard_map/ppermute | solution.py:567
  42.8 9.4 %collective-permute-start.11 = (bf16[64,256]{1,0:T(8,128)(2,1)S(1)}, bf16[64,256]{1,0:T(8,128)(2,1)S(1)}, u32[]{:S(2)}, u32[]{:S(2)}) collective-permute-start(bf16[64,256]{1,0:T(8,128)(2,1)S(1)} %get-tuple-element.35), channel_id=1, source_target_pairs={{0,4},{4,0},{8,12},{12,8},{1,5},{5,1},{9,13},{13,9},{2,6},{6,2},{1... | collective-permute-start | bytes 98312 | tf_op jit(solution)/shard_map/ppermute | solution.py:567
  44.8 8.0 %collective-permute-start.9 = (bf16[64,256]{1,0:T(8,128)(2,1)S(1)}, bf16[64,256]{1,0:T(8,128)(2,1)S(1)}, u32[]{:S(2)}, u32[]{:S(2)}) collective-permute-start(bf16[64,256]{1,0:T(8,128)(2,1)S(1)} %get-tuple-element.33), channel_id=1, source_target_pairs={{0,4},{4,0},{8,12},{12,8},{1,5},{5,1},{9,13},{13,9},{2,6},{6,2},{1... | collective-permute-start | bytes 98312 | tf_op jit(solution)/shard_map/ppermute | solution.py:567
  53.7 10.3 %all-to-all-start = ((bf16[4,96,128]{2,1,0:T(8,128)(2,1)}), bf16[4,96,128]{2,1,0:T(8,128)(2,1)S(1)}, u32[]{:S(2)}, u32[]{:S(2)}) async-start(bf16[4,96,128]{2,1,0:T(8,128)(2,1)} %bitcast.1), calls=%async_computation | async-start | bytes 196608 | tf_op jit(solution)/shard_map/all_to_all | solution.py:615

commit v20 on v19

--- a/solution.py
+++ b/solution.py
@@ -486,26 +486,23 @@
             kept = jnp.where(allowed[None], scores(some_keys).reshape(shape), MASKED)
             return kept.reshape(heads * block_rows, some_keys.shape[0])
 
-        chunks, sides = [], []
-        for c in range(b):
-            part = slice(c * block_keys, (c + 1) * block_keys)
-            chunks.append(scores(keys[part, :]))
-            sides.append(values[part, :])
         part = slice(b * block_keys, (b + 1) * block_keys)
         allowed = (slot_place + b * block_keys <= own_place) & (key_bias[:, part] == 0)
+        chunks = [scores(keys[: b * block_keys, :])] if b else []
         chunks.append(masked(keys[part, :], allowed))
-        sides.append(values[part, :])
         chunks.append(masked(fresh_k, key_place[...] <= own_place))
-        sides.append(fresh_v)
         lane_max = functools.reduce(
             jnp.maximum,
             [one[:, i : i + 128] for one in chunks for i in range(0, one.shape[1], 128)],
         )
         row_max = jnp.max(lane_max, axis=1, keepdims=True)
-        total = jnp.zeros((heads * block_rows, 2 * head_dim), jnp.float32)
-        for one, side in zip(chunks, sides):
-            powers = jnp.exp2(one - row_max).astype(jnp.bfloat16)
-            total += jnp.dot(powers, side, preferred_element_type=jnp.float32)
+        powers = [jnp.exp2(one - row_max).astype(jnp.bfloat16) for one in chunks]
+        total = jnp.dot(
+            jnp.concatenate(powers[:-1], axis=1),
+            values[: (b + 1) * block_keys, :],
+            preferred_element_type=jnp.float32,
+        )
+        total += jnp.dot(powers[-1], fresh_v, preferred_element_type=jnp.float32)
         result = (total[:, :head_dim] / total[:, head_dim:]).astype(mixed.dtype)
         for h in range(heads):
             mixed[0, rows, h * head_dim : (h + 1) * head_dim] = result[

time: 65.1 us -> 65.1 us (level)
  no operation moved by 1% of the time
where the time goes in v20:
time: 65.1 us; the launch traced here: 64.6 us
  waiting for transfers between devices  26.3 us (40%)
  starting transfers between devices  19.1 us (29%)
  Pallas kernels  17.8 us (27%)
  between operations  0.78 us (1%)
  local copies, waits for them, and re-layouts  0.67 us (1%)
    ppermute x14, waiting for transfers between devices, swap(): return lax.ppermute(array, axis, [(i, i ^ apart) for i in range(count)])  26.3 us
    ppermute x14, starting transfers between devices, swap(): return lax.ppermute(array, axis, [(i, i ^ apart) for i in range(count)])  15.8 us
    pallas_call x1, Pallas kernels, attend(): pl.pallas_call(functools.partial(attend_kernel, by_owner), out_shape=jax....  6.93 us
    all_to_all x1, starting transfers between devices, shards(): lax.all_to_all(outgoing, 'seq', split_axis=0, concat_axis=0, tiled=True)  3.3 us
    pallas_call x1, Pallas kernels, pick_docs(): pl.pallas_call(functools.partial(docs_kernel, by_owner), out_shape=tuple(...  2.12 us
    pallas_call x1, Pallas kernels, project(): pl.pallas_call(far_kernel, out_shape=(sums,) + (jax.ShapeDtypeStruct((row...  1.97 us
    pallas_call x1, Pallas kernels, project(): pl.pallas_call(neighbour_kernel, out_shape=sums, in_specs=[ANY] * (2 + le...  1.63 us
    pallas_call x1, Pallas kernels, project(): pl.pallas_call(near_kernel, out_shape=sums, in_specs=[ANY] * 4, out_specs...  1.61 us
  transfers between devices with their start and end apart: 15, of which 8 were waited for; matrix products, arithmetic and copies ran while one was open for 0% of the time, Pallas kernels for 26%

profile of v20, /device:TPU:0, one launch (start us, length us, event | category | flops | bytes accessed | tf_op | source)
XLA Modules:
  0.0 64.6 jit_solution(9118258815803439526)
XLA Ops:
  0.6 1.2 %pick_sent.1 = (bf16[448,128]{1,0:T(8,128)(2,1)S(1)}, bf16[1600,128]{1,0:T(8,128)(2,1)S(1)}, bf16[2,48,2048]{2,1,0:T(8,128)(2,1)S(1)}) custom-call(bf16[1,192,8192]{2,1,0:T(8,128)(2,1)} %hidden.5, bf16[2048,128]{1,0:T(8,128)(2,1)} %w_key.5, bf16[2048,128]{1,0:T(8,128)(2,1)} %w_value.5), custom_call_target="tpu_custom_call" | custom-call | tf_op jit(solution)/shard_map/pick_sent/pallas_call | solution.py:54
  1.9 3.1 %collective-permute-start.5 = (bf16[2,48,2048]{2,1,0:T(8,128)(2,1)S(1)}, bf16[2,48,2048]{2,1,0:T(8,128)(2,1)S(1)}, u32[]{:S(2)}, u32[]{:S(2)}) collective-permute-start(bf16[2,48,2048]{2,1,0:T(8,128)(2,1)S(1)} %get-tuple-element.31), channel_id=1, source_target_pairs={{0,4},{4,0},{8,12},{12,8},{1,5},{5,1},{9,13},{13,9},{2,6},{6,2},{1... | collective-permute-start | bytes 1179656 | tf_op jit(solution)/shard_map/ppermute | solution.py:564
  5.0 2.6 %collective-permute-start = (bf16[448,128]{1,0:T(8,128)(2,1)S(1)}, bf16[448,128]{1,0:T(8,128)(2,1)S(1)}, u32[]{:S(2)}, u32[]{:S(2)}) collective-permute-start(bf16[448,128]{1,0:T(8,128)(2,1)S(1)} %get-tuple-element.25), channel_id=1, source_target_pairs={{0,8},{4,12},{8,0},{12,4},{1,9},{5,13},{9,1},{13,5},{2,10},{6,14},... | collective-permute-start | bytes 344072 | tf_op jit(solution)/shard_map/ppermute | solution.py:564
  7.9 2.1 %pick_docs.1 = (bf16[4,2,128,128]{3,2,1,0:T(8,128)(2,1)S(1)}, bf16[4,2,128,128]{3,2,1,0:T(8,128)(2,1)S(1)}, bf16[4,2,128,128]{3,2,1,0:T(8,128)(2,1)S(1)}) custom-call(s32[4,16]{1,0:T(4,128)S(1)} %copy-done.2, bf16[8,128,128]{2,1,0:T(8,128)(2,1)} %rest_0_.1, bf16[8,128,128]{2,1,0:T(8,128)(2,1)} %rest_1_.1), custom_call_target="tpu_custom_call" | custom-call | tf_op jit(solution)/shard_map/pick_docs/pallas_call | solution.py:137
  10.2 6.8 %collective-permute-done.w_far_0 = bf16[448,128]{1,0:T(8,128)(2,1)S(1)} collective-permute-done((bf16[448,128]{1,0:T(8,128)(2,1)S(1)}, bf16[448,128]{1,0:T(8,128)(2,1)S(1)}, u32[]{:S(2)}, u32[]{:S(2)}) %collective-permute-start) | collective-permute-done | bytes 114720 | tf_op jit(solution)/shard_map/ppermute | solution.py:564
  17.0 1.5 %collective-permute-start.2 = (bf16[448,128]{1,0:T(8,128)(2,1)S(1)}, bf16[448,128]{1,0:T(8,128)(2,1)S(1)}, u32[]{:S(2)}, u32[]{:S(2)}) collective-permute-start(bf16[448,128]{1,0:T(8,128)(2,1)S(1)} %collective-permute-done.w_far_0), channel_id=1, source_target_pairs={{0,16},{16,0},{1,17},{17,1},{2,18},{18,2},{3,19},{19,3},{4,20},{20... | collective-permute-start | bytes 344072 | tf_op jit(solution)/shard_map/ppermute | solution.py:564
  18.5 4.6 %collective-permute-done.5.refs_0_ = bf16[2,48,2048]{2,1,0:T(8,128)(2,1)S(1)} collective-permute-done((bf16[2,48,2048]{2,1,0:T(8,128)(2,1)S(1)}, bf16[2,48,2048]{2,1,0:T(8,128)(2,1)S(1)}, u32[]{:S(2)}, u32[]{:S(2)}) %collective-permute-start.5) | collective-permute-done | bytes 393248 | tf_op jit(solution)/shard_map/ppermute | solution.py:564
  23.1 2.0 %collective-permute-start.7 = (bf16[2,48,2048]{2,1,0:T(8,128)(2,1)S(1)}, bf16[2,48,2048]{2,1,0:T(8,128)(2,1)S(1)}, u32[]{:S(2)}, u32[]{:S(2)}) collective-permute-start(bf16[2,48,2048]{2,1,0:T(8,128)(2,1)S(1)} %gate.3.rest_0_), channel_id=1, source_target_pairs={{0,2},{1,3},{2,0},{3,1},{4,6},{5,7},{6,4},{7,5},{8,10},{9,11},{10,... | collective-permute-start | bytes 1179656 | tf_op jit(solution)/shard_map/ppermute | solution.py:564
  25.1 5.7 %collective-permute-done.1.refs_2_ = bf16[1600,128]{1,0:T(8,128)(2,1)S(1)} collective-permute-done((bf16[1600,128]{1,0:T(8,128)(2,1)S(1)}, bf16[1600,128]{1,0:T(8,128)(2,1)S(1)}, u32[]{:S(2)}, u32[]{:S(2)}) %collective-permute-start.1) | collective-permute-done | bytes 409632 | tf_op jit(solution)/shard_map/ppermute | solution.py:564
  30.8 1.5 %collective-permute-start.3 = (bf16[1600,128]{1,0:T(8,128)(2,1)S(1)}, bf16[1600,128]{1,0:T(8,128)(2,1)S(1)}, u32[]{:S(2)}, u32[]{:S(2)}) collective-permute-start(bf16[1600,128]{1,0:T(8,128)(2,1)S(1)} %get-tuple-element.29.w_far_1), channel_id=1, source_target_pairs={{0,16},{16,0},{1,17},{17,1},{2,18},{18,2},{3,19},{19,3},{4,20},{20... | collective-permute-start | bytes 1228808 | tf_op jit(solution)/shard_map/ppermute | solution.py:564
  32.3 2.4 %collective-permute-start.13 = (bf16[4,2,128,128]{3,2,1,0:T(8,128)(2,1)S(1)}, bf16[4,2,128,128]{3,2,1,0:T(8,128)(2,1)S(1)}, u32[]{:S(2)}, u32[]{:S(2)}) collective-permute-start(bf16[4,2,128,128]{3,2,1,0:T(8,128)(2,1)S(1)} %get-tuple-element.44), channel_id=1, source_target_pairs={{0,12},{4,8},{8,4},{12,0},{1,13},{5,9},{9,5},{13,1},{2,14},{6,10},... | collective-permute-start | bytes 786440 | tf_op jit(solution)/shard_map/ppermute | solution.py:564
  34.7 1.6 %project_near.1.near = f32[192,256]{1,0:T(8,128)S(1)} custom-call(bf16[1,192,8192]{2,1,0:T(8,128)(2,1)S(1)} %copy-done, bf16[2048,128]{1,0:T(8,128)(2,1)} %w_key.5, bf16[2048,128]{1,0:T(8,128)(2,1)} %w_value.5, bf16[4,2,128,128]{3,2,1,0:T(8,128)(2,1)S(1)} %collective-permute-done.4._.rest_4_), custom_call_target="tpu_custom_call" | custom-call | flops 10000000000 | bytes 1 | tf_op jit(solution)/shard_map/project_near/pallas_call | solution.py:227
  36.4 1.6 %project_neighbour.1.neighbour = f32[192,256]{1,0:T(8,128)S(1)} custom-call(bf16[2048,128]{1,0:T(8,128)(2,1)} %w_key.5, bf16[2048,128]{1,0:T(8,128)(2,1)} %w_value.5, bf16[2,48,2048]{2,1,0:T(8,128)(2,1)S(1)} %gate.3.rest_0_, bf16[2,48,2048]{2,1,0:T(8,128)(2,1)S(1)} %collective-permute-done.6.rest_1_, ...), custom_call_target="tpu_custom_call" | custom-call | flops 1 | bytes 1 | tf_op jit(solution)/shard_map/project_neighbour/pallas_call | solution.py:237
  38.1 2.6 %collective-permute-done.3.w_swapped_1 = bf16[1600,128]{1,0:T(8,128)(2,1)S(1)} collective-permute-done((bf16[1600,128]{1,0:T(8,128)(2,1)S(1)}, bf16[1600,128]{1,0:T(8,128)(2,1)S(1)}, u32[]{:S(2)}, u32[]{:S(2)}) %collective-permute-start.3) | collective-permute-done | bytes 409632 | tf_op jit(solution)/shard_map/ppermute | solution.py:564
  40.7 2.0 %project_far.1 = (f32[192,256]{1,0:T(8,128)S(1)}, bf16[64,256]{1,0:T(8,128)(2,1)S(1)}, bf16[64,256]{1,0:T(8,128)(2,1)S(1)}, bf16[64,256]{1,0:T(8,128)(2,1)S(1)}) custom-call(bf16[1,192,8192]{2,1,0:T(8,128)(2,1)S(1)} %copy-done, bf16[448,128]{1,0:T(8,128)(2,1)S(1)} %collective-permute-done.w_far_0, bf16[1600,128]{1,0:T(8,128)(2,1)S(1)} %get-tuple-element.29.w_far_1, ...), custom_call_target="tpu_custom_call" | custom-call | flops 1 | bytes 1 | tf_op jit(solution)/shard_map/project_far/pallas_call | solution.py:251
  42.8 2.0 %collective-permute-start.11 = (bf16[64,256]{1,0:T(8,128)(2,1)S(1)}, bf16[64,256]{1,0:T(8,128)(2,1)S(1)}, u32[]{:S(2)}, u32[]{:S(2)}) collective-permute-start(bf16[64,256]{1,0:T(8,128)(2,1)S(1)} %get-tuple-element.35), channel_id=1, source_target_pairs={{0,4},{4,0},{8,12},{12,8},{1,5},{5,1},{9,13},{13,9},{2,6},{6,2},{1... | collective-permute-start | bytes 98312 | tf_op jit(solution)/shard_map/ppermute | solution.py:564
  44.9 1.4 %plan.1 = (bf16[1536,256]{1,0:T(8,128)(2,1)S(1)}, bf16[2048,128]{1,0:T(8,128)(2,1)S(1)}, bf16[16,2048]{1,0:T(8,128)(2,1)S(1)}, f32[1,2048]{1,0:T(1,128)S(1)}, s3...) custom-call(s32[4,16]{1,0:T(4,128)S(1)} %copy-done.2, s32[32]{0:T(128)S(1)} %copy-done.4, ...), custom_call_target="tpu_custom_call" | custom-call | tf_op jit(solution)/shard_map/plan/pallas_call | solution.py:356
  46.3 5.2 %collective-permute-done.10.arrived_1 = bf16[64,256]{1,0:T(8,128)(2,1)S(1)} collective-permute-done((bf16[64,256]{1,0:T(8,128)(2,1)S(1)}, bf16[64,256]{1,0:T(8,128)(2,1)S(1)}, u32[]{:S(2)}, u32[]{:S(2)}) %collective-permute-start.10) | collective-permute-done | bytes 32800 | tf_op jit(solution)/shard_map/ppermute | solution.py:564
  51.5 0.7 %collective-permute-done.11.arrived_2 = bf16[64,256]{1,0:T(8,128)(2,1)S(1)} collective-permute-done((bf16[64,256]{1,0:T(8,128)(2,1)S(1)}, bf16[64,256]{1,0:T(8,128)(2,1)S(1)}, u32[]{:S(2)}, u32[]{:S(2)}) %collective-permute-start.11) | collective-permute-done | bytes 32800 | tf_op jit(solution)/shard_map/ppermute | solution.py:564
  52.2 0.6 collective-permute-done.9.arrived_0
  52.8 0.9 %finish.1 = (bf16[192,256]{1,0:T(8,128)(2,1)S(1)}, bf16[384,128]{1,0:T(8,128)(2,1)}) custom-call(f32[192,256]{1,0:T(8,128)S(1)} %get-tuple-element.32.own, bf16[64,256]{1,0:T(8,128)(2,1)S(1)} %collective-permute-done.9.arrived_0, bf16[64,256]{1,0:T(8,128)(2,1)S(1)} %collective-permute-done.10.arrived_1, ...), custom_call_target="tpu_custom_call" | custom-call | tf_op jit(solution)/shard_map/finish/pallas_call | solution.py:383
  53.7 3.3 %all-to-all-start = ((bf16[4,96,128]{2,1,0:T(8,128)(2,1)}), bf16[4,96,128]{2,1,0:T(8,128)(2,1)S(1)}, u32[]{:S(2)}, u32[]{:S(2)}) async-start(bf16[4,96,128]{2,1,0:T(8,128)(2,1)} %bitcast.1), calls=%async_computation | async-start | bytes 196608 | tf_op jit(solution)/shard_map/all_to_all | solution.py:612
  57.0 6.9 %attend.1 = bf16[1,192,1024]{2,1,0:T(8,128)(2,1)} custom-call(s32[4,16]{1,0:T(4,128)S(1)} %copy-done.2, bf16[1536,256]{1,0:T(8,128)(2,1)S(1)} %get-tuple-element.24.q, bf16[192,256]{1,0:T(8,128)(2,1)S(1)} %get-tuple-element.37.fresh, bf16[2048,128]{1,0:T(8,128)(2,1)S(1)} %get-tuple-element.38.held, bf16[16,2048]{1,0:T(8,128)(2,1)S(1)} %get-tuple-element.39.spare, ...), custom_call_target="tpu_custom_call" | custom-call | tf_op jit(solution)/shard_map/attend/pallas_call | solution.py:517
  64.0 0.6 copy.20
  (27 shorter events, 0.8 us)
Async XLA Ops:
  0.6 7.3 %copy-start.2 = (s32[4,16]{1,0:T(4,128)S(1)}, s32[4,16]{1,0:T(4,128)}, u32[]{:S(2)}) copy-start(s32[4,16]{1,0:T(4,128)} %request_docs.5) | copy-start | bytes 772
  1.9 21.2 %collective-permute-start.5 = (bf16[2,48,2048]{2,1,0:T(8,128)(2,1)S(1)}, bf16[2,48,2048]{2,1,0:T(8,128)(2,1)S(1)}, u32[]{:S(2)}, u32[]{:S(2)}) collective-permute-start(bf16[2,48,2048]{2,1,0:T(8,128)(2,1)S(1)} %get-tuple-element.31), channel_id=1, source_target_pairs={{0,4},{4,0},{8,12},{12,8},{1,5},{5,1},{9,13},{13,9},{2,6},{6,2},{1... | collective-permute-start | bytes 1179656 | tf_op jit(solution)/shard_map/ppermute | solution.py:564
  5.0 12.0 %collective-permute-start = (bf16[448,128]{1,0:T(8,128)(2,1)S(1)}, bf16[448,128]{1,0:T(8,128)(2,1)S(1)}, u32[]{:S(2)}, u32[]{:S(2)}) collective-permute-start(bf16[448,128]{1,0:T(8,128)(2,1)S(1)} %get-tuple-element.25), channel_id=1, source_target_pairs={{0,8},{4,12},{8,0},{12,4},{1,9},{5,13},{9,1},{13,5},{2,10},{6,14},... | collective-permute-start | bytes 344072 | tf_op jit(solution)/shard_map/ppermute | solution.py:564
  7.5 23.2 %collective-permute-start.1 = (bf16[1600,128]{1,0:T(8,128)(2,1)S(1)}, bf16[1600,128]{1,0:T(8,128)(2,1)S(1)}, u32[]{:S(2)}, u32[]{:S(2)}) collective-permute-start(bf16[1600,128]{1,0:T(8,128)(2,1)S(1)} %get-tuple-element.28), channel_id=1, source_target_pairs={{0,8},{4,12},{8,0},{12,4},{1,9},{5,13},{9,1},{13,5},{2,10},{6,14},... | collective-permute-start | bytes 1228808 | tf_op jit(solution)/shard_map/ppermute | solution.py:564
  10.0 22.3 %collective-permute-start.4 = (bf16[4,2,128,128]{3,2,1,0:T(8,128)(2,1)S(1)}, bf16[4,2,128,128]{3,2,1,0:T(8,128)(2,1)S(1)}, u32[]{:S(2)}, u32[]{:S(2)}) collective-permute-start(bf16[4,2,128,128]{3,2,1,0:T(8,128)(2,1)S(1)} %get-tuple-element.30.refs_1_), channel_id=1, source_target_pairs={{0,4},{4,0},{8,12},{12,8},{1,5},{5,1},{9,13},{13,9},{2,6},{6,2},{1... | collective-permute-start | bytes 786440 | tf_op jit(solution)/shard_map/ppermute | solution.py:564
  17.0 8.1 %collective-permute-start.2 = (bf16[448,128]{1,0:T(8,128)(2,1)S(1)}, bf16[448,128]{1,0:T(8,128)(2,1)S(1)}, u32[]{:S(2)}, u32[]{:S(2)}) collective-permute-start(bf16[448,128]{1,0:T(8,128)(2,1)S(1)} %collective-permute-done.w_far_0), channel_id=1, source_target_pairs={{0,16},{16,0},{1,17},{17,1},{2,18},{18,2},{3,19},{19,3},{4,20},{20... | collective-permute-start | bytes 344072 | tf_op jit(solution)/shard_map/ppermute | solution.py:564
  23.1 11.6 %collective-permute-start.7 = (bf16[2,48,2048]{2,1,0:T(8,128)(2,1)S(1)}, bf16[2,48,2048]{2,1,0:T(8,128)(2,1)S(1)}, u32[]{:S(2)}, u32[]{:S(2)}) collective-permute-start(bf16[2,48,2048]{2,1,0:T(8,128)(2,1)S(1)} %gate.3.rest_0_), channel_id=1, source_target_pairs={{0,2},{1,3},{2,0},{3,1},{4,6},{5,7},{6,4},{7,5},{8,10},{9,11},{10,... | collective-permute-start | bytes 1179656 | tf_op jit(solution)/shard_map/ppermute | solution.py:564
  25.0 11.3 %collective-permute-start.6 = (bf16[2,48,2048]{2,1,0:T(8,128)(2,1)S(1)}, bf16[2,48,2048]{2,1,0:T(8,128)(2,1)S(1)}, u32[]{:S(2)}, u32[]{:S(2)}) collective-permute-start(bf16[2,48,2048]{2,1,0:T(8,128)(2,1)S(1)} %gate.3.rest_0_), channel_id=1, source_target_pairs={{0,1},{1,0},{2,3},{3,2},{4,5},{5,4},{6,7},{7,6},{8,9},{9,8},{10,11... | collective-permute-start | bytes 1179656 | tf_op jit(solution)/shard_map/ppermute | solution.py:564
  30.8 3.9 %copy-start = (bf16[1,192,8192]{2,1,0:T(8,128)(2,1)S(1)}, bf16[1,192,8192]{2,1,0:T(8,128)(2,1)}, u32[]{:S(2)}) copy-start(bf16[1,192,8192]{2,1,0:T(8,128)(2,1)} %hidden.5) | copy-start | bytes 9437188
  30.8 9.9 %collective-permute-start.3 = (bf16[1600,128]{1,0:T(8,128)(2,1)S(1)}, bf16[1600,128]{1,0:T(8,128)(2,1)S(1)}, u32[]{:S(2)}, u32[]{:S(2)}) collective-permute-start(bf16[1600,128]{1,0:T(8,128)(2,1)S(1)} %get-tuple-element.29.w_far_1), channel_id=1, source_target_pairs={{0,16},{16,0},{1,17},{17,1},{2,18},{18,2},{3,19},{19,3},{4,20},{20... | collective-permute-start | bytes 1228808 | tf_op jit(solution)/shard_map/ppermute | solution.py:564
  32.3 24.7 %collective-permute-start.12 = (bf16[4,2,128,128]{3,2,1,0:T(8,128)(2,1)S(1)}, bf16[4,2,128,128]{3,2,1,0:T(8,128)(2,1)S(1)}, u32[]{:S(2)}, u32[]{:S(2)}) collective-permute-start(bf16[4,2,128,128]{3,2,1,0:T(8,128)(2,1)S(1)} %get-tuple-element.43), channel_id=1, source_target_pairs={{0,8},{4,12},{8,0},{12,4},{1,9},{5,13},{9,1},{13,5},{2,10},{6,14},... | collective-permute-start | bytes 786440 | tf_op jit(solution)/shard_map/ppermute | solution.py:564
  32.3 24.7 %collective-permute-start.13 = (bf16[4,2,128,128]{3,2,1,0:T(8,128)(2,1)S(1)}, bf16[4,2,128,128]{3,2,1,0:T(8,128)(2,1)S(1)}, u32[]{:S(2)}, u32[]{:S(2)}) collective-permute-start(bf16[4,2,128,128]{3,2,1,0:T(8,128)(2,1)S(1)} %get-tuple-element.44), channel_id=1, source_target_pairs={{0,12},{4,8},{8,4},{12,0},{1,13},{5,9},{9,5},{13,1},{2,14},{6,10},... | collective-permute-start | bytes 786440 | tf_op jit(solution)/shard_map/ppermute | solution.py:564
  34.7 1.7 %collective-permute-start.8 = (bf16[2,48,2048]{2,1,0:T(8,128)(2,1)S(1)}, bf16[2,48,2048]{2,1,0:T(8,128)(2,1)S(1)}, u32[]{:S(2)}, u32[]{:S(2)}) collective-permute-start(bf16[2,48,2048]{2,1,0:T(8,128)(2,1)S(1)} %collective-permute-done.7.rest_2_), channel_id=1, source_target_pairs={{0,1},{1,0},{2,3},{3,2},{4,5},{5,4},{6,7},{7,6},{8,9},{9,8},{10,11... | collective-permute-start | bytes 1179656 | tf_op jit(solution)/shard_map/ppermute | solution.py:564
  38.1 6.8 %copy-start.1 = (bf16[1,192,1024]{2,1,0:T(8,128)(2,1)S(1)}, bf16[1,192,1024]{2,1,0:T(8,128)(2,1)}, u32[]{:S(2)}) copy-start(bf16[1,192,1024]{2,1,0:T(8,128)(2,1)} %queries.1) | copy-start | bytes 1179652
  38.1 6.8 %copy-start.3 = (s32[1,16,12]{1,0,2:T(1,128)S(1)}, s32[1,16,12]{1,0,2:T(1,128)}, u32[]{:S(2)}) copy-start(s32[1,16,12]{1,0,2:T(1,128)} %param.17) | copy-start | bytes 2308
  38.1 6.8 %copy-start.4 = (s32[32]{0:T(128)S(1)}, s32[32]{0:T(128)}, u32[]{:S(2)}) copy-start(s32[32]{0:T(128)} %doc_lengths.1) | copy-start | bytes 388
  42.7 8.8 %collective-permute-start.10 = (bf16[64,256]{1,0:T(8,128)(2,1)S(1)}, bf16[64,256]{1,0:T(8,128)(2,1)S(1)}, u32[]{:S(2)}, u32[]{:S(2)}) collective-permute-start(bf16[64,256]{1,0:T(8,128)(2,1)S(1)} %get-tuple-element.34), channel_id=1, source_target_pairs={{0,4},{4,0},{8,12},{12,8},{1,5},{5,1},{9,13},{13,9},{2,6},{6,2},{1... | collective-permute-start | bytes 98312 | tf_op jit(solution)/shard_map/ppermute | solution.py:564
  42.8 9.4 %collective-permute-start.11 = (bf16[64,256]{1,0:T(8,128)(2,1)S(1)}, bf16[64,256]{1,0:T(8,128)(2,1)S(1)}, u32[]{:S(2)}, u32[]{:S(2)}) collective-permute-start(bf16[64,256]{1,0:T(8,128)(2,1)S(1)} %get-tuple-element.35), channel_id=1, source_target_pairs={{0,4},{4,0},{8,12},{12,8},{1,5},{5,1},{9,13},{13,9},{2,6},{6,2},{1... | collective-permute-start | bytes 98312 | tf_op jit(solution)/shard_map/ppermute | solution.py:564
  44.8 8.0 %collective-permute-start.9 = (bf16[64,256]{1,0:T(8,128)(2,1)S(1)}, bf16[64,256]{1,0:T(8,128)(2,1)S(1)}, u32[]{:S(2)}, u32[]{:S(2)}) collective-permute-start(bf16[64,256]{1,0:T(8,128)(2,1)S(1)} %get-tuple-element.33), channel_id=1, source_target_pairs={{0,4},{4,0},{8,12},{12,8},{1,5},{5,1},{9,13},{13,9},{2,6},{6,2},{1... | collective-permute-start | bytes 98312 | tf_op jit(solution)/shard_map/ppermute | solution.py:564
  53.7 10.3 %all-to-all-start = ((bf16[4,96,128]{2,1,0:T(8,128)(2,1)}), bf16[4,96,128]{2,1,0:T(8,128)(2,1)S(1)}, u32[]{:S(2)}, u32[]{:S(2)}) async-start(bf16[4,96,128]{2,1,0:T(8,128)(2,1)} %bitcast.1), calls=%async_computation | async-start | bytes 196608 | tf_op jit(solution)/shard_map/all_to_all | solution.py:612

commit v21 on v20

--- a/solution.py
+++ b/solution.py
@@ -115,6 +115,10 @@
             pltpu.make_async_copy(store_keys.at[slot], out.at[c, 0], sem).start()
             pltpu.make_async_copy(store_values.at[slot], out.at[c, 1], sem).start()
 
+    def send_one(r, store, out, sem):
+        for c in range(capacity):
+            pltpu.make_async_copy(store.at[picks[r, c]], out.at[c], sem).start()
+
     if by_owner:
 
         def one_send(r, carry):
@@ -123,8 +127,10 @@
 
         lax.fori_loop(0, requests, one_send, 0)
     else:
-        for i, out in enumerate(outs):
-            send(lax.bitwise_xor(me, i + 1), out, sems.at[i])
+        send(lax.bitwise_xor(me, 1), outs[0], sems.at[0])
+        send_one(lax.bitwise_xor(me, 2), store_keys, outs[1], sems.at[1])
+        send_one(lax.bitwise_xor(me, 2), store_values, outs[2], sems.at[2])
+        send(lax.bitwise_xor(me, 3), outs[3], sems.at[3])
     for i, out in enumerate(outs):
         pltpu.make_async_copy(out, out, sems.at[i]).wait()
 
@@ -133,7 +139,8 @@
     requests = request_docs.shape[0]
     capacity = store_keys.shape[0] // 2
     one = (capacity, 2) + store_keys.shape[1:]
-    shapes = ((requests,) + one,) if by_owner else (one,) * (requests - 1)
+    half = (capacity,) + store_keys.shape[1:]
+    shapes = ((requests,) + one,) if by_owner else (one, half, half, one)
     return pl.pallas_call(
         functools.partial(docs_kernel, by_owner),
         out_shape=tuple(jax.ShapeDtypeStruct(one, jnp.bfloat16) for one in shapes),
@@ -187,7 +194,7 @@
     total[...] = jnp.dot(n[...], w[...], preferred_element_type=jnp.float32)
 
 
-def far_kernel(hidden, w_far_0, w_far_1, w_swapped_0, w_swapped_1, near, neighbour, *rest):
+def far_kernel(hidden, w_far_0, w_far_1, w_swapped_0, w_swapped_1, near, neighbour, _, __, *rest):
     *quarters, own, part_0, part_1, part_2, w, h, n, sems = rest
     group = lax.axis_index("groups")
     start, width = w_far_0.shape
@@ -233,7 +240,7 @@
         compiler_params=limit,
         cost_estimate=pl.CostEstimate(flops=10**10, bytes_accessed=1, transcendentals=0),
         name="project_near",
-    )(hidden, w_key, w_value, first)
+    )(hidden, w_key, w_value, first[0])
     neighbour = pl.pallas_call(
         neighbour_kernel,
         out_shape=sums,
@@ -251,7 +258,7 @@
     return pl.pallas_call(
         far_kernel,
         out_shape=(sums,) + (jax.ShapeDtypeStruct((rows // 3, 2 * width), jnp.bfloat16),) * 3,
-        in_specs=[ANY] * 5 + [VMEM] * 2 + [ANY] * len(quarters),
+        in_specs=[ANY] * 5 + [VMEM] * 2 + [ANY] * (2 + len(quarters)),
         out_specs=(VMEM,) * 4,
         scratch_shapes=[
             w_scratch,
@@ -262,7 +269,7 @@
         compiler_params=limit,
         cost_estimate=cheap,
         name="project_far",
-    )(hidden, *w_far, *w_swapped, near, neighbour, *quarters)
+    )(hidden, *w_far, *w_swapped, near, neighbour, *first[1:], *quarters)
 
 
 def plan_kernel(
@@ -432,7 +439,11 @@
                 slot = lax.rem(doc, slots)
                 fetch(sources[0].at[slot], sources[1].at[slot])
 
-            for k, source in zip((2, 3, 1), sources[2:]):
+            @pl.when(away == 2)
+            def _():
+                fetch(sources[2].at[rank], sources[3].at[rank])
+
+            for k, source in zip((3, 1), sources[4:]):
 
                 @pl.when(away == k)
                 def _():
@@ -566,19 +577,19 @@
         *w_send, h_send = pick_sent(hidden, w_key, w_value)
         w_far = [swap(part, "seq", 2) for part in w_send]
         h_mine = swap(h_send, "seq", 1)
-        doc_1, doc_2, doc_3 = pick_docs(request_docs, store_keys, store_values, False)
+        doc_1, keys_2, values_2, doc_3 = pick_docs(request_docs, store_keys, store_values, False)
         (h_mine,) = gate((h_mine,), (doc_1,), cost=8000000000)
         h_chip = swap(h_mine, "tp", 2)
         h_core = swap(h_mine, "tp", 1)
         w_swapped = [swap(w_far[0], "groups", 1)]
-        doc_2, doc_3, w_far[1] = gate(
-            (doc_2, doc_3, w_far[1]), (w_swapped[0],), cost=8 * 10**9
+        keys_2, values_2, doc_3, w_far[1] = gate(
+            (keys_2, values_2, doc_3, w_far[1]), (w_swapped[0],), cost=8 * 10**9
         )
         w_swapped.append(swap(w_far[1], "groups", 1))
         doc_1 = swap(doc_1, "seq", 1)
-        docs = (swap(doc_2, "seq", 2), swap(doc_3, "seq", 3), doc_1)
+        docs = (swap(keys_2, "seq", 2), swap(values_2, "seq", 2), swap(doc_3, "seq", 3), doc_1)
         quarters = (h_mine, h_core, h_chip, swap(h_chip, "tp", 1))
-        own, *parts = project(hidden, w_key, w_value, w_far, w_swapped, quarters, doc_1)
+        own, *parts = project(hidden, w_key, w_value, w_far, w_swapped, quarters, (doc_1, docs[0], docs[1]))
         arrived = [swap(one, "seq", 1) for one in parts]
         sources = (store_keys, store_values, *docs)
     else:

time: 65.1 us -> 72.1 us (1.11)
  waiting for transfers between devices: 26.3 us -> 30.4 us
  starting transfers between devices: 19.1 us -> 22 us
    ppermute x14 -> x15, waiting for transfers between devices: 26.3 us -> 30.4 us  [swap(): return lax.ppermute(array, axis, [(i, i ^ apart) for i in range(count)])]
    ppermute x14 -> x15, starting transfers between devices: 15.8 us -> 18.7 us  [swap(): return lax.ppermute(array, axis, [(i, i ^ apart) for i in range(count)])]
  transfers between devices with their start and end apart: 15 -> 16, of which waited for: 8 -> 9; matrix products, arithmetic and copies ran while one was open for 0% -> 0% of each run, Pallas kernels for 26% -> 23%
where the time goes in v21:
time: 72.1 us; the launch traced here: 71.5 us
  waiting for transfers between devices  30.4 us (42%)
  starting transfers between devices  22 us (31%)
  Pallas kernels  17.7 us (25%)
  between operations  0.77 us (1%)
    ppermute x15, waiting for transfers between devices, swap(): return lax.ppermute(array, axis, [(i, i ^ apart) for i in range(count)])  30.4 us
    ppermute x15, starting transfers between devices, swap(): return lax.ppermute(array, axis, [(i, i ^ apart) for i in range(count)])  18.7 us
    pallas_call x1, Pallas kernels, attend(): pl.pallas_call(functools.partial(attend_kernel, by_owner), out_shape=jax....  6.9 us
    all_to_all x1, starting transfers between devices, shards(): lax.all_to_all(outgoing, 'seq', split_axis=0, concat_axis=0, tiled=True)  3.3 us
    pallas_call x1, Pallas kernels, pick_docs(): pl.pallas_call(functools.partial(docs_kernel, by_owner), out_shape=tuple(...  2.13 us
    pallas_call x1, Pallas kernels, project(): pl.pallas_call(far_kernel, out_shape=(sums,) + (jax.ShapeDtypeStruct((row...  1.97 us
    pallas_call x1, Pallas kernels, project(): pl.pallas_call(neighbour_kernel, out_shape=sums, in_specs=[ANY] * (2 + le...  1.64 us
    pallas_call x1, Pallas kernels, project(): pl.pallas_call(near_kernel, out_shape=sums, in_specs=[ANY] * 4, out_specs...  1.61 us
  transfers between devices with their start and end apart: 16, of which 9 were waited for; matrix products, arithmetic and copies ran while one was open for 0% of the time, Pallas kernels for 23%

profile of v21, /device:TPU:0, one launch (start us, length us, event | category | flops | bytes accessed | tf_op | source)
XLA Modules:
  0.0 71.5 jit_solution(7091680087813672467)
XLA Ops:
  0.6 1.2 %pick_sent.1 = (bf16[448,128]{1,0:T(8,128)(2,1)S(1)}, bf16[1600,128]{1,0:T(8,128)(2,1)S(1)}, bf16[2,48,2048]{2,1,0:T(8,128)(2,1)S(1)}) custom-call(bf16[1,192,8192]{2,1,0:T(8,128)(2,1)} %hidden.5, bf16[2048,128]{1,0:T(8,128)(2,1)} %w_key.5, bf16[2048,128]{1,0:T(8,128)(2,1)} %w_value.5), custom_call_target="tpu_custom_call" | custom-call | tf_op jit(solution)/shard_map/pick_sent/pallas_call | solution.py:54
  1.9 3.1 %collective-permute-start.5 = (bf16[2,48,2048]{2,1,0:T(8,128)(2,1)S(1)}, bf16[2,48,2048]{2,1,0:T(8,128)(2,1)S(1)}, u32[]{:S(2)}, u32[]{:S(2)}) collective-permute-start(bf16[2,48,2048]{2,1,0:T(8,128)(2,1)S(1)} %get-tuple-element.34), channel_id=1, source_target_pairs={{0,4},{4,0},{8,12},{12,8},{1,5},{5,1},{9,13},{13,9},{2,6},{6,2},{1... | collective-permute-start | bytes 1179656 | tf_op jit(solution)/shard_map/ppermute | solution.py:575
  5.0 2.6 %collective-permute-start = (bf16[448,128]{1,0:T(8,128)(2,1)S(1)}, bf16[448,128]{1,0:T(8,128)(2,1)S(1)}, u32[]{:S(2)}, u32[]{:S(2)}) collective-permute-start(bf16[448,128]{1,0:T(8,128)(2,1)S(1)} %get-tuple-element.27), channel_id=1, source_target_pairs={{0,8},{4,12},{8,0},{12,4},{1,9},{5,13},{9,1},{13,5},{2,10},{6,14},... | collective-permute-start | bytes 344072 | tf_op jit(solution)/shard_map/ppermute | solution.py:575
  7.9 2.1 %pick_docs.1 = (bf16[4,2,128,128]{3,2,1,0:T(8,128)(2,1)S(1)}, bf16[4,128,128]{2,1,0:T(8,128)(2,1)S(1)}, bf16[4,128,128]{2,1,0:T(8,128)(2,1)S(1)}, bf16[4,2,128,128]{3,2,1,0:T(8,128)(2,1)S(1)}) custom-call(s32[4,16]{1,0:T(4,128)S(1)} %copy-done.2, bf16[8,128,128]{2,1,0:T(8,128)(2,1)} %rest_0_.1, bf16[8,128,128]{2,1,0:T(8,128)(2,1)} %rest_1_.1), custom_call_target="tpu_custom_call" | custom-call | tf_op jit(solution)/shard_map/pick_docs/pallas_call | solution.py:144
  10.2 6.7 %collective-permute-done.w_far_0 = bf16[448,128]{1,0:T(8,128)(2,1)S(1)} collective-permute-done((bf16[448,128]{1,0:T(8,128)(2,1)S(1)}, bf16[448,128]{1,0:T(8,128)(2,1)S(1)}, u32[]{:S(2)}, u32[]{:S(2)}) %collective-permute-start) | collective-permute-done | bytes 114720 | tf_op jit(solution)/shard_map/ppermute | solution.py:575
  17.0 1.5 %collective-permute-start.2 = (bf16[448,128]{1,0:T(8,128)(2,1)S(1)}, bf16[448,128]{1,0:T(8,128)(2,1)S(1)}, u32[]{:S(2)}, u32[]{:S(2)}) collective-permute-start(bf16[448,128]{1,0:T(8,128)(2,1)S(1)} %collective-permute-done.w_far_0), channel_id=1, source_target_pairs={{0,16},{16,0},{1,17},{17,1},{2,18},{18,2},{3,19},{19,3},{4,20},{20... | collective-permute-start | bytes 344072 | tf_op jit(solution)/shard_map/ppermute | solution.py:575
  18.5 4.6 %collective-permute-done.5.refs_0_ = bf16[2,48,2048]{2,1,0:T(8,128)(2,1)S(1)} collective-permute-done((bf16[2,48,2048]{2,1,0:T(8,128)(2,1)S(1)}, bf16[2,48,2048]{2,1,0:T(8,128)(2,1)S(1)}, u32[]{:S(2)}, u32[]{:S(2)}) %collective-permute-start.5) | collective-permute-done | bytes 393248 | tf_op jit(solution)/shard_map/ppermute | solution.py:575
  23.1 2.0 %collective-permute-start.7 = (bf16[2,48,2048]{2,1,0:T(8,128)(2,1)S(1)}, bf16[2,48,2048]{2,1,0:T(8,128)(2,1)S(1)}, u32[]{:S(2)}, u32[]{:S(2)}) collective-permute-start(bf16[2,48,2048]{2,1,0:T(8,128)(2,1)S(1)} %gate.3.rest_0_), channel_id=1, source_target_pairs={{0,2},{1,3},{2,0},{3,1},{4,6},{5,7},{6,4},{7,5},{8,10},{9,11},{10,... | collective-permute-start | bytes 1179656 | tf_op jit(solution)/shard_map/ppermute | solution.py:575
  25.1 5.7 %collective-permute-done.1.refs_3_ = bf16[1600,128]{1,0:T(8,128)(2,1)S(1)} collective-permute-done((bf16[1600,128]{1,0:T(8,128)(2,1)S(1)}, bf16[1600,128]{1,0:T(8,128)(2,1)S(1)}, u32[]{:S(2)}, u32[]{:S(2)}) %collective-permute-start.1) | collective-permute-done | bytes 409632 | tf_op jit(solution)/shard_map/ppermute | solution.py:575
  30.8 1.5 %collective-permute-start.3 = (bf16[1600,128]{1,0:T(8,128)(2,1)S(1)}, bf16[1600,128]{1,0:T(8,128)(2,1)S(1)}, u32[]{:S(2)}, u32[]{:S(2)}) collective-permute-start(bf16[1600,128]{1,0:T(8,128)(2,1)S(1)} %get-tuple-element.32.w_far_1), channel_id=1, source_target_pairs={{0,16},{16,0},{1,17},{17,1},{2,18},{18,2},{3,19},{19,3},{4,20},{20... | collective-permute-start | bytes 1228808 | tf_op jit(solution)/shard_map/ppermute | solution.py:575
  32.3 2.9 %collective-permute-start.9 = (bf16[4,128,128]{2,1,0:T(8,128)(2,1)S(1)}, bf16[4,128,128]{2,1,0:T(8,128)(2,1)S(1)}, u32[]{:S(2)}, u32[]{:S(2)}) collective-permute-start(bf16[4,128,128]{2,1,0:T(8,128)(2,1)S(1)} %get-tuple-element.35), channel_id=1, source_target_pairs={{0,8},{4,12},{8,0},{12,4},{1,9},{5,13},{9,1},{13,5},{2,10},{6,14},... | collective-permute-start | bytes 393224 | tf_op jit(solution)/shard_map/ppermute | solution.py:575
  35.2 2.3 %collective-permute-start.14 = (bf16[4,2,128,128]{3,2,1,0:T(8,128)(2,1)S(1)}, bf16[4,2,128,128]{3,2,1,0:T(8,128)(2,1)S(1)}, u32[]{:S(2)}, u32[]{:S(2)}) collective-permute-start(bf16[4,2,128,128]{3,2,1,0:T(8,128)(2,1)S(1)} %get-tuple-element.48), channel_id=1, source_target_pairs={{0,12},{4,8},{8,4},{12,0},{1,13},{5,9},{9,5},{13,1},{2,14},{6,10},... | collective-permute-start | bytes 786440 | tf_op jit(solution)/shard_map/ppermute | solution.py:575
  37.6 1.6 %project_near.1.near = f32[192,256]{1,0:T(8,128)S(1)} custom-call(bf16[1,192,8192]{2,1,0:T(8,128)(2,1)S(1)} %copy-done, bf16[2048,128]{1,0:T(8,128)(2,1)} %w_key.5, bf16[2048,128]{1,0:T(8,128)(2,1)} %w_value.5, bf16[4,2,128,128]{3,2,1,0:T(8,128)(2,1)S(1)} %collective-permute-done.4._.rest_5_), custom_call_target="tpu_custom_call" | custom-call | flops 10000000000 | bytes 1 | tf_op jit(solution)/shard_map/project_near/pallas_call | solution.py:234
  39.3 1.6 %project_neighbour.1.neighbour = f32[192,256]{1,0:T(8,128)S(1)} custom-call(bf16[2048,128]{1,0:T(8,128)(2,1)} %w_key.5, bf16[2048,128]{1,0:T(8,128)(2,1)} %w_value.5, bf16[2,48,2048]{2,1,0:T(8,128)(2,1)S(1)} %gate.3.rest_0_, bf16[2,48,2048]{2,1,0:T(8,128)(2,1)S(1)} %collective-permute-done.6.rest_1_, ...), custom_call_target="tpu_custom_call" | custom-call | flops 1 | bytes 1 | tf_op jit(solution)/shard_map/project_neighbour/pallas_call | solution.py:244
  41.0 8.0 %collective-permute-done.10.__.rest_3_ = bf16[4,128,128]{2,1,0:T(8,128)(2,1)S(1)} collective-permute-done((bf16[4,128,128]{2,1,0:T(8,128)(2,1)S(1)}, bf16[4,128,128]{2,1,0:T(8,128)(2,1)S(1)}, u32[]{:S(2)}, u32[]{:S(2)}) %collective-permute-start.10) | collective-permute-done | bytes 131104 | tf_op jit(solution)/shard_map/ppermute | solution.py:575
  49.0 2.8 %collective-permute-done.9._.rest_2_ = bf16[4,128,128]{2,1,0:T(8,128)(2,1)S(1)} collective-permute-done((bf16[4,128,128]{2,1,0:T(8,128)(2,1)S(1)}, bf16[4,128,128]{2,1,0:T(8,128)(2,1)S(1)}, u32[]{:S(2)}, u32[]{:S(2)}) %collective-permute-start.9) | collective-permute-done | bytes 131104 | tf_op jit(solution)/shard_map/ppermute | solution.py:575
  51.8 2.0 %project_far.1 = (f32[192,256]{1,0:T(8,128)S(1)}, bf16[64,256]{1,0:T(8,128)(2,1)S(1)}, bf16[64,256]{1,0:T(8,128)(2,1)S(1)}, bf16[64,256]{1,0:T(8,128)(2,1)S(1)}) custom-call(bf16[1,192,8192]{2,1,0:T(8,128)(2,1)S(1)} %copy-done, bf16[448,128]{1,0:T(8,128)(2,1)S(1)} %collective-permute-done.w_far_0, bf16[1600,128]{1,0:T(8,128)(2,1)S(1)} %get-tuple-element.32.w_far_1, ...), custom_call_target="tpu_custom_call" | custom-call | flops 1 | bytes 1 | tf_op jit(solution)/shard_map/project_far/pallas_call | solution.py:258
  53.8 2.0 %collective-permute-start.12 = (bf16[64,256]{1,0:T(8,128)(2,1)S(1)}, bf16[64,256]{1,0:T(8,128)(2,1)S(1)}, u32[]{:S(2)}, u32[]{:S(2)}) collective-permute-start(bf16[64,256]{1,0:T(8,128)(2,1)S(1)} %get-tuple-element.39), channel_id=1, source_target_pairs={{0,4},{4,0},{8,12},{12,8},{1,5},{5,1},{9,13},{13,9},{2,6},{6,2},{1... | collective-permute-start | bytes 98312 | tf_op jit(solution)/shard_map/ppermute | solution.py:575
  55.9 1.4 %plan.1 = (bf16[1536,256]{1,0:T(8,128)(2,1)S(1)}, bf16[2048,128]{1,0:T(8,128)(2,1)S(1)}, bf16[16,2048]{1,0:T(8,128)(2,1)S(1)}, f32[1,2048]{1,0:T(1,128)S(1)}, s3...) custom-call(s32[4,16]{1,0:T(4,128)S(1)} %copy-done.2, s32[32]{0:T(128)S(1)} %copy-done.4, ...), custom_call_target="tpu_custom_call" | custom-call | tf_op jit(solution)/shard_map/plan/pallas_call | solution.py:363
  58.1 1.7 %collective-permute-done.13.arrived_2 = bf16[64,256]{1,0:T(8,128)(2,1)S(1)} collective-permute-done((bf16[64,256]{1,0:T(8,128)(2,1)S(1)}, bf16[64,256]{1,0:T(8,128)(2,1)S(1)}, u32[]{:S(2)}, u32[]{:S(2)}) %collective-permute-start.13) | collective-permute-done | bytes 32800 | tf_op jit(solution)/shard_map/ppermute | solution.py:575
  59.8 0.9 %finish.1 = (bf16[192,256]{1,0:T(8,128)(2,1)S(1)}, bf16[384,128]{1,0:T(8,128)(2,1)}) custom-call(f32[192,256]{1,0:T(8,128)S(1)} %get-tuple-element.37.own, bf16[64,256]{1,0:T(8,128)(2,1)S(1)} %collective-permute-done.11.arrived_0, bf16[64,256]{1,0:T(8,128)(2,1)S(1)} %collective-permute-done.12.arrived_1, ...), custom_call_target="tpu_custom_call" | custom-call | tf_op jit(solution)/shard_map/finish/pallas_call | solution.py:390
  60.7 3.3 %all-to-all-start = ((bf16[4,96,128]{2,1,0:T(8,128)(2,1)}), bf16[4,96,128]{2,1,0:T(8,128)(2,1)S(1)}, u32[]{:S(2)}, u32[]{:S(2)}) async-start(bf16[4,96,128]{2,1,0:T(8,128)(2,1)} %bitcast.1), calls=%async_computation | async-start | bytes 196608 | tf_op jit(solution)/shard_map/all_to_all | solution.py:623
  64.0 6.9 %attend.1 = bf16[1,192,1024]{2,1,0:T(8,128)(2,1)} custom-call(s32[4,16]{1,0:T(4,128)S(1)} %copy-done.2, bf16[1536,256]{1,0:T(8,128)(2,1)S(1)} %get-tuple-element.26.q, bf16[192,256]{1,0:T(8,128)(2,1)S(1)} %get-tuple-element.42.fresh, bf16[2048,128]{1,0:T(8,128)(2,1)S(1)} %get-tuple-element.43.held, bf16[16,2048]{1,0:T(8,128)(2,1)S(1)} %get-tuple-element.44.spare, ...), custom_call_target="tpu_custom_call" | custom-call | tf_op jit(solution)/shard_map/attend/pallas_call | solution.py:528
  70.9 0.6 copy.22
  (29 shorter events, 1.6 us)
Async XLA Ops:
  0.6 7.3 %copy-start.2 = (s32[4,16]{1,0:T(4,128)S(1)}, s32[4,16]{1,0:T(4,128)}, u32[]{:S(2)}) copy-start(s32[4,16]{1,0:T(4,128)} %request_docs.5) | copy-start | bytes 772
  1.9 21.2 %collective-permute-start.5 = (bf16[2,48,2048]{2,1,0:T(8,128)(2,1)S(1)}, bf16[2,48,2048]{2,1,0:T(8,128)(2,1)S(1)}, u32[]{:S(2)}, u32[]{:S(2)}) collective-permute-start(bf16[2,48,2048]{2,1,0:T(8,128)(2,1)S(1)} %get-tuple-element.34), channel_id=1, source_target_pairs={{0,4},{4,0},{8,12},{12,8},{1,5},{5,1},{9,13},{13,9},{2,6},{6,2},{1... | collective-permute-start | bytes 1179656 | tf_op jit(solution)/shard_map/ppermute | solution.py:575
  5.0 12.0 %collective-permute-start = (bf16[448,128]{1,0:T(8,128)(2,1)S(1)}, bf16[448,128]{1,0:T(8,128)(2,1)S(1)}, u32[]{:S(2)}, u32[]{:S(2)}) collective-permute-start(bf16[448,128]{1,0:T(8,128)(2,1)S(1)} %get-tuple-element.27), channel_id=1, source_target_pairs={{0,8},{4,12},{8,0},{12,4},{1,9},{5,13},{9,1},{13,5},{2,10},{6,14},... | collective-permute-start | bytes 344072 | tf_op jit(solution)/shard_map/ppermute | solution.py:575
  7.5 23.2 %collective-permute-start.1 = (bf16[1600,128]{1,0:T(8,128)(2,1)S(1)}, bf16[1600,128]{1,0:T(8,128)(2,1)S(1)}, u32[]{:S(2)}, u32[]{:S(2)}) collective-permute-start(bf16[1600,128]{1,0:T(8,128)(2,1)S(1)} %get-tuple-element.31), channel_id=1, source_target_pairs={{0,8},{4,12},{8,0},{12,4},{1,9},{5,13},{9,1},{13,5},{2,10},{6,14},... | collective-permute-start | bytes 1228808 | tf_op jit(solution)/shard_map/ppermute | solution.py:575
  10.0 22.3 %collective-permute-start.4 = (bf16[4,2,128,128]{3,2,1,0:T(8,128)(2,1)S(1)}, bf16[4,2,128,128]{3,2,1,0:T(8,128)(2,1)S(1)}, u32[]{:S(2)}, u32[]{:S(2)}) collective-permute-start(bf16[4,2,128,128]{3,2,1,0:T(8,128)(2,1)S(1)} %get-tuple-element.33.refs_1_), channel_id=1, source_target_pairs={{0,4},{4,0},{8,12},{12,8},{1,5},{5,1},{9,13},{13,9},{2,6},{6,2},{1... | collective-permute-start | bytes 786440 | tf_op jit(solution)/shard_map/ppermute | solution.py:575
  17.0 8.1 %collective-permute-start.2 = (bf16[448,128]{1,0:T(8,128)(2,1)S(1)}, bf16[448,128]{1,0:T(8,128)(2,1)S(1)}, u32[]{:S(2)}, u32[]{:S(2)}) collective-permute-start(bf16[448,128]{1,0:T(8,128)(2,1)S(1)} %collective-permute-done.w_far_0), channel_id=1, source_target_pairs={{0,16},{16,0},{1,17},{17,1},{2,18},{18,2},{3,19},{19,3},{4,20},{20... | collective-permute-start | bytes 344072 | tf_op jit(solution)/shard_map/ppermute | solution.py:575
  23.1 12.2 %collective-permute-start.7 = (bf16[2,48,2048]{2,1,0:T(8,128)(2,1)S(1)}, bf16[2,48,2048]{2,1,0:T(8,128)(2,1)S(1)}, u32[]{:S(2)}, u32[]{:S(2)}) collective-permute-start(bf16[2,48,2048]{2,1,0:T(8,128)(2,1)S(1)} %gate.3.rest_0_), channel_id=1, source_target_pairs={{0,2},{1,3},{2,0},{3,1},{4,6},{5,7},{6,4},{7,5},{8,10},{9,11},{10,... | collective-permute-start | bytes 1179656 | tf_op jit(solution)/shard_map/ppermute | solution.py:575
  25.0 12.5 %collective-permute-start.6 = (bf16[2,48,2048]{2,1,0:T(8,128)(2,1)S(1)}, bf16[2,48,2048]{2,1,0:T(8,128)(2,1)S(1)}, u32[]{:S(2)}, u32[]{:S(2)}) collective-permute-start(bf16[2,48,2048]{2,1,0:T(8,128)(2,1)S(1)} %gate.3.rest_0_), channel_id=1, source_target_pairs={{0,1},{1,0},{2,3},{3,2},{4,5},{5,4},{6,7},{7,6},{8,9},{9,8},{10,11... | collective-permute-start | bytes 1179656 | tf_op jit(solution)/shard_map/ppermute | solution.py:575
  30.8 6.8 %copy-start = (bf16[1,192,8192]{2,1,0:T(8,128)(2,1)S(1)}, bf16[1,192,8192]{2,1,0:T(8,128)(2,1)}, u32[]{:S(2)}) copy-start(bf16[1,192,8192]{2,1,0:T(8,128)(2,1)} %hidden.5) | copy-start | bytes 9437188
  30.8 21.0 %collective-permute-start.3 = (bf16[1600,128]{1,0:T(8,128)(2,1)S(1)}, bf16[1600,128]{1,0:T(8,128)(2,1)S(1)}, u32[]{:S(2)}, u32[]{:S(2)}) collective-permute-start(bf16[1600,128]{1,0:T(8,128)(2,1)S(1)} %get-tuple-element.32.w_far_1), channel_id=1, source_target_pairs={{0,16},{16,0},{1,17},{17,1},{2,18},{18,2},{3,19},{19,3},{4,20},{20... | collective-permute-start | bytes 1228808 | tf_op jit(solution)/shard_map/ppermute | solution.py:575
  32.3 16.7 %collective-permute-start.10 = (bf16[4,128,128]{2,1,0:T(8,128)(2,1)S(1)}, bf16[4,128,128]{2,1,0:T(8,128)(2,1)S(1)}, u32[]{:S(2)}, u32[]{:S(2)}) collective-permute-start(bf16[4,128,128]{2,1,0:T(8,128)(2,1)S(1)} %get-tuple-element.36), channel_id=1, source_target_pairs={{0,8},{4,12},{8,0},{12,4},{1,9},{5,13},{9,1},{13,5},{2,10},{6,14},... | collective-permute-start | bytes 393224 | tf_op jit(solution)/shard_map/ppermute | solution.py:575
  32.3 19.5 %collective-permute-start.9 = (bf16[4,128,128]{2,1,0:T(8,128)(2,1)S(1)}, bf16[4,128,128]{2,1,0:T(8,128)(2,1)S(1)}, u32[]{:S(2)}, u32[]{:S(2)}) collective-permute-start(bf16[4,128,128]{2,1,0:T(8,128)(2,1)S(1)} %get-tuple-element.35), channel_id=1, source_target_pairs={{0,8},{4,12},{8,0},{12,4},{1,9},{5,13},{9,1},{13,5},{2,10},{6,14},... | collective-permute-start | bytes 393224 | tf_op jit(solution)/shard_map/ppermute | solution.py:575
  35.2 28.7 %collective-permute-start.14 = (bf16[4,2,128,128]{3,2,1,0:T(8,128)(2,1)S(1)}, bf16[4,2,128,128]{3,2,1,0:T(8,128)(2,1)S(1)}, u32[]{:S(2)}, u32[]{:S(2)}) collective-permute-start(bf16[4,2,128,128]{3,2,1,0:T(8,128)(2,1)S(1)} %get-tuple-element.48), channel_id=1, source_target_pairs={{0,12},{4,8},{8,4},{12,0},{1,13},{5,9},{9,5},{13,1},{2,14},{6,10},... | collective-permute-start | bytes 786440 | tf_op jit(solution)/shard_map/ppermute | solution.py:575
  37.6 1.7 %collective-permute-start.8 = (bf16[2,48,2048]{2,1,0:T(8,128)(2,1)S(1)}, bf16[2,48,2048]{2,1,0:T(8,128)(2,1)S(1)}, u32[]{:S(2)}, u32[]{:S(2)}) collective-permute-start(bf16[2,48,2048]{2,1,0:T(8,128)(2,1)S(1)} %collective-permute-done.7.rest_2_), channel_id=1, source_target_pairs={{0,1},{1,0},{2,3},{3,2},{4,5},{5,4},{6,7},{7,6},{8,9},{9,8},{10,11... | collective-permute-start | bytes 1179656 | tf_op jit(solution)/shard_map/ppermute | solution.py:575
  40.9 15.0 %copy-start.1 = (bf16[1,192,1024]{2,1,0:T(8,128)(2,1)S(1)}, bf16[1,192,1024]{2,1,0:T(8,128)(2,1)}, u32[]{:S(2)}) copy-start(bf16[1,192,1024]{2,1,0:T(8,128)(2,1)} %queries.1) | copy-start | bytes 1179652
  40.9 15.0 %copy-start.3 = (s32[1,16,12]{1,0,2:T(1,128)S(1)}, s32[1,16,12]{1,0,2:T(1,128)}, u32[]{:S(2)}) copy-start(s32[1,16,12]{1,0,2:T(1,128)} %param.17) | copy-start | bytes 2308
  41.0 15.0 %copy-start.4 = (s32[32]{0:T(128)S(1)}, s32[32]{0:T(128)}, u32[]{:S(2)}) copy-start(s32[32]{0:T(128)} %doc_lengths.1) | copy-start | bytes 388
  53.7 4.0 %collective-permute-start.11 = (bf16[64,256]{1,0:T(8,128)(2,1)S(1)}, bf16[64,256]{1,0:T(8,128)(2,1)S(1)}, u32[]{:S(2)}, u32[]{:S(2)}) collective-permute-start(bf16[64,256]{1,0:T(8,128)(2,1)S(1)} %get-tuple-element.38), channel_id=1, source_target_pairs={{0,4},{4,0},{8,12},{12,8},{1,5},{5,1},{9,13},{13,9},{2,6},{6,2},{1... | collective-permute-start | bytes 98312 | tf_op jit(solution)/shard_map/ppermute | solution.py:575
  53.8 4.3 %collective-permute-start.12 = (bf16[64,256]{1,0:T(8,128)(2,1)S(1)}, bf16[64,256]{1,0:T(8,128)(2,1)S(1)}, u32[]{:S(2)}, u32[]{:S(2)}) collective-permute-start(bf16[64,256]{1,0:T(8,128)(2,1)S(1)} %get-tuple-element.39), channel_id=1, source_target_pairs={{0,4},{4,0},{8,12},{12,8},{1,5},{5,1},{9,13},{13,9},{2,6},{6,2},{1... | collective-permute-start | bytes 98312 | tf_op jit(solution)/shard_map/ppermute | solution.py:575
  55.8 3.9 %collective-permute-start.13 = (bf16[64,256]{1,0:T(8,128)(2,1)S(1)}, bf16[64,256]{1,0:T(8,128)(2,1)S(1)}, u32[]{:S(2)}, u32[]{:S(2)}) collective-permute-start(bf16[64,256]{1,0:T(8,128)(2,1)S(1)} %get-tuple-element.40), channel_id=1, source_target_pairs={{0,4},{4,0},{8,12},{12,8},{1,5},{5,1},{9,13},{13,9},{2,6},{6,2},{1... | collective-permute-start | bytes 98312 | tf_op jit(solution)/shard_map/ppermute | solution.py:575
  60.7 10.2 %all-to-all-start = ((bf16[4,96,128]{2,1,0:T(8,128)(2,1)}), bf16[4,96,128]{2,1,0:T(8,128)(2,1)S(1)}, u32[]{:S(2)}, u32[]{:S(2)}) async-start(bf16[4,96,128]{2,1,0:T(8,128)(2,1)} %bitcast.1), calls=%async_computation | async-start | bytes 196608 | tf_op jit(solution)/shard_map/all_to_all | solution.py:623

commit v22 on v20

--- a/solution.py
+++ b/solution.py
@@ -541,6 +541,24 @@
     )
 
 
+def store_kernel(rows, out, sem):
+    copy = pltpu.make_async_copy(rows, out, sem)
+    copy.start()
+    copy.wait()
+
+
+def store(rows):
+    return pl.pallas_call(
+        store_kernel,
+        out_shape=jax.ShapeDtypeStruct(rows.shape, rows.dtype),
+        in_specs=[VMEM],
+        out_specs=ANY,
+        scratch_shapes=[pltpu.SemaphoreType.DMA],
+        compiler_params=pltpu.CompilerParams(vmem_limit_bytes=1024 * 1024),
+        name="store",
+    )(rows)
+
+
 def shards(
     pairs,
     hidden,
@@ -610,6 +628,8 @@
 
     outgoing = outgoing.reshape(seq_count, capacity * per_doc * 2, head_dim)
     returned = lax.all_to_all(outgoing, "seq", split_axis=0, concat_axis=0, tiled=True)
+    if pairs:
+        returned = store(returned)
     returned = returned.reshape(seq_count, capacity, per_doc, 2, head_dim)
     return (mixed, returned[None])
 

time: 65.1 us -> 65.1 us (level)
  Pallas kernels: 17.8 us -> 18.5 us
    pallas_call x0 -> x1, Pallas kernels: none -> 0.65 us  [store(): pl.pallas_call(store_kernel, out_shape=jax.ShapeDtypeStruct(rows.shape, r...]
where the time goes in v22:
time: 65.1 us; the launch traced here: 64.7 us
  waiting for transfers between devices  26.3 us (40%)
  starting transfers between devices  19.1 us (29%)
  Pallas kernels  18.5 us (28%)
  between operations  0.78 us (1%)
    ppermute x14, waiting for transfers between devices, swap(): return lax.ppermute(array, axis, [(i, i ^ apart) for i in range(count)])  26.3 us
    ppermute x14, starting transfers between devices, swap(): return lax.ppermute(array, axis, [(i, i ^ apart) for i in range(count)])  15.8 us
    pallas_call x1, Pallas kernels, attend(): pl.pallas_call(functools.partial(attend_kernel, by_owner), out_shape=jax....  6.97 us
    all_to_all x1, starting transfers between devices, shards(): lax.all_to_all(outgoing, 'seq', split_axis=0, concat_axis=0, tiled=True)  3.3 us
    pallas_call x1, Pallas kernels, pick_docs(): pl.pallas_call(functools.partial(docs_kernel, by_owner), out_shape=tuple(...  2.14 us
    pallas_call x1, Pallas kernels, project(): pl.pallas_call(far_kernel, out_shape=(sums,) + (jax.ShapeDtypeStruct((row...  1.97 us
    pallas_call x1, Pallas kernels, project(): pl.pallas_call(neighbour_kernel, out_shape=sums, in_specs=[ANY] * (2 + le...  1.63 us
    pallas_call x1, Pallas kernels, project(): pl.pallas_call(near_kernel, out_shape=sums, in_specs=[ANY] * 4, out_specs...  1.61 us
  transfers between devices with their start and end apart: 15, of which 8 were waited for; matrix products, arithmetic and copies ran while one was open for 0% of the time, Pallas kernels for 26%

profile of v22, /device:TPU:0, one launch (start us, length us, event | category | flops | bytes accessed | tf_op | source)
XLA Modules:
  0.0 64.7 jit_solution(16164257047804026705)
XLA Ops:
  0.6 1.2 %pick_sent.1 = (bf16[448,128]{1,0:T(8,128)(2,1)S(1)}, bf16[1600,128]{1,0:T(8,128)(2,1)S(1)}, bf16[2,48,2048]{2,1,0:T(8,128)(2,1)S(1)}) custom-call(bf16[1,192,8192]{2,1,0:T(8,128)(2,1)} %hidden.5, bf16[2048,128]{1,0:T(8,128)(2,1)} %w_key.5, bf16[2048,128]{1,0:T(8,128)(2,1)} %w_value.5), custom_call_target="tpu_custom_call" | custom-call | tf_op jit(solution)/shard_map/pick_sent/pallas_call | solution.py:54
  1.9 3.1 %collective-permute-start.5 = (bf16[2,48,2048]{2,1,0:T(8,128)(2,1)S(1)}, bf16[2,48,2048]{2,1,0:T(8,128)(2,1)S(1)}, u32[]{:S(2)}, u32[]{:S(2)}) collective-permute-start(bf16[2,48,2048]{2,1,0:T(8,128)(2,1)S(1)} %get-tuple-element.31), channel_id=1, source_target_pairs={{0,4},{4,0},{8,12},{12,8},{1,5},{5,1},{9,13},{13,9},{2,6},{6,2},{1... | collective-permute-start | bytes 1179656 | tf_op jit(solution)/shard_map/ppermute | solution.py:582
  5.0 2.6 %collective-permute-start = (bf16[448,128]{1,0:T(8,128)(2,1)S(1)}, bf16[448,128]{1,0:T(8,128)(2,1)S(1)}, u32[]{:S(2)}, u32[]{:S(2)}) collective-permute-start(bf16[448,128]{1,0:T(8,128)(2,1)S(1)} %get-tuple-element.25), channel_id=1, source_target_pairs={{0,8},{4,12},{8,0},{12,4},{1,9},{5,13},{9,1},{13,5},{2,10},{6,14},... | collective-permute-start | bytes 344072 | tf_op jit(solution)/shard_map/ppermute | solution.py:582
  7.9 2.1 %pick_docs.1 = (bf16[4,2,128,128]{3,2,1,0:T(8,128)(2,1)S(1)}, bf16[4,2,128,128]{3,2,1,0:T(8,128)(2,1)S(1)}, bf16[4,2,128,128]{3,2,1,0:T(8,128)(2,1)S(1)}) custom-call(s32[4,16]{1,0:T(4,128)S(1)} %copy-done.2, bf16[8,128,128]{2,1,0:T(8,128)(2,1)} %rest_0_.1, bf16[8,128,128]{2,1,0:T(8,128)(2,1)} %rest_1_.1), custom_call_target="tpu_custom_call" | custom-call | tf_op jit(solution)/shard_map/pick_docs/pallas_call | solution.py:137
  10.2 6.8 %collective-permute-done.w_far_0 = bf16[448,128]{1,0:T(8,128)(2,1)S(1)} collective-permute-done((bf16[448,128]{1,0:T(8,128)(2,1)S(1)}, bf16[448,128]{1,0:T(8,128)(2,1)S(1)}, u32[]{:S(2)}, u32[]{:S(2)}) %collective-permute-start) | collective-permute-done | bytes 114720 | tf_op jit(solution)/shard_map/ppermute | solution.py:582
  17.0 1.5 %collective-permute-start.2 = (bf16[448,128]{1,0:T(8,128)(2,1)S(1)}, bf16[448,128]{1,0:T(8,128)(2,1)S(1)}, u32[]{:S(2)}, u32[]{:S(2)}) collective-permute-start(bf16[448,128]{1,0:T(8,128)(2,1)S(1)} %collective-permute-done.w_far_0), channel_id=1, source_target_pairs={{0,16},{16,0},{1,17},{17,1},{2,18},{18,2},{3,19},{19,3},{4,20},{20... | collective-permute-start | bytes 344072 | tf_op jit(solution)/shard_map/ppermute | solution.py:582
  18.5 4.6 %collective-permute-done.5.refs_0_ = bf16[2,48,2048]{2,1,0:T(8,128)(2,1)S(1)} collective-permute-done((bf16[2,48,2048]{2,1,0:T(8,128)(2,1)S(1)}, bf16[2,48,2048]{2,1,0:T(8,128)(2,1)S(1)}, u32[]{:S(2)}, u32[]{:S(2)}) %collective-permute-start.5) | collective-permute-done | bytes 393248 | tf_op jit(solution)/shard_map/ppermute | solution.py:582
  23.1 2.0 %collective-permute-start.7 = (bf16[2,48,2048]{2,1,0:T(8,128)(2,1)S(1)}, bf16[2,48,2048]{2,1,0:T(8,128)(2,1)S(1)}, u32[]{:S(2)}, u32[]{:S(2)}) collective-permute-start(bf16[2,48,2048]{2,1,0:T(8,128)(2,1)S(1)} %gate.3.rest_0_), channel_id=1, source_target_pairs={{0,2},{1,3},{2,0},{3,1},{4,6},{5,7},{6,4},{7,5},{8,10},{9,11},{10,... | collective-permute-start | bytes 1179656 | tf_op jit(solution)/shard_map/ppermute | solution.py:582
  25.1 5.7 %collective-permute-done.1.refs_2_ = bf16[1600,128]{1,0:T(8,128)(2,1)S(1)} collective-permute-done((bf16[1600,128]{1,0:T(8,128)(2,1)S(1)}, bf16[1600,128]{1,0:T(8,128)(2,1)S(1)}, u32[]{:S(2)}, u32[]{:S(2)}) %collective-permute-start.1) | collective-permute-done | bytes 409632 | tf_op jit(solution)/shard_map/ppermute | solution.py:582
  30.8 1.5 %collective-permute-start.3 = (bf16[1600,128]{1,0:T(8,128)(2,1)S(1)}, bf16[1600,128]{1,0:T(8,128)(2,1)S(1)}, u32[]{:S(2)}, u32[]{:S(2)}) collective-permute-start(bf16[1600,128]{1,0:T(8,128)(2,1)S(1)} %get-tuple-element.29.w_far_1), channel_id=1, source_target_pairs={{0,16},{16,0},{1,17},{17,1},{2,18},{18,2},{3,19},{19,3},{4,20},{20... | collective-permute-start | bytes 1228808 | tf_op jit(solution)/shard_map/ppermute | solution.py:582
  32.3 2.4 %collective-permute-start.13 = (bf16[4,2,128,128]{3,2,1,0:T(8,128)(2,1)S(1)}, bf16[4,2,128,128]{3,2,1,0:T(8,128)(2,1)S(1)}, u32[]{:S(2)}, u32[]{:S(2)}) collective-permute-start(bf16[4,2,128,128]{3,2,1,0:T(8,128)(2,1)S(1)} %get-tuple-element.44), channel_id=1, source_target_pairs={{0,12},{4,8},{8,4},{12,0},{1,13},{5,9},{9,5},{13,1},{2,14},{6,10},... | collective-permute-start | bytes 786440 | tf_op jit(solution)/shard_map/ppermute | solution.py:582
  34.7 1.6 %project_near.1.near = f32[192,256]{1,0:T(8,128)S(1)} custom-call(bf16[1,192,8192]{2,1,0:T(8,128)(2,1)S(1)} %copy-done, bf16[2048,128]{1,0:T(8,128)(2,1)} %w_key.5, bf16[2048,128]{1,0:T(8,128)(2,1)} %w_value.5, bf16[4,2,128,128]{3,2,1,0:T(8,128)(2,1)S(1)} %collective-permute-done.4._.rest_4_), custom_call_target="tpu_custom_call" | custom-call | flops 10000000000 | bytes 1 | tf_op jit(solution)/shard_map/project_near/pallas_call | solution.py:227
  36.4 1.6 %project_neighbour.1.neighbour = f32[192,256]{1,0:T(8,128)S(1)} custom-call(bf16[2048,128]{1,0:T(8,128)(2,1)} %w_key.5, bf16[2048,128]{1,0:T(8,128)(2,1)} %w_value.5, bf16[2,48,2048]{2,1,0:T(8,128)(2,1)S(1)} %gate.3.rest_0_, bf16[2,48,2048]{2,1,0:T(8,128)(2,1)S(1)} %collective-permute-done.6.rest_1_, ...), custom_call_target="tpu_custom_call" | custom-call | flops 1 | bytes 1 | tf_op jit(solution)/shard_map/project_neighbour/pallas_call | solution.py:237
  38.1 2.6 %collective-permute-done.3.w_swapped_1 = bf16[1600,128]{1,0:T(8,128)(2,1)S(1)} collective-permute-done((bf16[1600,128]{1,0:T(8,128)(2,1)S(1)}, bf16[1600,128]{1,0:T(8,128)(2,1)S(1)}, u32[]{:S(2)}, u32[]{:S(2)}) %collective-permute-start.3) | collective-permute-done | bytes 409632 | tf_op jit(solution)/shard_map/ppermute | solution.py:582
  40.7 2.0 %project_far.1 = (f32[192,256]{1,0:T(8,128)S(1)}, bf16[64,256]{1,0:T(8,128)(2,1)S(1)}, bf16[64,256]{1,0:T(8,128)(2,1)S(1)}, bf16[64,256]{1,0:T(8,128)(2,1)S(1)}) custom-call(bf16[1,192,8192]{2,1,0:T(8,128)(2,1)S(1)} %copy-done, bf16[448,128]{1,0:T(8,128)(2,1)S(1)} %collective-permute-done.w_far_0, bf16[1600,128]{1,0:T(8,128)(2,1)S(1)} %get-tuple-element.29.w_far_1, ...), custom_call_target="tpu_custom_call" | custom-call | flops 1 | bytes 1 | tf_op jit(solution)/shard_map/project_far/pallas_call | solution.py:251
  42.8 2.0 %collective-permute-start.11 = (bf16[64,256]{1,0:T(8,128)(2,1)S(1)}, bf16[64,256]{1,0:T(8,128)(2,1)S(1)}, u32[]{:S(2)}, u32[]{:S(2)}) collective-permute-start(bf16[64,256]{1,0:T(8,128)(2,1)S(1)} %get-tuple-element.35), channel_id=1, source_target_pairs={{0,4},{4,0},{8,12},{12,8},{1,5},{5,1},{9,13},{13,9},{2,6},{6,2},{1... | collective-permute-start | bytes 98312 | tf_op jit(solution)/shard_map/ppermute | solution.py:582
  44.9 1.4 %plan.1 = (bf16[1536,256]{1,0:T(8,128)(2,1)S(1)}, bf16[2048,128]{1,0:T(8,128)(2,1)S(1)}, bf16[16,2048]{1,0:T(8,128)(2,1)S(1)}, f32[1,2048]{1,0:T(1,128)S(1)}, s3...) custom-call(s32[4,16]{1,0:T(4,128)S(1)} %copy-done.2, s32[32]{0:T(128)S(1)} %copy-done.4, ...), custom_call_target="tpu_custom_call" | custom-call | tf_op jit(solution)/shard_map/plan/pallas_call | solution.py:356
  46.3 5.2 %collective-permute-done.10.arrived_1 = bf16[64,256]{1,0:T(8,128)(2,1)S(1)} collective-permute-done((bf16[64,256]{1,0:T(8,128)(2,1)S(1)}, bf16[64,256]{1,0:T(8,128)(2,1)S(1)}, u32[]{:S(2)}, u32[]{:S(2)}) %collective-permute-start.10) | collective-permute-done | bytes 32800 | tf_op jit(solution)/shard_map/ppermute | solution.py:582
  51.5 0.7 %collective-permute-done.11.arrived_2 = bf16[64,256]{1,0:T(8,128)(2,1)S(1)} collective-permute-done((bf16[64,256]{1,0:T(8,128)(2,1)S(1)}, bf16[64,256]{1,0:T(8,128)(2,1)S(1)}, u32[]{:S(2)}, u32[]{:S(2)}) %collective-permute-start.11) | collective-permute-done | bytes 32800 | tf_op jit(solution)/shard_map/ppermute | solution.py:582
  52.2 0.6 collective-permute-done.9.arrived_0
  52.8 0.9 %finish.1 = (bf16[192,256]{1,0:T(8,128)(2,1)S(1)}, bf16[384,128]{1,0:T(8,128)(2,1)}) custom-call(f32[192,256]{1,0:T(8,128)S(1)} %get-tuple-element.32.own, bf16[64,256]{1,0:T(8,128)(2,1)S(1)} %collective-permute-done.9.arrived_0, bf16[64,256]{1,0:T(8,128)(2,1)S(1)} %collective-permute-done.10.arrived_1, ...), custom_call_target="tpu_custom_call" | custom-call | tf_op jit(solution)/shard_map/finish/pallas_call | solution.py:383
  53.7 3.3 %all-to-all-start = ((bf16[4,96,128]{2,1,0:T(8,128)(2,1)}), bf16[4,96,128]{2,1,0:T(8,128)(2,1)S(1)}, u32[]{:S(2)}, u32[]{:S(2)}) async-start(bf16[4,96,128]{2,1,0:T(8,128)(2,1)} %bitcast.1), calls=%async_computation | async-start | bytes 196608 | tf_op jit(solution)/shard_map/all_to_all | solution.py:630
  57.0 7.0 %attend.1 = bf16[1,192,1024]{2,1,0:T(8,128)(2,1)} custom-call(s32[4,16]{1,0:T(4,128)S(1)} %copy-done.2, bf16[1536,256]{1,0:T(8,128)(2,1)S(1)} %get-tuple-element.24.q, bf16[192,256]{1,0:T(8,128)(2,1)S(1)} %get-tuple-element.37.fresh, bf16[2048,128]{1,0:T(8,128)(2,1)S(1)} %get-tuple-element.38.held, bf16[16,2048]{1,0:T(8,128)(2,1)S(1)} %get-tuple-element.39.spare, ...), custom_call_target="tpu_custom_call" | custom-call | tf_op jit(solution)/shard_map/attend/pallas_call | solution.py:517
  64.0 0.7 %store.1 = bf16[4,96,128]{2,1,0:T(8,128)(2,1)} custom-call(bf16[4,96,128]{2,1,0:T(8,128)(2,1)S(1)} %all-to-all-done.rows), custom_call_target="tpu_custom_call" | custom-call | tf_op jit(solution)/shard_map/store/pallas_call | solution.py:551
  (27 shorter events, 0.8 us)
Async XLA Ops:
  0.6 7.3 %copy-start.2 = (s32[4,16]{1,0:T(4,128)S(1)}, s32[4,16]{1,0:T(4,128)}, u32[]{:S(2)}) copy-start(s32[4,16]{1,0:T(4,128)} %request_docs.5) | copy-start | bytes 772
  1.9 21.2 %collective-permute-start.5 = (bf16[2,48,2048]{2,1,0:T(8,128)(2,1)S(1)}, bf16[2,48,2048]{2,1,0:T(8,128)(2,1)S(1)}, u32[]{:S(2)}, u32[]{:S(2)}) collective-permute-start(bf16[2,48,2048]{2,1,0:T(8,128)(2,1)S(1)} %get-tuple-element.31), channel_id=1, source_target_pairs={{0,4},{4,0},{8,12},{12,8},{1,5},{5,1},{9,13},{13,9},{2,6},{6,2},{1... | collective-permute-start | bytes 1179656 | tf_op jit(solution)/shard_map/ppermute | solution.py:582
  5.0 12.0 %collective-permute-start = (bf16[448,128]{1,0:T(8,128)(2,1)S(1)}, bf16[448,128]{1,0:T(8,128)(2,1)S(1)}, u32[]{:S(2)}, u32[]{:S(2)}) collective-permute-start(bf16[448,128]{1,0:T(8,128)(2,1)S(1)} %get-tuple-element.25), channel_id=1, source_target_pairs={{0,8},{4,12},{8,0},{12,4},{1,9},{5,13},{9,1},{13,5},{2,10},{6,14},... | collective-permute-start | bytes 344072 | tf_op jit(solution)/shard_map/ppermute | solution.py:582
  7.5 23.2 %collective-permute-start.1 = (bf16[1600,128]{1,0:T(8,128)(2,1)S(1)}, bf16[1600,128]{1,0:T(8,128)(2,1)S(1)}, u32[]{:S(2)}, u32[]{:S(2)}) collective-permute-start(bf16[1600,128]{1,0:T(8,128)(2,1)S(1)} %get-tuple-element.28), channel_id=1, source_target_pairs={{0,8},{4,12},{8,0},{12,4},{1,9},{5,13},{9,1},{13,5},{2,10},{6,14},... | collective-permute-start | bytes 1228808 | tf_op jit(solution)/shard_map/ppermute | solution.py:582
  10.0 22.3 %collective-permute-start.4 = (bf16[4,2,128,128]{3,2,1,0:T(8,128)(2,1)S(1)}, bf16[4,2,128,128]{3,2,1,0:T(8,128)(2,1)S(1)}, u32[]{:S(2)}, u32[]{:S(2)}) collective-permute-start(bf16[4,2,128,128]{3,2,1,0:T(8,128)(2,1)S(1)} %get-tuple-element.30.refs_1_), channel_id=1, source_target_pairs={{0,4},{4,0},{8,12},{12,8},{1,5},{5,1},{9,13},{13,9},{2,6},{6,2},{1... | collective-permute-start | bytes 786440 | tf_op jit(solution)/shard_map/ppermute | solution.py:582
  17.0 8.1 %collective-permute-start.2 = (bf16[448,128]{1,0:T(8,128)(2,1)S(1)}, bf16[448,128]{1,0:T(8,128)(2,1)S(1)}, u32[]{:S(2)}, u32[]{:S(2)}) collective-permute-start(bf16[448,128]{1,0:T(8,128)(2,1)S(1)} %collective-permute-done.w_far_0), channel_id=1, source_target_pairs={{0,16},{16,0},{1,17},{17,1},{2,18},{18,2},{3,19},{19,3},{4,20},{20... | collective-permute-start | bytes 344072 | tf_op jit(solution)/shard_map/ppermute | solution.py:582
  23.1 11.6 %collective-permute-start.7 = (bf16[2,48,2048]{2,1,0:T(8,128)(2,1)S(1)}, bf16[2,48,2048]{2,1,0:T(8,128)(2,1)S(1)}, u32[]{:S(2)}, u32[]{:S(2)}) collective-permute-start(bf16[2,48,2048]{2,1,0:T(8,128)(2,1)S(1)} %gate.3.rest_0_), channel_id=1, source_target_pairs={{0,2},{1,3},{2,0},{3,1},{4,6},{5,7},{6,4},{7,5},{8,10},{9,11},{10,... | collective-permute-start | bytes 1179656 | tf_op jit(solution)/shard_map/ppermute | solution.py:582
  25.0 11.3 %collective-permute-start.6 = (bf16[2,48,2048]{2,1,0:T(8,128)(2,1)S(1)}, bf16[2,48,2048]{2,1,0:T(8,128)(2,1)S(1)}, u32[]{:S(2)}, u32[]{:S(2)}) collective-permute-start(bf16[2,48,2048]{2,1,0:T(8,128)(2,1)S(1)} %gate.3.rest_0_), channel_id=1, source_target_pairs={{0,1},{1,0},{2,3},{3,2},{4,5},{5,4},{6,7},{7,6},{8,9},{9,8},{10,11... | collective-permute-start | bytes 1179656 | tf_op jit(solution)/shard_map/ppermute | solution.py:582
  30.8 3.9 %copy-start = (bf16[1,192,8192]{2,1,0:T(8,128)(2,1)S(1)}, bf16[1,192,8192]{2,1,0:T(8,128)(2,1)}, u32[]{:S(2)}) copy-start(bf16[1,192,8192]{2,1,0:T(8,128)(2,1)} %hidden.5) | copy-start | bytes 9437188
  30.8 9.9 %collective-permute-start.3 = (bf16[1600,128]{1,0:T(8,128)(2,1)S(1)}, bf16[1600,128]{1,0:T(8,128)(2,1)S(1)}, u32[]{:S(2)}, u32[]{:S(2)}) collective-permute-start(bf16[1600,128]{1,0:T(8,128)(2,1)S(1)} %get-tuple-element.29.w_far_1), channel_id=1, source_target_pairs={{0,16},{16,0},{1,17},{17,1},{2,18},{18,2},{3,19},{19,3},{4,20},{20... | collective-permute-start | bytes 1228808 | tf_op jit(solution)/shard_map/ppermute | solution.py:582
  32.3 24.7 %collective-permute-start.12 = (bf16[4,2,128,128]{3,2,1,0:T(8,128)(2,1)S(1)}, bf16[4,2,128,128]{3,2,1,0:T(8,128)(2,1)S(1)}, u32[]{:S(2)}, u32[]{:S(2)}) collective-permute-start(bf16[4,2,128,128]{3,2,1,0:T(8,128)(2,1)S(1)} %get-tuple-element.43), channel_id=1, source_target_pairs={{0,8},{4,12},{8,0},{12,4},{1,9},{5,13},{9,1},{13,5},{2,10},{6,14},... | collective-permute-start | bytes 786440 | tf_op jit(solution)/shard_map/ppermute | solution.py:582
  32.3 24.7 %collective-permute-start.13 = (bf16[4,2,128,128]{3,2,1,0:T(8,128)(2,1)S(1)}, bf16[4,2,128,128]{3,2,1,0:T(8,128)(2,1)S(1)}, u32[]{:S(2)}, u32[]{:S(2)}) collective-permute-start(bf16[4,2,128,128]{3,2,1,0:T(8,128)(2,1)S(1)} %get-tuple-element.44), channel_id=1, source_target_pairs={{0,12},{4,8},{8,4},{12,0},{1,13},{5,9},{9,5},{13,1},{2,14},{6,10},... | collective-permute-start | bytes 786440 | tf_op jit(solution)/shard_map/ppermute | solution.py:582
  34.7 1.7 %collective-permute-start.8 = (bf16[2,48,2048]{2,1,0:T(8,128)(2,1)S(1)}, bf16[2,48,2048]{2,1,0:T(8,128)(2,1)S(1)}, u32[]{:S(2)}, u32[]{:S(2)}) collective-permute-start(bf16[2,48,2048]{2,1,0:T(8,128)(2,1)S(1)} %collective-permute-done.7.rest_2_), channel_id=1, source_target_pairs={{0,1},{1,0},{2,3},{3,2},{4,5},{5,4},{6,7},{7,6},{8,9},{9,8},{10,11... | collective-permute-start | bytes 1179656 | tf_op jit(solution)/shard_map/ppermute | solution.py:582
  38.1 6.8 %copy-start.1 = (bf16[1,192,1024]{2,1,0:T(8,128)(2,1)S(1)}, bf16[1,192,1024]{2,1,0:T(8,128)(2,1)}, u32[]{:S(2)}) copy-start(bf16[1,192,1024]{2,1,0:T(8,128)(2,1)} %queries.1) | copy-start | bytes 1179652
  38.1 6.8 %copy-start.3 = (s32[1,16,12]{1,0,2:T(1,128)S(1)}, s32[1,16,12]{1,0,2:T(1,128)}, u32[]{:S(2)}) copy-start(s32[1,16,12]{1,0,2:T(1,128)} %param.17) | copy-start | bytes 2308
  38.1 6.8 %copy-start.4 = (s32[32]{0:T(128)S(1)}, s32[32]{0:T(128)}, u32[]{:S(2)}) copy-start(s32[32]{0:T(128)} %doc_lengths.1) | copy-start | bytes 388
  42.7 8.8 %collective-permute-start.10 = (bf16[64,256]{1,0:T(8,128)(2,1)S(1)}, bf16[64,256]{1,0:T(8,128)(2,1)S(1)}, u32[]{:S(2)}, u32[]{:S(2)}) collective-permute-start(bf16[64,256]{1,0:T(8,128)(2,1)S(1)} %get-tuple-element.34), channel_id=1, source_target_pairs={{0,4},{4,0},{8,12},{12,8},{1,5},{5,1},{9,13},{13,9},{2,6},{6,2},{1... | collective-permute-start | bytes 98312 | tf_op jit(solution)/shard_map/ppermute | solution.py:582
  42.8 9.4 %collective-permute-start.11 = (bf16[64,256]{1,0:T(8,128)(2,1)S(1)}, bf16[64,256]{1,0:T(8,128)(2,1)S(1)}, u32[]{:S(2)}, u32[]{:S(2)}) collective-permute-start(bf16[64,256]{1,0:T(8,128)(2,1)S(1)} %get-tuple-element.35), channel_id=1, source_target_pairs={{0,4},{4,0},{8,12},{12,8},{1,5},{5,1},{9,13},{13,9},{2,6},{6,2},{1... | collective-permute-start | bytes 98312 | tf_op jit(solution)/shard_map/ppermute | solution.py:582
  44.8 8.0 %collective-permute-start.9 = (bf16[64,256]{1,0:T(8,128)(2,1)S(1)}, bf16[64,256]{1,0:T(8,128)(2,1)S(1)}, u32[]{:S(2)}, u32[]{:S(2)}) collective-permute-start(bf16[64,256]{1,0:T(8,128)(2,1)S(1)} %get-tuple-element.33), channel_id=1, source_target_pairs={{0,4},{4,0},{8,12},{12,8},{1,5},{5,1},{9,13},{13,9},{2,6},{6,2},{1... | collective-permute-start | bytes 98312 | tf_op jit(solution)/shard_map/ppermute | solution.py:582
  53.7 10.3 %all-to-all-start = ((bf16[4,96,128]{2,1,0:T(8,128)(2,1)}), bf16[4,96,128]{2,1,0:T(8,128)(2,1)S(1)}, u32[]{:S(2)}, u32[]{:S(2)}) async-start(bf16[4,96,128]{2,1,0:T(8,128)(2,1)} %bitcast.1), calls=%async_computation | async-start | bytes 196608 | tf_op jit(solution)/shard_map/all_to_all | solution.py:630
